TPU v7x, 32 devices: a whole 2x2x4 slice. The times are simulated.
32 devices in a mesh: dp: 8 (over z, x), tensor: 4 (over y, core).
Axes of the slice: x: 2, y: 2, z: 4, core: 2. Of those that a mesh axis runs over, the one named last changes fastest.
Arguments:
- inputs: bfloat16 [64, 512, 768], P('dp', 'tensor'), may hold values from -6 to 6
- lengths: int32 [64], P('dp'), may hold values from 51 to 512, as said below
- cotangent: bfloat16 [64, 512, 768], P('dp', 'tensor'), may hold values from -8 to 8
- ln1_gain: float32 [768], replicated, may hold values from 0.5 to 1.5
- ln1_bias: float32 [768], replicated, may hold values from -1.75 to 1.75
- w_qkv: bfloat16 [3, 768, 768], P(None, None, 'tensor'), may hold values from -0.21875 to 0.21875
- b_qv: float32 [2, 768], P(None, 'tensor'), may hold values from -3 to 3
- w_out: bfloat16 [768, 768], P('tensor'), may hold values from -0.875 to 0.875
- b_out: float32 [768], replicated, may hold values from -1.75 to 1.75
- ln2_gain: float32 [768], replicated, may hold values from 0.5 to 1.5
- ln2_bias: float32 [768], replicated, may hold values from -1.75 to 1.75
- w_up: bfloat16 [768, 3072], P(None, 'tensor'), may hold values from -0.21875 to 0.21875
- b_up: float32 [3072], P('tensor'), may hold values from -3 to 3
- w_down: bfloat16 [3072, 768], P('tensor'), may hold values from -0.109375 to 0.109375
- b_down: float32 [768], replicated, may hold values from -1.75 to 1.75
Outputs:
- layer_out: bfloat16 [64, 512, 768], P('dp', 'tensor')
- grad_input: bfloat16 [64, 512, 768], P('dp', 'tensor')
- grad_ln1_gain: float32 [768], replicated
- grad_ln1_bias: float32 [768], replicated
- grad_qkv: float32 [3, 768, 768], P(None, 'dp', 'tensor')
- grad_qv_bias: float32 [2, 768], P(None, 'tensor')
- grad_out_weight: float32 [768, 768], P('tensor', 'dp')
- grad_out_bias: float32 [768], replicated
- grad_ln2_gain: float32 [768], replicated
- grad_ln2_bias: float32 [768], replicated
- grad_up_weight: float32 [768, 3072], P('dp', 'tensor')
- grad_up_bias: float32 [3072], P('tensor')
- grad_down_weight: float32 [3072, 768], P('tensor', 'dp')
- grad_down_bias: float32 [768], replicated
Inputs may be any that keep to these rules, and one draw needn't show every extreme that they name: `lengths`: in each aligned block of 8 texts one text, drawn from the seed, has all 512 molecules.
All inputs are finite; a program needn't handle non-finite values.
Results may differ from a plain program's by a relative error of at most 0.018.
Values may be sent and summed in bfloat16 or wider, within the bound.
No kernel may reach another device: no remote copies, remote signals or barrier semaphores. Data moves between devices by JAX's collectives and lax.ppermute only.
A program may use at most 192 MiB of HBM per device.

v0:
```python
import jax
import jax.numpy as jnp
from jax import lax
from jax.sharding import PartitionSpec as P

D = 768
HD = 64
FF = 3072
MICRO = 4


def norm_rows(values, gain, shift):
    center = values - jnp.mean(values, -1, keepdims=True)
    rstd = lax.rsqrt(jnp.mean(center * center, -1, keepdims=True) + 1e-05)
    normal = center * rstd
    return (normal * gain + shift, normal, rstd)


def norm_back(grad_norm, normal, rstd, gain):
    scaled = grad_norm * gain
    return rstd * (
        scaled
        - jnp.mean(scaled, -1, keepdims=True)
        - normal * jnp.mean(scaled * normal, -1, keepdims=True)
    )


def gelu_exact(values):
    return jax.nn.gelu(values, approximate=False)


def reduce_texts(matrices):
    return (
        lax.psum_scatter(matrices[0], "dp", scatter_dimension=1, tiled=True),
        lax.psum_scatter(matrices[1], "dp", scatter_dimension=1, tiled=True),
        lax.psum_scatter(matrices[2], "dp", scatter_dimension=0, tiled=True),
        lax.psum_scatter(matrices[3], "dp", scatter_dimension=1, tiled=True),
    )


def layer_rows(x_rows, text_lens, cot_rows, row_positions, weights, moves):
    (
        ln1_gain,
        ln1_bias,
        w_qkv,
        b_qv,
        w_out,
        b_out,
        ln2_gain,
        ln2_bias,
        w_up,
        b_up,
        w_down,
        b_down,
    ) = weights
    spread_one, collect_one, spread_two, collect_two, collect_three, spread_three, collect_four = (
        moves
    )
    bf16 = jnp.bfloat16
    f32 = jnp.float32
    texts_step = x_rows.shape[0]
    local_width = w_qkv.shape[2]
    heads_here = local_width // HD
    score_scale = HD ** (-0.5)
    normed, normal_one, rstd_one = norm_rows(x_rows, ln1_gain, ln1_bias)
    normed_full = spread_one(normed.astype(bf16))
    text_len = normed_full.shape[1]
    key_positions = jnp.arange(text_len)
    projected = jnp.einsum("tmd,cde->ctme", normed_full, w_qkv, preferred_element_type=f32)
    head_shape = (texts_step, text_len, heads_here, HD)
    query = (projected[0] + b_qv[0]).astype(bf16).reshape(head_shape)
    keys = projected[1].astype(bf16).reshape(head_shape)
    values = (projected[2] + b_qv[1]).astype(bf16).reshape(head_shape)
    key_live = (key_positions[None, :] < text_lens[:, None])[:, None, None, :]
    scores = jnp.einsum("tqhd,tkhd->thqk", query, keys, preferred_element_type=f32) * score_scale
    scores = jnp.where(key_live, scores, -1e30)
    row_max = jnp.max(scores, -1, keepdims=True)
    shifted = jnp.exp(scores - row_max)
    row_total = jnp.sum(shifted, -1, keepdims=True)
    attn_probs = shifted / row_total
    log_total = row_max + jnp.log(row_total)
    context = jnp.einsum(
        "thqk,tkhd->tqhd", attn_probs.astype(bf16), values, preferred_element_type=f32
    )
    context = context.reshape(texts_step, text_len, local_width).astype(bf16)
    attn_part = jnp.einsum("tmf,fd->tmd", context, w_out, preferred_element_type=f32)
    attn_rows = collect_one(attn_part)
    resid = x_rows + attn_rows + b_out
    normed_two, normal_two, rstd_two = norm_rows(resid, ln2_gain, ln2_bias)
    row_live = (row_positions[None, :] < text_lens[:, None]).astype(f32)[:, :, None]
    grad_output = cot_rows.astype(f32) * row_live
    normed_two_full, grad_full = spread_two((normed_two.astype(bf16), grad_output.astype(bf16)))
    upper = jnp.einsum("tmd,df->tmf", normed_two_full, w_up, preferred_element_type=f32) + b_up
    active, gelu_pullback = jax.vjp(gelu_exact, upper)
    active_low = active.astype(bf16)
    down_part = jnp.einsum("tmf,fd->tmd", active_low, w_down, preferred_element_type=f32)
    down_rows = collect_two(down_part)
    out_rows = (resid + down_rows + b_down).astype(bf16)
    grad_down = jnp.einsum("tmf,tmd->fd", active_low, grad_full, preferred_element_type=f32)
    grad_active = jnp.einsum("tmd,fd->tmf", grad_full, w_down, preferred_element_type=f32)
    (grad_upper,) = gelu_pullback(grad_active)
    bias_up = jnp.sum(grad_upper, (0, 1))
    grad_upper_low = grad_upper.astype(bf16)
    grad_up = jnp.einsum("tmd,tmf->df", normed_two_full, grad_upper_low, preferred_element_type=f32)
    norm_two_part = jnp.einsum("tmf,df->tmd", grad_upper_low, w_up, preferred_element_type=f32)
    grad_norm_two = collect_three(norm_two_part)
    gain_two = jnp.sum(grad_norm_two * normal_two, (0, 1))
    shift_two = jnp.sum(grad_norm_two, (0, 1))
    grad_resid = grad_output + norm_back(grad_norm_two, normal_two, rstd_two, ln2_gain)
    bias_attn = jnp.sum(grad_resid, (0, 1))
    bias_down = jnp.sum(grad_output, (0, 1))
    grad_resid_full = spread_three(grad_resid.astype(bf16))
    grad_out = jnp.einsum("tmf,tmd->fd", context, grad_resid_full, preferred_element_type=f32)
    grad_context = jnp.einsum("tmd,fd->tmf", grad_resid_full, w_out, preferred_element_type=f32)
    grad_context = grad_context.astype(bf16).reshape(head_shape)
    again = jnp.einsum("tqhd,tkhd->thqk", query, keys, preferred_element_type=f32) * score_scale
    again = jnp.where(key_live, again, -1e30)
    probs_again = jnp.exp(again - log_total)
    grad_probs = jnp.einsum("tqhd,tkhd->thqk", grad_context, values, preferred_element_type=f32)
    inner_sum = jnp.sum(probs_again * grad_probs, -1, keepdims=True)
    grad_scores = (probs_again * (grad_probs - inner_sum)).astype(bf16)
    grad_query = (
        jnp.einsum("thqk,tkhd->tqhd", grad_scores, keys, preferred_element_type=f32) * score_scale
    )
    grad_keys = (
        jnp.einsum("thqk,tqhd->tkhd", grad_scores, query, preferred_element_type=f32) * score_scale
    )
    grad_values = jnp.einsum(
        "thqk,tqhd->tkhd", probs_again.astype(bf16), grad_context, preferred_element_type=f32
    )
    flat_shape = (texts_step, text_len, local_width)
    grad_proj = jnp.stack(
        [
            grad_query.astype(bf16).reshape(flat_shape),
            grad_keys.astype(bf16).reshape(flat_shape),
            grad_values.astype(bf16).reshape(flat_shape),
        ]
    )
    bias_qv = jnp.stack(
        [jnp.sum(grad_proj[0].astype(f32), (0, 1)), jnp.sum(grad_proj[2].astype(f32), (0, 1))]
    )
    grad_qkv = jnp.einsum("tmd,ctme->cde", normed_full, grad_proj, preferred_element_type=f32)
    norm_one_part = jnp.einsum("ctme,cde->tmd", grad_proj, w_qkv, preferred_element_type=f32)
    grad_norm_one = collect_four(norm_one_part)
    gain_one = jnp.sum(grad_norm_one * normal_one, (0, 1))
    shift_one = jnp.sum(grad_norm_one, (0, 1))
    grad_in = (grad_resid + norm_back(grad_norm_one, normal_one, rstd_one, ln1_gain)).astype(bf16)
    shared = (gain_one, shift_one, gain_two, shift_two, bias_attn, bias_down)
    return (out_rows, grad_in, (grad_qkv, grad_out, grad_up, grad_down), (bias_qv, bias_up), shared)


def on_device(
    inputs,
    lengths,
    cotangent,
    ln1_gain,
    ln1_bias,
    w_qkv,
    b_qv,
    w_out,
    b_out,
    ln2_gain,
    ln2_bias,
    w_up,
    b_up,
    w_down,
    b_down,
):
    f32 = jnp.float32
    tensor_index = lax.axis_index("tensor")

    def spread_one(values):
        return lax.all_gather(values, "tensor", axis=1, tiled=True)

    def collect_one(values):
        return lax.psum_scatter(
            values.astype(jnp.bfloat16), "tensor", scatter_dimension=1, tiled=True
        ).astype(jnp.float32)

    def spread_two(pair):
        return (
            lax.all_gather(pair[0], "tensor", axis=1, tiled=True),
            lax.all_gather(pair[1], "tensor", axis=1, tiled=True),
        )

    def collect_two(values):
        return lax.psum_scatter(
            values.astype(jnp.bfloat16), "tensor", scatter_dimension=1, tiled=True
        ).astype(jnp.float32)

    def collect_three(values):
        return lax.psum_scatter(
            values.astype(jnp.bfloat16), "tensor", scatter_dimension=1, tiled=True
        ).astype(jnp.float32)

    def spread_three(values):
        return lax.all_gather(values, "tensor", axis=1, tiled=True)

    def collect_four(values):
        return lax.psum_scatter(
            values.astype(jnp.bfloat16), "tensor", scatter_dimension=1, tiled=True
        ).astype(jnp.float32)

    moves = (
        spread_one,
        collect_one,
        spread_two,
        collect_two,
        collect_three,
        spread_three,
        collect_four,
    )
    weights = (
        ln1_gain,
        ln1_bias,
        w_qkv,
        b_qv,
        w_out,
        b_out,
        ln2_gain,
        ln2_bias,
        w_up,
        b_up,
        w_down,
        b_down,
    )
    x_all, cot_all, lens_all = (inputs, cotangent, lengths)
    groups = MICRO
    texts_step = inputs.shape[0] // MICRO
    row_positions = tensor_index * inputs.shape[1] + jnp.arange(inputs.shape[1])
    outputs = []
    grad_rows = []
    summed = None
    biases = None
    shared = None
    for group in range(groups):
        lower = group * texts_step
        out_rows, grad_in, matrices, bias_terms, shared_terms = layer_rows(
            x_all[lower : lower + texts_step].astype(f32),
            lens_all[lower : lower + texts_step],
            cot_all[lower : lower + texts_step],
            row_positions,
            weights,
            moves,
        )
        outputs.append(out_rows)
        grad_rows.append(grad_in)
        if summed is None:
            summed, biases, shared = (matrices, bias_terms, shared_terms)
        else:
            summed = tuple((left + right for left, right in zip(summed, matrices)))
            biases = tuple((left + right for left, right in zip(biases, bias_terms)))
            shared = tuple((left + right for left, right in zip(shared, shared_terms)))
    summed = reduce_texts(summed)
    layer_out = jnp.concatenate(outputs, 0)
    grad_input = jnp.concatenate(grad_rows, 0)
    local_qv = b_qv.shape[1]
    local_up = b_up.shape[0]
    bias_qv, bias_up = biases
    bias_qv = lax.dynamic_update_slice_in_dim(
        jnp.zeros((2, D), f32), bias_qv, tensor_index * local_qv, 1
    )
    bias_up = lax.dynamic_update_slice_in_dim(
        jnp.zeros((FF,), f32), bias_up, tensor_index * local_up, 0
    )
    gain_one, shift_one, gain_two, shift_two, bias_attn, bias_down, total_qv, total_up = lax.psum(
        (shared[0], shared[1], shared[2], shared[3], shared[4], shared[5], bias_qv, bias_up),
        ("dp", "tensor"),
    )
    grad_qv_bias = lax.dynamic_slice_in_dim(total_qv, tensor_index * local_qv, local_qv, 1)
    grad_up_bias = lax.dynamic_slice_in_dim(total_up, tensor_index * local_up, local_up, 0)
    return (
        layer_out,
        grad_input,
        gain_one,
        shift_one,
        summed[0],
        grad_qv_bias,
        summed[1],
        bias_attn,
        gain_two,
        shift_two,
        summed[2],
        grad_up_bias,
        summed[3],
        bias_down,
    )


def solution(mesh):
    return jax.shard_map(
        on_device,
        mesh=mesh,
        in_specs=(
            P("dp", "tensor", None),
            P("dp"),
            P("dp", "tensor", None),
            P(),
            P(),
            P(None, None, "tensor"),
            P(None, "tensor"),
            P("tensor", None),
            P(),
            P(),
            P(),
            P(None, "tensor"),
            P("tensor"),
            P("tensor", None),
            P(),
        ),
        out_specs=(
            P("dp", "tensor", None),
            P("dp", "tensor", None),
            P(),
            P(),
            P(None, "dp", "tensor"),
            P(None, "tensor"),
            P("tensor", "dp"),
            P(),
            P(),
            P(),
            P("dp", "tensor"),
            P("tensor"),
            P("tensor", "dp"),
            P(),
        ),
        check_vma=False,
    )
```

profile of v0, /device:TPU:0, one launch (start us, length us, event | category | flops | bytes accessed | tf_op | source)
XLA Modules:
  0.0 1178.2 jit_solution(9756855672257540588)
XLA Ops:
  14.6 20.8 %all-gather.25.cloned.1.call-done = bf16[2,512,768]{2,1,0:T(8,128)(2,1)} async-done(((bf16[2,128,768]{2,1,0:T(8,128)(2,1)}), bf16[2,512,768]{2,1,0:T(8,128)(2,1)}) %all-gather.25.cloned.1.call-update) | async-done | bytes 1572880 | tf_op jit(solution)/shard_map/all_gather | solution.py:173
  46.4 10.2 all-gather.17.cloned.1.call-done
  67.8 20.2 %reduce-scatter.33.cloned.1.call-done = bf16[2,128,768]{2,1,0:T(8,128)(2,1)} async-done(((bf16[2,512,768]{2,1,0:T(8,128)(2,1)}), bf16[2,128,768]{2,1,0:T(8,128)(2,1)}) %reduce-scatter.33.cloned.1.call-update) | async-done | bytes 393232 | tf_op jit(solution)/shard_map/reduce_scatter | solution.py:176
  88.0 31.3 %reduce-scatter.25.cloned.1.call-done = bf16[2,128,768]{2,1,0:T(8,128)(2,1)} async-done(((bf16[2,512,768]{2,1,0:T(8,128)(2,1)}), bf16[2,128,768]{2,1,0:T(8,128)(2,1)}) %reduce-scatter.25.cloned.1.call-update) | async-done | bytes 393232 | tf_op jit(solution)/shard_map/reduce_scatter | solution.py:176
  122.6 19.8 %all-gather.21.cloned.1.call-done = bf16[2,512,768]{2,1,0:T(8,128)(2,1)} async-done(((bf16[2,128,768]{2,1,0:T(8,128)(2,1)}), bf16[2,512,768]{2,1,0:T(8,128)(2,1)}) %all-gather.21.cloned.1.call-update) | async-done | bytes 1572880 | tf_op jit(solution)/shard_map/all_gather | solution.py:173
  157.2 24.5 %reduce-scatter.29.cloned.1.call-done = bf16[2,128,768]{2,1,0:T(8,128)(2,1)} async-done(((bf16[2,512,768]{2,1,0:T(8,128)(2,1)}), bf16[2,128,768]{2,1,0:T(8,128)(2,1)}) %reduce-scatter.29.cloned.1.call-update) | async-done | bytes 393232 | tf_op jit(solution)/shard_map/reduce_scatter | solution.py:176
  193.3 13.1 %all-gather.29.cloned.1.call-done = bf16[2,512,768]{2,1,0:T(8,128)(2,1)} async-done(((bf16[2,128,768]{2,1,0:T(8,128)(2,1)}), bf16[2,512,768]{2,1,0:T(8,128)(2,1)}) %all-gather.29.cloned.1.call-update) | async-done | bytes 1572880 | tf_op jit(solution)/shard_map/all_gather | solution.py:173
  232.8 17.5 %all-gather.19.cloned.1.call-done = bf16[2,512,768]{2,1,0:T(8,128)(2,1)} async-done(((bf16[2,128,768]{2,1,0:T(8,128)(2,1)}), bf16[2,512,768]{2,1,0:T(8,128)(2,1)}) %all-gather.19.cloned.1.call-update) | async-done | bytes 1572880 | tf_op jit(solution)/shard_map/all_gather | solution.py:182
  257.7 15.8 %multiply_convert_fusion.7 = (bf16[2,512,768]{2,1,0:T(8,128)(2,1)}, f32[2,512,768]{2,1,0:T(8,128)}, bf16[2,512,768]{2,1,0:T(8,128)(2,1)}, f32[2,512,768]{2,1,0:T(8,128)}) fusion(f32[2,512,768]{2,1,0:T(8,128)S(1)} %get-tuple-element.185, f32[768]{0:T(1024)S(1)} %copy-done.125, u8[512,768]{1,0:T(8,128)(4,1)S(1)} %get-tuple-element.43, ...), kind=kLoop, calls=%fused_computation.112 | loop fusion | flops 110886912 | bytes 17304576 | tf_op jit(solution)/shard_map/convert_element_type | solution.py:95
  308.8 14.7 %reduce-scatter.37.cloned.1.call-done = bf16[2,128,768]{2,1,0:T(8,128)(2,1)} async-done(((bf16[2,512,768]{2,1,0:T(8,128)(2,1)}), bf16[2,128,768]{2,1,0:T(8,128)(2,1)}) %reduce-scatter.37.cloned.1.call-update) | async-done | bytes 393232 | tf_op jit(solution)/shard_map/reduce_scatter | solution.py:176
  323.5 30.7 %reduce-scatter.49.cloned.1.call-done = bf16[2,128,768]{2,1,0:T(8,128)(2,1)} async-done(((bf16[2,512,768]{2,1,0:T(8,128)(2,1)}), bf16[2,128,768]{2,1,0:T(8,128)(2,1)}) %reduce-scatter.49.cloned.1.call-update) | async-done | bytes 393232 | tf_op jit(solution)/shard_map/reduce_scatter | solution.py:192
  354.2 30.8 %reduce-scatter.41.cloned.1.call-done = bf16[2,128,768]{2,1,0:T(8,128)(2,1)} async-done(((bf16[2,512,768]{2,1,0:T(8,128)(2,1)}), bf16[2,128,768]{2,1,0:T(8,128)(2,1)}) %reduce-scatter.41.cloned.1.call-update) | async-done | bytes 393232 | tf_op jit(solution)/shard_map/reduce_scatter | solution.py:192
  388.2 27.3 %reduce-scatter.35.cloned.1.call-done = bf16[2,128,768]{2,1,0:T(8,128)(2,1)} async-done(((bf16[2,512,768]{2,1,0:T(8,128)(2,1)}), bf16[2,128,768]{2,1,0:T(8,128)(2,1)}) %reduce-scatter.35.cloned.1.call-update) | async-done | bytes 393232 | tf_op jit(solution)/shard_map/reduce_scatter | solution.py:187
  420.8 19.5 %all-gather.43.cloned.1.call-done = bf16[2,512,768]{2,1,0:T(8,128)(2,1)} async-done(((bf16[2,128,768]{2,1,0:T(8,128)(2,1)}), bf16[2,512,768]{2,1,0:T(8,128)(2,1)}) %all-gather.43.cloned.1.call-update) | async-done | bytes 1572880 | tf_op jit(solution)/shard_map/all_gather | solution.py:197
  463.7 25.9 %reduce-scatter.51.cloned.1.call-done = bf16[2,128,768]{2,1,0:T(8,128)(2,1)} async-done(((bf16[2,512,768]{2,1,0:T(8,128)(2,1)}), bf16[2,128,768]{2,1,0:T(8,128)(2,1)}) %reduce-scatter.51.cloned.1.call-update) | async-done | bytes 393232 | tf_op jit(solution)/shard_map/reduce_scatter | solution.py:200
  501.2 13.1 %all-gather.31.cloned.1.call-done = bf16[2,512,768]{2,1,0:T(8,128)(2,1)} async-done(((bf16[2,128,768]{2,1,0:T(8,128)(2,1)}), bf16[2,512,768]{2,1,0:T(8,128)(2,1)}) %all-gather.31.cloned.1.call-update) | async-done | bytes 1572880 | tf_op jit(solution)/shard_map/all_gather | solution.py:182
  518.7 16.8 %all-gather.23.cloned.1.call-done = bf16[2,512,768]{2,1,0:T(8,128)(2,1)} async-done(((bf16[2,128,768]{2,1,0:T(8,128)(2,1)}), bf16[2,512,768]{2,1,0:T(8,128)(2,1)}) %all-gather.23.cloned.1.call-update) | async-done | bytes 1572880 | tf_op jit(solution)/shard_map/all_gather | solution.py:182
  542.9 15.9 %multiply_convert_fusion.6 = (bf16[2,512,768]{2,1,0:T(8,128)(2,1)}, f32[2,512,768]{2,1,0:T(8,128)}, bf16[2,512,768]{2,1,0:T(8,128)(2,1)}, f32[2,512,768]{2,1,0:T(8,128)}) fusion(f32[2,512,768]{2,1,0:T(8,128)S(1)} %get-tuple-element.190, f32[768]{0:T(1024)S(1)} %copy-done.127, u8[512,768]{1,0:T(8,128)(4,1)S(1)} %get-tuple-element.45, ...), kind=kLoop, calls=%fused_computation.99 | loop fusion | flops 110886912 | bytes 17304576 | tf_op jit(solution)/shard_map/convert_element_type | solution.py:95
  598.3 10.3 reduce-scatter.27.cloned.1.call-done
  612.7 26.9 %reduce-scatter.45.cloned.1.call-done = bf16[2,128,768]{2,1,0:T(8,128)(2,1)} async-done(((bf16[2,512,768]{2,1,0:T(8,128)(2,1)}), bf16[2,128,768]{2,1,0:T(8,128)(2,1)}) %reduce-scatter.45.cloned.1.call-update) | async-done | bytes 393232 | tf_op jit(solution)/shard_map/reduce_scatter | solution.py:192
  639.5 30.6 %reduce-scatter.53.cloned.1.call-done = bf16[2,128,768]{2,1,0:T(8,128)(2,1)} async-done(((bf16[2,512,768]{2,1,0:T(8,128)(2,1)}), bf16[2,128,768]{2,1,0:T(8,128)(2,1)}) %reduce-scatter.53.cloned.1.call-update) | async-done | bytes 393232 | tf_op jit(solution)/shard_map/reduce_scatter | solution.py:192
  672.8 28.2 %reduce-scatter.39.cloned.1.call-done = bf16[2,128,768]{2,1,0:T(8,128)(2,1)} async-done(((bf16[2,512,768]{2,1,0:T(8,128)(2,1)}), bf16[2,128,768]{2,1,0:T(8,128)(2,1)}) %reduce-scatter.39.cloned.1.call-update) | async-done | bytes 393232 | tf_op jit(solution)/shard_map/reduce_scatter | solution.py:187
  705.9 25.7 %reduce-scatter.31.cloned.1.call-done = bf16[2,128,768]{2,1,0:T(8,128)(2,1)} async-done(((bf16[2,512,768]{2,1,0:T(8,128)(2,1)}), bf16[2,128,768]{2,1,0:T(8,128)(2,1)}) %reduce-scatter.31.cloned.1.call-update) | async-done | bytes 393232 | tf_op jit(solution)/shard_map/reduce_scatter | solution.py:187
  738.7 14.1 %all-gather.35.cloned.1.call-done = bf16[2,512,768]{2,1,0:T(8,128)(2,1)} async-done(((bf16[2,128,768]{2,1,0:T(8,128)(2,1)}), bf16[2,512,768]{2,1,0:T(8,128)(2,1)}) %all-gather.35.cloned.1.call-update) | async-done | bytes 1572880 | tf_op jit(solution)/shard_map/all_gather | solution.py:197
  763.2 10.9 all-gather.47.cloned.1.call-done
  777.0 18.5 %all-gather.39.cloned.1.call-done = bf16[2,512,768]{2,1,0:T(8,128)(2,1)} async-done(((bf16[2,128,768]{2,1,0:T(8,128)(2,1)}), bf16[2,512,768]{2,1,0:T(8,128)(2,1)}) %all-gather.39.cloned.1.call-update) | async-done | bytes 1572880 | tf_op jit(solution)/shard_map/all_gather | solution.py:197
  865.3 12.1 %reduce-scatter.57.cloned.1.call-start = ((), (), s32[]{:S(2)}) async-start(), calls=%async_computation.52 | async-start | bytes 2654208 | tf_op jit(solution)/shard_map/reduce_scatter | solution.py:36
  925.6 30.6 %reduce-scatter.47.cloned.1.call-done = bf16[2,128,768]{2,1,0:T(8,128)(2,1)} async-done(((bf16[2,512,768]{2,1,0:T(8,128)(2,1)}), bf16[2,128,768]{2,1,0:T(8,128)(2,1)}) %reduce-scatter.47.cloned.1.call-update) | async-done | bytes 393232 | tf_op jit(solution)/shard_map/reduce_scatter | solution.py:200
  960.0 41.4 %all-reduce = (f32[768]{0:T(1024)}, f32[768]{0:T(1024)}, f32[2,768]{1,0:T(2,128)S(1)}, f32[768]{0:T(1024)}, f32[768]{0:T(1024)}, /*index=5*/f32[768]{0:T(1024)}, f32[3072]{0:T(1024)S(1)}, f32[768]{0:T(1024)}) all-reduce(f32[768]{0:T(1024)S(1)} %add_add_fusion.5, ...), channel_id=1, replica_groups=mesh['dp'=8,'tensor'=4] {'dp','tensor'}, use_global_device_ids=true, to_apply=%region_64.65 | all-reduce | flops 9216 | bytes 73728 | tf_op jit(solution)/shard_map/psum | solution.py:266
  1007.9 19.4 %reduce-scatter.61.cloned.1.call-done = f32[96,576]{1,0:T(8,128)} async-done(((f32[768,576]{1,0:T(8,128)}), f32[96,576]{1,0:T(8,128)}) %reduce-scatter.61.cloned.1.call-update) | async-done | bytes 221200
  1029.2 70.3 %reduce-scatter.57.cloned.1.call-done = f32[96,768]{1,0:T(8,128)} async-done(((f32[768,768]{1,0:T(8,128)}), f32[96,768]{1,0:T(8,128)}) %reduce-scatter.57.cloned.1.call-update) | async-done | bytes 294928 | tf_op jit(solution)/shard_map/reduce_scatter | solution.py:36
  1099.6 71.9 %reduce-scatter.59.cloned.1.call-done = f32[768,96]{0,1:T(8,128)} async-done(((f32[768,768]{0,1:T(8,128)}), f32[768,96]{0,1:T(8,128)}) %reduce-scatter.59.cloned.1.call-update) | async-done | bytes 294928 | tf_op jit(solution)/shard_map/reduce_scatter | solution.py:37
  (614 shorter events, 382.8 us)
Async XLA Ops:
  13.6 74.4 %reduce-scatter.33.cloned.1.call-start = ((), (), s32[]{:S(2)}) async-start(), calls=%async_computation.29 | async-start | bytes 1966080 | tf_op jit(solution)/shard_map/reduce_scatter | solution.py:176
  46.3 73.0 %reduce-scatter.25.cloned.1.call-start = ((), (), s32[]{:S(2)}) async-start(), calls=%async_computation.21 | async-start | bytes 1966080 | tf_op jit(solution)/shard_map/reduce_scatter | solution.py:176
  67.5 74.9 %all-gather.21.cloned.1.call-start = ((), (), s32[]{:S(2)}) async-start(), calls=%async_computation.24 | async-start | bytes 1966080 | tf_op jit(solution)/shard_map/all_gather | solution.py:173
  122.5 59.2 %reduce-scatter.29.cloned.1.call-start = ((), (), s32[]{:S(2)}) async-start(), calls=%async_computation.25 | async-start | bytes 1966080 | tf_op jit(solution)/shard_map/reduce_scatter | solution.py:176
  153.4 53.0 %all-gather.29.cloned.1.call-start = ((), (), s32[]{:S(2)}) async-start(), calls=%async_computation.32 | async-start | bytes 1966080 | tf_op jit(solution)/shard_map/all_gather | solution.py:173
  187.4 62.9 %all-gather.19.cloned.1.call-start = ((), (), s32[]{:S(2)}) async-start(), calls=%async_computation.22 | async-start | bytes 1966080 | tf_op jit(solution)/shard_map/all_gather | solution.py:182
  188.1 85.3 %all-gather.41.cloned.1.call-start = ((), (), s32[]{:S(2)}) async-start(), calls=%async_computation.44 | async-start | bytes 1966080 | tf_op jit(solution)/shard_map/all_gather | solution.py:183
  192.5 100.2 %all-gather.33.cloned.1.call-start = ((), (), s32[]{:S(2)}) async-start(), calls=%async_computation.36 | async-start | bytes 1966080 | tf_op jit(solution)/shard_map/all_gather | solution.py:183
  193.3 130.2 %reduce-scatter.37.cloned.1.call-start = ((), (), s32[]{:S(2)}) async-start(), calls=%async_computation.33 | async-start | bytes 1966080 | tf_op jit(solution)/shard_map/reduce_scatter | solution.py:176
  218.0 136.2 %reduce-scatter.49.cloned.1.call-start = ((), (), s32[]{:S(2)}) async-start(), calls=%async_computation.45 | async-start | bytes 1966080 | tf_op jit(solution)/shard_map/reduce_scatter | solution.py:192
  283.7 101.3 %reduce-scatter.41.cloned.1.call-start = ((), (), s32[]{:S(2)}) async-start(), calls=%async_computation.37 | async-start | bytes 1966080 | tf_op jit(solution)/shard_map/reduce_scatter | solution.py:192
  303.0 112.6 %reduce-scatter.35.cloned.1.call-start = ((), (), s32[]{:S(2)}) async-start(), calls=%async_computation.31 | async-start | bytes 1966080 | tf_op jit(solution)/shard_map/reduce_scatter | solution.py:187
  307.5 132.8 %all-gather.43.cloned.1.call-start = ((), (), s32[]{:S(2)}) async-start(), calls=%async_computation.46 | async-start | bytes 1966080 | tf_op jit(solution)/shard_map/all_gather | solution.py:197
  420.5 69.0 %reduce-scatter.51.cloned.1.call-start = ((), (), s32[]{:S(2)}) async-start(), calls=%async_computation.47 | async-start | bytes 1966080 | tf_op jit(solution)/shard_map/reduce_scatter | solution.py:200
  461.3 53.0 %all-gather.31.cloned.1.call-start = ((), (), s32[]{:S(2)}) async-start(), calls=%async_computation.34 | async-start | bytes 1966080 | tf_op jit(solution)/shard_map/all_gather | solution.py:182
  495.2 63.6 %all-gather.37.cloned.1.call-start = ((), (), s32[]{:S(2)}) async-start(), calls=%async_computation.40 | async-start | bytes 1966080 | tf_op jit(solution)/shard_map/all_gather | solution.py:183
  495.8 82.1 %all-gather.45.cloned.1.call-start = ((), (), s32[]{:S(2)}) async-start(), calls=%async_computation.48 | async-start | bytes 1966080 | tf_op jit(solution)/shard_map/all_gather | solution.py:183
  496.5 112.1 %reduce-scatter.27.cloned.1.call-start = ((), (), s32[]{:S(2)}) async-start(), calls=%async_computation.23 | async-start | bytes 1966080 | tf_op jit(solution)/shard_map/reduce_scatter | solution.py:187
  500.9 138.6 %reduce-scatter.45.cloned.1.call-start = ((), (), s32[]{:S(2)}) async-start(), calls=%async_computation.41 | async-start | bytes 1966080 | tf_op jit(solution)/shard_map/reduce_scatter | solution.py:192
  569.0 101.1 %reduce-scatter.53.cloned.1.call-start = ((), (), s32[]{:S(2)}) async-start(), calls=%async_computation.49 | async-start | bytes 1966080 | tf_op jit(solution)/shard_map/reduce_scatter | solution.py:192
  588.2 112.8 %reduce-scatter.39.cloned.1.call-start = ((), (), s32[]{:S(2)}) async-start(), calls=%async_computation.35 | async-start | bytes 1966080 | tf_op jit(solution)/shard_map/reduce_scatter | solution.py:187
  592.6 139.0 %reduce-scatter.31.cloned.1.call-start = ((), (), s32[]{:S(2)}) async-start(), calls=%async_computation.27 | async-start | bytes 1966080 | tf_op jit(solution)/shard_map/reduce_scatter | solution.py:187
  597.1 155.7 %all-gather.35.cloned.1.call-start = ((), (), s32[]{:S(2)}) async-start(), calls=%async_computation.38 | async-start | bytes 1966080 | tf_op jit(solution)/shard_map/all_gather | solution.py:197
  612.6 161.5 %all-gather.47.cloned.1.call-start = ((), (), s32[]{:S(2)}) async-start(), calls=%async_computation.50 | async-start | bytes 1966080 | tf_op jit(solution)/shard_map/all_gather | solution.py:197
  705.8 89.6 %all-gather.39.cloned.1.call-start = ((), (), s32[]{:S(2)}) async-start(), calls=%async_computation.42 | async-start | bytes 1966080 | tf_op jit(solution)/shard_map/all_gather | solution.py:197
  735.6 181.2 %reduce-scatter.63.cloned.1.call-start = ((), (), s32[]{:S(2)}) async-start(), calls=%async_computation.55 | async-start | bytes 884736
  802.3 116.1 %reduce-scatter.43.cloned.1.call-start = ((), (), s32[]{:S(2)}) async-start(), calls=%async_computation.39 | async-start | bytes 1966080 | tf_op jit(solution)/shard_map/reduce_scatter | solution.py:200
  815.0 110.6 %reduce-scatter.55.cloned.1.call-start = ((), (), s32[]{:S(2)}) async-start(), calls=%async_computation.51 | async-start | bytes 1966080 | tf_op jit(solution)/shard_map/reduce_scatter | solution.py:200
  831.8 124.4 %reduce-scatter.47.cloned.1.call-start = ((), (), s32[]{:S(2)}) async-start(), calls=%async_computation.43 | async-start | bytes 1966080 | tf_op jit(solution)/shard_map/reduce_scatter | solution.py:200
  847.8 179.5 %reduce-scatter.61.cloned.1.call-start = ((), (), s32[]{:S(2)}) async-start(), calls=%async_computation.54 | async-start | bytes 2211840
  865.3 234.2 %reduce-scatter.57.cloned.1.call-start = ((), (), s32[]{:S(2)}) async-start(), calls=%async_computation.52 | async-start | bytes 2654208 | tf_op jit(solution)/shard_map/reduce_scatter | solution.py:36
  887.9 283.6 %reduce-scatter.59.cloned.1.call-start = ((), (), s32[]{:S(2)}) async-start(), calls=%async_computation.53 | async-start | bytes 2654208 | tf_op jit(solution)/shard_map/reduce_scatter | solution.py:37
  (178 other events, 2531.6 us)
Sparse Core Ops, SparseCore 0:
  13.0 22.3 all-gather.24
  37.0 19.6 all-gather.16
  59.8 28.1 reduce-scatter.32
  91.1 28.1 reduce-scatter.24
  122.6 19.6 all-gather.20
  153.6 28.1 reduce-scatter.28
  208.6 19.6 all-gather.26
  251.7 19.6 all-gather.40
  295.3 28.1 reduce-scatter.36
  326.1 28.1 reduce-scatter.48
  356.8 28.1 reduce-scatter.40
  387.4 28.1 reduce-scatter.34
  420.7 19.6 all-gather.42
  461.4 28.1 reduce-scatter.50
  494.6 19.6 all-gather.30
  515.8 19.6 all-gather.22
  536.9 19.6 all-gather.36
  558.2 19.6 all-gather.44
  580.4 28.1 reduce-scatter.26
  611.3 28.1 reduce-scatter.44
  641.9 28.1 reduce-scatter.52
  672.8 28.1 reduce-scatter.38
  703.4 28.1 reduce-scatter.30
  733.1 19.6 all-gather.34
  775.8 19.6 all-gather.38
  802.4 62.4 reduce-scatter.62
  867.4 27.1 reduce-scatter.42
  897.4 28.1 reduce-scatter.54
  928.0 28.1 reduce-scatter.46
  960.1 67.1 reduce-scatter.60
  1031.4 68.1 reduce-scatter.56
  1103.5 67.9 reduce-scatter.58
  (4 shorter events, 78.4 us)
where the time goes:
time: 1190 us; the launch traced here: 1180 us
  waiting for transfers between devices  733 us (62%)
  matrix products  202 us (17%)
  other arithmetic  116 us (10%)
  local copies, waits for them, and re-layouts  53 us (4%)
  blocking collectives  41.4 us (3%)
  between operations  16.6 us (1%)
  starting transfers between devices  16 us (1%)
    reduce_scatter x4, waiting for transfers between devices, collect_three(): lax.psum_scatter(values.astype(jnp.bfloat16), 'tensor', scatter_dimension...  119 us
    reduce_scatter x4, waiting for transfers between devices, collect_two(): lax.psum_scatter(values.astype(jnp.bfloat16), 'tensor', scatter_dimension...  91.5 us
    reduce_scatter x4, waiting for transfers between devices, collect_one(): lax.psum_scatter(values.astype(jnp.bfloat16), 'tensor', scatter_dimension...  90.8 us
    reduce_scatter x1, waiting for transfers between devices, reduce_texts(): lax.psum_scatter(matrices[3], 'dp', scatter_dimension=1, tiled=True)  71.9 us
    reduce_scatter x1, waiting for transfers between devices, reduce_texts(): lax.psum_scatter(matrices[2], 'dp', scatter_dimension=0, tiled=True)  70.3 us
    all_gather x4, waiting for transfers between devices, spread_one(): return lax.all_gather(values, 'tensor', axis=1, tiled=True)  63.9 us
    reduce_scatter x4, waiting for transfers between devices, collect_four(): lax.psum_scatter(values.astype(jnp.bfloat16), 'tensor', scatter_dimension...  63.7 us
    all_gather x4, waiting for transfers between devices, spread_three(): return lax.all_gather(values, 'tensor', axis=1, tiled=True)  63.1 us
  transfers between devices with their start and end apart: 36, of which 32 were waited for; matrix products, arithmetic and copies ran while one was open for 24% of the time, Pallas kernels for 0%

commit v1 on v0

v1 whole, which is shorter than its diff:
```python
import functools

import jax
import jax.numpy as jnp
from jax import lax
from jax.experimental import pallas as pl
from jax.experimental.pallas import tpu as pltpu
from jax.sharding import PartitionSpec as P

D = 768
HD = 64
BF = jnp.bfloat16
F32 = jnp.float32
SCALE = HD**-0.5
LOG2E = 1.4426950408889634


def dot(left, right, left_dim, right_dim):
    return lax.dot_general(
        left, right, (((left_dim,), (right_dim,)), ((), ())), preferred_element_type=F32
    )


def attend_body(lens, q_ref, k_ref, v_ref, ctx_ref, p_ref, inv_ref, *, step):
    n = lens[pl.program_id(0)]
    length = q_ref.shape[0]

    def rows(live):
        edge = lax.broadcasted_iota(jnp.int32, (step, length), 0) < n - (live - step)
        for head in range(2):
            cols = slice(head * HD, head * HD + HD)
            keys = k_ref[:live, cols]
            values = v_ref[:live, cols]
            scores = dot(keys, q_ref[:, cols], 1, 1)
            last = jnp.where(edge, scores[live - step :], -1e30)
            if live > step:
                scores = jnp.concatenate([scores[: live - step], last], 0)
            else:
                scores = last
            top = jnp.max(scores, 0, keepdims=True)
            power = jnp.exp2((scores - top) * (SCALE * LOG2E))
            inverse = 1.0 / jnp.sum(power, 0, keepdims=True)
            low = power.astype(BF)
            p_ref[0, 0, head, :live, :] = low
            inv_ref[0, 0, head : head + 1, :] = inverse
            mixed = dot(low, values, 0, 0)
            ctx_ref[:, cols] = (mixed * inverse.reshape(length, 1)).astype(BF)

    for live in range(step, length + 1, step):
        pl.when((n > live - step) & (n <= live))(functools.partial(rows, live))


def attend_back_body(
    lens, q_ref, k_ref, v_ref, do_ref, p_ref, inv_ref, dq_ref, dk_ref, dv_ref, *, step
):
    n = lens[pl.program_id(0)]
    length = q_ref.shape[0]

    def rows(live):
        for head in range(2):
            cols = slice(head * HD, head * HD + HD)
            queries = q_ref[:live, cols]
            keys = k_ref[:live, cols]
            inverse = inv_ref[0, 0, head : head + 1, :live]
            grad = (do_ref[:live, cols].astype(F32) * inverse.reshape(live, 1)).astype(BF)
            low = p_ref[0, 0, head, :live, :live]
            grad_probs = dot(v_ref[:live, cols], grad, 1, 1)
            power = low.astype(F32)
            product = power * grad_probs
            inner = jnp.sum(product, 0, keepdims=True) * inverse
            grad_scores = (product - power * inner).astype(BF)
            dv_ref[:live, cols] = dot(low, grad, 1, 0).astype(BF)
            dk_ref[:live, cols] = (dot(grad_scores, queries, 1, 0) * SCALE).astype(BF)
            dq_ref[:live, cols] = (dot(grad_scores, keys, 0, 0) * SCALE).astype(BF)
        if live < length:
            for ref in (dq_ref, dk_ref, dv_ref):
                ref[live:, :] = jnp.zeros((length - live, 2 * HD), BF)

    for live in range(step, length + 1, step):
        pl.when((n > live - step) & (n <= live))(functools.partial(rows, live))


def attend_specs(texts, length, width):
    pairs = width // (2 * HD)
    cols = pl.BlockSpec((length, 2 * HD), lambda i, j, *_: (i, j))
    probs = pl.BlockSpec((1, 1, 2, length, length), lambda i, j, *_: (i, j, 0, 0, 0))
    inverse = pl.BlockSpec((1, 1, 2, length), lambda i, j, *_: (i, j, 0, 0))
    shapes = (
        jax.ShapeDtypeStruct((texts * length, width), BF),
        jax.ShapeDtypeStruct((texts, pairs, 2, length, length), BF),
        jax.ShapeDtypeStruct((texts, pairs, 2, length), F32),
    )
    return pairs, cols, probs, inverse, shapes


def attend(lens, q, k, v, length):
    texts = lens.shape[0]
    pairs, cols, probs, inverse, shapes = attend_specs(texts, length, q.shape[1])
    return pl.pallas_call(
        functools.partial(attend_body, step=length // 4),
        grid_spec=pltpu.PrefetchScalarGridSpec(
            num_scalar_prefetch=1,
            grid=(texts, pairs),
            in_specs=[cols] * 3,
            out_specs=[cols, probs, inverse],
        ),
        out_shape=shapes,
        compiler_params=pltpu.CompilerParams(vmem_limit_bytes=40 << 20),
        cost_estimate=pl.CostEstimate(
            flops=16 * texts * length * length * q.shape[1],
            bytes_accessed=2 * texts * length * length * q.shape[1] // HD,
            transcendentals=texts * length * length * q.shape[1] // HD,
        ),
        name="attend",
    )(lens, q, k, v)


def attend_back(lens, q, k, v, do, p, inv, length):
    texts = lens.shape[0]
    pairs, cols, probs, inverse, shapes = attend_specs(texts, length, q.shape[1])
    return pl.pallas_call(
        functools.partial(attend_back_body, step=length // 4),
        grid_spec=pltpu.PrefetchScalarGridSpec(
            num_scalar_prefetch=1,
            grid=(texts, pairs),
            in_specs=[cols] * 4 + [probs, inverse],
            out_specs=[cols] * 3,
        ),
        out_shape=[shapes[0]] * 3,
        compiler_params=pltpu.CompilerParams(vmem_limit_bytes=40 << 20),
        cost_estimate=pl.CostEstimate(
            flops=32 * texts * length * length * q.shape[1],
            bytes_accessed=2 * texts * length * length * q.shape[1] // HD,
            transcendentals=0,
        ),
        name="attend_back",
    )(lens, q, k, v, do, p, inv)


def norm_stats(values):
    center = values - jnp.mean(values, -1, keepdims=True)
    rstd = lax.rsqrt(jnp.mean(center * center, -1, keepdims=True) + 1e-05)
    return center * rstd, rstd


def norm_back(grad_norm, normal, rstd, gain):
    scaled = grad_norm * gain
    return rstd * (
        scaled
        - jnp.mean(scaled, -1, keepdims=True)
        - normal * jnp.mean(scaled * normal, -1, keepdims=True)
    )


def program(dp_size, tensor_size):
    bits = []
    while (1 << len(bits)) < dp_size:
        bits.append(1 << len(bits))

    def pp_tensor(values, flip):
        return lax.ppermute(values, "tensor", [(i, i ^ flip) for i in range(tensor_size)])

    def pp_dp(values, flip):
        return lax.ppermute(values, "dp", [(i, i ^ flip) for i in range(dp_size)])

    def on_device(
        inputs,
        lengths,
        cotangent,
        ln1_gain,
        ln1_bias,
        w_qkv,
        b_qv,
        w_out,
        b_out,
        ln2_gain,
        ln2_bias,
        w_up,
        b_up,
        w_down,
        b_down,
    ):
        t = lax.axis_index("tensor")
        d = lax.axis_index("dp")
        texts_all, part = inputs.shape[:2]
        texts = texts_all // tensor_size
        length = part * tensor_size
        rows = texts * length
        rels = range(tensor_size)

        def pick(values, index, axis):
            return lax.dynamic_index_in_dim(values, index, axis, keepdims=False)

        def to_texts(values):
            blocks = values.reshape(tensor_size, texts, part, D)
            out = jnp.zeros((texts, tensor_size, part, D), values.dtype)
            for r in rels:
                block = pick(blocks, t ^ r, 0)
                if r:
                    block = pp_tensor(block, r)
                out = lax.dynamic_update_slice(out, block[:, None], (0, t ^ r, 0, 0))
            return out.reshape(rows, D)

        def to_rows(values):
            blocks = values.reshape(texts, tensor_size, part, D)
            out = jnp.zeros((tensor_size, texts, part, D), values.dtype)
            for r in rels:
                block = pick(blocks, t ^ r, 1)
                if r:
                    block = pp_tensor(block, r)
                out = lax.dynamic_update_slice(out, block[None], (t ^ r, 0, 0, 0))
            return out.reshape(texts_all, part, D)

        def spread(shard):
            near = pp_tensor(shard, 1)
            far = pp_tensor(shard, 2)
            return [shard, near, far, pp_tensor(far, 1)]

        def after(values, *waits):
            return lax.optimization_barrier((values,) + waits)[0]

        x = to_texts(inputs).astype(F32)
        wq = spread(w_qkv)
        small = jnp.concatenate([b_qv.reshape(-1), b_up])
        small = [small] + [pp_tensor(small, r) for r in rels[1:]]
        local = w_qkv.shape[2]
        units = b_up.shape[0]
        bqv = [s[: 2 * local].reshape(2, local) for s in small]
        bup = [s[2 * local :] for s in small]
        wo = spread(after(w_out, wq[2]))
        wu = spread(after(w_up, wq[2]))
        wd = spread(after(w_down, wu[2]))
        cot = to_texts(after(cotangent, wd[2]))
        lens = lax.dynamic_slice_in_dim(lengths, t * texts, texts)

        normal_one, rstd_one = norm_stats(x)
        h1 = (normal_one * ln1_gain + ln1_bias).astype(BF)
        pairs = [(0, 1), (2, 3)]
        heads = []
        for a, b in pairs:
            w = jnp.concatenate([wq[a], wq[b]], 2)
            bias = jnp.concatenate([bqv[a], bqv[b]], 1)
            q = (dot(h1, w[0], 1, 0) + bias[0]).astype(BF)
            k = dot(h1, w[1], 1, 0).astype(BF)
            v = (dot(h1, w[2], 1, 0) + bias[1]).astype(BF)
            ctx, p, inv = attend(lens, q, k, v, length)
            heads.append((q, k, v, ctx, p, inv, w, jnp.concatenate([wo[a], wo[b]], 0)))
        resid = x + b_out
        for q, k, v, ctx, p, inv, w, w_o in heads:
            resid = resid + dot(ctx, w_o, 1, 0)
        normal_two, rstd_two = norm_stats(resid)
        h2 = (normal_two * ln2_gain + ln2_bias).astype(BF)
        acts, slopes = [], []
        out = resid + b_down
        for r in rels:
            upper = dot(h2, wu[r], 1, 0) + bup[r]
            below = 0.5 * (1.0 + lax.erf(upper * (0.5**0.5)))
            acts.append((upper * below).astype(BF))
            density = jnp.exp(-0.5 * upper * upper) * 0.3989422804014327
            slopes.append((below + upper * density).astype(BF))
            out = out + dot(acts[r], wd[r], 1, 0)
        layer_out = to_rows(out.astype(BF))

        def collect(parts):
            near = pp_tensor(jnp.concatenate([parts[1], parts[3]], 1).astype(BF), 1)
            width = parts[0].shape[1]
            far = pp_tensor((parts[2] + near[:, width:]).astype(BF), 2)
            total = parts[0] + near[:, :width] + far
            for bit in bits:
                block = total.shape[0] // 2
                inner = D // dp_size
                view = total.reshape(-1, 2, inner, width)
                mine = (d // bit) % 2
                send = pick(view, 1 - mine, 1).astype(BF)
                keep = pick(view, mine, 1)
                total = (keep + pp_dp(send, bit)).reshape(block, width)
            return total

        def all_sum(values):
            for flip in (1, 2):
                values = values + pp_tensor(values, flip)
            for bit in bits:
                values = values + pp_dp(values, bit)
            return values

        place = jnp.arange(length)
        live = (place[None, :] < lens[:, None]).reshape(rows, 1)
        g_low = jnp.where(live, cot, jnp.zeros_like(cot))
        g = g_low.astype(F32)
        bias_down = jnp.sum(g, 0)
        grad_down = collect([dot(g_low, acts[r], 0, 0) for r in rels])
        dups, bias_up = [], []
        dh2 = 0.0
        for r in rels:
            dup = dot(g_low, wd[r], 1, 1) * slopes[r].astype(F32)
            bias_up.append(jnp.sum(dup, 0))
            dups.append(dup.astype(BF))
            dh2 = dh2 + dot(dups[r], wu[r], 1, 1)
        grad_up = collect([dot(h2, dups[r], 0, 0) for r in rels])
        gain_two = jnp.sum(dh2 * normal_two, 0)
        shift_two = jnp.sum(dh2, 0)
        dres = g + norm_back(dh2, normal_two, rstd_two, ln2_gain)
        bias_attn = jnp.sum(dres, 0)
        dres_low = dres.astype(BF)
        grad_out_parts = []
        for q, k, v, ctx, p, inv, w, w_o in heads:
            both = dot(dres_low, ctx, 0, 0)
            grad_out_parts += [both[:, :local], both[:, local:]]
        grad_out = collect(grad_out_parts)
        up_full = jnp.zeros((tensor_size, units), F32)
        for r in rels:
            up_full = lax.dynamic_update_slice(up_full, bias_up[r][None], (t ^ r, 0))
        early = all_sum(
            jnp.concatenate([bias_down, gain_two, shift_two, bias_attn, up_full.reshape(-1)])
        )
        dh1 = 0.0
        qkv_parts = []
        qv_full = jnp.zeros((tensor_size, 2, local), F32)
        for (a, b), (q, k, v, ctx, p, inv, w, w_o) in list(zip(pairs, heads)):
            dctx = dot(dres_low, w_o, 1, 1).astype(BF)
            grads = attend_back(lens, q, k, v, dctx, p, inv, length)
            sums = [jnp.sum(grads[c].astype(F32), 0) for c in (0, 2)]
            mats = [dot(h1, grads[c], 0, 0) for c in range(3)]
            for index, r in enumerate((a, b)):
                cols = slice(index * local, index * local + local)
                qkv_parts.append(jnp.concatenate([m[:, cols] for m in mats], 1))
                qv = jnp.stack([s[cols] for s in sums])
                qv_full = lax.dynamic_update_slice(qv_full, qv[None], (t ^ r, 0, 0))
            for c in range(3):
                dh1 = dh1 + dot(grads[c], w[c], 1, 1)
        grad_qkv = collect(qkv_parts)
        gain_one = jnp.sum(dh1 * normal_one, 0)
        shift_one = jnp.sum(dh1, 0)
        grad_in = (dres + norm_back(dh1, normal_one, rstd_one, ln1_gain)).astype(BF)
        grad_input = to_rows(grad_in)
        late = all_sum(jnp.concatenate([gain_one, shift_one, qv_full.reshape(-1)]))
        grad_qv_bias = pick(late[2 * D :].reshape(tensor_size, 2, local), t, 0)
        grad_up_bias = pick(early[4 * D :].reshape(tensor_size, units), t, 0)
        return (
            layer_out,
            grad_input,
            late[:D],
            late[D : 2 * D],
            jnp.stack([grad_qkv[:, c * local : c * local + local] for c in range(3)]),
            grad_qv_bias,
            grad_out.T,
            early[3 * D : 4 * D],
            early[D : 2 * D],
            early[2 * D : 3 * D],
            grad_up,
            grad_up_bias,
            grad_down.T,
            early[:D],
        )

    return on_device


def solution(mesh):
    return jax.shard_map(
        program(mesh.shape["dp"], mesh.shape["tensor"]),
        mesh=mesh,
        in_specs=(
            P("dp", "tensor", None),
            P("dp"),
            P("dp", "tensor", None),
            P(),
            P(),
            P(None, None, "tensor"),
            P(None, "tensor"),
            P("tensor", None),
            P(),
            P(),
            P(),
            P(None, "tensor"),
            P("tensor"),
            P("tensor", None),
            P(),
        ),
        out_specs=(
            P("dp", "tensor", None),
            P("dp", "tensor", None),
            P(),
            P(),
            P(None, "dp", "tensor"),
            P(None, "tensor"),
            P("tensor", "dp"),
            P(),
            P(),
            P(),
            P("dp", "tensor"),
            P("tensor"),
            P("tensor", "dp"),
            P(),
        ),
        check_vma=False,
    )
```

time: 1190 us -> 479 us (0.40)
  waiting for transfers between devices: 733 us -> 176 us
  matrix products: 202 us -> 108 us
  other arithmetic: 116 us -> 31.9 us
  starting transfers between devices: 16 us -> 64.9 us
  blocking collectives: 41.4 us -> 0 us
  Pallas kernels: 0 us -> 30 us
  between operations: 16.6 us -> 2.78 us
    reduce_scatter x18 -> x0, waiting for transfers between devices: 507 us -> none  [the longest x4 119 us: collect_three(): lax.psum_scatter(values.astype(jnp.bfloat16), 'tensor', scatter_dimension...]
    all_gather x16 -> x0, waiting for transfers between devices: 201 us -> none  [the longest x4 63.9 us: spread_one(): return lax.all_gather(values, 'tensor', axis=1, tiled=True)]
    ppermute x0 -> x57, waiting for transfers between devices: none -> 176 us  [the longest x39 136 us: pp_tensor(): lax.ppermute(values, 'tensor', [(i, i ^ flip) for i in range(tensor_size)])]
    dot_general x72 -> x48, matrix products: 202 us -> 108 us  [dot(): lax.dot_general(left, right, (((left_dim,), (right_dim,)), ((), ())), pre...]
    ppermute x0 -> x57, starting transfers between devices: none -> 64.9 us  [the longest x39 33.1 us: pp_tensor(): lax.ppermute(values, 'tensor', [(i, i ^ flip) for i in range(tensor_size)])]
    convert_element_type x17 -> x6, other arithmetic: 56.3 us -> 7.49 us  [the longest x1 3.77 us: on_device(): grad_in = (dres + norm_back(dh1, normal_one, rstd_one, ln1_gain)).astype(BF)]
    psum x1 -> x0, blocking collectives: 41.4 us -> none  [on_device(): lax.psum((shared[0], shared[1], shared[2], shared[3], shared[4], shared[5...]
    reduce_sum x17 -> x9, other arithmetic: 37.8 us -> 4.06 us  [the longest x1 1.6 us: on_device(): bias_attn = jnp.sum(dres, 0)]
  transfers between devices with their start and end apart: 36 -> 57, of which waited for: 32 -> 24; matrix products, arithmetic and copies ran while one was open for 24% -> 39% of each run, Pallas kernels for 0% -> 6%
where the time goes in v1:
time: 479 us; the launch traced here: 473 us
  waiting for transfers between devices  176 us (37%)
  matrix products  108 us (23%)
  starting transfers between devices  64.9 us (14%)
  local copies, waits for them, and re-layouts  60.2 us (13%)
  other arithmetic  31.9 us (7%)
  Pallas kernels  30 us (6%)
    ppermute x39, waiting for transfers between devices, pp_tensor(): lax.ppermute(values, 'tensor', [(i, i ^ flip) for i in range(tensor_size)])  136 us
    dot_general x48, matrix products, dot(): lax.dot_general(left, right, (((left_dim,), (right_dim,)), ((), ())), pre...  108 us
    ppermute x18, waiting for transfers between devices, pp_dp(): return lax.ppermute(values, 'dp', [(i, i ^ flip) for i in range(dp_size)])  39.1 us
    ppermute x39, starting transfers between devices, pp_tensor(): lax.ppermute(values, 'tensor', [(i, i ^ flip) for i in range(tensor_size)])  33.1 us
    ppermute x18, starting transfers between devices, pp_dp(): return lax.ppermute(values, 'dp', [(i, i ^ flip) for i in range(dp_size)])  31.8 us
    unnamed x208, local copies, waits for them, and re-layouts  26.7 us
    pallas_call x2, Pallas kernels, attend_back(): pl.pallas_call(functools.partial(attend_back_body, step=length // 4), gri...  15.3 us
    pallas_call x2, Pallas kernels, attend(): pl.pallas_call(functools.partial(attend_body, step=length // 4), grid_spe...  14.7 us
  transfers between devices with their start and end apart: 57, of which 24 were waited for; matrix products, arithmetic and copies ran while one was open for 39% of the time, Pallas kernels for 6%

profile of v1, /device:TPU:0, one launch (start us, length us, event | category | flops | bytes accessed | tf_op | source)
XLA Modules:
  0.0 473.3 jit_solution(10205092436482557861)
XLA Ops:
  14.7 5.3 %collective-permute-done.1 = bf16[2,128,768]{2,1,0:T(8,128)(2,1)} collective-permute-done((bf16[2,128,768]{2,1,0:T(8,128)(2,1)}, bf16[2,128,768]{2,1,0:T(8,128)(2,1)}, u32[]{:S(2)}, u32[]{:S(2)}) %collective-permute-start.1) | collective-permute-done | bytes 393248 | tf_op jit(solution)/shard_map/ppermute | solution.py:161
  21.0 25.4 %collective-permute-done.2 = bf16[2,128,768]{2,1,0:T(8,128)(2,1)} collective-permute-done((bf16[2,128,768]{2,1,0:T(8,128)(2,1)}, bf16[2,128,768]{2,1,0:T(8,128)(2,1)}, u32[]{:S(2)}, u32[]{:S(2)}) %collective-permute-start.2) | collective-permute-done | bytes 393248 | tf_op jit(solution)/shard_map/ppermute | solution.py:161
  56.5 7.3 %attend.2 = (bf16[1024,384]{1,0:T(8,128)(2,1)S(1)}, bf16[2,3,2,512,512]{4,3,2,1,0:T(8,128)(2,1)S(1)}, f32[2,3,2,512]{3,2,1,0:T(2,128)S(1)}) custom-call(s32[2]{0:T(128)S(1)} %dynamic_slice.130.lens, bf16[1024,384]{1,0:T(8,128)(2,1)S(1)} %add_convert_fusion.7.q_ref, bf16[1024,384]{1,0:T(8,128)(2,1)S(1)} %convolution_convert_fusion.7.k_ref, ...), custom_call_target="tpu_custom_call" | custom-call | flops 3221225472 | bytes 6291456 | tf_op jit(solution)/shard_map/attend/pallas_call | solution.py:99
  70.8 7.4 %attend.3 = (bf16[1024,384]{1,0:T(8,128)(2,1)S(1)}, bf16[2,3,2,512,512]{4,3,2,1,0:T(8,128)(2,1)S(1)}, f32[2,3,2,512]{3,2,1,0:T(2,128)S(1)}) custom-call(s32[2]{0:T(128)S(1)} %dynamic_slice.130.lens, bf16[1024,384]{1,0:T(8,128)(2,1)S(1)} %add_convert_fusion.5.q_ref, bf16[1024,384]{1,0:T(8,128)(2,1)S(1)} %convolution_convert_fusion.6.k_ref, ...), custom_call_target="tpu_custom_call" | custom-call | flops 3221225472 | bytes 6291456 | tf_op jit(solution)/shard_map/attend/pallas_call | solution.py:99
  78.2 5.8 %collective-permute-done.12 = bf16[768,768]{1,0:T(8,128)(2,1)S(1)} collective-permute-done((bf16[768,768]{1,0:T(8,128)(2,1)S(1)}, bf16[768,768]{1,0:T(8,128)(2,1)S(1)}, u32[]{:S(2)}, u32[]{:S(2)}) %collective-permute-start.12) | collective-permute-done | bytes 1179680 | tf_op jit(solution)/shard_map/ppermute | solution.py:161
  88.5 22.9 %collective-permute-done.15 = bf16[768,768]{1,0:T(8,128)(2,1)} collective-permute-done((bf16[768,768]{1,0:T(8,128)(2,1)S(1)}, bf16[768,768]{1,0:T(8,128)(2,1)}, u32[]{:S(2)}, u32[]{:S(2)}) %collective-permute-start.15) | collective-permute-done | bytes 1179680 | tf_op jit(solution)/shard_map/ppermute | solution.py:161
  115.4 8.1 %collective-permute-done.22 = bf16[2,128,768]{2,1,0:T(8,128)(2,1)S(1)} collective-permute-done((bf16[2,128,768]{2,1,0:T(8,128)(2,1)S(1)}, bf16[2,128,768]{2,1,0:T(8,128)(2,1)S(1)}, u32[]{:S(2)}, u32[]{:S(2)}) %collective-permute-start.22) | collective-permute-done | bytes 393248 | tf_op jit(solution)/shard_map/ppermute | solution.py:161
  123.6 7.5 %collective-permute-done.23 = bf16[2,128,768]{2,1,0:T(8,128)(2,1)S(1)} collective-permute-done((bf16[2,128,768]{2,1,0:T(8,128)(2,1)S(1)}, bf16[2,128,768]{2,1,0:T(8,128)(2,1)S(1)}, u32[]{:S(2)}, u32[]{:S(2)}) %collective-permute-start.23) | collective-permute-done | bytes 393248 | tf_op jit(solution)/shard_map/ppermute | solution.py:161
  144.1 4.5 fusion.43
  158.0 4.5 fusion.45
  166.0 4.9 %fusion.109 = f32[1024,768]{1,0:T(8,128)} fusion(bf16[1024,768]{1,0:T(8,128)(2,1)} %copy-done.91, bf16[768,768]{1,0:T(8,128)(2,1)} %copy-done.87), kind=kOutput, calls=%fused_computation.269 | convolution fusion | flops 1207959552 | bytes 5898240 | tf_op jit(solution)/shard_map/dot_general | solution.py:19
  175.0 4.5 fusion.110
  186.8 5.6 %fusion.47 = (f32[768]{0:T(1024)S(1)}, bf16[1024,768]{1,0:T(8,128)(2,1)S(1)}, f32[1024,768]{1,0:T(8,128)S(1)}) fusion(f32[1024,768]{1,0:T(8,128)S(1)} %copy-done.39, f32[768]{0:T(1024)S(1)} %slice.311, bf16[1024,768]{1,0:T(8,128)(2,1)S(1)} %copy-done.47, bf16[768,768]{1,0:T(8,128)(2,1)} %collective-permute-done.17), kind=kOutput, calls=%fused_computation.85 | convolution fusion | flops 1218182400 | bytes 10622976 | tf_op jit(solution)/shard_map/dot_general | solution.py:19
  208.2 7.8 %attend_back.2 = (bf16[1024,384]{1,0:T(8,128)(2,1)S(1)}, bf16[1024,384]{1,0:T(8,128)(2,1)S(1)}, bf16[1024,384]{1,0:T(8,128)(2,1)S(1)}) custom-call(s32[2]{0:T(128)S(1)} %dynamic_slice.130.lens, bf16[1024,384]{1,0:T(8,128)(2,1)S(1)} %copy-done.3, bf16[1024,384]{1,0:T(8,128)(2,1)S(1)} %convolution_convert_fusion.7.k_ref, bf16[1024,384]{1,0:T(8,128)(2,1)S(1)} %copy-done.1, ...), custom_call_target="tpu_custom_call" | custom-call | flops 6442450944 | bytes 6291456 | tf_op jit(solution)/shard_map/attend_back/pallas_call | solution.py:121
  220.2 7.5 %attend_back.3 = (bf16[1024,384]{1,0:T(8,128)(2,1)S(1)}, bf16[1024,384]{1,0:T(8,128)(2,1)S(1)}, bf16[1024,384]{1,0:T(8,128)(2,1)S(1)}) custom-call(s32[2]{0:T(128)S(1)} %dynamic_slice.130.lens, bf16[1024,384]{1,0:T(8,128)(2,1)S(1)} %copy-done.7, bf16[1024,384]{1,0:T(8,128)(2,1)S(1)} %convolution_convert_fusion.6.k_ref, bf16[1024,384]{1,0:T(8,128)(2,1)S(1)} %copy-done.5, ...), custom_call_target="tpu_custom_call" | custom-call | flops 6442450944 | bytes 6291456 | tf_op jit(solution)/shard_map/attend_back/pallas_call | solution.py:121
  231.3 4.3 fusion.38
  265.1 3.8 fusion.37
  270.8 4.6 add_convert_fusion
  276.1 7.1 %collective-permute-start.28 = (f32[3072]{0:T(1024)S(1)}, f32[3072]{0:T(1024)S(1)}, u32[]{:S(2)}, u32[]{:S(2)}) collective-permute-start(f32[3072]{0:T(1024)S(1)} %fusion.198), channel_id=1, source_target_pairs={{0,2},{1,3},{2,0},{3,1},{4,6},{5,7},{6,4},{7,5},{8,10},{9,11},{10,... | collective-permute-start | bytes 36872 | tf_op jit(solution)/shard_map/ppermute | solution.py:161
  290.2 3.9 collective-permute-start.30
  318.0 6.1 %collective-permute-done.25 = bf16[2,128,768]{2,1,0:T(8,128)(2,1)} collective-permute-done((bf16[2,128,768]{2,1,0:T(8,128)(2,1)}, bf16[2,128,768]{2,1,0:T(8,128)(2,1)}, u32[]{:S(2)}, u32[]{:S(2)}) %collective-permute-start.25) | collective-permute-done | bytes 393248 | tf_op jit(solution)/shard_map/ppermute | solution.py:161
  333.7 8.8 %collective-permute-done.19 = bf16[2,128,768]{2,1,0:T(8,128)(2,1)S(1)} collective-permute-done((bf16[2,128,768]{2,1,0:T(8,128)(2,1)S(1)}, bf16[2,128,768]{2,1,0:T(8,128)(2,1)S(1)}, u32[]{:S(2)}, u32[]{:S(2)}) %collective-permute-start.19) | collective-permute-done | bytes 393248 | tf_op jit(solution)/shard_map/ppermute | solution.py:161
  343.7 5.1 %collective-permute-done.38 = bf16[768,192]{0,1:T(8,128)(2,1)S(1)} collective-permute-done((bf16[768,192]{0,1:T(8,128)(2,1)S(1)}, bf16[768,192]{0,1:T(8,128)(2,1)S(1)}, u32[]{:S(2)}, u32[]{:S(2)}) %collective-permute-start.38) | collective-permute-done | bytes 294944 | tf_op jit(solution)/shard_map/ppermute | solution.py:161
  362.7 4.1 add_convert_fusion.2
  371.6 3.8 add_convert_fusion.3
  376.0 8.6 %collective-permute-done.33 = bf16[768,576]{0,1:T(8,128)(2,1)S(1)} collective-permute-done((bf16[768,576]{0,1:T(8,128)(2,1)S(1)}, bf16[768,576]{0,1:T(8,128)(2,1)S(1)}, u32[]{:S(2)}, u32[]{:S(2)}) %collective-permute-start.33) | collective-permute-done | bytes 884768 | tf_op jit(solution)/shard_map/ppermute | solution.py:161
  389.9 19.9 %collective-permute-done.53 = bf16[768,768]{1,0:T(8,128)(2,1)S(1)} collective-permute-done((bf16[768,768]{1,0:T(8,128)(2,1)}, bf16[768,768]{1,0:T(8,128)(2,1)S(1)}, u32[]{:S(2)}, u32[]{:S(2)}) %collective-permute-start.53) | collective-permute-done | bytes 1179680 | tf_op jit(solution)/shard_map/ppermute | solution.py:161
  416.9 5.2 %collective-permute-done.35 = bf16[2,96,576]{2,1,0:T(8,128)(2,1)} collective-permute-done((bf16[2,96,576]{2,1,0:T(8,128)(2,1)}, bf16[2,96,576]{2,1,0:T(8,128)(2,1)}, u32[]{:S(2)}, u32[]{:S(2)}) %collective-permute-start.35) | collective-permute-done | bytes 221216 | tf_op jit(solution)/shard_map/ppermute | solution.py:164
  429.7 5.4 %collective-permute-done.48 = bf16[768,768]{1,0:T(8,128)(2,1)} collective-permute-done((bf16[768,768]{1,0:T(8,128)(2,1)}, bf16[768,768]{1,0:T(8,128)(2,1)}, u32[]{:S(2)}, u32[]{:S(2)}) %collective-permute-start.48) | collective-permute-done | bytes 1179680 | tf_op jit(solution)/shard_map/ppermute | solution.py:161
  439.6 12.8 %collective-permute-done.49 = bf16[4,96,768]{2,1,0:T(8,128)(2,1)S(1)} collective-permute-done((bf16[4,96,768]{2,1,0:T(8,128)(2,1)S(1)}, bf16[4,96,768]{2,1,0:T(8,128)(2,1)S(1)}, u32[]{:S(2)}, u32[]{:S(2)}) %collective-permute-start.49) | collective-permute-done | bytes 589856 | tf_op jit(solution)/shard_map/ppermute | solution.py:164
  456.1 7.7 %collective-permute-done.50 = bf16[2,96,768]{2,1,0:T(8,128)(2,1)S(1)} collective-permute-done((bf16[2,96,768]{2,1,0:T(8,128)(2,1)S(1)}, bf16[2,96,768]{2,1,0:T(8,128)(2,1)S(1)}, u32[]{:S(2)}, u32[]{:S(2)}) %collective-permute-start.50) | collective-permute-done | bytes 294944 | tf_op jit(solution)/shard_map/ppermute | solution.py:164
  465.9 6.4 %collective-permute-done.51 = bf16[1,96,768]{2,1,0:T(8,128)(2,1)S(1)} collective-permute-done((bf16[1,96,768]{2,1,0:T(8,128)(2,1)S(1)}, bf16[1,96,768]{2,1,0:T(8,128)(2,1)S(1)}, u32[]{:S(2)}, u32[]{:S(2)}) %collective-permute-start.51) | collective-permute-done | bytes 147488 | tf_op jit(solution)/shard_map/ppermute | solution.py:164
  (506 shorter events, 223.9 us)
Async XLA Ops:
  7.7 12.2 %collective-permute-start.1 = (bf16[2,128,768]{2,1,0:T(8,128)(2,1)}, bf16[2,128,768]{2,1,0:T(8,128)(2,1)}, u32[]{:S(2)}, u32[]{:S(2)}) collective-permute-start(bf16[2,128,768]{2,1,0:T(8,128)(2,1)} %get-tuple-element.96), channel_id=1, source_target_pairs={{0,2},{1,3},{2,0},{3,1},{4,6},{5,7},{6,4},{7,5},{8,10},{9,11},{10,... | collective-permute-start | bytes 1179656 | tf_op jit(solution)/shard_map/ppermute | solution.py:161
  11.2 40.4 %collective-permute-start.3 = (bf16[3,768,192]{1,2,0:T(8,128)(2,1)}, bf16[3,768,192]{1,2,0:T(8,128)(2,1)}, u32[]{:S(2)}, u32[]{:S(2)}) collective-permute-start(bf16[3,768,192]{1,2,0:T(8,128)(2,1)} %param.20), channel_id=1, source_target_pairs={{0,1},{1,0},{2,3},{3,2},{4,5},{5,4},{6,7},{7,6},{8,9},{9,8},{10,11... | collective-permute-start | bytes 2654216 | tf_op jit(solution)/shard_map/ppermute | solution.py:161
  11.4 37.7 %collective-permute-start.5 = (bf16[3,768,192]{1,2,0:T(8,128)(2,1)}, bf16[3,768,192]{1,2,0:T(8,128)(2,1)}, u32[]{:S(2)}, u32[]{:S(2)}) collective-permute-start(bf16[3,768,192]{1,2,0:T(8,128)(2,1)} %param.20), channel_id=1, source_target_pairs={{0,2},{1,3},{2,0},{3,1},{4,6},{5,7},{6,4},{7,5},{8,10},{9,11},{10,... | collective-permute-start | bytes 2654216 | tf_op jit(solution)/shard_map/ppermute | solution.py:161
  11.8 34.6 %collective-permute-start.2 = (bf16[2,128,768]{2,1,0:T(8,128)(2,1)}, bf16[2,128,768]{2,1,0:T(8,128)(2,1)}, u32[]{:S(2)}, u32[]{:S(2)}) collective-permute-start(bf16[2,128,768]{2,1,0:T(8,128)(2,1)} %get-tuple-element.95), channel_id=1, source_target_pairs={{0,3},{1,2},{2,1},{3,0},{4,7},{5,6},{6,5},{7,4},{8,11},{9,10},{10,... | collective-permute-start | bytes 1179656 | tf_op jit(solution)/shard_map/ppermute | solution.py:161
  49.3 17.1 %collective-permute-start.6 = (bf16[192,768]{1,0:T(8,128)(2,1)S(1)}, bf16[192,768]{1,0:T(8,128)(2,1)S(1)}, u32[]{:S(2)}, u32[]{:S(2)}) collective-permute-start(bf16[192,768]{1,0:T(8,128)(2,1)S(1)} %copy-done.76), channel_id=1, source_target_pairs={{0,1},{1,0},{2,3},{3,2},{4,5},{5,4},{6,7},{7,6},{8,9},{9,8},{10,11... | collective-permute-start | bytes 884744 | tf_op jit(solution)/shard_map/ppermute | solution.py:161
  49.6 16.2 %collective-permute-start.10 = (bf16[192,768]{1,0:T(8,128)(2,1)S(1)}, bf16[192,768]{1,0:T(8,128)(2,1)S(1)}, u32[]{:S(2)}, u32[]{:S(2)}) collective-permute-start(bf16[192,768]{1,0:T(8,128)(2,1)S(1)} %copy-done.76), channel_id=1, source_target_pairs={{0,2},{1,3},{2,0},{3,1},{4,6},{5,7},{6,4},{7,5},{8,10},{9,11},{10,... | collective-permute-start | bytes 884744 | tf_op jit(solution)/shard_map/ppermute | solution.py:161
  51.3 32.7 %collective-permute-start.12 = (bf16[768,768]{1,0:T(8,128)(2,1)S(1)}, bf16[768,768]{1,0:T(8,128)(2,1)S(1)}, u32[]{:S(2)}, u32[]{:S(2)}) collective-permute-start(bf16[768,768]{1,0:T(8,128)(2,1)S(1)} %copy-done.61), channel_id=1, source_target_pairs={{0,2},{1,3},{2,0},{3,1},{4,6},{5,7},{6,4},{7,5},{8,10},{9,11},{10,... | collective-permute-start | bytes 3538952 | tf_op jit(solution)/shard_map/ppermute | solution.py:161
  51.6 92.4 %collective-permute-start.13 = (bf16[768,768]{1,0:T(8,128)(2,1)S(1)}, bf16[768,768]{1,0:T(8,128)(2,1)S(1)}, u32[]{:S(2)}, u32[]{:S(2)}) collective-permute-start(bf16[768,768]{1,0:T(8,128)(2,1)S(1)} %copy-done.61), channel_id=1, source_target_pairs={{0,1},{1,0},{2,3},{3,2},{4,5},{5,4},{6,7},{7,6},{8,9},{9,8},{10,11... | collective-permute-start | bytes 3538952 | tf_op jit(solution)/shard_map/ppermute | solution.py:161
  84.0 27.4 %collective-permute-start.15 = (bf16[768,768]{1,0:T(8,128)(2,1)S(1)}, bf16[768,768]{1,0:T(8,128)(2,1)}, u32[]{:S(2)}, u32[]{:S(2)}) collective-permute-start(bf16[768,768]{1,0:T(8,128)(2,1)S(1)} %copy-done.86), channel_id=1, source_target_pairs={{0,2},{1,3},{2,0},{3,1},{4,6},{5,7},{6,4},{7,5},{8,10},{9,11},{10,... | collective-permute-start | bytes 3538952 | tf_op jit(solution)/shard_map/ppermute | solution.py:161
  86.7 26.2 %collective-permute-start.16 = (bf16[768,768]{1,0:T(8,128)(2,1)S(1)}, bf16[768,768]{1,0:T(8,128)(2,1)S(1)}, u32[]{:S(2)}, u32[]{:S(2)}) collective-permute-start(bf16[768,768]{1,0:T(8,128)(2,1)S(1)} %collective-permute-done.12), channel_id=1, source_target_pairs={{0,1},{1,0},{2,3},{3,2},{4,5},{5,4},{6,7},{7,6},{8,9},{9,8},{10,11... | collective-permute-start | bytes 3538952 | tf_op jit(solution)/shard_map/ppermute | solution.py:161
  88.4 51.4 %collective-permute-start.14 = (bf16[768,768]{1,0:T(8,128)(2,1)S(1)}, bf16[768,768]{1,0:T(8,128)(2,1)S(1)}, u32[]{:S(2)}, u32[]{:S(2)}) collective-permute-start(bf16[768,768]{1,0:T(8,128)(2,1)S(1)} %copy-done.86), channel_id=1, source_target_pairs={{0,1},{1,0},{2,3},{3,2},{4,5},{5,4},{6,7},{7,6},{8,9},{9,8},{10,11... | collective-permute-start | bytes 3538952 | tf_op jit(solution)/shard_map/ppermute | solution.py:161
  112.9 18.2 %collective-permute-start.23 = (bf16[2,128,768]{2,1,0:T(8,128)(2,1)S(1)}, bf16[2,128,768]{2,1,0:T(8,128)(2,1)S(1)}, u32[]{:S(2)}, u32[]{:S(2)}) collective-permute-start(bf16[2,128,768]{2,1,0:T(8,128)(2,1)S(1)} %get-tuple-element.89), channel_id=1, source_target_pairs={{0,3},{1,2},{2,1},{3,0},{4,7},{5,6},{6,5},{7,4},{8,11},{9,10},{10,... | collective-permute-start | bytes 1179656 | tf_op jit(solution)/shard_map/ppermute | solution.py:161
  115.0 71.8 %collective-permute-start.17 = (bf16[768,768]{1,0:T(8,128)(2,1)}, bf16[768,768]{1,0:T(8,128)(2,1)}, u32[]{:S(2)}, u32[]{:S(2)}) collective-permute-start(bf16[768,768]{1,0:T(8,128)(2,1)} %collective-permute-done.15), channel_id=1, source_target_pairs={{0,1},{1,0},{2,3},{3,2},{4,5},{5,4},{6,7},{7,6},{8,9},{9,8},{10,11... | collective-permute-start | bytes 3538952 | tf_op jit(solution)/shard_map/ppermute | solution.py:161
  155.0 207.7 %collective-permute-start.52 = (bf16[768,1536]{1,0:T(8,128)(2,1)}, bf16[768,1536]{1,0:T(8,128)(2,1)}, u32[]{:S(2)}, u32[]{:S(2)}) collective-permute-start(bf16[768,1536]{1,0:T(8,128)(2,1)} %pad_maximum_fusion.1), channel_id=1, source_target_pairs={{0,1},{1,0},{2,3},{3,2},{4,5},{5,4},{6,7},{7,6},{8,9},{9,8},{10,11... | collective-permute-start | bytes 7077896 | tf_op jit(solution)/shard_map/ppermute | solution.py:161
  248.9 122.7 %collective-permute-start.47 = (bf16[768,1536]{1,0:T(8,128)(2,1)}, bf16[768,1536]{1,0:T(8,128)(2,1)}, u32[]{:S(2)}, u32[]{:S(2)}) collective-permute-start(bf16[768,1536]{1,0:T(8,128)(2,1)} %pad_maximum_fusion), channel_id=1, source_target_pairs={{0,1},{1,0},{2,3},{3,2},{4,5},{5,4},{6,7},{7,6},{8,9},{9,8},{10,11... | collective-permute-start | bytes 7077896 | tf_op jit(solution)/shard_map/ppermute | solution.py:161
  255.0 32.4 %collective-permute-start.42 = (f32[6144]{0:T(1024)}, f32[6144]{0:T(1024)S(1)}, u32[]{:S(2)}, u32[]{:S(2)}) collective-permute-start(f32[6144]{0:T(1024)} %constant_dynamic-update-slice_fusion.16), channel_id=1, source_target_pairs={{0,1},{1,0},{2,3},{3,2},{4,5},{5,4},{6,7},{7,6},{8,9},{9,8},{10,11... | collective-permute-start | bytes 73736 | tf_op jit(solution)/shard_map/ppermute | solution.py:161
  258.1 72.4 %collective-permute-start.37 = (bf16[768,384]{0,1:T(8,128)(2,1)}, bf16[768,384]{0,1:T(8,128)(2,1)}, u32[]{:S(2)}, u32[]{:S(2)}) collective-permute-start(bf16[768,384]{0,1:T(8,128)(2,1)} %pad_maximum_fusion.2), channel_id=1, source_target_pairs={{0,1},{1,0},{2,3},{3,2},{4,5},{5,4},{6,7},{7,6},{8,9},{9,8},{10,11... | collective-permute-start | bytes 1769480 | tf_op jit(solution)/shard_map/ppermute | solution.py:161
  259.8 16.3 %collective-permute-start.27 = (f32[3072]{0:T(1024)S(1)}, f32[3072]{0:T(1024)S(1)}, u32[]{:S(2)}, u32[]{:S(2)}) collective-permute-start(f32[3072]{0:T(1024)S(1)} %pad_maximum_fusion.4), channel_id=1, source_target_pairs={{0,1},{1,0},{2,3},{3,2},{4,5},{5,4},{6,7},{7,6},{8,9},{9,8},{10,11... | collective-permute-start | bytes 36872 | tf_op jit(solution)/shard_map/ppermute | solution.py:161
  301.5 15.4 %collective-permute-start.24 = (bf16[2,128,768]{2,1,0:T(8,128)(2,1)}, bf16[2,128,768]{2,1,0:T(8,128)(2,1)}, u32[]{:S(2)}, u32[]{:S(2)}) collective-permute-start(bf16[2,128,768]{2,1,0:T(8,128)(2,1)} %get-tuple-element.88), channel_id=1, source_target_pairs={{0,1},{1,0},{2,3},{3,2},{4,5},{5,4},{6,7},{7,6},{8,9},{9,8},{10,11... | collective-permute-start | bytes 1179656 | tf_op jit(solution)/shard_map/ppermute | solution.py:161
  324.1 36.4 %collective-permute-start.32 = (bf16[768,1152]{0,1:T(8,128)(2,1)}, bf16[768,1152]{0,1:T(8,128)(2,1)}, u32[]{:S(2)}, u32[]{:S(2)}) collective-permute-start(bf16[768,1152]{0,1:T(8,128)(2,1)} %fusion.69), channel_id=1, source_target_pairs={{0,1},{1,0},{2,3},{3,2},{4,5},{5,4},{6,7},{7,6},{8,9},{9,8},{10,11... | collective-permute-start | bytes 5308424 | tf_op jit(solution)/shard_map/ppermute | solution.py:161
  330.5 12.0 %collective-permute-start.19 = (bf16[2,128,768]{2,1,0:T(8,128)(2,1)S(1)}, bf16[2,128,768]{2,1,0:T(8,128)(2,1)S(1)}, u32[]{:S(2)}, u32[]{:S(2)}) collective-permute-start(bf16[2,128,768]{2,1,0:T(8,128)(2,1)S(1)} %copy-done.75), channel_id=1, source_target_pairs={{0,2},{1,3},{2,0},{3,1},{4,6},{5,7},{6,4},{7,5},{8,10},{9,11},{10,... | collective-permute-start | bytes 1179656 | tf_op jit(solution)/shard_map/ppermute | solution.py:161
  332.3 16.5 %collective-permute-start.38 = (bf16[768,192]{0,1:T(8,128)(2,1)S(1)}, bf16[768,192]{0,1:T(8,128)(2,1)S(1)}, u32[]{:S(2)}, u32[]{:S(2)}) collective-permute-start(bf16[768,192]{0,1:T(8,128)(2,1)S(1)} %fusion.53), channel_id=1, source_target_pairs={{0,2},{1,3},{2,0},{3,1},{4,6},{5,7},{6,4},{7,5},{8,10},{9,11},{10,... | collective-permute-start | bytes 884744 | tf_op jit(solution)/shard_map/ppermute | solution.py:161
  342.5 12.9 %collective-permute-start.20 = (bf16[2,128,768]{2,1,0:T(8,128)(2,1)S(1)}, bf16[2,128,768]{2,1,0:T(8,128)(2,1)}, u32[]{:S(2)}, u32[]{:S(2)}) collective-permute-start(bf16[2,128,768]{2,1,0:T(8,128)(2,1)S(1)} %get-tuple-element.92), channel_id=1, source_target_pairs={{0,3},{1,2},{2,1},{3,0},{4,7},{5,6},{6,5},{7,4},{8,11},{9,10},{10,... | collective-permute-start | bytes 1179656 | tf_op jit(solution)/shard_map/ppermute | solution.py:161
  362.0 22.6 %collective-permute-start.33 = (bf16[768,576]{0,1:T(8,128)(2,1)S(1)}, bf16[768,576]{0,1:T(8,128)(2,1)S(1)}, u32[]{:S(2)}, u32[]{:S(2)}) collective-permute-start(bf16[768,576]{0,1:T(8,128)(2,1)S(1)} %fusion.50), channel_id=1, source_target_pairs={{0,2},{1,3},{2,0},{3,1},{4,6},{5,7},{6,4},{7,5},{8,10},{9,11},{10,... | collective-permute-start | bytes 2654216 | tf_op jit(solution)/shard_map/ppermute | solution.py:161
  366.8 43.0 %collective-permute-start.53 = (bf16[768,768]{1,0:T(8,128)(2,1)}, bf16[768,768]{1,0:T(8,128)(2,1)S(1)}, u32[]{:S(2)}, u32[]{:S(2)}) collective-permute-start(bf16[768,768]{1,0:T(8,128)(2,1)} %add_convert_fusion.2), channel_id=1, source_target_pairs={{0,2},{1,3},{2,0},{3,1},{4,6},{5,7},{6,4},{7,5},{8,10},{9,11},{10,... | collective-permute-start | bytes 3538952 | tf_op jit(solution)/shard_map/ppermute | solution.py:161
  368.9 46.5 %collective-permute-start.41 = (bf16[1,96,192]{2,1,0:T(8,128)(2,1)}, bf16[1,96,192]{2,1,0:T(8,128)(2,1)}, u32[]{:S(2)}, u32[]{:S(2)}) collective-permute-start(bf16[1,96,192]{2,1,0:T(8,128)(2,1)} %dynamic-slice_convert_fusion.8), channel_id=1, source_target_pairs={{0,16},{4,20},{8,24},{12,28},{16,0},{20,4},{24,8},{28,12},{1,17},{... | collective-permute-start | bytes 110600 | tf_op jit(solution)/shard_map/ppermute | solution.py:164
  375.4 59.6 %collective-permute-start.48 = (bf16[768,768]{1,0:T(8,128)(2,1)}, bf16[768,768]{1,0:T(8,128)(2,1)}, u32[]{:S(2)}, u32[]{:S(2)}) collective-permute-start(bf16[768,768]{1,0:T(8,128)(2,1)} %add_convert_fusion.3), channel_id=1, source_target_pairs={{0,2},{1,3},{2,0},{3,1},{4,6},{5,7},{6,4},{7,5},{8,10},{9,11},{10,... | collective-permute-start | bytes 3538952 | tf_op jit(solution)/shard_map/ppermute | solution.py:161
  389.3 24.4 %collective-permute-start.34 = (bf16[4,96,576]{2,1,0:T(8,128)(2,1)S(1)}, bf16[4,96,576]{2,1,0:T(8,128)(2,1)S(1)}, u32[]{:S(2)}, u32[]{:S(2)}) collective-permute-start(bf16[4,96,576]{2,1,0:T(8,128)(2,1)S(1)} %fusion.61), channel_id=1, source_target_pairs={{0,4},{4,0},{8,12},{12,8},{16,20},{20,16},{24,28},{28,24},{1,5},{5... | collective-permute-start | bytes 1327112 | tf_op jit(solution)/shard_map/ppermute | solution.py:164
  413.2 15.3 %collective-permute-start.54 = (bf16[4,96,768]{2,1,0:T(8,128)(2,1)}, bf16[4,96,768]{2,1,0:T(8,128)(2,1)}, u32[]{:S(2)}, u32[]{:S(2)}) collective-permute-start(bf16[4,96,768]{2,1,0:T(8,128)(2,1)} %fusion.52), channel_id=1, source_target_pairs={{0,4},{4,0},{8,12},{12,8},{16,20},{20,16},{24,28},{28,24},{1,5},{5... | collective-permute-start | bytes 1769480 | tf_op jit(solution)/shard_map/ppermute | solution.py:164
  423.1 15.6 %collective-permute-start.36 = (bf16[1,96,576]{2,1,0:T(8,128)(2,1)S(1)}, bf16[1,96,576]{2,1,0:T(8,128)(2,1)S(1)}, u32[]{:S(2)}, u32[]{:S(2)}) collective-permute-start(bf16[1,96,576]{2,1,0:T(8,128)(2,1)S(1)} %dynamic-slice_convert_fusion.6), channel_id=1, source_target_pairs={{0,16},{4,20},{8,24},{12,28},{16,0},{20,4},{24,8},{28,12},{1,17},{... | collective-permute-start | bytes 331784 | tf_op jit(solution)/shard_map/ppermute | solution.py:164
  437.2 15.2 %collective-permute-start.49 = (bf16[4,96,768]{2,1,0:T(8,128)(2,1)S(1)}, bf16[4,96,768]{2,1,0:T(8,128)(2,1)S(1)}, u32[]{:S(2)}, u32[]{:S(2)}) collective-permute-start(bf16[4,96,768]{2,1,0:T(8,128)(2,1)S(1)} %fusion.51), channel_id=1, source_target_pairs={{0,4},{4,0},{8,12},{12,8},{16,20},{20,16},{24,28},{28,24},{1,5},{5... | collective-permute-start | bytes 1769480 | tf_op jit(solution)/shard_map/ppermute | solution.py:164
  437.8 15.5 %collective-permute-start.55 = (bf16[2,96,768]{2,1,0:T(8,128)(2,1)S(1)}, bf16[2,96,768]{2,1,0:T(8,128)(2,1)S(1)}, u32[]{:S(2)}, u32[]{:S(2)}) collective-permute-start(bf16[2,96,768]{2,1,0:T(8,128)(2,1)S(1)} %fusion.63), channel_id=1, source_target_pairs={{0,8},{4,12},{8,0},{12,4},{16,24},{20,28},{24,16},{28,20},{1,9},{5... | collective-permute-start | bytes 884744 | tf_op jit(solution)/shard_map/ppermute | solution.py:164
  (127 other events, 1059.0 us)

commit v2 on v1

v2 whole, which is shorter than its diff:
```python
import functools

import jax
import jax.numpy as jnp
from jax import lax
from jax.experimental import pallas as pl
from jax.experimental.pallas import tpu as pltpu
from jax.sharding import PartitionSpec as P

D = 768
HD = 64
BF = jnp.bfloat16
F32 = jnp.float32
SCALE = HD**-0.5
LOG2E = 1.4426950408889634


def dot(left, right, left_dim, right_dim):
    return lax.dot_general(
        left, right, (((left_dim,), (right_dim,)), ((), ())), preferred_element_type=F32
    )


def norm_stats(values):
    center = values - jnp.mean(values, -1, keepdims=True)
    rstd = lax.rsqrt(jnp.mean(center * center, -1, keepdims=True) + 1e-05)
    return center * rstd, rstd


def norm_back(grad_norm, normal, rstd, gain):
    scaled = grad_norm * gain
    return rstd * (
        scaled
        - jnp.mean(scaled, -1, keepdims=True)
        - normal * jnp.mean(scaled * normal, -1, keepdims=True)
    )


class Clock:
    def __init__(self):
        self.last = None

    def after(self, values):
        return values if self.last is None else tie(values, self.last)

    def then(self, values):
        self.last = jax.tree.leaves(values)[0]
        return values


def tie(value, *waits):
    return lax.optimization_barrier((value,) + waits)[0]


def call(clock, body, out_shape, operands, *, grid=(), in_specs=None, out_specs=None, scalars=(), scratch=(),
         name=None):
    operands = (clock.after(operands[0]),) + tuple(operands[1:])
    out = pl.pallas_call(
        body,
        out_shape=out_shape,
        grid_spec=pltpu.PrefetchScalarGridSpec(
            num_scalar_prefetch=len(scalars),
            grid=grid,
            in_specs=in_specs,
            out_specs=out_specs,
            scratch_shapes=scratch,
        ),
        compiler_params=pltpu.CompilerParams(vmem_limit_bytes=48 << 20),
        cost_estimate=pl.CostEstimate(flops=0, bytes_accessed=0, transcendentals=0),
        name=name,
    )(*scalars, *operands)
    return clock.then(out)


def shape_of(dims, dtype=BF):
    return jax.ShapeDtypeStruct(tuple(dims), dtype)


def whole(values):
    return pl.BlockSpec(values.shape, lambda *_: (0,) * len(values.shape))


def side_by_side(clock, w):
    half, width = w.shape[1] // 2, w.shape[2]

    def body(w_ref, *refs):
        for i in range(2):
            for c in range(3):
                refs[i][:, c * width : (c + 1) * width] = w_ref[c, i * half : (i + 1) * half, :]

    out = [shape_of((half, 3 * width))] * 2
    return call(
        clock, body, out, (w,), grid=(1,), in_specs=[whole(w)], out_specs=[whole(v) for v in out],
        name="side_by_side",
    )


def order_halves(clock, mine, other, index):
    def body(at, mine_ref, other_ref, first_ref, second_ref):
        keep = at[0] == 0
        first_ref[...] = jnp.where(keep, mine_ref[...], other_ref[...])
        second_ref[...] = jnp.where(keep, other_ref[...], mine_ref[...])

    return call(
        clock, body, [shape_of(mine.shape)] * 2, (mine, other), grid=(1,), in_specs=[whole(mine), whole(other)],
        out_specs=[whole(mine), whole(mine)], scalars=(index.reshape(1),), name="order_halves",
    )


def times(left, pieces):
    total, start = None, 0
    for ref in pieces:
        part = dot(left[:, start : start + ref.shape[0]], ref[...], 1, 0)
        start += ref.shape[0]
        total = part if total is None else total + part
    return total


def times_turned(left, pieces):
    parts = [dot(left, ref[...], 1, 1) for ref in pieces]
    return parts[0] if len(parts) == 1 else jnp.concatenate(parts, 1)


def split_refs(refs, counts):
    out = []
    for count in counts:
        out.append(refs[:count])
        refs = refs[count:]
    return out


def row_block(values, steps):
    return pl.BlockSpec((values.shape[0] // steps, values.shape[1]), lambda i, *_: (i, 0))


def project(clock, h, w, bias):
    def body(h_ref, bias_ref, *refs):
        refs[-1][...] = (times(h_ref[...], refs[:-1]) + bias_ref[...]).astype(BF)

    bias = bias.reshape(1, -1)
    out = shape_of((h.shape[0], bias.shape[1]))
    return call(
        clock, body, out, (h, bias, *w), grid=(4,), in_specs=[row_block(h, 4), whole(bias)] + [whole(v) for v in w],
        out_specs=row_block(out, 4), name="project",
    )


def attention_out(clock, x, ctx, w, vectors):
    count = len(ctx)

    def body(x_ref, *refs):
        ctx_refs, w_refs, (bias_ref, gain_ref, shift_ref), (out_ref, h_ref) = split_refs(refs, (count, count, 3, 2))
        total = x_ref[...].astype(F32) + bias_ref[...]
        for r in range(count):
            total = total + dot(ctx_refs[r][...], w_refs[r][...], 1, 0)
        out_ref[...] = total
        normal, _ = norm_stats(total)
        h_ref[...] = (normal * gain_ref[...] + shift_ref[...]).astype(BF)

    vectors = [v.reshape(1, -1) for v in vectors]
    out = [shape_of(x.shape, F32), shape_of(x.shape)]
    return call(
        clock, body, out, (x, *ctx, *w, *vectors), grid=(4,),
        in_specs=[row_block(v, 4) for v in (x, *ctx)] + [whole(v) for v in (*w, *vectors)],
        out_specs=[row_block(v, 4) for v in out], name="attention_out",
    )


def up(clock, h, w, bias):
    def body(h_ref, bias_ref, *refs):
        upper = times(h_ref[...], refs[:-2]) + bias_ref[...]
        below = 0.5 * (1.0 + lax.erf(upper * (0.5**0.5)))
        density = jnp.exp(-0.5 * upper * upper) * 0.3989422804014327
        refs[-2][...] = (upper * below).astype(BF)
        refs[-1][...] = (below + upper * density).astype(BF)

    bias = bias.reshape(1, -1)
    out = [shape_of((h.shape[0], bias.shape[1]))] * 2
    return call(
        clock, body, out, (h, bias, *w), grid=(4,), in_specs=[row_block(h, 4), whole(bias)] + [whole(v) for v in w],
        out_specs=[row_block(v, 4) for v in out], name="up",
    )


def to_owner(refs, at, values, scratch, count):
    text, late = pl.program_id(0) // 2, pl.program_id(0) % 2
    part = values.shape[0] * 2 // count
    scratch[...] = values.astype(BF)
    for r in range(count):
        place = at[0] ^ r

        @pl.when(place // (count // 2) == late)
        def _():
            start = pl.multiple_of((place % (count // 2)) * part, part)
            refs[r][pl.ds(text, 1)] = scratch[pl.ds(start, part), :][None]


def down_out(clock, resid, acts, w, bias, me, texts):
    count = len(acts)
    steps = texts * 2

    def body(at, resid_ref, *refs):
        act_refs, w_refs, (bias_ref,), outs, (scratch,) = split_refs(refs, (count, count, 1, count, 1))
        total = resid_ref[...] + bias_ref[...]
        for r in range(count):
            total = total + dot(act_refs[r][...], w_refs[r][...], 1, 0)
        to_owner(outs, at, total, scratch, count)

    bias = bias.reshape(1, -1)
    out = [shape_of((texts, resid.shape[0] // texts // count, resid.shape[1]))] * count
    return call(
        clock, body, out, (resid, *acts, *w, bias), grid=(steps,),
        in_specs=[row_block(v, steps) for v in (resid, *acts)] + [whole(v) for v in (*w, bias)],
        out_specs=[whole(v) for v in out], scalars=(me.reshape(1),),
        scratch=[pltpu.VMEM((resid.shape[0] // steps, resid.shape[1]), BF)], name="down_out",
    )


def norm_one_back(clock, x, dres, dqkv, w, gain, me, texts):
    count = len(dqkv)
    steps = texts * 2
    sizes = [len(pieces) for pieces in w]
    flat = [v for pieces in w for v in pieces]

    def body(at, x_ref, dres_ref, *refs):
        grads, w_refs, (gain_ref,), outs, (gain_sum, shift_sum, scratch) = split_refs(
            refs, (count, len(flat), 1, count, 3)
        )
        w_refs = split_refs(w_refs, sizes)
        total = None
        for r in range(count):
            part = times_turned(grads[r][...], w_refs[r])
            total = part if total is None else total + part
        normal, rstd = norm_stats(x_ref[...].astype(F32))

        @pl.when(pl.program_id(0) == 0)
        def _():
            gain_sum[...] = jnp.zeros_like(gain_sum)
            shift_sum[...] = jnp.zeros_like(shift_sum)

        gain_sum[...] += jnp.sum(total * normal, 0, keepdims=True)
        shift_sum[...] += jnp.sum(total, 0, keepdims=True)
        to_owner(outs, at, dres_ref[...] + norm_back(total, normal, rstd, gain_ref[...]), scratch, count)

    gain = gain.reshape(1, -1)
    out = [shape_of((texts, x.shape[0] // texts // count, x.shape[1]))] * count + [shape_of(gain.shape, F32)] * 2
    out = call(
        clock, body, out, (x, dres, *dqkv, *flat, gain), grid=(steps,),
        in_specs=[row_block(v, steps) for v in (x, dres, *dqkv)] + [whole(v) for v in (*flat, gain)],
        out_specs=[whole(v) for v in out], scalars=(me.reshape(1),),
        scratch=[pltpu.VMEM((x.shape[0] // steps, x.shape[1]), BF)], name="norm_one_back",
    )
    return out[:count], out[count], out[count + 1]


def join_norm(clock, blocks, me, gain, shift):
    texts, part, width = blocks[0].shape
    count = len(blocks)

    def body(at, *refs):
        ins, (gain_ref, shift_ref, x_ref, h_ref) = refs[:count], refs[count:]
        for r in range(count):
            for i in range(texts):
                start = pl.multiple_of(i * count * part + (at[0] ^ r) * part, part)
                low = ins[r][i]
                normal, _ = norm_stats(low.astype(F32))
                x_ref[pl.ds(start, part), :] = low
                h_ref[pl.ds(start, part), :] = (normal * gain_ref[...] + shift_ref[...]).astype(BF)

    out = [shape_of((texts * count * part, width))] * 2
    operands = (*blocks, gain.reshape(1, -1), shift.reshape(1, -1))
    return call(
        clock, body, out, operands, grid=(1,), in_specs=[whole(v) for v in operands], out_specs=[whole(v) for v in out],
        scalars=(me.reshape(1),), name="join_norm",
    )


def join_mask(clock, blocks, me, lens):
    texts, part, width = blocks[0].shape
    count = len(blocks)

    def body(at, n, *refs):
        ins, (g_ref, sum_ref) = refs[:count], refs[count:]
        total = jnp.zeros((1, width), F32)
        for r in range(count):
            for i in range(texts):
                place = (at[0] ^ r) * part
                start = pl.multiple_of(i * count * part + place, part)
                live = lax.broadcasted_iota(jnp.int32, (part, width), 0) + place < n[i]
                values = jnp.where(live, ins[r][i].astype(F32), 0.0)
                total = total + jnp.sum(values, 0, keepdims=True)
                g_ref[pl.ds(start, part), :] = values.astype(BF)
        sum_ref[...] = total

    out = [shape_of((texts * count * part, width)), shape_of((1, width), F32)]
    return call(
        clock, body, out, blocks, grid=(1,), in_specs=[whole(v) for v in blocks], out_specs=[whole(v) for v in out],
        scalars=(me.reshape(1), lens), name="join_mask",
    )


def join_rows(clock, blocks, me):
    texts = blocks[0].shape[0]
    count = len(blocks)

    def body(at, *refs):
        for r in range(count):
            refs[count][pl.ds((at[0] ^ r) * texts, texts)] = refs[r][...]

    out = shape_of((texts * count,) + blocks[0].shape[1:])
    return call(
        clock, body, out, blocks, grid=(1,), in_specs=[whole(v) for v in blocks], out_specs=whole(out),
        scalars=(me.reshape(1),), name="join_rows",
    )


def up_back(clock, g, ups, downs, slopes, base, resid, gain):
    rows, width = g.shape
    count = len(ups)
    units = downs[0].shape[0]
    sizes = [len(pieces) for pieces in ups]
    flat = [v for pieces in ups for v in pieces]
    last = base is not None

    def body(g_ref, *refs):
        up_refs, down_refs, slope_refs, more, grad_refs, sum_refs, outs = split_refs(
            refs, (len(flat), count, count, 3 if last else 0, count, count, 5 if last else 1)
        )
        up_refs = split_refs(up_refs, sizes)
        grad = g_ref[...]
        total = more[0][...] if last else None

        @pl.when(pl.program_id(0) == 0)
        def _():
            for ref in list(sum_refs) + list(outs[2:]):
                ref[...] = jnp.zeros_like(ref)

        for s in range(count):
            upper = dot(grad, down_refs[s][...], 1, 1) * slope_refs[s][...].astype(F32)
            sum_refs[s][...] += jnp.sum(upper, 0, keepdims=True)
            low = upper.astype(BF)
            grad_refs[s][...] = low
            part = times_turned(low, up_refs[s])
            total = part if total is None else total + part
        if last:
            normal, rstd = norm_stats(more[1][...])
            outs[2][...] += jnp.sum(total * normal, 0, keepdims=True)
            outs[3][...] += jnp.sum(total, 0, keepdims=True)
            total = grad.astype(F32) + norm_back(total, normal, rstd, more[2][...])
            outs[4][...] += jnp.sum(total, 0, keepdims=True)
            outs[1][...] = total.astype(BF)
        outs[0][...] = total

    sums, vector = shape_of((1, units), F32), shape_of((1, width), F32)
    unit = pl.BlockSpec((rows // 4, units), lambda i: (i, 0))
    operands = (g, *flat, *downs, *slopes)
    in_specs = [row_block(g, 4)] + [whole(v) for v in (*flat, *downs)] + [unit] * count
    outs = [shape_of((rows, width), F32)]
    out_specs = [row_block(g, 4)]
    if last:
        gain = gain.reshape(1, -1)
        operands += (base, resid, gain)
        in_specs += [row_block(g, 4)] * 2 + [whole(gain)]
        outs += [shape_of((rows, width))] + [vector] * 3
        out_specs += [row_block(g, 4)] + [whole(vector)] * 3
    out = call(
        clock, body,
        [shape_of((rows, units))] * count + [sums] * count + outs,
        operands,
        grid=(4,),
        in_specs=in_specs,
        out_specs=[unit] * count + [whole(sums)] * count + out_specs,
        name="up_back",
    )
    return list(out[:count]), list(out[count : 2 * count]), out[2 * count :]


def weight_grads(clock, lefts, slots, near=None, split=None, apart=False, pieces=False):
    rows, width = lefts[0].shape
    columns = sum(right.shape[1] for _, right in slots[0])
    count = len(slots)
    half = width // 2
    rights = [right for slot in slots for _, right in slot]

    def body(*refs):
        if split is not None:
            at, refs = refs[0], refs[1:]
        left_refs, refs = refs[: len(lefts)], refs[len(lefts) :]
        right_refs, refs = list(refs[: len(rights)]), refs[len(rights) :]
        if near is not None:
            near_refs, refs = refs[: 2 * count], refs[2 * count :]
        for s, slot in enumerate(slots):
            start = 0
            for which, right in slot:
                product = dot(left_refs[which][...], right_refs.pop(0)[...], 0, 0)
                cols = slice(start, start + right.shape[1])
                start = cols.stop
                for i in range(2):
                    low, high = max(cols.start, i * columns // 2), min(cols.stop, (i + 1) * columns // 2)
                    if low < high:
                        here = slice(low - cols.start, high - cols.start)
                        there = slice(low - i * columns // 2, high - i * columns // 2)
                        value = product[:, here]
                        if near is not None:
                            value = value + near_refs[2 * s + i][:, there].astype(F32)
                        if pieces:
                            refs[2 * s + i][:, there] = value.astype(BF)
                        elif apart:
                            refs[s][0, :, low:high] = value.astype(BF)
                        elif split is None:
                            refs[0][s, :, low:high] = value.astype(BF)
                        else:
                            refs[2][:, low:high] = value
            if split is not None:
                outer, inner = split[0] // 2, width // split[0] // 2
                for a in range(outer):
                    for ref, bit in ((refs[0], 1 - at[0]), (refs[1], at[0])):
                        place = pl.multiple_of((2 * a + bit) * inner, inner)
                        ref[s, a * inner : (a + 1) * inner, :] = refs[2][pl.ds(place, inner), :].astype(BF)

    left = pl.BlockSpec((rows, half), lambda i, *_: (0, i))
    tall = pl.BlockSpec((count, half, columns), lambda i, *_: (0, i, 0))
    narrow = pl.BlockSpec((half, columns // 2), lambda i, *_: (i, 0))
    short = pl.BlockSpec((count, half // 2, columns), lambda i, *_: (0, i, 0))
    operands = (*lefts, *rights) + (() if near is None else tuple(near))
    if pieces:
        out_shape = [shape_of((width, columns // 2))] * (2 * count)
        out_specs = [narrow] * (2 * count)
    elif apart:
        out_shape = [shape_of((1, width, columns))] * count
        out_specs = [pl.BlockSpec((1, half, columns), lambda i, *_: (0, i, 0))] * count
    elif split is None:
        out_shape, out_specs = shape_of((count, width, columns)), tall
    else:
        out_shape, out_specs = [shape_of((count, half, columns))] * 2, [short] * 2
    return call(
        clock, body,
        out_shape,
        operands,
        grid=(2,),
        in_specs=[left] * len(lefts) + [whole(v) for v in rights] + ([] if near is None else [narrow] * len(near)),
        out_specs=out_specs,
        scalars=() if split is None else (split[1].reshape(1),),
        scratch=[] if split is None else [pltpu.VMEM((half, columns), F32)],
        name="weight_grads",
    )


def add_split(clock, keep, arrived, outer, index):
    columns = keep.shape[-1]
    inner = keep.size // columns // outer // 2

    def body(at, keep_ref, arrived_ref, send_ref, out_ref):
        for ref, bit in ((send_ref, 1 - at[0]), (out_ref, at[0])):
            ref[0] = (keep_ref[0, bit].astype(F32) + arrived_ref[0, bit].astype(F32)).astype(BF)

    tall = pl.BlockSpec((1, 2, inner, columns), lambda i, *_: (i, 0, 0, 0))
    short = pl.BlockSpec((1, inner, columns), lambda i, *_: (i, 0, 0))
    return call(
        clock, body,
        [shape_of((outer, inner, columns))] * 2,
        (keep.reshape(outer, 2, inner, columns), arrived.reshape(outer, 2, inner, columns)),
        grid=(outer,),
        in_specs=[tall] * 2,
        out_specs=[short] * 2,
        scalars=(jnp.asarray(index, jnp.int32).reshape(1),),
        name="add_split",
    )


def attend_body(lens, *refs, step, heads):
    ins, outs, (p_ref, inv_ref) = refs[:2], refs[2:4], refs[4:]
    n = lens[pl.program_id(0)]
    length = ins[0].shape[0]
    width = heads * HD

    def rows(live):
        edge = lax.broadcasted_iota(jnp.int32, (step, length), 0) < n - (live - step)
        for which in range(2):
            ref, ctx_ref = ins[which], outs[which]
            for head in range(heads):
                slot = which * heads + head
                cols = slice(head * HD, head * HD + HD)
                keys = ref[:live, width + head * HD : width + head * HD + HD]
                values = ref[:live, 2 * width + head * HD : 2 * width + head * HD + HD]
                scores = dot(keys, ref[:, cols], 1, 1)
                last = jnp.where(edge, scores[live - step :], -1e30)
                if live > step:
                    scores = jnp.concatenate([scores[: live - step], last], 0)
                else:
                    scores = last
                top = jnp.max(scores, 0, keepdims=True)
                power = jnp.exp2((scores - top) * (SCALE * LOG2E))
                inverse = 1.0 / jnp.sum(power, 0, keepdims=True)
                low = power.astype(BF)
                p_ref[0, slot, :live, :] = low
                inv_ref[0, slot : slot + 1, :] = inverse
                mixed = dot(low, values, 0, 0)
                ctx_ref[:, cols] = (mixed * inverse.reshape(length, 1)).astype(BF)

    for live in range(step, length + 1, step):
        pl.when((n > live - step) & (n <= live))(functools.partial(rows, live))


def attend_back_body(lens, *refs, step, heads):
    ins, (grad_ref,), w_refs, (p_ref, inv_ref) = refs[:2], refs[2:3], refs[3:5], refs[5:7]
    outs, sums, do_ref = refs[7:9], refs[9:11], refs[11]
    n = lens[pl.program_id(0)]
    length = ins[0].shape[0]
    width = heads * HD

    def rows(live):
        for which in range(2):
            ref, out_ref = ins[which], outs[which]
            do_ref[:live, :] = dot(grad_ref[:live, :], w_refs[which][...], 1, 1)
            for head in range(heads):
                slot = which * heads + head
                at = [slice(c * width + head * HD, c * width + head * HD + HD) for c in range(3)]
                inverse = inv_ref[0, slot : slot + 1, :live]
                grad = (do_ref[:live, at[0]] * inverse.reshape(live, 1)).astype(BF)
                low = p_ref[0, slot, :live, :live]
                grad_probs = dot(ref[:live, at[2]], grad, 1, 1)
                power = low.astype(F32)
                product = power * grad_probs
                inner = jnp.sum(product, 0, keepdims=True) * inverse
                grad_scores = (product - power * inner).astype(BF)
                out_ref[:live, at[2]] = dot(low, grad, 1, 0).astype(BF)
                out_ref[:live, at[1]] = (dot(grad_scores, ref[:live, at[0]], 1, 0) * SCALE).astype(BF)
                out_ref[:live, at[0]] = (dot(grad_scores, ref[:live, at[1]], 0, 0) * SCALE).astype(BF)
            if live < length:
                out_ref[live:, :] = jnp.zeros((length - live, 3 * width), BF)
            sums[which][...] += jnp.sum(out_ref[:live, :].astype(F32), 0, keepdims=True)

    @pl.when(pl.program_id(0) == 0)
    def _():
        for ref in sums:
            ref[...] = jnp.zeros_like(ref)

    for live in range(step, length + 1, step):
        pl.when((n > live - step) & (n <= live))(functools.partial(rows, live))


def attend_call(clock, lens, qkv, back, length):
    texts = lens.shape[0]
    width = qkv[0].shape[1] // 3
    heads = width // HD
    wide = pl.BlockSpec((length, 3 * width), lambda i, *_: (i, 0))
    slim = pl.BlockSpec((length, width), lambda i, *_: (i, 0))
    full = pl.BlockSpec((length, D), lambda i, *_: (i, 0))
    probs = pl.BlockSpec((1, 2 * heads, length, length), lambda i, *_: (i, 0, 0, 0))
    inverse = pl.BlockSpec((1, 2 * heads, length), lambda i, *_: (i, 0, 0))
    rows = texts * length
    if back is None:
        return call(
            clock,
            functools.partial(attend_body, step=length // 4, heads=heads),
            [shape_of((rows, width))] * 2
            + [shape_of((texts, 2 * heads, length, length)), shape_of((texts, 2 * heads, length), F32)],
            tuple(qkv),
            grid=(texts,),
            in_specs=[wide] * 2,
            out_specs=[slim] * 2 + [probs, inverse],
            scalars=(lens,),
            name="attend",
        )
    return call(
        clock,
        functools.partial(attend_back_body, step=length // 4, heads=heads),
        [shape_of((rows, 3 * width))] * 2 + [shape_of((1, 3 * width), F32)] * 2,
        tuple(qkv) + tuple(back),
        grid=(texts,),
        in_specs=[wide] * 2 + [full] + [whole(w) for w in back[1:3]] + [probs, inverse],
        out_specs=[wide] * 2 + [pl.BlockSpec((1, 3 * width), lambda i, *_: (0, 0))] * 2,
        scalars=(lens,),
        scratch=[pltpu.VMEM((length, width), F32)],
        name="attend_back",
    )


def program(dp_size, tensor_size):
    bits = dp_size.bit_length() - 1

    def pp_tensor(values, flip):
        return lax.ppermute(values, "tensor", [(i, i ^ flip) for i in range(tensor_size)])

    def pp_dp(values, bit):
        return lax.ppermute(values, "dp", [(i, i ^ (1 << bit)) for i in range(dp_size)])

    def on_device(
        inputs,
        lengths,
        cotangent,
        ln1_gain,
        ln1_bias,
        w_qkv,
        b_qv,
        w_out,
        b_out,
        ln2_gain,
        ln2_bias,
        w_up,
        b_up,
        w_down,
        b_down,
    ):
        t = lax.axis_index("tensor")
        d = lax.axis_index("dp")
        texts_all, part = inputs.shape[:2]
        texts = texts_all // tensor_size
        length = part * tensor_size
        rows = texts * length
        rels = range(tensor_size)
        local = w_qkv.shape[2]
        units = b_up.shape[0]
        inner = D // dp_size
        bit_of = [(d >> b) & 1 for b in range(bits)]
        clock = Clock()

        def pick(values, index, axis):
            return lax.dynamic_index_in_dim(values, index, axis, keepdims=False)

        def text_blocks(values):
            return [
                lax.dynamic_slice(values, ((t ^ r) * texts, 0, 0), (texts, part, D)) for r in rels
            ]

        def row_blocks(values):
            blocks = values.reshape(texts, tensor_size, part, D)
            return [pick(blocks, t ^ r, 1) for r in rels]

        def exchange(blocks):
            far = {r: pp_tensor(blocks[r], r) for r in (3, 2, 1)}
            return [blocks[0]] + [far[r] for r in (1, 2, 3)]

        def half(values):
            count = values.shape[0] // 2
            return lax.dynamic_slice_in_dim(values, bit_of[0] * count, count)

        class Chain:
            def __init__(self, lefts, slots, near, steps):
                self.steps = list(steps)
                self.dims = [len(slots)] + [2] * bits
                step = self.steps.pop(0)
                outer, index = self.place(step)
                if step == "y":
                    self.keep, self.sent = weight_grads(clock, lefts, slots, near, apart=True)
                elif inner % 16 == 0 and outer > len(slots):
                    split = (outer // len(slots), index)
                    self.sent, self.keep = weight_grads(clock, lefts, slots, near, split)
                else:
                    total = weight_grads(clock, lefts, slots, near)
                    self.sent, self.keep = self.halves(total, outer, index)
                self.fly(step)

            def place(self, step):
                axis = 0 if step == "y" else bits - step
                outer = 1
                for size in self.dims[:axis]:
                    outer *= size
                self.dims[axis] = 1
                return outer, 0 * t if step == "y" else bit_of[step]

            def halves(self, total, outer, index):
                view = total.reshape(outer, 2, -1, total.shape[-1])
                return pick(view, 1 - index, 1), pick(view, index, 1)

            def fly(self, step):
                self.flight = pp_tensor(self.sent, 2) if step == "y" else pp_dp(self.sent, step)

            def step(self):
                arrived = clock.after(self.flight)
                step = self.steps.pop(0)
                outer, index = self.place(step)
                if inner % 16 == 0:
                    self.sent, self.keep = add_split(clock, self.keep, arrived, outer, index)
                else:
                    total = (self.keep.astype(F32) + arrived.astype(F32)).astype(BF)
                    self.sent, self.keep = self.halves(total, outer, index)
                self.fly(step)

            def last(self):
                total = self.keep.astype(F32) + clock.after(self.flight).astype(F32)
                return total.reshape(-1, total.shape[-1])

        high = list(range(2, bits))

        def from_near(lefts, slots):
            return [pp_tensor(v, 1) for v in weight_grads(clock, lefts, slots, pieces=True)]

        x_own = text_blocks(inputs)
        x_blocks = exchange(x_own)
        wq_own = side_by_side(clock, tie(w_qkv, x_own[1]))
        wq_near = [pp_tensor(v, 1) for v in wq_own]
        small = jnp.concatenate([b_qv.reshape(-1), tie(b_up, wq_own[0])])
        small = [small] + [pp_tensor(small, r) for r in (1, 2, 3)]
        bqkv = [
            jnp.concatenate([s[:local], jnp.zeros((local,), F32), s[local : 2 * local]]) for s in small
        ]
        bup = [s[2 * local :] for s in small]
        lens = lax.dynamic_slice_in_dim(lengths, t * texts, texts)

        x, h1 = join_norm(clock, x_blocks, t, ln1_gain, ln1_bias)
        wq_far = [pp_tensor(clock.after(v), 2) for v in wq_own]
        wu_half = pp_tensor(half(clock.after(w_up)), 2)
        wo_near = pp_tensor(clock.after(w_out), 1)
        wq = [wq_own, wq_near]
        qkv = [project(clock, h1, wq[r], bqkv[r]) for r in (0, 1)]
        qkv[0] = tie(qkv[0], wo_near)
        attn_a = attend_call(clock, lens, qkv[:2], None, length)
        wo_far = pp_tensor(clock.after(w_out), 2)
        wu_near = pp_tensor(clock.after(w_up), 1)
        wd_near = pp_tensor(clock.after(w_down), 1)
        wq_far = [clock.after(v) for v in wq_far]
        wq += [wq_far, [pp_tensor(v, 1) for v in wq_far]]
        qkv += [project(clock, h1, wq[r], bqkv[r]) for r in (2, 3)]
        qkv[2] = tie(qkv[2], wu_near, wd_near)
        attn_b = attend_call(clock, lens, qkv[2:], None, length)
        wu_half = clock.after(wu_half)
        wu_other = pp_dp(wu_half, 0)
        cot_blocks = exchange(text_blocks(tie(cotangent, wu_half)))
        wo_far = clock.after(wo_far)
        wo = [w_out, wo_near, wo_far, pp_tensor(wo_far, 1)]
        ctx = [attn_a[0], attn_a[1], attn_b[0], attn_b[1]]
        resid, h2 = attention_out(clock, x, ctx, wo, (b_out, ln2_gain, ln2_bias))
        wu = [[w_up], [wu_near]]
        acts, slopes = [], []
        for r in rels:
            if r == 2:
                g_low, bias_down = join_mask(clock, [cot_blocks[0]] + [clock.after(b) for b in cot_blocks[1:]], t, lens)
                wd_far = pp_tensor(clock.after(w_down), 2)
                wu_far = order_halves(clock, wu_half, clock.after(wu_other), bit_of[0])
                wu += [wu_far, [pp_tensor(v, 1) for v in wu_far]]
            act, slope = up(clock, h2, wu[r], bup[r])
            acts.append(act)
            slopes.append(slope)

        near = from_near([g_low], [[(0, acts[1])], [(0, acts[3])]])
        down = Chain([g_low], [[(0, acts[0])], [(0, acts[2])]], near, [0, 1, "y"] + high)
        wd_far = clock.after(wd_far)
        wd = [w_down, wd_near, wd_far, pp_tensor(wd_far, 1)]
        dups_a, sums_a, dh2 = up_back(clock, g_low, wu[:2], wd[:2], slopes[:2], None, None, None)
        dups_b, sums_b, rest = up_back(clock, g_low, wu[2:], wd[2:], slopes[2:], dh2[0], resid, ln2_gain)
        dres, dres_low, gain_two, shift_two, bias_attn = rest
        dups, bias_up = dups_a + dups_b, sums_a + sums_b
        up_near = from_near([h2], [[(0, dups[1])], [(0, dups[3])]])
        down.step()
        grads_up = Chain([h2], [[(0, dups[0])], [(0, dups[2])]], up_near, ["y", 0, 1] + high)
        back = attend_call(clock, lens, qkv[2:], [dres_low] + wo[2:] + list(attn_b[2:]), length)
        dqkv_far, qkv_sums_far = back[:2], back[2:]
        near = from_near([h1, dres_low], [[(0, dqkv_far[1]), (1, ctx[3])]])
        down.step()
        q_far = Chain([h1, dres_low], [[(0, dqkv_far[0]), (1, ctx[2])]], near, [1, 0])
        back = attend_call(clock, lens, qkv[:2], [dres_low] + wo[:2] + list(attn_a[2:]), length)
        dqkv, qkv_sums = list(back[:2]) + list(dqkv_far), list(back[2:]) + list(qkv_sums_far)
        grads_up.step()
        if high:
            down.step()
        near = from_near([h1, dres_low], [[(0, dqkv[1]), (1, ctx[1])]])
        out_blocks = exchange(down_out(clock, resid, acts, wd, b_down, t, texts))
        q_own = Chain([h1, dres_low], [[(0, dqkv[0]), (1, ctx[0])]], near, [1, 0] + high)
        q_far.step()
        in_blocks, gain_one, shift_one = norm_one_back(clock, x, dres, dqkv, wq, ln1_gain, t, texts)
        in_blocks = exchange(in_blocks)
        layer_out = join_rows(clock, [out_blocks[0]] + [clock.after(b) for b in out_blocks[1:]], t)
        grads_up.step()
        up_full = jnp.zeros((tensor_size, units), F32)
        qv_full = jnp.zeros((tensor_size, 2, local), F32)
        for r in rels:
            up_full = lax.dynamic_update_slice(up_full, bias_up[r], (t ^ r, 0))
            sums = qkv_sums[r].reshape(3, local)
            sums = jnp.concatenate([sums[:1], sums[2:]], 0)
            qv_full = lax.dynamic_update_slice(qv_full, sums[None], (t ^ r, 0, 0))
        vectors = [gain_one, shift_one, gain_two, shift_two, bias_attn, bias_down]
        total = jnp.concatenate([v.reshape(-1) for v in vectors] + [qv_full.reshape(-1), up_full.reshape(-1)])

        def reduced(flip, tensor):
            moved = pp_tensor(total, flip) if tensor else pp_dp(total, flip)
            return clock.then(total + clock.after(moved))

        total = reduced(1, True)
        q_own.step()
        total = reduced(2, True)
        q_far_all = pp_tensor(q_far.last().astype(BF), 2)
        total = reduced(0, False)
        for bit in high:
            if bit != high[0]:
                down.step()
            grads_up.step()
            if bit == high[0]:
                arrived = clock.after(q_far_all).reshape(q_own.keep.shape)
                q_own.keep = (q_own.keep.astype(F32) + arrived.astype(F32)).astype(BF)
            q_own.step()
        total = reduced(1, False)
        grad_input = join_rows(clock, [in_blocks[0]] + [clock.after(b) for b in in_blocks[1:]], t)
        for bit in high:
            total = reduced(bit, False)
        grad_down, grad_up, both = down.last(), grads_up.last(), q_own.last()
        grad_qkv, grad_out = both[:, : 3 * local], both[:, 3 * local :]
        vector = [total[i * D : (i + 1) * D] for i in range(6)]
        rest = total[6 * D :]
        return (
            layer_out,
            grad_input,
            vector[0],
            vector[1],
            jnp.stack([grad_qkv[:, c * local : c * local + local] for c in range(3)]),
            pick(rest[: 2 * D].reshape(tensor_size, 2, local), t, 0),
            grad_out.T,
            vector[4],
            vector[2],
            vector[3],
            grad_up,
            pick(rest[2 * D :].reshape(tensor_size, units), t, 0),
            grad_down.T,
            vector[5],
        )

    return on_device


def solution(mesh):
    return jax.shard_map(
        program(mesh.shape["dp"], mesh.shape["tensor"]),
        mesh=mesh,
        in_specs=(
            P("dp", "tensor", None),
            P("dp"),
            P("dp", "tensor", None),
            P(),
            P(),
            P(None, None, "tensor"),
            P(None, "tensor"),
            P("tensor", None),
            P(),
            P(),
            P(),
            P(None, "tensor"),
            P("tensor"),
            P("tensor", None),
            P(),
        ),
        out_specs=(
            P("dp", "tensor", None),
            P("dp", "tensor", None),
            P(),
            P(),
            P(None, "dp", "tensor"),
            P(None, "tensor"),
            P("tensor", "dp"),
            P(),
            P(),
            P(),
            P("dp", "tensor"),
            P("tensor"),
            P("tensor", "dp"),
            P(),
        ),
        check_vma=False,
    )
```

time: 479 us -> 337 us (0.70)
  Pallas kernels: 30 us -> 170 us
  waiting for transfers between devices: 176 us -> 65.3 us
  matrix products: 108 us -> 0 us
  other arithmetic: 31.9 us -> 5.05 us
  starting transfers between devices: 64.9 us -> 47.2 us
  local copies, waits for them, and re-layouts: 60.2 us -> 43.2 us
    pallas_call x4 -> x40, Pallas kernels: 30 us -> 170 us  [call(): pl.pallas_call(body, out_shape=out_shape, grid_spec=pltpu.PrefetchScalarG...]
    dot_general x48 -> x0, matrix products: 108 us -> none  [dot(): lax.dot_general(left, right, (((left_dim,), (right_dim,)), ((), ())), pre...]
    ppermute x39 -> x48, waiting for transfers between devices: 136 us -> 49.8 us  [pp_tensor(): lax.ppermute(values, 'tensor', [(i, i ^ flip) for i in range(tensor_size)])]
    ppermute x18 -> x15, waiting for transfers between devices: 39.1 us -> 15.5 us  [pp_dp(): lax.ppermute(values, 'dp', [(i, i ^ 1 << bit) for i in range(dp_size)])]
    add x22 -> x5, other arithmetic: 12.6 us -> 0.03 us  [reduced(): return clock.then(total + clock.after(moved))]
    ppermute x18 -> x15, starting transfers between devices: 31.8 us -> 22.8 us  [pp_dp(): lax.ppermute(values, 'dp', [(i, i ^ 1 << bit) for i in range(dp_size)])]
    ppermute x39 -> x48, starting transfers between devices: 33.1 us -> 24.4 us  [pp_tensor(): lax.ppermute(values, 'tensor', [(i, i ^ flip) for i in range(tensor_size)])]
    dynamic_update_slice x20 -> x4, local copies, waits for them, and re-layouts: 8.58 us -> 0.24 us  [on_device(): up_full = lax.dynamic_update_slice(up_full, bias_up[r], (t ^ r, 0))]
  transfers between devices with their start and end apart: 57 -> 63, of which waited for: 24 -> 18; matrix products, arithmetic and copies ran while one was open for 39% -> 6% of each run, Pallas kernels for 6% -> 46%
where the time goes in v2:
time: 337 us; the launch traced here: 334 us
  Pallas kernels  170 us (50%)
  waiting for transfers between devices  65.3 us (19%)
  starting transfers between devices  47.2 us (14%)
  local copies, waits for them, and re-layouts  43.2 us (13%)
  other arithmetic  5.05 us (1%)
    pallas_call x40, Pallas kernels, call(): pl.pallas_call(body, out_shape=out_shape, grid_spec=pltpu.PrefetchScalarG...  170 us
    ppermute x48, waiting for transfers between devices, pp_tensor(): lax.ppermute(values, 'tensor', [(i, i ^ flip) for i in range(tensor_size)])  49.8 us
    unnamed x237, local copies, waits for them, and re-layouts  34.4 us
    ppermute x48, starting transfers between devices, pp_tensor(): lax.ppermute(values, 'tensor', [(i, i ^ flip) for i in range(tensor_size)])  24.4 us
    ppermute x15, starting transfers between devices, pp_dp(): lax.ppermute(values, 'dp', [(i, i ^ 1 << bit) for i in range(dp_size)])  22.8 us
    ppermute x15, waiting for transfers between devices, pp_dp(): lax.ppermute(values, 'dp', [(i, i ^ 1 << bit) for i in range(dp_size)])  15.5 us
  transfers between devices with their start and end apart: 63, of which 18 were waited for; matrix products, arithmetic and copies ran while one was open for 6% of the time, Pallas kernels for 46%

profile of v2, /device:TPU:0, one launch (start us, length us, event | category | flops | bytes accessed | tf_op | source)
XLA Modules:
  0.0 333.7 jit_solution(18324145150506832029)
XLA Ops:
  11.7 9.1 %collective-permute-done.1.refs_2_ = bf16[2,128,768]{2,1,0:T(8,128)(2,1)S(1)} collective-permute-done((bf16[2,128,768]{2,1,0:T(8,128)(2,1)}, bf16[2,128,768]{2,1,0:T(8,128)(2,1)S(1)}, u32[]{:S(2)}, u32[]{:S(2)}) %collective-permute-start.1) | collective-permute-done | bytes 393248 | tf_op jit(solution)/shard_map/ppermute | solution.py:584
  20.8 6.9 %collective-permute-done.2.refs_3_ = bf16[2,128,768]{2,1,0:T(8,128)(2,1)S(1)} collective-permute-done((bf16[2,128,768]{2,1,0:T(8,128)(2,1)}, bf16[2,128,768]{2,1,0:T(8,128)(2,1)S(1)}, u32[]{:S(2)}, u32[]{:S(2)}) %collective-permute-start.2) | collective-permute-done | bytes 393248 | tf_op jit(solution)/shard_map/ppermute | solution.py:584
  31.2 3.2 project.4.refs_0_
  37.5 8.9 %attend.2 = (bf16[1024,192]{1,0:T(8,128)(2,1)S(1)}, bf16[1024,192]{1,0:T(8,128)(2,1)S(1)}, bf16[2,6,512,512]{3,2,1,0:T(8,128)(2,1)}, f32[2,6,512]{2,1,0:T(8,128)S(1)}) custom-call(s32[2]{0:T(128)S(1)} %dynamic_slice.42.lens.n, bf16[1024,576]{1,0:T(8,128)(2,1)S(1)} %project.4.refs_0_, bf16[1024,576]{1,0:T(8,128)(2,1)S(1)} %project.5.refs_1_), custom_call_target="tpu_custom_call" | custom-call | tf_op jit(solution)/shard_map/attend/pallas_call | solution.py:58
  51.5 12.0 %collective-permute-done.9.refs_1_.refs_9_ = bf16[384,576]{1,0:T(8,128)(2,1)} collective-permute-done((bf16[384,576]{1,0:T(8,128)(2,1)}, bf16[384,576]{1,0:T(8,128)(2,1)}, u32[]{:S(2)}, u32[]{:S(2)}) %collective-permute-start.9) | collective-permute-done | bytes 442400 | tf_op jit(solution)/shard_map/ppermute | solution.py:584
  63.6 10.5 %collective-permute-done.8.refs_0_.refs_8_ = bf16[384,576]{1,0:T(8,128)(2,1)} collective-permute-done((bf16[384,576]{1,0:T(8,128)(2,1)S(1)}, bf16[384,576]{1,0:T(8,128)(2,1)}, u32[]{:S(2)}, u32[]{:S(2)}) %collective-permute-start.8) | collective-permute-done | bytes 442400 | tf_op jit(solution)/shard_map/ppermute | solution.py:584
  75.0 3.4 %project.6.refs_0_ = bf16[1024,576]{1,0:T(8,128)(2,1)S(1)} custom-call(bf16[1024,768]{1,0:T(8,128)(2,1)S(1)} %get-tuple-element.311.h_ref.refs_0_.refs_1_, f32[1,576]{1,0:T(1,128)S(1)} %reshape.231.bias_ref, bf16[384,576]{1,0:T(8,128)(2,1)} %collective-permute-done.8.refs_0_.refs_8_, bf16[384,576]{1,0:T(8,128)(2,1)} %collective-permute-done.9.refs_1_.refs_9_), custom_call_target="tpu_custom_call" | custom-call | tf_op jit(solution)/shard_map/project/pallas_call | solution.py:58
  80.7 9.0 %attend.3 = (bf16[1024,192]{1,0:T(8,128)(2,1)S(1)}, bf16[1024,192]{1,0:T(8,128)(2,1)S(1)}, bf16[2,6,512,512]{3,2,1,0:T(8,128)(2,1)}, f32[2,6,512]{2,1,0:T(8,128)S(1)}) custom-call(s32[2]{0:T(128)S(1)} %dynamic_slice.42.lens.n, bf16[1024,576]{1,0:T(8,128)(2,1)S(1)} %project.6.refs_0_, bf16[1024,576]{1,0:T(8,128)(2,1)S(1)} %project.7.refs_1_), custom_call_target="tpu_custom_call" | custom-call | tf_op jit(solution)/shard_map/attend/pallas_call | solution.py:58
  97.3 5.3 %attention_out.1 = (f32[1024,768]{1,0:T(8,128)}, bf16[1024,768]{1,0:T(8,128)(2,1)S(1)}) custom-call(bf16[1024,768]{1,0:T(8,128)(2,1)} %copy-done.16, bf16[1024,192]{1,0:T(8,128)(2,1)S(1)} %copy-done.33, bf16[1024,192]{1,0:T(8,128)(2,1)S(1)} %copy-done.36, bf16[1024,192]{1,0:T(8,128)(2,1)S(1)} %get-tuple-element.219.refs_2_.refs_4_, ...), custom_call_target="tpu_custom_call" | custom-call | tf_op jit(solution)/shard_map/attention_out/pallas_call | solution.py:58
  106.5 4.7 %up.5 = (bf16[1024,768]{1,0:T(8,128)(2,1)S(1)}, bf16[1024,768]{1,0:T(8,128)(2,1)S(1)}) custom-call(bf16[1024,768]{1,0:T(8,128)(2,1)S(1)} %get-tuple-element.274.h_ref.refs_0_, f32[1,768]{1,0:T(1,128)S(1)} %reshape.240.bias_ref, bf16[768,768]{1,0:T(8,128)(2,1)} %collective-permute-done.10.refs_0_.refs_1_), custom_call_target="tpu_custom_call" | custom-call | tf_op jit(solution)/shard_map/up/pallas_call | solution.py:58
  118.9 3.3 up.6
  124.4 3.3 up.7
  130.1 4.4 %weight_grads.8 = (bf16[768,384]{1,0:T(8,128)(2,1)S(1)}, bf16[768,384]{1,0:T(8,128)(2,1)S(1)}, bf16[768,384]{1,0:T(8,128)(2,1)S(1)}, bf16[768,384]{1,0:T(8,128)(2,1)S(1)}) custom-call(bf16[1024,768]{1,0:T(8,128)(2,1)S(1)} %get-tuple-element.259.refs_0_.refs_1_.g_ref, bf16[1024,768]{1,0:T(8,128)(2,1)S(1)} %get-tuple-element.233.refs_1_, ...), custom_call_target="tpu_custom_call" | custom-call | tf_op jit(solution)/shard_map/weight_grads/pallas_call | solution.py:58
  139.1 6.2 %weight_grads.9 = (bf16[2,384,768]{2,1,0:T(8,128)(2,1)}, bf16[2,384,768]{2,1,0:T(8,128)(2,1)S(1)}) custom-call(s32[1]{0:T(128)} %bitcast.5.at.refs_0_, bf16[1024,768]{1,0:T(8,128)(2,1)} %copy-done.3, bf16[1024,768]{1,0:T(8,128)(2,1)} %copy-done.14, bf16[1024,768]{1,0:T(8,128)(2,1)} %copy-done.15, bf16[768,384]{1,0:T(8,128)(2,1)S(1)} %collective-permute-done.24.refs_4_, ...), custom_call_target="tpu_custom_call" | custom-call | tf_op jit(solution)/shard_map/weight_grads/pallas_call | solution.py:58
  146.9 10.6 %up_back.2 = (bf16[1024,768]{1,0:T(8,128)(2,1)}, bf16[1024,768]{1,0:T(8,128)(2,1)}, f32[1,768]{1,0:T(1,128)S(1)}, f32[1,768]{1,0:T(1,128)S(1)}, f32[1024,768]{1,0:T(8,128)}) custom-call(bf16[1024,768]{1,0:T(8,128)(2,1)} %copy-done.3, bf16[768,768]{1,0:T(8,128)(2,1)S(1)} %copy-done.13, bf16[768,768]{1,0:T(8,128)(2,1)} %collective-permute-done.10.refs_0_.refs_1_, ...), custom_call_target="tpu_custom_call" | custom-call | tf_op jit(solution)/shard_map/up_back/pallas_call | solution.py:58
  157.6 12.1 %up_back.3 = (bf16[1024,768]{1,0:T(8,128)(2,1)}, bf16[1024,768]{1,0:T(8,128)(2,1)}, f32[1,768]{1,0:T(1,128)S(1)}, f32[1,768]{1,0:T(1,128)S(1)}, f32[1024,768]{1,...) custom-call(bf16[1024,768]{1,0:T(8,128)(2,1)} %copy-done.3, ...), custom_call_target="tpu_custom_call" | custom-call | tf_op jit(solution)/shard_map/up_back/pallas_call | solution.py:58
  169.6 5.2 %weight_grads.10 = (bf16[768,384]{1,0:T(8,128)(2,1)}, bf16[768,384]{1,0:T(8,128)(2,1)}, bf16[768,384]{1,0:T(8,128)(2,1)}, bf16[768,384]{1,0:T(8,128)(2,1)}) custom-call(bf16[1024,768]{1,0:T(8,128)(2,1)S(1)} %get-tuple-element.274.h_ref.refs_0_, bf16[1024,768]{1,0:T(8,128)(2,1)S(1)} %copy-done.56, bf16[1024,768]{1,0:T(8,128)(2,1)} %get-tuple-element.268.refs_2_), custom_call_target="tpu_custom_call" | custom-call | tf_op jit(solution)/shard_map/weight_grads/pallas_call | solution.py:58
  179.8 6.2 %weight_grads.11 = (bf16[1,768,768]{2,1,0:T(8,128)(2,1)S(1)}, bf16[1,768,768]{2,1,0:T(8,128)(2,1)}) custom-call(bf16[1024,768]{1,0:T(8,128)(2,1)} %copy-done, bf16[1024,768]{1,0:T(8,128)(2,1)} %get-tuple-element.258.refs_1_, bf16[1024,768]{1,0:T(8,128)(2,1)} %get-tuple-element.265.refs_2_, bf16[768,384]{1,0:T(8,128)(2,1)S(1)} %collective-permute-done.31.refs_3_, ...), custom_call_target="tpu_custom_call" | custom-call | tf_op jit(solution)/shard_map/weight_grads/pallas_call | solution.py:58
  190.5 11.9 %attend_back.2 = (bf16[1024,576]{1,0:T(8,128)(2,1)S(1)}, bf16[1024,576]{1,0:T(8,128)(2,1)S(1)}, f32[1,576]{1,0:T(1,128)S(1)}, f32[1,576]{1,0:T(1,128)S(1)}) custom-call(s32[2]{0:T(128)S(1)} %dynamic_slice.42.lens.n, bf16[1024,576]{1,0:T(8,128)(2,1)S(1)} %copy-done.9, bf16[1024,576]{1,0:T(8,128)(2,1)S(1)} %copy-done.11, ...), custom_call_target="tpu_custom_call" | custom-call | tf_op jit(solution)/shard_map/attend_back/pallas_call | solution.py:58
  203.6 3.4 %weight_grads.12 = (bf16[768,384]{1,0:T(8,128)(2,1)}, bf16[768,384]{1,0:T(8,128)(2,1)}) custom-call(bf16[1024,768]{1,0:T(8,128)(2,1)S(1)} %get-tuple-element.311.h_ref.refs_0_.refs_1_, bf16[1024,768]{1,0:T(8,128)(2,1)S(1)} %copy-done.1, bf16[1024,576]{1,0:T(8,128)(2,1)S(1)} %get-tuple-element.285.refs_2_.refs_3_, bf16[1024,192]{1,0:T(8,128)(2,1)S(1)} %copy-done.41), custom_call_target="tpu_custom_call" | custom-call | tf_op jit(solution)/shard_map/weight_grads/pallas_call | solution.py:58
  213.5 4.4 %weight_grads.13 = (bf16[1,384,768]{2,1,0:T(8,128)(2,1)}, bf16[1,384,768]{2,1,0:T(8,128)(2,1)S(1)}) custom-call(s32[1]{0:T(128)} %bitcast.4.at.refs_0_, bf16[1024,768]{1,0:T(8,128)(2,1)S(1)} %get-tuple-element.311.h_ref.refs_0_.refs_1_, bf16[1024,768]{1,0:T(8,128)(2,1)} %get-tuple-element.280.refs_2_.refs_1_, bf16[1024,576]{1,0:T(8,128)(2,1)S(1)} %copy-done.20, ...), custom_call_target="tpu_custom_call" | custom-call | tf_op jit(solution)/shard_map/weight_grads/pallas_call | solution.py:58
  219.1 11.5 %attend_back.3 = (bf16[1024,576]{1,0:T(8,128)(2,1)S(1)}, bf16[1024,576]{1,0:T(8,128)(2,1)S(1)}, f32[1,576]{1,0:T(1,128)S(1)}, f32[1,576]{1,0:T(1,128)S(1)}) custom-call(s32[2]{0:T(128)S(1)} %dynamic_slice.42.lens.n, bf16[1024,576]{1,0:T(8,128)(2,1)S(1)} %copy-done.5, bf16[1024,576]{1,0:T(8,128)(2,1)S(1)} %copy-done.7, ...), custom_call_target="tpu_custom_call" | custom-call | tf_op jit(solution)/shard_map/attend_back/pallas_call | solution.py:58
  235.7 3.5 %weight_grads.14 = (bf16[768,384]{1,0:T(8,128)(2,1)}, bf16[768,384]{1,0:T(8,128)(2,1)}) custom-call(bf16[1024,768]{1,0:T(8,128)(2,1)S(1)} %get-tuple-element.311.h_ref.refs_0_.refs_1_, bf16[1024,768]{1,0:T(8,128)(2,1)S(1)} %copy-done.2, bf16[1024,576]{1,0:T(8,128)(2,1)S(1)} %get-tuple-element.306.refs_2_.refs_1_, bf16[1024,192]{1,0:T(8,128)(2,1)S(1)} %copy-done.37), custom_call_target="tpu_custom_call" | custom-call | tf_op jit(solution)/shard_map/weight_grads/pallas_call | solution.py:58
  243.5 10.1 %down_out.1 = (bf16[2,128,768]{2,1,0:T(8,128)(2,1)S(1)}, bf16[2,128,768]{2,1,0:T(8,128)(2,1)}, bf16[2,128,768]{2,1,0:T(8,128)(2,1)}, bf16[2,128,768]{2,1,0:T(8,128)(2,1)}) custom-call(s32[1]{0:T(128)} %bitcast.at, f32[1024,768]{1,0:T(8,128)} %get-tuple-element.308.refs_9_.resid_ref, bf16[1024,768]{1,0:T(8,128)(2,1)} %copy-done.14, ...), custom_call_target="tpu_custom_call" | custom-call | tf_op jit(solution)/shard_map/down_out/pallas_call | solution.py:58
  255.6 4.6 %weight_grads.15 = (bf16[1,384,768]{2,1,0:T(8,128)(2,1)}, bf16[1,384,768]{2,1,0:T(8,128)(2,1)S(1)}) custom-call(s32[1]{0:T(128)} %bitcast.4.at.refs_0_, bf16[1024,768]{1,0:T(8,128)(2,1)S(1)} %get-tuple-element.311.h_ref.refs_0_.refs_1_, bf16[1024,768]{1,0:T(8,128)(2,1)} %get-tuple-element.280.refs_2_.refs_1_, bf16[1024,576]{1,0:T(8,128)(2,1)S(1)} %copy-done.23, ...), custom_call_target="tpu_custom_call" | custom-call | tf_op jit(solution)/shard_map/weight_grads/pallas_call | solution.py:58
  261.7 12.2 %norm_one_back.1 = (bf16[2,128,768]{2,1,0:T(8,128)(2,1)S(1)}, bf16[2,128,768]{2,1,0:T(8,128)(2,1)S(1)}, bf16[2,128,768]{2,1,0:T(8,128)(2,1)S(1)}, bf16[2,128,768...) custom-call(s32[1]{0:T(128)} %bitcast.at, bf16[1024,768]{1,0:T(8,128)(2,1)} %copy-done.16, ...), custom_call_target="tpu_custom_call" | custom-call | tf_op jit(solution)/shard_map/norm_one_back/pallas_call | solution.py:58
  299.4 3.7 %collective-permute-done.50 = f32[9216]{0:T(1024)S(1)} collective-permute-done((f32[9216]{0:T(1024)S(1)}, f32[9216]{0:T(1024)S(1)}, u32[]{:S(2)}, u32[]{:S(2)}) %collective-permute-start.50) | collective-permute-done | bytes 36896 | tf_op jit(solution)/shard_map/ppermute | solution.py:587
  303.4 3.7 %collective-permute-done.51 = f32[9216]{0:T(1024)S(1)} collective-permute-done((f32[9216]{0:T(1024)S(1)}, f32[9216]{0:T(1024)S(1)}, u32[]{:S(2)}, u32[]{:S(2)}) %collective-permute-start.51) | collective-permute-done | bytes 36896 | tf_op jit(solution)/shard_map/ppermute | solution.py:587
  307.1 3.7 %collective-permute-start.62 = (bf16[1,96,768]{2,1,0:T(8,128)(2,1)S(1)}, bf16[1,96,768]{2,1,0:T(8,128)(2,1)S(1)}, u32[]{:S(2)}, u32[]{:S(2)}) collective-permute-start(bf16[1,96,768]{2,1,0:T(8,128)(2,1)S(1)} %copy-done.91), channel_id=1, source_target_pairs={{0,16},{4,20},{8,24},{12,28},{16,0},{20,4},{24,8},{28,12},{1,17},{... | collective-permute-start | bytes 442376 | tf_op jit(solution)/shard_map/ppermute | solution.py:587
  314.0 3.6 %collective-permute-done.57.refs_2_ = bf16[2,128,768]{2,1,0:T(8,128)(2,1)S(1)} collective-permute-done((bf16[2,128,768]{2,1,0:T(8,128)(2,1)S(1)}, bf16[2,128,768]{2,1,0:T(8,128)(2,1)S(1)}, u32[]{:S(2)}, u32[]{:S(2)}) %collective-permute-start.57) | collective-permute-done | bytes 393248 | tf_op jit(solution)/shard_map/ppermute | solution.py:584
  317.7 4.4 %collective-permute-start.60 = (bf16[1,96,768]{2,1,0:T(8,128)(2,1)S(1)}, bf16[1,96,768]{2,1,0:T(8,128)(2,1)S(1)}, u32[]{:S(2)}, u32[]{:S(2)}) collective-permute-start(bf16[1,96,768]{2,1,0:T(8,128)(2,1)S(1)} %get-tuple-element.362), channel_id=1, source_target_pairs={{0,16},{4,20},{8,24},{12,28},{16,0},{20,4},{24,8},{28,12},{1,17},{... | collective-permute-start | bytes 442376 | tf_op jit(solution)/shard_map/ppermute | solution.py:587
  323.3 5.1 %collective-permute-done.59 = f32[9216]{0:T(1024)S(1)} collective-permute-done((f32[9216]{0:T(1024)S(1)}, f32[9216]{0:T(1024)S(1)}, u32[]{:S(2)}, u32[]{:S(2)}) %collective-permute-start.59) | collective-permute-done | bytes 36896 | tf_op jit(solution)/shard_map/ppermute | solution.py:587
  (443 shorter events, 121.0 us)
Async XLA Ops:
  8.1 22.4 %collective-permute-start.4 = (f32[1152]{0:T(1024)S(1)}, f32[1152]{0:T(1024)S(1)}, u32[]{:S(2)}, u32[]{:S(2)}) collective-permute-start(f32[1152]{0:T(1024)S(1)} %constant_dynamic-update-slice_fusion.2), channel_id=1, source_target_pairs={{0,1},{1,0},{2,3},{3,2},{4,5},{5,4},{6,7},{7,6},{8,9},{9,8},{10,11... | collective-permute-start | bytes 13832 | tf_op jit(solution)/shard_map/ppermute | solution.py:584
  10.1 17.6 %collective-permute-start.2 = (bf16[2,128,768]{2,1,0:T(8,128)(2,1)}, bf16[2,128,768]{2,1,0:T(8,128)(2,1)S(1)}, u32[]{:S(2)}, u32[]{:S(2)}) collective-permute-start(bf16[2,128,768]{2,1,0:T(8,128)(2,1)} %get-tuple-element.396), channel_id=1, source_target_pairs={{0,3},{1,2},{2,1},{3,0},{4,7},{5,6},{6,5},{7,4},{8,11},{9,10},{10,... | collective-permute-start | bytes 1179656 | tf_op jit(solution)/shard_map/ppermute | solution.py:584
  11.1 23.4 %collective-permute-start.5 = (bf16[384,576]{1,0:T(8,128)(2,1)S(1)}, bf16[384,576]{1,0:T(8,128)(2,1)S(1)}, u32[]{:S(2)}, u32[]{:S(2)}) collective-permute-start(bf16[384,576]{1,0:T(8,128)(2,1)S(1)} %get-tuple-element.210.refs_0_.refs_4_), channel_id=1, source_target_pairs={{0,1},{1,0},{2,3},{3,2},{4,5},{5,4},{6,7},{7,6},{8,9},{9,8},{10,11... | collective-permute-start | bytes 1327112 | tf_op jit(solution)/shard_map/ppermute | solution.py:584
  11.3 23.1 %collective-permute-start.6 = (bf16[384,576]{1,0:T(8,128)(2,1)}, bf16[384,576]{1,0:T(8,128)(2,1)S(1)}, u32[]{:S(2)}, u32[]{:S(2)}) collective-permute-start(bf16[384,576]{1,0:T(8,128)(2,1)} %get-tuple-element.212.refs_1_.refs_5_), channel_id=1, source_target_pairs={{0,1},{1,0},{2,3},{3,2},{4,5},{5,4},{6,7},{7,6},{8,9},{9,8},{10,11... | collective-permute-start | bytes 1327112 | tf_op jit(solution)/shard_map/ppermute | solution.py:584
  48.6 32.1 %collective-permute-start.10 = (bf16[768,768]{1,0:T(8,128)(2,1)S(1)}, bf16[768,768]{1,0:T(8,128)(2,1)}, u32[]{:S(2)}, u32[]{:S(2)}) collective-permute-start(bf16[768,768]{1,0:T(8,128)(2,1)S(1)} %copy-done.12), channel_id=1, source_target_pairs={{0,1},{1,0},{2,3},{3,2},{4,5},{5,4},{6,7},{7,6},{8,9},{9,8},{10,11... | collective-permute-start | bytes 3538952 | tf_op jit(solution)/shard_map/ppermute | solution.py:584
  48.7 32.1 %collective-permute-start.11 = (bf16[768,768]{1,0:T(8,128)(2,1)}, bf16[768,768]{1,0:T(8,128)(2,1)}, u32[]{:S(2)}, u32[]{:S(2)}) collective-permute-start(bf16[768,768]{1,0:T(8,128)(2,1)} %refs_4_.3), channel_id=1, source_target_pairs={{0,1},{1,0},{2,3},{3,2},{4,5},{5,4},{6,7},{7,6},{8,9},{9,8},{10,11... | collective-permute-start | bytes 3538952 | tf_op jit(solution)/shard_map/ppermute | solution.py:584
  49.4 24.7 %collective-permute-start.8 = (bf16[384,576]{1,0:T(8,128)(2,1)S(1)}, bf16[384,576]{1,0:T(8,128)(2,1)}, u32[]{:S(2)}, u32[]{:S(2)}) collective-permute-start(bf16[384,576]{1,0:T(8,128)(2,1)S(1)} %get-tuple-element.210.refs_0_.refs_4_), channel_id=1, source_target_pairs={{0,2},{1,3},{2,0},{3,1},{4,6},{5,7},{6,4},{7,5},{8,10},{9,11},{10,... | collective-permute-start | bytes 1327112 | tf_op jit(solution)/shard_map/ppermute | solution.py:584
  51.2 38.6 %collective-permute-start.17 = (bf16[384,768]{1,0:T(8,128)(2,1)S(1)}, bf16[384,768]{1,0:T(8,128)(2,1)S(1)}, u32[]{:S(2)}, u32[]{:S(2)}) collective-permute-start(bf16[384,768]{1,0:T(8,128)(2,1)S(1)} %constant_dynamic-slice_fusion.6), channel_id=1, source_target_pairs={{0,2},{1,3},{2,0},{3,1},{4,6},{5,7},{6,4},{7,5},{8,10},{9,11},{10,... | collective-permute-start | bytes 1769480 | tf_op jit(solution)/shard_map/ppermute | solution.py:584
  74.1 21.4 %collective-permute-start.15 = (bf16[192,768]{1,0:T(8,128)(2,1)S(1)}, bf16[192,768]{1,0:T(8,128)(2,1)S(1)}, u32[]{:S(2)}, u32[]{:S(2)}) collective-permute-start(bf16[192,768]{1,0:T(8,128)(2,1)S(1)} %copy-done.61), channel_id=1, source_target_pairs={{0,2},{1,3},{2,0},{3,1},{4,6},{5,7},{6,4},{7,5},{8,10},{9,11},{10,... | collective-permute-start | bytes 884744 | tf_op jit(solution)/shard_map/ppermute | solution.py:584
  89.9 25.4 %collective-permute-start.21 = (bf16[384,768]{1,0:T(8,128)(2,1)S(1)}, bf16[384,768]{1,0:T(8,128)(2,1)S(1)}, u32[]{:S(2)}, u32[]{:S(2)}) collective-permute-start(bf16[384,768]{1,0:T(8,128)(2,1)S(1)} %collective-permute-done.17.mine_ref), channel_id=1, source_target_pairs={{0,4},{4,0},{8,12},{12,8},{16,20},{20,16},{24,28},{28,24},{1,5},{5... | collective-permute-start | bytes 1769480 | tf_op jit(solution)/shard_map/ppermute | solution.py:587
  93.7 18.8 %collective-permute-start.20 = (bf16[2,128,768]{2,1,0:T(8,128)(2,1)}, bf16[2,128,768]{2,1,0:T(8,128)(2,1)S(1)}, u32[]{:S(2)}, u32[]{:S(2)}) collective-permute-start(bf16[2,128,768]{2,1,0:T(8,128)(2,1)} %get-tuple-element.392), channel_id=1, source_target_pairs={{0,3},{1,2},{2,1},{3,0},{4,7},{5,6},{6,5},{7,4},{8,11},{9,10},{10,... | collective-permute-start | bytes 1179656 | tf_op jit(solution)/shard_map/ppermute | solution.py:584
  94.0 18.5 %collective-permute-start.19 = (bf16[2,128,768]{2,1,0:T(8,128)(2,1)}, bf16[2,128,768]{2,1,0:T(8,128)(2,1)S(1)}, u32[]{:S(2)}, u32[]{:S(2)}) collective-permute-start(bf16[2,128,768]{2,1,0:T(8,128)(2,1)} %get-tuple-element.393), channel_id=1, source_target_pairs={{0,2},{1,3},{2,0},{3,1},{4,6},{5,7},{6,4},{7,5},{8,10},{9,11},{10,... | collective-permute-start | bytes 1179656 | tf_op jit(solution)/shard_map/ppermute | solution.py:584
  94.0 18.4 %collective-permute-start.18 = (bf16[2,128,768]{2,1,0:T(8,128)(2,1)}, bf16[2,128,768]{2,1,0:T(8,128)(2,1)S(1)}, u32[]{:S(2)}, u32[]{:S(2)}) collective-permute-start(bf16[2,128,768]{2,1,0:T(8,128)(2,1)} %get-tuple-element.394), channel_id=1, source_target_pairs={{0,1},{1,0},{2,3},{3,2},{4,5},{5,4},{6,7},{7,6},{8,9},{9,8},{10,11... | collective-permute-start | bytes 1179656 | tf_op jit(solution)/shard_map/ppermute | solution.py:584
  118.0 28.5 %collective-permute-start.28 = (bf16[768,768]{1,0:T(8,128)(2,1)}, bf16[768,768]{1,0:T(8,128)(2,1)S(1)}, u32[]{:S(2)}, u32[]{:S(2)}) collective-permute-start(bf16[768,768]{1,0:T(8,128)(2,1)} %refs_4_.3), channel_id=1, source_target_pairs={{0,2},{1,3},{2,0},{3,1},{4,6},{5,7},{6,4},{7,5},{8,10},{9,11},{10,... | collective-permute-start | bytes 3538952 | tf_op jit(solution)/shard_map/ppermute | solution.py:584
  146.4 29.5 %collective-permute-start.30 = (bf16[2,384,768]{2,1,0:T(8,128)(2,1)}, bf16[2,384,768]{2,1,0:T(8,128)(2,1)}, u32[]{:S(2)}, u32[]{:S(2)}) collective-permute-start(bf16[2,384,768]{2,1,0:T(8,128)(2,1)} %get-tuple-element.254), channel_id=1, source_target_pairs={{0,4},{4,0},{8,12},{12,8},{16,20},{20,16},{24,28},{28,24},{1,5},{5... | collective-permute-start | bytes 3538952 | tf_op jit(solution)/shard_map/ppermute | solution.py:587
  187.0 44.6 %collective-permute-start.38 = (bf16[1,768,768]{2,1,0:T(8,128)(2,1)}, bf16[1,768,768]{2,1,0:T(8,128)(2,1)}, u32[]{:S(2)}, u32[]{:S(2)}) collective-permute-start(bf16[1,768,768]{2,1,0:T(8,128)(2,1)} %get-tuple-element.299), channel_id=1, source_target_pairs={{0,2},{1,3},{2,0},{3,1},{4,6},{5,7},{6,4},{7,5},{8,10},{9,11},{10,... | collective-permute-start | bytes 3538952 | tf_op jit(solution)/shard_map/ppermute | solution.py:584
  188.4 19.7 %collective-permute-start.35 = (bf16[4,96,768]{2,1,0:T(8,128)(2,1)S(1)}, bf16[4,96,768]{2,1,0:T(8,128)(2,1)S(1)}, u32[]{:S(2)}, u32[]{:S(2)}) collective-permute-start(bf16[4,96,768]{2,1,0:T(8,128)(2,1)S(1)} %get-tuple-element.273), channel_id=1, source_target_pairs={{0,8},{4,12},{8,0},{12,4},{16,24},{20,28},{24,16},{28,20},{1,9},{5... | collective-permute-start | bytes 1769480 | tf_op jit(solution)/shard_map/ppermute | solution.py:587
  209.6 24.8 %collective-permute-start.39 = (bf16[1,192,768]{2,1,0:T(8,128)(2,1)}, bf16[1,192,768]{2,1,0:T(8,128)(2,1)}, u32[]{:S(2)}, u32[]{:S(2)}) collective-permute-start(bf16[1,192,768]{2,1,0:T(8,128)(2,1)} %get-tuple-element.290), channel_id=1, source_target_pairs={{0,2},{1,3},{2,0},{3,1},{4,6},{5,7},{6,4},{7,5},{8,10},{9,11},{10,... | collective-permute-start | bytes 884744 | tf_op jit(solution)/shard_map/ppermute | solution.py:584
  218.0 42.2 %collective-permute-start.42 = (bf16[1,384,768]{2,1,0:T(8,128)(2,1)}, bf16[1,384,768]{2,1,0:T(8,128)(2,1)}, u32[]{:S(2)}, u32[]{:S(2)}) collective-permute-start(bf16[1,384,768]{2,1,0:T(8,128)(2,1)} %get-tuple-element.293), channel_id=1, source_target_pairs={{0,8},{4,12},{8,0},{12,4},{16,24},{20,28},{24,16},{28,20},{1,9},{5... | collective-permute-start | bytes 1769480 | tf_op jit(solution)/shard_map/ppermute | solution.py:587
  240.0 15.1 %collective-permute-start.41 = (bf16[768,384]{1,0:T(8,128)(2,1)}, bf16[768,384]{1,0:T(8,128)(2,1)S(1)}, u32[]{:S(2)}, u32[]{:S(2)}) collective-permute-start(bf16[768,384]{1,0:T(8,128)(2,1)} %get-tuple-element.312), channel_id=1, source_target_pairs={{0,1},{1,0},{2,3},{3,2},{4,5},{5,4},{6,7},{7,6},{8,9},{9,8},{10,11... | collective-permute-start | bytes 1769480 | tf_op jit(solution)/shard_map/ppermute | solution.py:584
  240.2 47.5 %collective-permute-start.47 = (bf16[4,96,768]{2,1,0:T(8,128)(2,1)}, bf16[4,96,768]{2,1,0:T(8,128)(2,1)S(1)}, u32[]{:S(2)}, u32[]{:S(2)}) collective-permute-start(bf16[4,96,768]{2,1,0:T(8,128)(2,1)} %copy-done.87), channel_id=1, source_target_pairs={{0,4},{4,0},{8,12},{12,8},{16,20},{20,16},{24,28},{28,24},{1,5},{5... | collective-permute-start | bytes 1769480 | tf_op jit(solution)/shard_map/ppermute | solution.py:587
  253.6 28.9 %collective-permute-start.45 = (bf16[2,128,768]{2,1,0:T(8,128)(2,1)}, bf16[2,128,768]{2,1,0:T(8,128)(2,1)}, u32[]{:S(2)}, u32[]{:S(2)}) collective-permute-start(bf16[2,128,768]{2,1,0:T(8,128)(2,1)} %get-tuple-element.325), channel_id=1, source_target_pairs={{0,3},{1,2},{2,1},{3,0},{4,7},{5,6},{6,5},{7,4},{8,11},{9,10},{10,... | collective-permute-start | bytes 1179656 | tf_op jit(solution)/shard_map/ppermute | solution.py:584
  253.6 31.5 %collective-permute-start.44 = (bf16[2,128,768]{2,1,0:T(8,128)(2,1)}, bf16[2,128,768]{2,1,0:T(8,128)(2,1)}, u32[]{:S(2)}, u32[]{:S(2)}) collective-permute-start(bf16[2,128,768]{2,1,0:T(8,128)(2,1)} %get-tuple-element.323), channel_id=1, source_target_pairs={{0,2},{1,3},{2,0},{3,1},{4,6},{5,7},{6,4},{7,5},{8,10},{9,11},{10,... | collective-permute-start | bytes 1179656 | tf_op jit(solution)/shard_map/ppermute | solution.py:584
  255.1 30.1 %collective-permute-start.43 = (bf16[2,128,768]{2,1,0:T(8,128)(2,1)}, bf16[2,128,768]{2,1,0:T(8,128)(2,1)}, u32[]{:S(2)}, u32[]{:S(2)}) collective-permute-start(bf16[2,128,768]{2,1,0:T(8,128)(2,1)} %get-tuple-element.321), channel_id=1, source_target_pairs={{0,1},{1,0},{2,3},{3,2},{4,5},{5,4},{6,7},{7,6},{8,9},{9,8},{10,11... | collective-permute-start | bytes 1179656 | tf_op jit(solution)/shard_map/ppermute | solution.py:584
  260.2 29.9 %collective-permute-start.49 = (bf16[1,384,768]{2,1,0:T(8,128)(2,1)}, bf16[1,384,768]{2,1,0:T(8,128)(2,1)S(1)}, u32[]{:S(2)}, u32[]{:S(2)}) collective-permute-start(bf16[1,384,768]{2,1,0:T(8,128)(2,1)} %get-tuple-element.313), channel_id=1, source_target_pairs={{0,8},{4,12},{8,0},{12,4},{16,24},{20,28},{24,16},{28,20},{1,9},{5... | collective-permute-start | bytes 1769480 | tf_op jit(solution)/shard_map/ppermute | solution.py:587
  294.0 16.8 %collective-permute-start.55 = (bf16[2,96,768]{2,1,0:T(8,128)(2,1)S(1)}, bf16[2,96,768]{2,1,0:T(8,128)(2,1)S(1)}, u32[]{:S(2)}, u32[]{:S(2)}) collective-permute-start(bf16[2,96,768]{2,1,0:T(8,128)(2,1)S(1)} %get-tuple-element.349), channel_id=1, source_target_pairs={{0,4},{4,0},{8,12},{12,8},{16,20},{20,16},{24,28},{28,24},{1,5},{5... | collective-permute-start | bytes 884744 | tf_op jit(solution)/shard_map/ppermute | solution.py:587
  296.0 15.1 %collective-permute-start.58 = (bf16[2,128,768]{2,1,0:T(8,128)(2,1)S(1)}, bf16[2,128,768]{2,1,0:T(8,128)(2,1)S(1)}, u32[]{:S(2)}, u32[]{:S(2)}) collective-permute-start(bf16[2,128,768]{2,1,0:T(8,128)(2,1)S(1)} %copy-done.89), channel_id=1, source_target_pairs={{0,3},{1,2},{2,1},{3,0},{4,7},{5,6},{6,5},{7,4},{8,11},{9,10},{10,... | collective-permute-start | bytes 1179656 | tf_op jit(solution)/shard_map/ppermute | solution.py:584
  299.0 18.7 %collective-permute-start.57 = (bf16[2,128,768]{2,1,0:T(8,128)(2,1)S(1)}, bf16[2,128,768]{2,1,0:T(8,128)(2,1)S(1)}, u32[]{:S(2)}, u32[]{:S(2)}) collective-permute-start(bf16[2,128,768]{2,1,0:T(8,128)(2,1)S(1)} %get-tuple-element.367), channel_id=1, source_target_pairs={{0,2},{1,3},{2,0},{3,1},{4,6},{5,7},{6,4},{7,5},{8,10},{9,11},{10,... | collective-permute-start | bytes 1179656 | tf_op jit(solution)/shard_map/ppermute | solution.py:584
  303.1 19.0 %collective-permute-start.56 = (bf16[2,128,768]{2,1,0:T(8,128)(2,1)S(1)}, bf16[2,128,768]{2,1,0:T(8,128)(2,1)S(1)}, u32[]{:S(2)}, u32[]{:S(2)}) collective-permute-start(bf16[2,128,768]{2,1,0:T(8,128)(2,1)S(1)} %get-tuple-element.365), channel_id=1, source_target_pairs={{0,1},{1,0},{2,3},{3,2},{4,5},{5,4},{6,7},{7,6},{8,9},{9,8},{10,11... | collective-permute-start | bytes 1179656 | tf_op jit(solution)/shard_map/ppermute | solution.py:584
  307.1 21.3 %collective-permute-start.62 = (bf16[1,96,768]{2,1,0:T(8,128)(2,1)S(1)}, bf16[1,96,768]{2,1,0:T(8,128)(2,1)S(1)}, u32[]{:S(2)}, u32[]{:S(2)}) collective-permute-start(bf16[1,96,768]{2,1,0:T(8,128)(2,1)S(1)} %copy-done.91), channel_id=1, source_target_pairs={{0,16},{4,20},{8,24},{12,28},{16,0},{20,4},{24,8},{28,12},{1,17},{... | collective-permute-start | bytes 442376 | tf_op jit(solution)/shard_map/ppermute | solution.py:587
  310.8 17.5 %collective-permute-start.61 = (bf16[1,96,768]{2,1,0:T(8,128)(2,1)S(1)}, bf16[1,96,768]{2,1,0:T(8,128)(2,1)S(1)}, u32[]{:S(2)}, u32[]{:S(2)}) collective-permute-start(bf16[1,96,768]{2,1,0:T(8,128)(2,1)S(1)} %get-tuple-element.358), channel_id=1, source_target_pairs={{0,16},{4,20},{8,24},{12,28},{16,0},{20,4},{24,8},{28,12},{1,17},{... | collective-permute-start | bytes 442376 | tf_op jit(solution)/shard_map/ppermute | solution.py:587
  311.1 17.3 %collective-permute-start.59 = (f32[9216]{0:T(1024)S(1)}, f32[9216]{0:T(1024)S(1)}, u32[]{:S(2)}, u32[]{:S(2)}) collective-permute-start(f32[9216]{0:T(1024)S(1)} %add.84), channel_id=1, source_target_pairs={{0,16},{4,20},{8,24},{12,28},{16,0},{20,4},{24,8},{28,12},{1,17},{... | collective-permute-start | bytes 110600 | tf_op jit(solution)/shard_map/ppermute | solution.py:587
  (145 other events, 1127.0 us)

commit v3 on v2

--- a/solution.py
+++ b/solution.py
@@ -53,11 +53,13 @@
 
 
 def call(clock, body, out_shape, operands, *, grid=(), in_specs=None, out_specs=None, scalars=(), scratch=(),
-         name=None):
+         name=None, flops=0, plain=False):
     operands = (clock.after(operands[0]),) + tuple(operands[1:])
+    if plain:
+        operands = [pltpu.with_memory_space_constraint(v, pltpu.HBM) for v in operands]
     out = pl.pallas_call(
         body,
-        out_shape=out_shape,
+        out_shape=jax.tree.map(lambda v: pltpu.HBM(v.shape, v.dtype), out_shape),
         grid_spec=pltpu.PrefetchScalarGridSpec(
             num_scalar_prefetch=len(scalars),
             grid=grid,
@@ -66,7 +68,7 @@
             scratch_shapes=scratch,
         ),
         compiler_params=pltpu.CompilerParams(vmem_limit_bytes=48 << 20),
-        cost_estimate=pl.CostEstimate(flops=0, bytes_accessed=0, transcendentals=0),
+        cost_estimate=pl.CostEstimate(flops=flops, bytes_accessed=0, transcendentals=0),
         name=name,
     )(*scalars, *operands)
     return clock.then(out)
@@ -92,18 +94,6 @@
     return call(
         clock, body, out, (w,), grid=(1,), in_specs=[whole(w)], out_specs=[whole(v) for v in out],
         name="side_by_side",
-    )
-
-
-def order_halves(clock, mine, other, index):
-    def body(at, mine_ref, other_ref, first_ref, second_ref):
-        keep = at[0] == 0
-        first_ref[...] = jnp.where(keep, mine_ref[...], other_ref[...])
-        second_ref[...] = jnp.where(keep, other_ref[...], mine_ref[...])
-
-    return call(
-        clock, body, [shape_of(mine.shape)] * 2, (mine, other), grid=(1,), in_specs=[whole(mine), whole(other)],
-        out_specs=[whole(mine), whole(mine)], scalars=(index.reshape(1),), name="order_halves",
     )
 
 
@@ -145,7 +135,7 @@
     )
 
 
-def attention_out(clock, x, ctx, w, vectors):
+def attention_out(clock, x, ctx, w, vectors, cost=0):
     count = len(ctx)
 
     def body(x_ref, *refs):
@@ -162,11 +152,11 @@
     return call(
         clock, body, out, (x, *ctx, *w, *vectors), grid=(4,),
         in_specs=[row_block(v, 4) for v in (x, *ctx)] + [whole(v) for v in (*w, *vectors)],
-        out_specs=[row_block(v, 4) for v in out], name="attention_out",
-    )
-
-
-def up(clock, h, w, bias):
+        out_specs=[row_block(v, 4) for v in out], name="attention_out", flops=cost, plain=True,
+    )
+
+
+def up(clock, h, w, bias, cost=0):
     def body(h_ref, bias_ref, *refs):
         upper = times(h_ref[...], refs[:-2]) + bias_ref[...]
         below = 0.5 * (1.0 + lax.erf(upper * (0.5**0.5)))
@@ -178,7 +168,7 @@
     out = [shape_of((h.shape[0], bias.shape[1]))] * 2
     return call(
         clock, body, out, (h, bias, *w), grid=(4,), in_specs=[row_block(h, 4), whole(bias)] + [whole(v) for v in w],
-        out_specs=[row_block(v, 4) for v in out], name="up",
+        out_specs=[row_block(v, 4) for v in out], name="up", flops=cost,
     )
 
 
@@ -192,22 +182,34 @@
         @pl.when(place // (count // 2) == late)
         def _():
             start = pl.multiple_of((place % (count // 2)) * part, part)
-            refs[r][pl.ds(text, 1)] = scratch[pl.ds(start, part), :][None]
+            rows = scratch[pl.ds(start, part), :]
+            if r < 2:
+                refs[r][pl.ds(text, 1)] = rows[None]
+            else:
+                refs[2][pl.ds(place % 2, 1), pl.ds(text, 1)] = rows[None, None]
+
+
+def owner_shapes(texts, count, rows, width):
+    block = (texts, rows // texts // count, width)
+    return [shape_of(block), shape_of(block), shape_of((2, *block))]
 
 
 def down_out(clock, resid, acts, w, bias, me, texts):
     count = len(acts)
+    sizes = [len(pieces) for pieces in w]
+    w = [v for pieces in w for v in pieces]
     steps = texts * 2
 
     def body(at, resid_ref, *refs):
-        act_refs, w_refs, (bias_ref,), outs, (scratch,) = split_refs(refs, (count, count, 1, count, 1))
+        act_refs, w_refs, (bias_ref,), outs, (scratch,) = split_refs(refs, (count, len(w), 1, 3, 1))
+        w_refs = split_refs(w_refs, sizes)
         total = resid_ref[...] + bias_ref[...]
         for r in range(count):
-            total = total + dot(act_refs[r][...], w_refs[r][...], 1, 0)
+            total = total + times(act_refs[r], w_refs[r])
         to_owner(outs, at, total, scratch, count)
 
     bias = bias.reshape(1, -1)
-    out = [shape_of((texts, resid.shape[0] // texts // count, resid.shape[1]))] * count
+    out = owner_shapes(texts, count, *resid.shape)
     return call(
         clock, body, out, (resid, *acts, *w, bias), grid=(steps,),
         in_specs=[row_block(v, steps) for v in (resid, *acts)] + [whole(v) for v in (*w, bias)],
@@ -224,7 +226,7 @@
 
     def body(at, x_ref, dres_ref, *refs):
         grads, w_refs, (gain_ref,), outs, (gain_sum, shift_sum, scratch) = split_refs(
-            refs, (count, len(flat), 1, count, 3)
+            refs, (count, len(flat), 1, 3, 3)
         )
         w_refs = split_refs(w_refs, sizes)
         total = None
@@ -243,14 +245,18 @@
         to_owner(outs, at, dres_ref[...] + norm_back(total, normal, rstd, gain_ref[...]), scratch, count)
 
     gain = gain.reshape(1, -1)
-    out = [shape_of((texts, x.shape[0] // texts // count, x.shape[1]))] * count + [shape_of(gain.shape, F32)] * 2
+    out = owner_shapes(texts, count, *x.shape) + [shape_of(gain.shape, F32)] * 2
     out = call(
         clock, body, out, (x, dres, *dqkv, *flat, gain), grid=(steps,),
         in_specs=[row_block(v, steps) for v in (x, dres, *dqkv)] + [whole(v) for v in (*flat, gain)],
         out_specs=[whole(v) for v in out], scalars=(me.reshape(1),),
         scratch=[pltpu.VMEM((x.shape[0] // steps, x.shape[1]), BF)], name="norm_one_back",
     )
-    return out[:count], out[count], out[count + 1]
+    return out[:3], out[3], out[4]
+
+
+def block_of(refs, at, r, i):
+    return refs[r][i] if refs[r].ndim == 3 else refs[r][at[0] % 2, i]
 
 
 def join_norm(clock, blocks, me, gain, shift):
@@ -287,7 +293,7 @@
                 place = (at[0] ^ r) * part
                 start = pl.multiple_of(i * count * part + place, part)
                 live = lax.broadcasted_iota(jnp.int32, (part, width), 0) + place < n[i]
-                values = jnp.where(live, ins[r][i].astype(F32), 0.0)
+                values = jnp.where(live, block_of(ins, at, r, i).astype(F32), 0.0)
                 total = total + jnp.sum(values, 0, keepdims=True)
                 g_ref[pl.ds(start, part), :] = values.astype(BF)
         sum_ref[...] = total
@@ -299,34 +305,38 @@
     )
 
 
-def join_rows(clock, blocks, me):
+def join_rows(clock, blocks, me, cost=0):
     texts = blocks[0].shape[0]
     count = len(blocks)
 
     def body(at, *refs):
         for r in range(count):
-            refs[count][pl.ds((at[0] ^ r) * texts, texts)] = refs[r][...]
+            for i in range(texts):
+                refs[count][pl.ds((at[0] ^ r) * texts + i, 1)] = block_of(refs, at, r, i)[None]
 
     out = shape_of((texts * count,) + blocks[0].shape[1:])
     return call(
         clock, body, out, blocks, grid=(1,), in_specs=[whole(v) for v in blocks], out_specs=whole(out),
-        scalars=(me.reshape(1),), name="join_rows",
+        scalars=(me.reshape(1),), name="join_rows", flops=cost,
     )
 
 
 def up_back(clock, g, ups, downs, slopes, base, resid, gain):
     rows, width = g.shape
     count = len(ups)
-    units = downs[0].shape[0]
+    units = slopes[0].shape[1]
+    down_sizes = [len(pieces) for pieces in downs]
+    downs = [v for pieces in downs for v in pieces]
     sizes = [len(pieces) for pieces in ups]
     flat = [v for pieces in ups for v in pieces]
     last = base is not None
 
     def body(g_ref, *refs):
         up_refs, down_refs, slope_refs, more, grad_refs, sum_refs, outs = split_refs(
-            refs, (len(flat), count, count, 3 if last else 0, count, count, 5 if last else 1)
+            refs, (len(flat), len(downs), count, 3 if last else 0, count, count, 5 if last else 1)
         )
         up_refs = split_refs(up_refs, sizes)
+        down_refs = split_refs(down_refs, down_sizes)
         grad = g_ref[...]
         total = more[0][...] if last else None
 
@@ -336,7 +346,7 @@
                 ref[...] = jnp.zeros_like(ref)
 
         for s in range(count):
-            upper = dot(grad, down_refs[s][...], 1, 1) * slope_refs[s][...].astype(F32)
+            upper = times_turned(grad, down_refs[s]) * slope_refs[s][...].astype(F32)
             sum_refs[s][...] += jnp.sum(upper, 0, keepdims=True)
             low = upper.astype(BF)
             grad_refs[s][...] = low
@@ -375,7 +385,7 @@
     return list(out[:count]), list(out[count : 2 * count]), out[2 * count :]
 
 
-def weight_grads(clock, lefts, slots, near=None, split=None, apart=False, pieces=False):
+def weight_grads(clock, lefts, slots, near=None, split=None, apart=False, pieces=False, extra=None):
     rows, width = lefts[0].shape
     columns = sum(right.shape[1] for _, right in slots[0])
     count = len(slots)
@@ -388,7 +398,9 @@
         left_refs, refs = refs[: len(lefts)], refs[len(lefts) :]
         right_refs, refs = list(refs[: len(rights)]), refs[len(rights) :]
         if near is not None:
-            near_refs, refs = refs[: 2 * count], refs[2 * count :]
+            near_refs, refs = refs[: len(near)], refs[len(near) :]
+        if extra is not None:
+            extra_ref, refs = refs[0], refs[1:]
         for s, slot in enumerate(slots):
             start = 0
             for which, right in slot:
@@ -403,6 +415,8 @@
                         value = product[:, here]
                         if near is not None:
                             value = value + near_refs[2 * s + i][:, there].astype(F32)
+                        if extra is not None:
+                            value = value + extra_ref[s, :, low:high].astype(F32)
                         if pieces:
                             refs[2 * s + i][:, there] = value.astype(BF)
                         elif apart:
@@ -422,7 +436,7 @@
     tall = pl.BlockSpec((count, half, columns), lambda i, *_: (0, i, 0))
     narrow = pl.BlockSpec((half, columns // 2), lambda i, *_: (i, 0))
     short = pl.BlockSpec((count, half // 2, columns), lambda i, *_: (0, i, 0))
-    operands = (*lefts, *rights) + (() if near is None else tuple(near))
+    operands = (*lefts, *rights) + (() if near is None else tuple(near)) + (() if extra is None else (extra,))
     if pieces:
         out_shape = [shape_of((width, columns // 2))] * (2 * count)
         out_specs = [narrow] * (2 * count)
@@ -438,7 +452,7 @@
         out_shape,
         operands,
         grid=(2,),
-        in_specs=[left] * len(lefts) + [whole(v) for v in rights] + ([] if near is None else [narrow] * len(near)),
+        in_specs=[left] * len(lefts) + [whole(v) for v in rights] + ([] if near is None else [narrow] * len(near)) + ([] if extra is None else [tall]),
         out_specs=out_specs,
         scalars=() if split is None else (split[1].reshape(1),),
         scratch=[] if split is None else [pltpu.VMEM((half, columns), F32)],
@@ -465,6 +479,31 @@
         out_specs=[short] * 2,
         scalars=(jnp.asarray(index, jnp.int32).reshape(1),),
         name="add_split",
+    )
+
+
+def pack(clock, shared, units, projected, me):
+    count = len(units)
+    first = len(shared)
+
+    def body(at, *refs):
+        shared_refs, unit_refs, q_refs, (out_ref,) = split_refs(refs, (first, count, count, 1))
+        out_ref[...] = jnp.zeros_like(out_ref)
+        for i in range(first):
+            out_ref[i : i + 1, :] = shared_refs[i][...]
+        for r in range(count):
+            width = q_refs[r].shape[1] // 3
+            row = pl.ds(first + (at[0] ^ r), 1)
+            out_ref[row, : unit_refs[r].shape[1]] = unit_refs[r][...]
+            row = pl.ds(first + count + (at[0] ^ r), 1)
+            out_ref[row, :width] = q_refs[r][:, :width]
+            out_ref[row, width : 2 * width] = q_refs[r][:, 2 * width :]
+
+    out = shape_of((first + 2 * count, max(D, units[0].shape[1])), F32)
+    operands = (*shared, *units, *projected)
+    return call(
+        clock, body, out, operands, grid=(1,), in_specs=[whole(v) for v in operands], out_specs=whole(out),
+        scalars=(me.reshape(1),), name="pack",
     )
 
 
@@ -540,7 +579,7 @@
         pl.when((n > live - step) & (n <= live))(functools.partial(rows, live))
 
 
-def attend_call(clock, lens, qkv, back, length):
+def attend_call(clock, lens, qkv, back, length, cost=0):
     texts = lens.shape[0]
     width = qkv[0].shape[1] // 3
     heads = width // HD
@@ -562,6 +601,7 @@
             out_specs=[slim] * 2 + [probs, inverse],
             scalars=(lens,),
             name="attend",
+            flops=cost,
         )
     return call(
         clock,
@@ -575,6 +615,9 @@
         scratch=[pltpu.VMEM((length, width), F32)],
         name="attend_back",
     )
+
+
+COST_FAR, COST_OUT, COST_END = 14 * 10**9, 6 * 10**9, 2 * 10**9
 
 
 def program(dp_size, tensor_size):
@@ -615,6 +658,7 @@
         inner = D // dp_size
         bit_of = [(d >> b) & 1 for b in range(bits)]
         clock = Clock()
+        chains = []
 
         def pick(values, index, axis):
             return lax.dynamic_index_in_dim(values, index, axis, keepdims=False)
@@ -624,20 +668,24 @@
                 lax.dynamic_slice(values, ((t ^ r) * texts, 0, 0), (texts, part, D)) for r in rels
             ]
 
-        def row_blocks(values):
-            blocks = values.reshape(texts, tensor_size, part, D)
-            return [pick(blocks, t ^ r, 1) for r in rels]
-
         def exchange(blocks):
             far = {r: pp_tensor(blocks[r], r) for r in (3, 2, 1)}
             return [blocks[0]] + [far[r] for r in (1, 2, 3)]
 
-        def half(values):
-            count = values.shape[0] // 2
-            return lax.dynamic_slice_in_dim(values, bit_of[0] * count, count)
+        class Exchange:
+            def __init__(self, own, near, far):
+                self.own, self.near, self.far = own, near, pp_tensor(far, 2)
+
+            def forward(self):
+                self.far = clock.after(self.far)
+                self.near = pp_tensor(clock.after(self.near), 1)
+                self.last = pp_tensor(pick(self.far, 1 - t % 2, 0), 1)
+
+            def blocks(self):
+                return [self.own, clock.after(self.near), self.far, clock.after(self.last)]
 
         class Chain:
-            def __init__(self, lefts, slots, near, steps):
+            def __init__(self, lefts, slots, near, steps, extra=None):
                 self.steps = list(steps)
                 self.dims = [len(slots)] + [2] * bits
                 step = self.steps.pop(0)
@@ -646,9 +694,9 @@
                     self.keep, self.sent = weight_grads(clock, lefts, slots, near, apart=True)
                 elif inner % 16 == 0 and outer > len(slots):
                     split = (outer // len(slots), index)
-                    self.sent, self.keep = weight_grads(clock, lefts, slots, near, split)
+                    self.sent, self.keep = weight_grads(clock, lefts, slots, near, split, extra=extra)
                 else:
-                    total = weight_grads(clock, lefts, slots, near)
+                    total = weight_grads(clock, lefts, slots, near, extra=extra)
                     self.sent, self.keep = self.halves(total, outer, index)
                 self.fly(step)
 
@@ -684,60 +732,87 @@
 
         high = list(range(2, bits))
 
+        always = (lengths[0] | 1) != 0
+
+        def block(steps, *operands):
+            operands = (clock.after(operands[0]),) + operands[1:]
+
+            def run(*values):
+                clock.last = None
+                return steps(*values)
+
+            saved = [(list(chain.steps), list(chain.dims)) for chain in chains]
+            shapes = jax.eval_shape(lambda *v: run(*v), *operands)
+            for chain, (left, dims) in zip(chains, saved):
+                chain.steps, chain.dims = left, dims
+            out = lax.cond(
+                always, run, lambda *_: jax.tree.map(lambda v: jnp.zeros(v.shape, v.dtype), shapes), *operands
+            )
+            clock.last = None
+            return clock.then(out)
+
         def from_near(lefts, slots):
             return [pp_tensor(v, 1) for v in weight_grads(clock, lefts, slots, pieces=True)]
 
         x_own = text_blocks(inputs)
         x_blocks = exchange(x_own)
-        wq_own = side_by_side(clock, tie(w_qkv, x_own[1]))
+        wq_own = side_by_side(clock, tie(w_qkv, *x_own[1:]))
         wq_near = [pp_tensor(v, 1) for v in wq_own]
-        small = jnp.concatenate([b_qv.reshape(-1), tie(b_up, wq_own[0])])
-        small = [small] + [pp_tensor(small, r) for r in (1, 2, 3)]
+        wo_near = pp_tensor(tie(w_out, x_blocks[1]), 1)
+        small = jnp.concatenate([b_qv.reshape(-1), tie(b_up, x_blocks[1])])
+        small = jnp.stack([small, pp_tensor(small, 1)])
+        small = list(small) + list(pp_tensor(small, 2))
         bqkv = [
             jnp.concatenate([s[:local], jnp.zeros((local,), F32), s[local : 2 * local]]) for s in small
         ]
         bup = [s[2 * local :] for s in small]
         lens = lax.dynamic_slice_in_dim(lengths, t * texts, texts)
 
+
+        x_blocks[0] = tie(x_blocks[0], wo_near, *wq_near)
+        wq_far = [pp_tensor(tie(v, x_blocks[3]), 2) for v in wq_own]
+        cut = w_up.shape[0] // 2
+        up_first, up_second = jnp.concatenate([w_up[:cut], w_out], 0), w_up[cut:]
+        first_far, second_far = [pp_tensor(tie(v, x_blocks[3]), 2) for v in (up_first, up_second)]
+        cot_far = lax.dynamic_slice_in_dim(cotangent, (t // 2 ^ 1) * 2 * texts, 2 * texts)
+        cot_own = text_blocks(cotangent)
+        cot = Exchange(cot_own[0], cot_own[1], tie(cot_far, x_blocks[3]).reshape(2, texts, part, D))
+        wd_far = pp_tensor(tie(w_down, x_blocks[3]), 2)
         x, h1 = join_norm(clock, x_blocks, t, ln1_gain, ln1_bias)
-        wq_far = [pp_tensor(clock.after(v), 2) for v in wq_own]
-        wu_half = pp_tensor(half(clock.after(w_up)), 2)
-        wo_near = pp_tensor(clock.after(w_out), 1)
         wq = [wq_own, wq_near]
         qkv = [project(clock, h1, wq[r], bqkv[r]) for r in (0, 1)]
-        qkv[0] = tie(qkv[0], wo_near)
         attn_a = attend_call(clock, lens, qkv[:2], None, length)
-        wo_far = pp_tensor(clock.after(w_out), 2)
-        wu_near = pp_tensor(clock.after(w_up), 1)
-        wd_near = pp_tensor(clock.after(w_down), 1)
         wq_far = [clock.after(v) for v in wq_far]
-        wq += [wq_far, [pp_tensor(v, 1) for v in wq_far]]
-        qkv += [project(clock, h1, wq[r], bqkv[r]) for r in (2, 3)]
-        qkv[2] = tie(qkv[2], wu_near, wd_near)
-        attn_b = attend_call(clock, lens, qkv[2:], None, length)
-        wu_half = clock.after(wu_half)
-        wu_other = pp_dp(wu_half, 0)
-        cot_blocks = exchange(text_blocks(tie(cotangent, wu_half)))
-        wo_far = clock.after(wo_far)
+
+        def project_far(values):
+            passed = [pp_tensor(v, 1) for v in wq_far]
+            return passed, project(clock, values, wq_far, bqkv[2])
+
+        passed, q_first = block(project_far, h1)
+        wq += [wq_far, passed]
+        qkv += [q_first, project(clock, h1, wq[3], bqkv[3])]
+        attn_b = attend_call(clock, lens, qkv[2:], None, length, COST_FAR)
+        wu_near = [pp_tensor(clock.after(v), 1) for v in (w_up[:cut], up_second)]
+        first_far = clock.after(first_far)
+        wo_far = first_far[cut:]
         wo = [w_out, wo_near, wo_far, pp_tensor(wo_far, 1)]
         ctx = [attn_a[0], attn_a[1], attn_b[0], attn_b[1]]
-        resid, h2 = attention_out(clock, x, ctx, wo, (b_out, ln2_gain, ln2_bias))
-        wu = [[w_up], [wu_near]]
-        acts, slopes = [], []
-        for r in rels:
-            if r == 2:
-                g_low, bias_down = join_mask(clock, [cot_blocks[0]] + [clock.after(b) for b in cot_blocks[1:]], t, lens)
-                wd_far = pp_tensor(clock.after(w_down), 2)
-                wu_far = order_halves(clock, wu_half, clock.after(wu_other), bit_of[0])
-                wu += [wu_far, [pp_tensor(v, 1) for v in wu_far]]
-            act, slope = up(clock, h2, wu[r], bup[r])
-            acts.append(act)
-            slopes.append(slope)
-
-        near = from_near([g_low], [[(0, acts[1])], [(0, acts[3])]])
-        down = Chain([g_low], [[(0, acts[0])], [(0, acts[2])]], near, [0, 1, "y"] + high)
+        resid, h2 = attention_out(clock, x, ctx, wo, (b_out, ln2_gain, ln2_bias), COST_OUT)
+        ups = [up(clock, h2, [w_up], bup[0])]
+        wu_far = [first_far[:cut], clock.after(second_far)]
+        wu = [[w_up], wu_near, wu_far, [pp_tensor(v, 1) for v in wu_far]]
+        ups.append(up(clock, h2, wu[1], bup[1], COST_OUT))
+        cot.forward()
+        ups.append(up(clock, h2, wu[3], bup[3]))
+        g_low, bias_down = join_mask(clock, cot.blocks(), t, lens)
+        wd_near = [pp_tensor(clock.after(v), 1) for v in (w_down[:cut], w_down[cut:])]
+
+        near = from_near([tie(g_low, *wd_near)], [[(0, ups[1][0])], [(0, ups[2][0])]])
+        ups.insert(2, up(clock, h2, wu[2], bup[2]))
+        acts, slopes = [u[0] for u in ups], [u[1] for u in ups]
+        down = Chain([g_low], [[(0, acts[0])], [(0, acts[2])]], near, ["y", 0, 1] + high)
         wd_far = clock.after(wd_far)
-        wd = [w_down, wd_near, wd_far, pp_tensor(wd_far, 1)]
+        wd = [[w_down], wd_near, [wd_far], [pp_tensor(wd_far, 1)]]
         dups_a, sums_a, dh2 = up_back(clock, g_low, wu[:2], wd[:2], slopes[:2], None, None, None)
         dups_b, sums_b, rest = up_back(clock, g_low, wu[2:], wd[2:], slopes[2:], dh2[0], resid, ln2_gain)
         dres, dres_low, gain_two, shift_two, bias_attn = rest
@@ -749,70 +824,71 @@
         dqkv_far, qkv_sums_far = back[:2], back[2:]
         near = from_near([h1, dres_low], [[(0, dqkv_far[1]), (1, ctx[3])]])
         down.step()
-        q_far = Chain([h1, dres_low], [[(0, dqkv_far[0]), (1, ctx[2])]], near, [1, 0])
+        q_far = weight_grads(clock, [h1, dres_low], [[(0, dqkv_far[0]), (1, ctx[2])]], near)
+        q_far = pp_tensor(q_far, 2)
         back = attend_call(clock, lens, qkv[:2], [dres_low] + wo[:2] + list(attn_a[2:]), length)
         dqkv, qkv_sums = list(back[:2]) + list(dqkv_far), list(back[2:]) + list(qkv_sums_far)
         grads_up.step()
-        if high:
+        for bit in high:
             down.step()
         near = from_near([h1, dres_low], [[(0, dqkv[1]), (1, ctx[1])]])
-        out_blocks = exchange(down_out(clock, resid, acts, wd, b_down, t, texts))
-        q_own = Chain([h1, dres_low], [[(0, dqkv[0]), (1, ctx[0])]], near, [1, 0] + high)
-        q_far.step()
+        out = Exchange(*down_out(clock, resid, acts, wd, b_down, t, texts))
+        grad_down = clock.then(down.last())
+        grads_up.step()
+        q_own = Chain([h1, dres_low], [[(0, dqkv[0]), (1, ctx[0])]], near, [1, 0] + high, clock.after(q_far))
         in_blocks, gain_one, shift_one = norm_one_back(clock, x, dres, dqkv, wq, ln1_gain, t, texts)
-        in_blocks = exchange(in_blocks)
-        layer_out = join_rows(clock, [out_blocks[0]] + [clock.after(b) for b in out_blocks[1:]], t)
-        grads_up.step()
-        up_full = jnp.zeros((tensor_size, units), F32)
-        qv_full = jnp.zeros((tensor_size, 2, local), F32)
-        for r in rels:
-            up_full = lax.dynamic_update_slice(up_full, bias_up[r], (t ^ r, 0))
-            sums = qkv_sums[r].reshape(3, local)
-            sums = jnp.concatenate([sums[:1], sums[2:]], 0)
-            qv_full = lax.dynamic_update_slice(qv_full, sums[None], (t ^ r, 0, 0))
-        vectors = [gain_one, shift_one, gain_two, shift_two, bias_attn, bias_down]
-        total = jnp.concatenate([v.reshape(-1) for v in vectors] + [qv_full.reshape(-1), up_full.reshape(-1)])
-
-        def reduced(flip, tensor):
-            moved = pp_tensor(total, flip) if tensor else pp_dp(total, flip)
-            return clock.then(total + clock.after(moved))
-
-        total = reduced(1, True)
-        q_own.step()
-        total = reduced(2, True)
-        q_far_all = pp_tensor(q_far.last().astype(BF), 2)
-        total = reduced(0, False)
-        for bit in high:
-            if bit != high[0]:
-                down.step()
-            grads_up.step()
-            if bit == high[0]:
-                arrived = clock.after(q_far_all).reshape(q_own.keep.shape)
-                q_own.keep = (q_own.keep.astype(F32) + arrived.astype(F32)).astype(BF)
+        gin = Exchange(*in_blocks)
+        shared = [gain_one, shift_one, gain_two, shift_two, bias_attn, bias_down]
+        out.forward()
+        total = pack(clock, shared, bias_up, qkv_sums, t)
+        chains += [grads_up, q_own]
+        for chain in chains:
+            chain.flight = clock.after(chain.flight)
+
+        def finish(total, state):
+            for chain, (keep, flight) in zip(chains, state):
+                chain.keep, chain.flight = keep, flight
+
+            def reduced(flip, tensor):
+                moved = pp_tensor(total, flip) if tensor else pp_dp(total, flip)
+                return clock.then(total + clock.after(moved))
+
             q_own.step()
-        total = reduced(1, False)
-        grad_input = join_rows(clock, [in_blocks[0]] + [clock.after(b) for b in in_blocks[1:]], t)
-        for bit in high:
-            total = reduced(bit, False)
-        grad_down, grad_up, both = down.last(), grads_up.last(), q_own.last()
-        grad_qkv, grad_out = both[:, : 3 * local], both[:, 3 * local :]
-        vector = [total[i * D : (i + 1) * D] for i in range(6)]
-        rest = total[6 * D :]
+            total = reduced(1, True)
+            total = reduced(0, False)
+            for bit in high:
+                q_own.step()
+                grads_up.step()
+            for bit in range(1, bits):
+                total = reduced(bit, False)
+            total = reduced(2, True)
+            both = q_own.last()
+            weights = jnp.stack([both[:, c * local : c * local + local] for c in range(3)])
+            return total, grads_up.last(), weights, both[:, 3 * local :].T
+
+        state = [(chain.keep, chain.flight) for chain in chains]
+        total, grad_up, grad_qkv, grad_out = block(finish, total, state)
+        layer_out = join_rows(clock, out.blocks(), t, COST_END)
+        gin.forward()
+        grad_input = join_rows(clock, gin.blocks(), t)
+        first = len(shared)
+        units_sum = lax.dynamic_slice_in_dim(total, first + t, 1)[0, :units]
+        qv_sum = lax.dynamic_slice_in_dim(total, first + tensor_size + t, 1)[0, : 2 * local]
         return (
             layer_out,
             grad_input,
-            vector[0],
-            vector[1],
-            jnp.stack([grad_qkv[:, c * local : c * local + local] for c in range(3)]),
-            pick(rest[: 2 * D].reshape(tensor_size, 2, local), t, 0),
-            grad_out.T,
-            vector[4],
-            vector[2],
-            vector[3],
+            total[0],
+            total[1],
+            grad_qkv,
+            qv_sum.reshape(2, local),
+            grad_out,
+            total[4],
+            total[2],
+            total[3],
             grad_up,
-            pick(rest[2 * D :].reshape(tensor_size, units), t, 0),
+            units_sum,
             grad_down.T,
-            vector[5],
+            total[5],
         )
 
     return on_device

time: 337 us -> 330 us (0.979)
  waiting for transfers between devices: 65.3 us -> 52.5 us
  local copies, waits for them, and re-layouts: 43.2 us -> 39.1 us
  Pallas kernels: 170 us -> 174 us
    ppermute x48 -> x49, waiting for transfers between devices: 49.8 us -> 32 us  [pp_tensor(): lax.ppermute(values, 'tensor', [(i, i ^ flip) for i in range(tensor_size)])]
    unnamed x237 -> x235, local copies, waits for them, and re-layouts: 34.4 us -> 21.2 us
    ppermute x15 -> x12, waiting for transfers between devices: 15.5 us -> 20.5 us  [pp_dp(): lax.ppermute(values, 'dp', [(i, i ^ 1 << bit) for i in range(dp_size)])]
    pallas_call x40 -> x39, Pallas kernels: 170 us -> 174 us  [call(): pl.pallas_call(body, out_shape=jax.tree.map(lambda v: pltpu.HBM(v.shape,...]
    ppermute x48 -> x49, starting transfers between devices: 24.4 us -> 27.1 us  [pp_tensor(): lax.ppermute(values, 'tensor', [(i, i ^ flip) for i in range(tensor_size)])]
    ppermute x15 -> x12, starting transfers between devices: 22.8 us -> 22.4 us  [pp_dp(): lax.ppermute(values, 'dp', [(i, i ^ 1 << bit) for i in range(dp_size)])]
  transfers between devices with their start and end apart: 63 -> 61, of which waited for: 18 -> 19; matrix products, arithmetic and copies ran while one was open for 6% -> 6% of each run, Pallas kernels for 46% -> 51%
where the time goes in v3:
time: 330 us; the launch traced here: 325 us
  Pallas kernels  174 us (53%)
  waiting for transfers between devices  52.5 us (16%)
  starting transfers between devices  49.6 us (15%)
  local copies, waits for them, and re-layouts  39.1 us (12%)
  other arithmetic  7.63 us (2%)
    pallas_call x39, Pallas kernels, call(): pl.pallas_call(body, out_shape=jax.tree.map(lambda v: pltpu.HBM(v.shape,...  174 us
    ppermute x49, waiting for transfers between devices, pp_tensor(): lax.ppermute(values, 'tensor', [(i, i ^ flip) for i in range(tensor_size)])  32 us
    ppermute x49, starting transfers between devices, pp_tensor(): lax.ppermute(values, 'tensor', [(i, i ^ flip) for i in range(tensor_size)])  27.1 us
    ppermute x12, starting transfers between devices, pp_dp(): lax.ppermute(values, 'dp', [(i, i ^ 1 << bit) for i in range(dp_size)])  22.4 us
    unnamed x235, local copies, waits for them, and re-layouts  21.2 us
    ppermute x12, waiting for transfers between devices, pp_dp(): lax.ppermute(values, 'dp', [(i, i ^ 1 << bit) for i in range(dp_size)])  20.5 us
  transfers between devices with their start and end apart: 61, of which 19 were waited for; matrix products, arithmetic and copies ran while one was open for 6% of the time, Pallas kernels for 51%

profile of v3, /device:TPU:0, one launch (start us, length us, event | category | flops | bytes accessed | tf_op | source)
XLA Modules:
  0.0 325.4 jit_solution(5329911531896632385)
XLA Ops:
  17.1 7.7 %collective-permute-done.19 = f32[2,1152]{1,0:T(2,128)S(1)} collective-permute-done((f32[2,1152]{1,0:T(2,128)S(1)}, f32[2,1152]{1,0:T(2,128)S(1)}, u32[]{:S(2)}, u32[]{:S(2)}) %collective-permute-start.19) | collective-permute-done | bytes 9248 | tf_op jit(solution)/shard_map/ppermute | solution.py:627
  32.3 4.7 %project.5.refs_0_ = bf16[1024,576]{1,0:T(8,128)(2,1)} custom-call(bf16[1024,768]{1,0:T(8,128)(2,1)} %get-tuple-element.369.h_ref.refs_0_.refs_1_, f32[1,576]{1,0:T(1,128)S(1)} %reshape.178.bias_ref, bf16[384,576]{1,0:T(8,128)(2,1)S(1)} %copy-done.39, bf16[384,576]{1,0:T(8,128)(2,1)S(1)} %copy-done.41), custom_call_target="tpu_custom_call" | custom-call | tf_op jit(solution)/shard_map/project/pallas_call | solution.py:60
  41.5 6.5 %attend.2 = (bf16[1024,192]{1,0:T(8,128)(2,1)}, bf16[1024,192]{1,0:T(8,128)(2,1)}, bf16[2,6,512,512]{3,2,1,0:T(8,128)(2,1)}, f32[2,6,512]{2,1,0:T(8,128)}) custom-call(s32[2]{0:T(128)S(1)} %dynamic_slice.45.lens.n, bf16[1024,576]{1,0:T(8,128)(2,1)S(1)} %copy-done.5, bf16[1024,576]{1,0:T(8,128)(2,1)S(1)} %copy-done.7), custom_call_target="tpu_custom_call" | custom-call | tf_op jit(solution)/shard_map/attend/pallas_call | solution.py:60
  48.0 5.5 %conditional.2 = (bf16[384,576]{1,0:T(8,128)(2,1)}, bf16[384,576]{1,0:T(8,128)(2,1)}, bf16[1024,576]{1,0:T(8,128)(2,1)}) conditional(s32[]{:T(128)} %bitcast.15, () %tuple.118, (bf16[384,576]{1,0:T(8,128)(2,1)}, bf16[384,576]{1,0:T(8,128)(2,1)}, f32[576]{0:T(1024)S(1)}, bf16[1024,768]{1,0:T(8,128)(2,1)S(1)}) %tuple.238), branch_computations={%region_0.1_spmd, %region_1.2_spmd} | conditional | bytes 3543656 | solution.py:748
  49.2 4.3 %project.4 = bf16[1024,576]{1,0:T(8,128)(2,1)} custom-call(bf16[1024,768]{1,0:T(8,128)(2,1)S(1)} %get-tuple-element.36.h_ref, f32[1,576]{1,0:T(1,128)S(1)} %reshape.136.bias_ref, bf16[384,576]{1,0:T(8,128)(2,1)} %get-tuple-element.34.refs_0_, bf16[384,576]{1,0:T(8,128)(2,1)} %get-tuple-element.35.refs_1_), custom_call_target="tpu_custom_call" | custom-call | tf_op jit(solution)/shard_map/cond/branch_1_fun/project/pallas_call | solution.py:60
  53.5 4.7 %project.7.refs_1_ = bf16[1024,576]{1,0:T(8,128)(2,1)} custom-call(bf16[1024,768]{1,0:T(8,128)(2,1)S(1)} %copy-done.92, f32[1,576]{1,0:T(1,128)S(1)} %reshape.181.bias_ref, bf16[384,576]{1,0:T(8,128)(2,1)} %get-tuple-element.267.refs_0_.refs_10_, bf16[384,576]{1,0:T(8,128)(2,1)} %get-tuple-element.269.refs_1_.refs_11_), custom_call_target="tpu_custom_call" | custom-call | tf_op jit(solution)/shard_map/project/pallas_call | solution.py:60
  59.6 7.3 %attend.3 = (bf16[1024,192]{1,0:T(8,128)(2,1)}, bf16[1024,192]{1,0:T(8,128)(2,1)}, bf16[2,6,512,512]{3,2,1,0:T(8,128)(2,1)}, f32[2,6,512]{2,1,0:T(8,128)}) custom-call(s32[2]{0:T(128)S(1)} %dynamic_slice.45.lens.n, bf16[1024,576]{1,0:T(8,128)(2,1)} %get-tuple-element.333.refs_0_, bf16[1024,576]{1,0:T(8,128)(2,1)S(1)} %copy-done.19), custom_call_target="tpu_custom_call" | custom-call | flops 14000000000 | tf_op jit(solution)/shard_map/attend/pallas_call | solution.py:60
  79.4 6.4 %attention_out.1 = (f32[1024,768]{1,0:T(8,128)}, bf16[1024,768]{1,0:T(8,128)(2,1)}) custom-call(bf16[1024,768]{1,0:T(8,128)(2,1)} %get-tuple-element.373.x_ref, bf16[1024,192]{1,0:T(8,128)(2,1)} %get-tuple-element.261.refs_0_.refs_4_, bf16[1024,192]{1,0:T(8,128)(2,1)} %get-tuple-element.273.refs_1_.refs_3_, ...), custom_call_target="tpu_custom_call" | custom-call | flops 6000000000 | tf_op jit(solution)/shard_map/attention_out/pallas_call | solution.py:60
  87.2 3.8 %up.4 = (bf16[1024,768]{1,0:T(8,128)(2,1)}, bf16[1024,768]{1,0:T(8,128)(2,1)}) custom-call(bf16[1024,768]{1,0:T(8,128)(2,1)S(1)} %copy-done.1, f32[1,768]{1,0:T(1,128)S(1)} %reshape.188.bias_ref, bf16[768,768]{1,0:T(8,128)(2,1)S(1)} %copy-done.11), custom_call_target="tpu_custom_call" | custom-call | tf_op jit(solution)/shard_map/up/pallas_call | solution.py:60
  91.1 6.0 %up.5 = (bf16[1024,768]{1,0:T(8,128)(2,1)}, bf16[1024,768]{1,0:T(8,128)(2,1)}) custom-call(bf16[1024,768]{1,0:T(8,128)(2,1)S(1)} %copy-done.1, f32[1,768]{1,0:T(1,128)S(1)} %reshape.189.bias_ref, bf16[384,768]{1,0:T(8,128)(2,1)S(1)} %collective-permute-done.22.refs_0_.refs_1_, bf16[384,768]{1,0:T(8,128)(2,1)} %collective-permute-done.23.refs_1_.refs_2_), custom_call_target="tpu_custom_call" | custom-call | flops 6000000000 | tf_op jit(solution)/shard_map/up/pallas_call | solution.py:60
  97.2 6.4 %collective-permute-done.28.refs_2_ = bf16[2,2,128,768]{3,2,1,0:T(8,128)(2,1)S(1)} collective-permute-done((bf16[2,2,128,768]{3,2,1,0:T(8,128)(2,1)}, bf16[2,2,128,768]{3,2,1,0:T(8,128)(2,1)S(1)}, u32[]{:S(2)}, u32[]{:S(2)}) %collective-permute-start.28) | collective-permute-done | bytes 786464 | tf_op jit(solution)/shard_map/ppermute | solution.py:627
  104.3 4.2 %up.6 = (bf16[1024,768]{1,0:T(8,128)(2,1)}, bf16[1024,768]{1,0:T(8,128)(2,1)}) custom-call(bf16[1024,768]{1,0:T(8,128)(2,1)S(1)} %copy-done.1, f32[1,768]{1,0:T(1,128)S(1)} %get-tuple-element.472.bias_ref, bf16[384,768]{1,0:T(8,128)(2,1)S(1)} %collective-permute-done.24.refs_0_.refs_2_, bf16[384,768]{1,0:T(8,128)(2,1)S(1)} %collective-permute-done.26.refs_1_.refs_3_), custom_call_target="tpu_custom_call" | custom-call | tf_op jit(solution)/shard_map/up/pallas_call | solution.py:60
  116.5 3.9 %weight_grads.8 = (bf16[768,384]{1,0:T(8,128)(2,1)}, bf16[768,384]{1,0:T(8,128)(2,1)}, bf16[768,384]{1,0:T(8,128)(2,1)}, bf16[768,384]{1,0:T(8,128)(2,1)}) custom-call(bf16[1024,768]{1,0:T(8,128)(2,1)S(1)} %copy-done.3, bf16[1024,768]{1,0:T(8,128)(2,1)S(1)} %copy-done.13, bf16[1024,768]{1,0:T(8,128)(2,1)S(1)} %copy-done.14), custom_call_target="tpu_custom_call" | custom-call | tf_op jit(solution)/shard_map/weight_grads/pallas_call | solution.py:60
  121.4 4.2 %up.7 = (bf16[1024,768]{1,0:T(8,128)(2,1)}, bf16[1024,768]{1,0:T(8,128)(2,1)}) custom-call(bf16[1024,768]{1,0:T(8,128)(2,1)S(1)} %copy-done.2, f32[1,768]{1,0:T(1,128)S(1)} %get-tuple-element.471.bias_ref, bf16[384,768]{1,0:T(8,128)(2,1)S(1)} %slice.148.refs_0_, bf16[384,768]{1,0:T(8,128)(2,1)S(1)} %copy-done.33), custom_call_target="tpu_custom_call" | custom-call | tf_op jit(solution)/shard_map/up/pallas_call | solution.py:60
  125.7 5.3 %weight_grads.9 = (bf16[1,768,768]{2,1,0:T(8,128)(2,1)}, bf16[1,768,768]{2,1,0:T(8,128)(2,1)}) custom-call(bf16[1024,768]{1,0:T(8,128)(2,1)S(1)} %copy-done.4, bf16[1024,768]{1,0:T(8,128)(2,1)S(1)} %copy-done.12, bf16[1024,768]{1,0:T(8,128)(2,1)} %get-tuple-element.302.refs_2_, bf16[768,384]{1,0:T(8,128)(2,1)S(1)} %collective-permute-done.32.refs_3_, ...), custom_call_target="tpu_custom_call" | custom-call | tf_op jit(solution)/shard_map/weight_grads/pallas_call | solution.py:60
  131.0 8.3 %collective-permute-done.36.refs_4_.refs_7_ = bf16[768,768]{1,0:T(8,128)(2,1)S(1)} collective-permute-done((bf16[768,768]{1,0:T(8,128)(2,1)S(1)}, bf16[768,768]{1,0:T(8,128)(2,1)S(1)}, u32[]{:S(2)}, u32[]{:S(2)}) %collective-permute-start.36) | collective-permute-done | bytes 1179680 | tf_op jit(solution)/shard_map/ppermute | solution.py:627
  140.2 9.5 %up_back.2 = (bf16[1024,768]{1,0:T(8,128)(2,1)}, bf16[1024,768]{1,0:T(8,128)(2,1)}, f32[1,768]{1,0:T(1,128)}, f32[1,768]{1,0:T(1,128)}, f32[1024,768]{1,0:T(8,128)}) custom-call(bf16[1024,768]{1,0:T(8,128)(2,1)} %get-tuple-element.312.refs_0_.g_ref, bf16[768,768]{1,0:T(8,128)(2,1)S(1)} %copy-done.11, bf16[384,768]{1,0:T(8,128)(2,1)S(1)} %copy-done.57, ...), custom_call_target="tpu_custom_call" | custom-call | tf_op jit(solution)/shard_map/up_back/pallas_call | solution.py:60
  149.7 11.9 %up_back.3 = (bf16[1024,768]{1,0:T(8,128)(2,1)}, bf16[1024,768]{1,0:T(8,128)(2,1)}, f32[1,768]{1,0:T(1,128)}, f32[1,768]{1,0:T(1,128)}, f32[1024,768]{1,0:T(8,12...) custom-call(bf16[1024,768]{1,0:T(8,128)(2,1)} %get-tuple-element.312.refs_0_.g_ref, ...), custom_call_target="tpu_custom_call" | custom-call | tf_op jit(solution)/shard_map/up_back/pallas_call | solution.py:60
  163.0 3.8 %weight_grads.10 = (bf16[768,384]{1,0:T(8,128)(2,1)}, bf16[768,384]{1,0:T(8,128)(2,1)}, bf16[768,384]{1,0:T(8,128)(2,1)}, bf16[768,384]{1,0:T(8,128)(2,1)}) custom-call(bf16[1024,768]{1,0:T(8,128)(2,1)S(1)} %copy-done.2, bf16[1024,768]{1,0:T(8,128)(2,1)S(1)} %copy-done.48, bf16[1024,768]{1,0:T(8,128)(2,1)S(1)} %copy-done.49), custom_call_target="tpu_custom_call" | custom-call | tf_op jit(solution)/shard_map/weight_grads/pallas_call | solution.py:60
  174.4 5.6 %weight_grads.11 = (bf16[1,768,768]{2,1,0:T(8,128)(2,1)}, bf16[1,768,768]{2,1,0:T(8,128)(2,1)}) custom-call(bf16[1024,768]{1,0:T(8,128)(2,1)S(1)} %copy-done.2, bf16[1024,768]{1,0:T(8,128)(2,1)S(1)} %copy-done.47, bf16[1024,768]{1,0:T(8,128)(2,1)} %get-tuple-element.318.refs_2_, bf16[768,384]{1,0:T(8,128)(2,1)} %collective-permute-done.39.refs_3_, ...), custom_call_target="tpu_custom_call" | custom-call | tf_op jit(solution)/shard_map/weight_grads/pallas_call | solution.py:60
  181.1 4.9 %collective-permute-start.43 = (bf16[4,96,768]{2,1,0:T(8,128)(2,1)}, bf16[4,96,768]{2,1,0:T(8,128)(2,1)S(1)}, u32[]{:S(2)}, u32[]{:S(2)}) collective-permute-start(bf16[4,96,768]{2,1,0:T(8,128)(2,1)} %get-tuple-element.327), channel_id=1, source_target_pairs={{0,4},{4,0},{8,12},{12,8},{16,20},{20,16},{24,28},{28,24},{1,5},{5... | collective-permute-start | bytes 1769480 | tf_op jit(solution)/shard_map/ppermute | solution.py:630
  186.0 9.1 %attend_back.2 = (bf16[1024,576]{1,0:T(8,128)(2,1)}, bf16[1024,576]{1,0:T(8,128)(2,1)}, f32[1,576]{1,0:T(1,128)}, f32[1,576]{1,0:T(1,128)}) custom-call(s32[2]{0:T(128)S(1)} %dynamic_slice.45.lens.n, bf16[1024,576]{1,0:T(8,128)(2,1)} %get-tuple-element.333.refs_0_, bf16[1024,576]{1,0:T(8,128)(2,1)S(1)} %copy-done.20, bf16[1024,768]{1,0:T(8,128)(2,1)S(1)} %copy-done, ...), custom_call_target="tpu_custom_call" | custom-call | tf_op jit(solution)/shard_map/attend_back/pallas_call | solution.py:60
  206.5 4.3 %weight_grads.13 = bf16[1,768,768]{2,1,0:T(8,128)(2,1)} custom-call(bf16[1024,768]{1,0:T(8,128)(2,1)} %get-tuple-element.369.h_ref.refs_0_.refs_1_, bf16[1024,768]{1,0:T(8,128)(2,1)S(1)} %copy-done, bf16[1024,576]{1,0:T(8,128)(2,1)S(1)} %copy-done.15, bf16[1024,192]{1,0:T(8,128)(2,1)S(1)} %copy-done.62, bf16[768,384]{1,0:T(8,128)(2,1)S(1)} %copy-done.59, ...), custom_call_target="tpu_custom_call" | custom-call | tf_op jit(solution)/shard_map/weight_grads/pallas_call | solution.py:60
  217.4 8.7 %attend_back.3 = (bf16[1024,576]{1,0:T(8,128)(2,1)}, bf16[1024,576]{1,0:T(8,128)(2,1)}, f32[1,576]{1,0:T(1,128)}, f32[1,576]{1,0:T(1,128)}) custom-call(s32[2]{0:T(128)S(1)} %dynamic_slice.45.lens.n, bf16[1024,576]{1,0:T(8,128)(2,1)S(1)} %copy-done.6, bf16[1024,576]{1,0:T(8,128)(2,1)S(1)} %copy-done.8, bf16[1024,768]{1,0:T(8,128)(2,1)S(1)} %copy-done, ...), custom_call_target="tpu_custom_call" | custom-call | tf_op jit(solution)/shard_map/attend_back/pallas_call | solution.py:60
  242.1 9.4 %down_out.1 = (bf16[2,128,768]{2,1,0:T(8,128)(2,1)}, bf16[2,128,768]{2,1,0:T(8,128)(2,1)}, bf16[2,2,128,768]{3,2,1,0:T(8,128)(2,1)}) custom-call(s32[1]{0:T(128)} %bitcast.14.at, f32[1024,768]{1,0:T(8,128)} %get-tuple-element.361.refs_9_.resid_ref, bf16[1024,768]{1,0:T(8,128)(2,1)} %get-tuple-element.280.refs_1_.refs_0_, ...), custom_call_target="tpu_custom_call" | custom-call | tf_op jit(solution)/shard_map/down_out/pallas_call | solution.py:60
  254.6 4.6 %weight_grads.15 = (bf16[1,384,768]{2,1,0:T(8,128)(2,1)}, bf16[1,384,768]{2,1,0:T(8,128)(2,1)}) custom-call(s32[1]{0:T(128)} %bitcast.23.at.refs_0_, bf16[1024,768]{1,0:T(8,128)(2,1)S(1)} %copy-done.94, bf16[1024,768]{1,0:T(8,128)(2,1)S(1)} %copy-done, bf16[1024,576]{1,0:T(8,128)(2,1)S(1)} %copy-done.21, bf16[1024,192]{1,0:T(8,128)(2,1)S(1)} %copy-done.65, ...), custom_call_target="tpu_custom_call" | custom-call | tf_op jit(solution)/shard_map/weight_grads/pallas_call | solution.py:60
  261.4 13.2 %norm_one_back.1 = (bf16[2,128,768]{2,1,0:T(8,128)(2,1)}, bf16[2,128,768]{2,1,0:T(8,128)(2,1)}, bf16[2,2,128,768]{3,2,1,0:T(8,128)(2,1)}, f32[1,768]{1,0:T(1,128)}, f32[1,768]{1,0:T(1,128)}) custom-call(s32[1]{0:T(128)} %bitcast.14.at, bf16[1024,768]{1,0:T(8,128)(2,1)} %get-tuple-element.373.x_ref, f32[1024,768]{1,0:T(8,128)} %get-tuple-element.374.dres_ref, ...), custom_call_target="tpu_custom_call" | custom-call | tf_op jit(solution)/shard_map/norm_one_back/pallas_call | solution.py:60
  276.9 4.0 %collective-permute-done.54 = bf16[2,96,768]{2,1,0:T(8,128)(2,1)S(1)} collective-permute-done((bf16[2,96,768]{2,1,0:T(8,128)(2,1)S(1)}, bf16[2,96,768]{2,1,0:T(8,128)(2,1)S(1)}, u32[]{:S(2)}, u32[]{:S(2)}) %collective-permute-start.54) | collective-permute-done | bytes 294944 | tf_op jit(solution)/shard_map/ppermute | solution.py:630
  280.9 35.5 %conditional.3 = (f32[14,768]{1,0:T(8,128)}, f32[96,768]{1,0:T(8,128)}, f32[3,96,192]{2,1,0:T(8,128)}, bf16[1,768]{1,0:T(2,128)(2,1)S(1)}, bf16[1,768]{1,0:T(2,1...) conditional(s32[]{:T(128)} %bitcast.15, () %tuple.173, ...), branch_computations={%region_2.3_spmd, %region_3.4_spmd} | conditional | flops 611328 | bytes 8039928 | solution.py:748
  286.1 5.0 %collective-permute-done.3 = f32[14,768]{1,0:T(8,128)S(1)} collective-permute-done((f32[14,768]{1,0:T(8,128)S(1)}, f32[14,768]{1,0:T(8,128)S(1)}, u32[]{:S(2)}, u32[]{:S(2)}) %collective-permute-start.3) | collective-permute-done | bytes 43040 | tf_op jit(solution)/shard_map/cond/branch_1_fun/ppermute | solution.py:630
  296.0 4.9 %collective-permute-done.6 = f32[14,768]{1,0:T(8,128)S(1)} collective-permute-done((f32[14,768]{1,0:T(8,128)S(1)}, f32[14,768]{1,0:T(8,128)S(1)}, u32[]{:S(2)}, u32[]{:S(2)}) %collective-permute-start.6) | collective-permute-done | bytes 43040 | tf_op jit(solution)/shard_map/cond/branch_1_fun/ppermute | solution.py:630
  306.6 5.4 %collective-permute-done.9 = bf16[1,96,768]{2,1,0:T(8,128)(2,1)S(1)} collective-permute-done((bf16[1,96,768]{2,1,0:T(8,128)(2,1)}, bf16[1,96,768]{2,1,0:T(8,128)(2,1)S(1)}, u32[]{:S(2)}, u32[]{:S(2)}) %collective-permute-start.9) | collective-permute-done | bytes 147488 | tf_op jit(solution)/shard_map/cond/branch_1_fun/ppermute | solution.py:630
  (423 shorter events, 135.2 us)
Async XLA Ops:
  3.5 12.4 %collective-permute-start.15 = (bf16[2,128,768]{2,1,0:T(8,128)(2,1)}, bf16[2,128,768]{2,1,0:T(8,128)(2,1)}, u32[]{:S(2)}, u32[]{:S(2)}) collective-permute-start(bf16[2,128,768]{2,1,0:T(8,128)(2,1)} %get-tuple-element.463), channel_id=1, source_target_pairs={{0,3},{1,2},{2,1},{3,0},{4,7},{5,6},{6,5},{7,4},{8,11},{9,10},{10,... | collective-permute-start | bytes 1179656 | tf_op jit(solution)/shard_map/ppermute | solution.py:627
  6.2 22.5 %collective-permute-start.14 = (bf16[2,128,768]{2,1,0:T(8,128)(2,1)}, bf16[2,128,768]{2,1,0:T(8,128)(2,1)}, u32[]{:S(2)}, u32[]{:S(2)}) collective-permute-start(bf16[2,128,768]{2,1,0:T(8,128)(2,1)} %get-tuple-element.466), channel_id=1, source_target_pairs={{0,2},{1,3},{2,0},{3,1},{4,6},{5,7},{6,4},{7,5},{8,10},{9,11},{10,... | collective-permute-start | bytes 1179656 | tf_op jit(solution)/shard_map/ppermute | solution.py:627
  8.9 18.1 %collective-permute-start.12 = (bf16[384,576]{1,0:T(8,128)(2,1)}, bf16[384,576]{1,0:T(8,128)(2,1)S(1)}, u32[]{:S(2)}, u32[]{:S(2)}) collective-permute-start(bf16[384,576]{1,0:T(8,128)(2,1)} %get-tuple-element.255.refs_0_.refs_4_), channel_id=1, source_target_pairs={{0,1},{1,0},{2,3},{3,2},{4,5},{5,4},{6,7},{7,6},{8,9},{9,8},{10,11... | collective-permute-start | bytes 1327112 | tf_op jit(solution)/shard_map/ppermute | solution.py:627
  9.0 18.2 %collective-permute-start.13 = (bf16[384,576]{1,0:T(8,128)(2,1)}, bf16[384,576]{1,0:T(8,128)(2,1)S(1)}, u32[]{:S(2)}, u32[]{:S(2)}) collective-permute-start(bf16[384,576]{1,0:T(8,128)(2,1)} %get-tuple-element.263.refs_1_.refs_5_), channel_id=1, source_target_pairs={{0,1},{1,0},{2,3},{3,2},{4,5},{5,4},{6,7},{7,6},{8,9},{9,8},{10,11... | collective-permute-start | bytes 1327112 | tf_op jit(solution)/shard_map/ppermute | solution.py:627
  11.8 13.1 %collective-permute-start.19 = (f32[2,1152]{1,0:T(2,128)S(1)}, f32[2,1152]{1,0:T(2,128)S(1)}, u32[]{:S(2)}, u32[]{:S(2)}) collective-permute-start(f32[2,1152]{1,0:T(2,128)S(1)} %pad_maximum_fusion.6), channel_id=1, source_target_pairs={{0,2},{1,3},{2,0},{3,1},{4,6},{5,7},{6,4},{7,5},{8,10},{9,11},{10,... | collective-permute-start | bytes 27656 | tf_op jit(solution)/shard_map/ppermute | solution.py:627
  16.0 32.0 %collective-permute-start.18 = (bf16[384,576]{1,0:T(8,128)(2,1)S(1)}, bf16[384,576]{1,0:T(8,128)(2,1)}, u32[]{:S(2)}, u32[]{:S(2)}) collective-permute-start(bf16[384,576]{1,0:T(8,128)(2,1)S(1)} %copy-done.41), channel_id=1, source_target_pairs={{0,2},{1,3},{2,0},{3,1},{4,6},{5,7},{6,4},{7,5},{8,10},{9,11},{10,... | collective-permute-start | bytes 1327112 | tf_op jit(solution)/shard_map/ppermute | solution.py:627
  24.9 23.2 %collective-permute-start.16 = (bf16[384,576]{1,0:T(8,128)(2,1)S(1)}, bf16[384,576]{1,0:T(8,128)(2,1)}, u32[]{:S(2)}, u32[]{:S(2)}) collective-permute-start(bf16[384,576]{1,0:T(8,128)(2,1)S(1)} %copy-done.39), channel_id=1, source_target_pairs={{0,2},{1,3},{2,0},{3,1},{4,6},{5,7},{6,4},{7,5},{8,10},{9,11},{10,... | collective-permute-start | bytes 1327112 | tf_op jit(solution)/shard_map/ppermute | solution.py:627
  27.3 39.6 %collective-permute-start.20 = (bf16[576,768]{1,0:T(8,128)(2,1)}, bf16[576,768]{1,0:T(8,128)(2,1)}, u32[]{:S(2)}, u32[]{:S(2)}) collective-permute-start(bf16[576,768]{1,0:T(8,128)(2,1)} %pad_maximum_fusion.1), channel_id=1, source_target_pairs={{0,2},{1,3},{2,0},{3,1},{4,6},{5,7},{6,4},{7,5},{8,10},{9,11},{10,... | collective-permute-start | bytes 2654216 | tf_op jit(solution)/shard_map/ppermute | solution.py:627
  67.9 10.8 %collective-permute-start.21 = (bf16[192,768]{1,0:T(8,128)(2,1)S(1)}, bf16[192,768]{1,0:T(8,128)(2,1)S(1)}, u32[]{:S(2)}, u32[]{:S(2)}) collective-permute-start(bf16[192,768]{1,0:T(8,128)(2,1)S(1)} %slice.144.refs_6_.refs_3_), channel_id=1, source_target_pairs={{0,1},{1,0},{2,3},{3,2},{4,5},{5,4},{6,7},{7,6},{8,9},{9,8},{10,11... | collective-permute-start | bytes 884744 | tf_op jit(solution)/shard_map/ppermute | solution.py:627
  71.2 19.8 %collective-permute-start.25 = (bf16[384,768]{1,0:T(8,128)(2,1)}, bf16[384,768]{1,0:T(8,128)(2,1)S(1)}, u32[]{:S(2)}, u32[]{:S(2)}) collective-permute-start(bf16[384,768]{1,0:T(8,128)(2,1)} %get-tuple-element.286), channel_id=1, source_target_pairs={{0,2},{1,3},{2,0},{3,1},{4,6},{5,7},{6,4},{7,5},{8,10},{9,11},{10,... | collective-permute-start | bytes 1769480 | tf_op jit(solution)/shard_map/ppermute | solution.py:627
  71.9 19.2 %collective-permute-start.22 = (bf16[384,768]{1,0:T(8,128)(2,1)}, bf16[384,768]{1,0:T(8,128)(2,1)S(1)}, u32[]{:S(2)}, u32[]{:S(2)}) collective-permute-start(bf16[384,768]{1,0:T(8,128)(2,1)} %copy-done.95), channel_id=1, source_target_pairs={{0,1},{1,0},{2,3},{3,2},{4,5},{5,4},{6,7},{7,6},{8,9},{9,8},{10,11... | collective-permute-start | bytes 1769480 | tf_op jit(solution)/shard_map/ppermute | solution.py:627
  71.9 19.2 %collective-permute-start.23 = (bf16[384,768]{1,0:T(8,128)(2,1)}, bf16[384,768]{1,0:T(8,128)(2,1)}, u32[]{:S(2)}, u32[]{:S(2)}) collective-permute-start(bf16[384,768]{1,0:T(8,128)(2,1)} %get-tuple-element.286), channel_id=1, source_target_pairs={{0,1},{1,0},{2,3},{3,2},{4,5},{5,4},{6,7},{7,6},{8,9},{9,8},{10,11... | collective-permute-start | bytes 1769480 | tf_op jit(solution)/shard_map/ppermute | solution.py:627
  76.2 27.4 %collective-permute-start.28 = (bf16[2,2,128,768]{3,2,1,0:T(8,128)(2,1)}, bf16[2,2,128,768]{3,2,1,0:T(8,128)(2,1)S(1)}, u32[]{:S(2)}, u32[]{:S(2)}) collective-permute-start(bf16[2,2,128,768]{3,2,1,0:T(8,128)(2,1)} %bitcast.63), channel_id=1, source_target_pairs={{0,2},{1,3},{2,0},{3,1},{4,6},{5,7},{6,4},{7,5},{8,10},{9,11},{10,... | collective-permute-start | bytes 2359304 | tf_op jit(solution)/shard_map/ppermute | solution.py:627
  78.7 25.6 %collective-permute-start.24 = (bf16[384,768]{1,0:T(8,128)(2,1)S(1)}, bf16[384,768]{1,0:T(8,128)(2,1)S(1)}, u32[]{:S(2)}, u32[]{:S(2)}) collective-permute-start(bf16[384,768]{1,0:T(8,128)(2,1)S(1)} %slice.148.refs_0_), channel_id=1, source_target_pairs={{0,1},{1,0},{2,3},{3,2},{4,5},{5,4},{6,7},{7,6},{8,9},{9,8},{10,11... | collective-permute-start | bytes 1769480 | tf_op jit(solution)/shard_map/ppermute | solution.py:627
  91.0 13.3 %collective-permute-start.26 = (bf16[384,768]{1,0:T(8,128)(2,1)S(1)}, bf16[384,768]{1,0:T(8,128)(2,1)S(1)}, u32[]{:S(2)}, u32[]{:S(2)}) collective-permute-start(bf16[384,768]{1,0:T(8,128)(2,1)S(1)} %collective-permute-done.25.refs_1_), channel_id=1, source_target_pairs={{0,1},{1,0},{2,3},{3,2},{4,5},{5,4},{6,7},{7,6},{8,9},{9,8},{10,11... | collective-permute-start | bytes 1769480 | tf_op jit(solution)/shard_map/ppermute | solution.py:627
  111.3 28.0 %collective-permute-start.36 = (bf16[768,768]{1,0:T(8,128)(2,1)S(1)}, bf16[768,768]{1,0:T(8,128)(2,1)S(1)}, u32[]{:S(2)}, u32[]{:S(2)}) collective-permute-start(bf16[768,768]{1,0:T(8,128)(2,1)S(1)} %copy-done.9), channel_id=1, source_target_pairs={{0,2},{1,3},{2,0},{3,1},{4,6},{5,7},{6,4},{7,5},{8,10},{9,11},{10,... | collective-permute-start | bytes 3538952 | tf_op jit(solution)/shard_map/ppermute | solution.py:627
  139.3 28.7 %collective-permute-start.38 = (bf16[1,768,768]{2,1,0:T(8,128)(2,1)}, bf16[1,768,768]{2,1,0:T(8,128)(2,1)}, u32[]{:S(2)}, u32[]{:S(2)}) collective-permute-start(bf16[1,768,768]{2,1,0:T(8,128)(2,1)} %get-tuple-element.324), channel_id=1, source_target_pairs={{0,2},{1,3},{2,0},{3,1},{4,6},{5,7},{6,4},{7,5},{8,10},{9,11},{10,... | collective-permute-start | bytes 3538952 | tf_op jit(solution)/shard_map/ppermute | solution.py:627
  180.0 46.1 %collective-permute-start.46 = (bf16[1,768,768]{2,1,0:T(8,128)(2,1)}, bf16[1,768,768]{2,1,0:T(8,128)(2,1)}, u32[]{:S(2)}, u32[]{:S(2)}) collective-permute-start(bf16[1,768,768]{2,1,0:T(8,128)(2,1)} %get-tuple-element.352), channel_id=1, source_target_pairs={{0,2},{1,3},{2,0},{3,1},{4,6},{5,7},{6,4},{7,5},{8,10},{9,11},{10,... | collective-permute-start | bytes 3538952 | tf_op jit(solution)/shard_map/ppermute | solution.py:627
  181.1 19.3 %collective-permute-start.43 = (bf16[4,96,768]{2,1,0:T(8,128)(2,1)}, bf16[4,96,768]{2,1,0:T(8,128)(2,1)S(1)}, u32[]{:S(2)}, u32[]{:S(2)}) collective-permute-start(bf16[4,96,768]{2,1,0:T(8,128)(2,1)} %get-tuple-element.327), channel_id=1, source_target_pairs={{0,4},{4,0},{8,12},{12,8},{16,20},{20,16},{24,28},{28,24},{1,5},{5... | collective-permute-start | bytes 1769480 | tf_op jit(solution)/shard_map/ppermute | solution.py:630
  210.8 43.8 %collective-permute-start.52 = (bf16[1,768,768]{2,1,0:T(8,128)(2,1)}, bf16[1,768,768]{2,1,0:T(8,128)(2,1)}, u32[]{:S(2)}, u32[]{:S(2)}) collective-permute-start(bf16[1,768,768]{2,1,0:T(8,128)(2,1)} %weight_grads.13), channel_id=1, source_target_pairs={{0,2},{1,3},{2,0},{3,1},{4,6},{5,7},{6,4},{7,5},{8,10},{9,11},{10,... | collective-permute-start | bytes 3538952 | tf_op jit(solution)/shard_map/ppermute | solution.py:627
  213.3 19.1 %collective-permute-start.47 = (bf16[2,96,768]{2,1,0:T(8,128)(2,1)}, bf16[2,96,768]{2,1,0:T(8,128)(2,1)}, u32[]{:S(2)}, u32[]{:S(2)}) collective-permute-start(bf16[2,96,768]{2,1,0:T(8,128)(2,1)} %get-tuple-element.344), channel_id=1, source_target_pairs={{0,8},{4,12},{8,0},{12,4},{16,24},{20,28},{24,16},{28,20},{1,9},{5... | collective-permute-start | bytes 884744 | tf_op jit(solution)/shard_map/ppermute | solution.py:630
  229.8 23.9 %collective-permute-start.49 = (bf16[4,96,768]{2,1,0:T(8,128)(2,1)}, bf16[4,96,768]{2,1,0:T(8,128)(2,1)S(1)}, u32[]{:S(2)}, u32[]{:S(2)}) collective-permute-start(bf16[4,96,768]{2,1,0:T(8,128)(2,1)} %get-tuple-element.354), channel_id=1, source_target_pairs={{0,4},{4,0},{8,12},{12,8},{16,20},{20,16},{24,28},{28,24},{1,5},{5... | collective-permute-start | bytes 1769480 | tf_op jit(solution)/shard_map/ppermute | solution.py:630
  237.8 16.8 %collective-permute-start.50 = (bf16[768,384]{1,0:T(8,128)(2,1)}, bf16[768,384]{1,0:T(8,128)(2,1)S(1)}, u32[]{:S(2)}, u32[]{:S(2)}) collective-permute-start(bf16[768,384]{1,0:T(8,128)(2,1)} %get-tuple-element.360), channel_id=1, source_target_pairs={{0,1},{1,0},{2,3},{3,2},{4,5},{5,4},{6,7},{7,6},{8,9},{9,8},{10,11... | collective-permute-start | bytes 1769480 | tf_op jit(solution)/shard_map/ppermute | solution.py:627
  237.8 16.8 %collective-permute-start.51 = (bf16[768,384]{1,0:T(8,128)(2,1)}, bf16[768,384]{1,0:T(8,128)(2,1)S(1)}, u32[]{:S(2)}, u32[]{:S(2)}) collective-permute-start(bf16[768,384]{1,0:T(8,128)(2,1)} %get-tuple-element.370), channel_id=1, source_target_pairs={{0,1},{1,0},{2,3},{3,2},{4,5},{5,4},{6,7},{7,6},{8,9},{9,8},{10,11... | collective-permute-start | bytes 1769480 | tf_op jit(solution)/shard_map/ppermute | solution.py:627
  238.3 13.2 %collective-permute-start.48 = (bf16[1,96,768]{2,1,0:T(8,128)(2,1)S(1)}, bf16[1,96,768]{2,1,0:T(8,128)(2,1)S(1)}, u32[]{:S(2)}, u32[]{:S(2)}) collective-permute-start(bf16[1,96,768]{2,1,0:T(8,128)(2,1)S(1)} %copy-done.117), channel_id=1, source_target_pairs={{0,16},{4,20},{8,24},{12,28},{16,0},{20,4},{24,8},{28,12},{1,17},{... | collective-permute-start | bytes 442376 | tf_op jit(solution)/shard_map/ppermute | solution.py:630
  251.5 25.3 %collective-permute-start.56 = (bf16[2,2,128,768]{3,2,1,0:T(8,128)(2,1)}, bf16[2,2,128,768]{3,2,1,0:T(8,128)(2,1)S(1)}, u32[]{:S(2)}, u32[]{:S(2)}) collective-permute-start(bf16[2,2,128,768]{3,2,1,0:T(8,128)(2,1)} %get-tuple-element.401), channel_id=1, source_target_pairs={{0,2},{1,3},{2,0},{3,1},{4,6},{5,7},{6,4},{7,5},{8,10},{9,11},{10,... | collective-permute-start | bytes 2359304 | tf_op jit(solution)/shard_map/ppermute | solution.py:627
  259.2 21.7 %collective-permute-start.53 = (bf16[1,384,768]{2,1,0:T(8,128)(2,1)}, bf16[1,384,768]{2,1,0:T(8,128)(2,1)S(1)}, u32[]{:S(2)}, u32[]{:S(2)}) collective-permute-start(bf16[1,384,768]{2,1,0:T(8,128)(2,1)} %get-tuple-element.372), channel_id=1, source_target_pairs={{0,8},{4,12},{8,0},{12,4},{16,24},{20,28},{24,16},{28,20},{1,9},{5... | collective-permute-start | bytes 1769480 | tf_op jit(solution)/shard_map/ppermute | solution.py:630
  259.2 21.7 %collective-permute-start.54 = (bf16[2,96,768]{2,1,0:T(8,128)(2,1)S(1)}, bf16[2,96,768]{2,1,0:T(8,128)(2,1)S(1)}, u32[]{:S(2)}, u32[]{:S(2)}) collective-permute-start(bf16[2,96,768]{2,1,0:T(8,128)(2,1)S(1)} %copy-done.116), channel_id=1, source_target_pairs={{0,8},{4,12},{8,0},{12,4},{16,24},{20,28},{24,16},{28,20},{1,9},{5... | collective-permute-start | bytes 884744 | tf_op jit(solution)/shard_map/ppermute | solution.py:630
  274.6 45.4 %collective-permute-start.59 = (bf16[2,2,128,768]{3,2,1,0:T(8,128)(2,1)}, bf16[2,2,128,768]{3,2,1,0:T(8,128)(2,1)S(1)}, u32[]{:S(2)}, u32[]{:S(2)}) collective-permute-start(bf16[2,2,128,768]{3,2,1,0:T(8,128)(2,1)} %get-tuple-element.408), channel_id=1, source_target_pairs={{0,2},{1,3},{2,0},{3,1},{4,6},{5,7},{6,4},{7,5},{8,10},{9,11},{10,... | collective-permute-start | bytes 2359304 | tf_op jit(solution)/shard_map/ppermute | solution.py:627
  276.8 39.7 %collective-permute-start.57 = (bf16[2,128,768]{2,1,0:T(8,128)(2,1)S(1)}, bf16[2,128,768]{2,1,0:T(8,128)(2,1)S(1)}, u32[]{:S(2)}, u32[]{:S(2)}) collective-permute-start(bf16[2,128,768]{2,1,0:T(8,128)(2,1)S(1)} %dynamic-slice_bitcast_fusion.1), channel_id=1, source_target_pairs={{0,1},{1,0},{2,3},{3,2},{4,5},{5,4},{6,7},{7,6},{8,9},{9,8},{10,11... | collective-permute-start | bytes 1179656 | tf_op jit(solution)/shard_map/ppermute | solution.py:627
  301.0 11.1 %collective-permute-start.9 = (bf16[1,96,768]{2,1,0:T(8,128)(2,1)}, bf16[1,96,768]{2,1,0:T(8,128)(2,1)S(1)}, u32[]{:S(2)}, u32[]{:S(2)}) collective-permute-start(bf16[1,96,768]{2,1,0:T(8,128)(2,1)} %get-tuple-element.50), channel_id=1, source_target_pairs={{0,16},{4,20},{8,24},{12,28},{16,0},{20,4},{24,8},{28,12},{1,17},{... | collective-permute-start | bytes 442376 | tf_op jit(solution)/shard_map/cond/branch_1_fun/ppermute | solution.py:630
  301.7 12.3 %collective-permute-start.8 = (bf16[1,96,768]{2,1,0:T(8,128)(2,1)}, bf16[1,96,768]{2,1,0:T(8,128)(2,1)}, u32[]{:S(2)}, u32[]{:S(2)}) collective-permute-start(bf16[1,96,768]{2,1,0:T(8,128)(2,1)} %get-tuple-element.54), channel_id=1, source_target_pairs={{0,16},{4,20},{8,24},{12,28},{16,0},{20,4},{24,8},{28,12},{1,17},{... | collective-permute-start | bytes 442376 | tf_op jit(solution)/shard_map/cond/branch_1_fun/ppermute | solution.py:630
  (148 other events, 1093.9 us)

commit v4 on v3

--- a/solution.py
+++ b/solution.py
@@ -59,7 +59,7 @@
         operands = [pltpu.with_memory_space_constraint(v, pltpu.HBM) for v in operands]
     out = pl.pallas_call(
         body,
-        out_shape=jax.tree.map(lambda v: pltpu.HBM(v.shape, v.dtype), out_shape),
+        out_shape=jax.tree.map(lambda v: pltpu.HBM(v.shape, v.dtype), out_shape) if name in ("up", "attend", "up_back") else out_shape,
         grid_spec=pltpu.PrefetchScalarGridSpec(
             num_scalar_prefetch=len(scalars),
             grid=grid,
@@ -617,7 +617,7 @@
     )
 
 
-COST_FAR, COST_OUT, COST_END = 14 * 10**9, 6 * 10**9, 2 * 10**9
+COST_FAR, COST_OUT, COST_END = 14 * 10**9, 4 * 10**9, 2 * 10**9
 
 
 def program(dp_size, tensor_size):
@@ -786,33 +786,32 @@
 
         def project_far(values):
             passed = [pp_tensor(v, 1) for v in wq_far]
-            return passed, project(clock, values, wq_far, bqkv[2])
-
-        passed, q_first = block(project_far, h1)
+            ups, downs = pp_tensor(w_up, 1), pp_tensor(w_down, 1)
+            return passed, project(clock, values, wq_far, bqkv[2]), ups, downs
+
+        passed, q_first, wu_near, wd_near = block(project_far, h1)
         wq += [wq_far, passed]
         qkv += [q_first, project(clock, h1, wq[3], bqkv[3])]
         attn_b = attend_call(clock, lens, qkv[2:], None, length, COST_FAR)
-        wu_near = [pp_tensor(clock.after(v), 1) for v in (w_up[:cut], up_second)]
         first_far = clock.after(first_far)
         wo_far = first_far[cut:]
         wo = [w_out, wo_near, wo_far, pp_tensor(wo_far, 1)]
         ctx = [attn_a[0], attn_a[1], attn_b[0], attn_b[1]]
-        resid, h2 = attention_out(clock, x, ctx, wo, (b_out, ln2_gain, ln2_bias), COST_OUT)
+        resid, h2 = attention_out(clock, x, ctx, wo, (b_out, ln2_gain, ln2_bias))
         ups = [up(clock, h2, [w_up], bup[0])]
         wu_far = [first_far[:cut], clock.after(second_far)]
-        wu = [[w_up], wu_near, wu_far, [pp_tensor(v, 1) for v in wu_far]]
+        wu = [[w_up], [wu_near], wu_far, [pp_tensor(v, 1) for v in wu_far]]
         ups.append(up(clock, h2, wu[1], bup[1], COST_OUT))
         cot.forward()
         ups.append(up(clock, h2, wu[3], bup[3]))
         g_low, bias_down = join_mask(clock, cot.blocks(), t, lens)
-        wd_near = [pp_tensor(clock.after(v), 1) for v in (w_down[:cut], w_down[cut:])]
-
-        near = from_near([tie(g_low, *wd_near)], [[(0, ups[1][0])], [(0, ups[2][0])]])
+
+        near = from_near([g_low], [[(0, ups[1][0])], [(0, ups[2][0])]])
         ups.insert(2, up(clock, h2, wu[2], bup[2]))
         acts, slopes = [u[0] for u in ups], [u[1] for u in ups]
         down = Chain([g_low], [[(0, acts[0])], [(0, acts[2])]], near, ["y", 0, 1] + high)
         wd_far = clock.after(wd_far)
-        wd = [[w_down], wd_near, [wd_far], [pp_tensor(wd_far, 1)]]
+        wd = [[w_down], [wd_near], [wd_far], [pp_tensor(wd_far, 1)]]
         dups_a, sums_a, dh2 = up_back(clock, g_low, wu[:2], wd[:2], slopes[:2], None, None, None)
         dups_b, sums_b, rest = up_back(clock, g_low, wu[2:], wd[2:], slopes[2:], dh2[0], resid, ln2_gain)
         dres, dres_low, gain_two, shift_two, bias_attn = rest

time: 330 us -> 303 us (0.918)
  Pallas kernels: 174 us -> 163 us
  waiting for transfers between devices: 52.5 us -> 42.2 us
  local copies, waits for them, and re-layouts: 39.1 us -> 34.9 us
    ppermute x49 -> x47, waiting for transfers between devices: 32 us -> 19.7 us  [pp_tensor(): lax.ppermute(values, 'tensor', [(i, i ^ flip) for i in range(tensor_size)])]
    pallas_call x39, Pallas kernels: 174 us -> 163 us  [call(): pl.pallas_call(body, out_shape=jax.tree.map(lambda v: pltpu.HBM(v.shape,...]
    ppermute x12, starting transfers between devices: 22.4 us -> 12.5 us  [pp_dp(): lax.ppermute(values, 'dp', [(i, i ^ 1 << bit) for i in range(dp_size)])]
    ppermute x49 -> x47, starting transfers between devices: 27.1 us -> 36.5 us  [pp_tensor(): lax.ppermute(values, 'tensor', [(i, i ^ flip) for i in range(tensor_size)])]
    unnamed x235 -> x191, local copies, waits for them, and re-layouts: 21.2 us -> 15.1 us
  transfers between devices with their start and end apart: 61 -> 59, of which waited for: 19 -> 19; matrix products, arithmetic and copies ran while one was open for 6% -> 8% of each run, Pallas kernels for 51% -> 52%
where the time goes in v4:
time: 303 us; the launch traced here: 299 us
  Pallas kernels  163 us (54%)
  starting transfers between devices  49 us (16%)
  waiting for transfers between devices  42.2 us (14%)
  local copies, waits for them, and re-layouts  34.9 us (12%)
  other arithmetic  7.54 us (2%)
    pallas_call x39, Pallas kernels, call(): pl.pallas_call(body, out_shape=jax.tree.map(lambda v: pltpu.HBM(v.shape,...  163 us
    ppermute x47, starting transfers between devices, pp_tensor(): lax.ppermute(values, 'tensor', [(i, i ^ flip) for i in range(tensor_size)])  36.5 us
    ppermute x12, waiting for transfers between devices, pp_dp(): lax.ppermute(values, 'dp', [(i, i ^ 1 << bit) for i in range(dp_size)])  22.5 us
    ppermute x47, waiting for transfers between devices, pp_tensor(): lax.ppermute(values, 'tensor', [(i, i ^ flip) for i in range(tensor_size)])  19.7 us
    unnamed x191, local copies, waits for them, and re-layouts  15.1 us
    ppermute x12, starting transfers between devices, pp_dp(): lax.ppermute(values, 'dp', [(i, i ^ 1 << bit) for i in range(dp_size)])  12.5 us
  transfers between devices with their start and end apart: 59, of which 19 were waited for; matrix products, arithmetic and copies ran while one was open for 8% of the time, Pallas kernels for 52%

profile of v4, /device:TPU:0, one launch (start us, length us, event | category | flops | bytes accessed | tf_op | source)
XLA Modules:
  0.0 298.9 jit_solution(13053219455477440875)
XLA Ops:
  17.3 7.7 %collective-permute-done.21 = f32[2,1152]{1,0:T(2,128)S(1)} collective-permute-done((f32[2,1152]{1,0:T(2,128)S(1)}, f32[2,1152]{1,0:T(2,128)S(1)}, u32[]{:S(2)}, u32[]{:S(2)}) %collective-permute-start.21) | collective-permute-done | bytes 9248 | tf_op jit(solution)/shard_map/ppermute | solution.py:627
  37.0 7.5 %attend.2 = (bf16[1024,192]{1,0:T(8,128)(2,1)}, bf16[1024,192]{1,0:T(8,128)(2,1)}, bf16[2,6,512,512]{3,2,1,0:T(8,128)(2,1)}, f32[2,6,512]{2,1,0:T(8,128)}) custom-call(s32[2]{0:T(128)S(1)} %dynamic_slice.44.lens.n, bf16[1024,576]{1,0:T(8,128)(2,1)S(1)} %project.5.refs_0_, bf16[1024,576]{1,0:T(8,128)(2,1)S(1)} %project.6.refs_1_), custom_call_target="tpu_custom_call" | custom-call | tf_op jit(solution)/shard_map/attend/pallas_call | solution.py:60
  46.9 6.3 %conditional.2 = (bf16[384,576]{1,0:T(8,128)(2,1)}, bf16[384,576]{1,0:T(8,128)(2,1)}, bf16[1024,576]{1,0:T(8,128)(2,1)S(1)}, bf16[768,768]{1,0:T(8,128)(2,1)}, bf16[768,768]{1,0:T(8,128)(2,1)}) conditional(s32[]{:T(128)} %bitcast.15, () %tuple.113, (bf16[384,576]{1,0:T(8,128)(2,1)S(1)}, bf16[384,576]{1,0:T(8,128)(2,1)S(1)}, f32[576]{0:T(1024)S(1)}, ...), branch_computations={%region_0.1_spmd, %region_1.2_spmd} | conditional | bytes 12980936 | solution.py:748
  55.2 4.5 %project.7.refs_1_ = bf16[1024,576]{1,0:T(8,128)(2,1)S(1)} custom-call(bf16[1024,768]{1,0:T(8,128)(2,1)} %copy-done.68, f32[1,576]{1,0:T(1,128)S(1)} %reshape.181.bias_ref, bf16[384,576]{1,0:T(8,128)(2,1)} %get-tuple-element.270.refs_0_.refs_10_, bf16[384,576]{1,0:T(8,128)(2,1)} %get-tuple-element.272.refs_1_.refs_11_), custom_call_target="tpu_custom_call" | custom-call | tf_op jit(solution)/shard_map/project/pallas_call | solution.py:60
  59.8 7.2 %attend.3 = (bf16[1024,192]{1,0:T(8,128)(2,1)}, bf16[1024,192]{1,0:T(8,128)(2,1)}, bf16[2,6,512,512]{3,2,1,0:T(8,128)(2,1)}, f32[2,6,512]{2,1,0:T(8,128)}) custom-call(s32[2]{0:T(128)S(1)} %dynamic_slice.44.lens.n, bf16[1024,576]{1,0:T(8,128)(2,1)S(1)} %get-tuple-element.333.refs_0_, bf16[1024,576]{1,0:T(8,128)(2,1)S(1)} %project.7.refs_1_), custom_call_target="tpu_custom_call" | custom-call | flops 14000000000 | tf_op jit(solution)/shard_map/attend/pallas_call | solution.py:60
  76.7 5.4 %attention_out.1 = (f32[1024,768]{1,0:T(8,128)S(1)}, bf16[1024,768]{1,0:T(8,128)(2,1)S(1)}) custom-call(bf16[1024,768]{1,0:T(8,128)(2,1)} %copy-done.11, bf16[1024,192]{1,0:T(8,128)(2,1)} %get-tuple-element.264.refs_0_.refs_4_, bf16[1024,192]{1,0:T(8,128)(2,1)} %get-tuple-element.276.refs_1_.refs_3_, bf16[1024,192]{1,0:T(8,128)(2,1)} %get-tuple-element.274.refs_2_.refs_3_, ...), custom_call_target="tpu_custom_call" | custom-call | tf_op jit(solution)/shard_map/attention_out/pallas_call | solution.py:60
  83.8 3.8 %up.4 = (bf16[1024,768]{1,0:T(8,128)(2,1)}, bf16[1024,768]{1,0:T(8,128)(2,1)}) custom-call(bf16[1024,768]{1,0:T(8,128)(2,1)S(1)} %get-tuple-element.328.h_ref.refs_0_, f32[1,768]{1,0:T(1,128)S(1)} %reshape.188.bias_ref, bf16[768,768]{1,0:T(8,128)(2,1)S(1)} %copy-done.71), custom_call_target="tpu_custom_call" | custom-call | tf_op jit(solution)/shard_map/up/pallas_call | solution.py:60
  88.0 5.2 %up.5 = (bf16[1024,768]{1,0:T(8,128)(2,1)}, bf16[1024,768]{1,0:T(8,128)(2,1)}) custom-call(bf16[1024,768]{1,0:T(8,128)(2,1)S(1)} %get-tuple-element.328.h_ref.refs_0_, f32[1,768]{1,0:T(1,128)S(1)} %reshape.189.bias_ref, bf16[768,768]{1,0:T(8,128)(2,1)} %get-tuple-element.285.refs_0_.refs_1_), custom_call_target="tpu_custom_call" | custom-call | flops 4000000000 | tf_op jit(solution)/shard_map/up/pallas_call | solution.py:60
  96.3 4.3 %up.6 = (bf16[1024,768]{1,0:T(8,128)(2,1)}, bf16[1024,768]{1,0:T(8,128)(2,1)}) custom-call(bf16[1024,768]{1,0:T(8,128)(2,1)S(1)} %get-tuple-element.328.h_ref.refs_0_, f32[1,768]{1,0:T(1,128)S(1)} %get-tuple-element.470.bias_ref, bf16[384,768]{1,0:T(8,128)(2,1)S(1)} %collective-permute-done.24.refs_0_.refs_2_, ...), custom_call_target="tpu_custom_call" | custom-call | tf_op jit(solution)/shard_map/up/pallas_call | solution.py:60
  102.8 4.8 %weight_grads.8 = (bf16[768,384]{1,0:T(8,128)(2,1)S(1)}, bf16[768,384]{1,0:T(8,128)(2,1)S(1)}, bf16[768,384]{1,0:T(8,128)(2,1)S(1)}, bf16[768,384]{1,0:T(8,128)(2,1)S(1)}) custom-call(bf16[1024,768]{1,0:T(8,128)(2,1)S(1)} %get-tuple-element.312.refs_0_.g_ref, bf16[1024,768]{1,0:T(8,128)(2,1)S(1)} %copy-done.12, ...), custom_call_target="tpu_custom_call" | custom-call | tf_op jit(solution)/shard_map/weight_grads/pallas_call | solution.py:60
  108.7 4.2 %up.7 = (bf16[1024,768]{1,0:T(8,128)(2,1)}, bf16[1024,768]{1,0:T(8,128)(2,1)}) custom-call(bf16[1024,768]{1,0:T(8,128)(2,1)S(1)} %get-tuple-element.328.h_ref.refs_0_, f32[1,768]{1,0:T(1,128)S(1)} %get-tuple-element.469.bias_ref, bf16[384,768]{1,0:T(8,128)(2,1)S(1)} %slice.140.refs_0_, bf16[384,768]{1,0:T(8,128)(2,1)S(1)} %collective-permute-done.25.refs_1_), custom_call_target="tpu_custom_call" | custom-call | tf_op jit(solution)/shard_map/up/pallas_call | solution.py:60
  113.0 6.0 %weight_grads.9 = (bf16[1,768,768]{2,1,0:T(8,128)(2,1)S(1)}, bf16[1,768,768]{2,1,0:T(8,128)(2,1)}) custom-call(bf16[1024,768]{1,0:T(8,128)(2,1)} %copy-done.3, bf16[1024,768]{1,0:T(8,128)(2,1)} %get-tuple-element.283.refs_1_.refs_0_, bf16[1024,768]{1,0:T(8,128)(2,1)} %get-tuple-element.301.refs_2_, bf16[768,384]{1,0:T(8,128)(2,1)S(1)} %collective-permute-done.30.refs_3_, ...), custom_call_target="tpu_custom_call" | custom-call | tf_op jit(solution)/shard_map/weight_grads/pallas_call | solution.py:60
  122.7 10.3 %up_back.2 = (bf16[1024,768]{1,0:T(8,128)(2,1)}, bf16[1024,768]{1,0:T(8,128)(2,1)}, f32[1,768]{1,0:T(1,128)}, f32[1,768]{1,0:T(1,128)}, f32[1024,768]{1,0:T(8,128)}) custom-call(bf16[1024,768]{1,0:T(8,128)(2,1)S(1)} %copy-done.4, bf16[768,768]{1,0:T(8,128)(2,1)} %refs_0_.3, bf16[768,768]{1,0:T(8,128)(2,1)} %get-tuple-element.285.refs_0_.refs_1_, ...), custom_call_target="tpu_custom_call" | custom-call | tf_op jit(solution)/shard_map/up_back/pallas_call | solution.py:60
  133.1 11.9 %up_back.3 = (bf16[1024,768]{1,0:T(8,128)(2,1)}, bf16[1024,768]{1,0:T(8,128)(2,1)}, f32[1,768]{1,0:T(1,128)}, f32[1,768]{1,0:T(1,128)}, f32[1024,768]{1,0:T(8,12...) custom-call(bf16[1024,768]{1,0:T(8,128)(2,1)} %copy-done.3, ...), custom_call_target="tpu_custom_call" | custom-call | tf_op jit(solution)/shard_map/up_back/pallas_call | solution.py:60
  145.0 5.3 %weight_grads.10 = (bf16[768,384]{1,0:T(8,128)(2,1)}, bf16[768,384]{1,0:T(8,128)(2,1)}, bf16[768,384]{1,0:T(8,128)(2,1)}, bf16[768,384]{1,0:T(8,128)(2,1)}) custom-call(bf16[1024,768]{1,0:T(8,128)(2,1)S(1)} %get-tuple-element.328.h_ref.refs_0_, bf16[1024,768]{1,0:T(8,128)(2,1)S(1)} %copy-done.40, bf16[1024,768]{1,0:T(8,128)(2,1)} %get-tuple-element.321.refs_2_), custom_call_target="tpu_custom_call" | custom-call | tf_op jit(solution)/shard_map/weight_grads/pallas_call | solution.py:60
  151.3 3.3 %add_split.11 = (bf16[4,96,768]{2,1,0:T(8,128)(2,1)}, bf16[4,96,768]{2,1,0:T(8,128)(2,1)S(1)}) custom-call(s32[1]{0:T(128)} %bitcast.24.at, bf16[4,2,96,768]{3,2,1,0:T(8,128)(2,1)S(1)} %bitcast.55, bf16[4,2,96,768]{3,2,1,0:T(8,128)(2,1)} %bitcast.28.arrived_ref), custom_call_target="tpu_custom_call" | custom-call | tf_op jit(solution)/shard_map/add_split/pallas_call | solution.py:60
  155.0 6.3 %weight_grads.11 = (bf16[1,768,768]{2,1,0:T(8,128)(2,1)S(1)}, bf16[1,768,768]{2,1,0:T(8,128)(2,1)}) custom-call(bf16[1024,768]{1,0:T(8,128)(2,1)} %copy-done.2, bf16[1024,768]{1,0:T(8,128)(2,1)} %get-tuple-element.311.refs_1_, bf16[1024,768]{1,0:T(8,128)(2,1)} %get-tuple-element.318.refs_2_, bf16[768,384]{1,0:T(8,128)(2,1)S(1)} %collective-permute-done.37.refs_3_, ...), custom_call_target="tpu_custom_call" | custom-call | tf_op jit(solution)/shard_map/weight_grads/pallas_call | solution.py:60
  164.4 8.1 %attend_back.2 = (bf16[1024,576]{1,0:T(8,128)(2,1)S(1)}, bf16[1024,576]{1,0:T(8,128)(2,1)S(1)}, f32[1,576]{1,0:T(1,128)S(1)}, f32[1,576]{1,0:T(1,128)S(1)}) custom-call(s32[2]{0:T(128)S(1)} %dynamic_slice.44.lens.n, bf16[1024,576]{1,0:T(8,128)(2,1)S(1)} %copy-done.73, bf16[1024,576]{1,0:T(8,128)(2,1)S(1)} %copy-done.17, bf16[1024,768]{1,0:T(8,128)(2,1)S(1)} %copy-done, ...), custom_call_target="tpu_custom_call" | custom-call | tf_op jit(solution)/shard_map/attend_back/pallas_call | solution.py:60
  173.6 3.6 %weight_grads.12 = (bf16[768,384]{1,0:T(8,128)(2,1)}, bf16[768,384]{1,0:T(8,128)(2,1)}) custom-call(bf16[1024,768]{1,0:T(8,128)(2,1)S(1)} %copy-done.69, bf16[1024,768]{1,0:T(8,128)(2,1)S(1)} %copy-done, bf16[1024,576]{1,0:T(8,128)(2,1)S(1)} %get-tuple-element.339.refs_2_.refs_3_, bf16[1024,192]{1,0:T(8,128)(2,1)S(1)} %copy-done.28), custom_call_target="tpu_custom_call" | custom-call | tf_op jit(solution)/shard_map/weight_grads/pallas_call | solution.py:60
  177.3 4.3 %collective-permute-start.42 = (bf16[768,384]{1,0:T(8,128)(2,1)}, bf16[768,384]{1,0:T(8,128)(2,1)S(1)}, u32[]{:S(2)}, u32[]{:S(2)}) collective-permute-start(bf16[768,384]{1,0:T(8,128)(2,1)} %get-tuple-element.340), channel_id=1, source_target_pairs={{0,1},{1,0},{2,3},{3,2},{4,5},{5,4},{6,7},{7,6},{8,9},{9,8},{10,11... | collective-permute-start | bytes 1769480 | tf_op jit(solution)/shard_map/ppermute | solution.py:627
  187.8 4.3 %weight_grads.13 = bf16[1,768,768]{2,1,0:T(8,128)(2,1)} custom-call(bf16[1024,768]{1,0:T(8,128)(2,1)} %copy-done.68, bf16[1024,768]{1,0:T(8,128)(2,1)S(1)} %copy-done, bf16[1024,576]{1,0:T(8,128)(2,1)S(1)} %copy-done.14, bf16[1024,192]{1,0:T(8,128)(2,1)S(1)} %copy-done.26, bf16[768,384]{1,0:T(8,128)(2,1)S(1)} %copy-done.51, ...), custom_call_target="tpu_custom_call" | custom-call | tf_op jit(solution)/shard_map/weight_grads/pallas_call | solution.py:60
  196.0 8.1 %attend_back.3 = (bf16[1024,576]{1,0:T(8,128)(2,1)S(1)}, bf16[1024,576]{1,0:T(8,128)(2,1)S(1)}, f32[1,576]{1,0:T(1,128)S(1)}, f32[1,576]{1,0:T(1,128)S(1)}) custom-call(s32[2]{0:T(128)S(1)} %dynamic_slice.44.lens.n, bf16[1024,576]{1,0:T(8,128)(2,1)S(1)} %copy-done.7, bf16[1024,576]{1,0:T(8,128)(2,1)S(1)} %copy-done.9, ...), custom_call_target="tpu_custom_call" | custom-call | tf_op jit(solution)/shard_map/attend_back/pallas_call | solution.py:60
  206.8 3.9 %weight_grads.14 = (bf16[768,384]{1,0:T(8,128)(2,1)}, bf16[768,384]{1,0:T(8,128)(2,1)S(1)}) custom-call(bf16[1024,768]{1,0:T(8,128)(2,1)} %copy-done.68, bf16[1024,768]{1,0:T(8,128)(2,1)S(1)} %copy-done.1, bf16[1024,576]{1,0:T(8,128)(2,1)S(1)} %get-tuple-element.359.refs_2_.refs_1_, bf16[1024,192]{1,0:T(8,128)(2,1)S(1)} %copy-done.27), custom_call_target="tpu_custom_call" | custom-call | tf_op jit(solution)/shard_map/weight_grads/pallas_call | solution.py:60
  210.7 4.1 %collective-permute-start.48 = (bf16[768,384]{1,0:T(8,128)(2,1)}, bf16[768,384]{1,0:T(8,128)(2,1)S(1)}, u32[]{:S(2)}, u32[]{:S(2)}) collective-permute-start(bf16[768,384]{1,0:T(8,128)(2,1)} %get-tuple-element.360), channel_id=1, source_target_pairs={{0,1},{1,0},{2,3},{3,2},{4,5},{5,4},{6,7},{7,6},{8,9},{9,8},{10,11... | collective-permute-start | bytes 1769480 | tf_op jit(solution)/shard_map/ppermute | solution.py:627
  216.2 9.4 %down_out.1 = (bf16[2,128,768]{2,1,0:T(8,128)(2,1)S(1)}, bf16[2,128,768]{2,1,0:T(8,128)(2,1)}, bf16[2,2,128,768]{3,2,1,0:T(8,128)(2,1)}) custom-call(s32[1]{0:T(128)} %bitcast.14.at, f32[1024,768]{1,0:T(8,128)} %copy-done.5, bf16[1024,768]{1,0:T(8,128)(2,1)S(1)} %copy-done.10, bf16[1024,768]{1,0:T(8,128)(2,1)} %get-tuple-element.286.refs_1_, ...), custom_call_target="tpu_custom_call" | custom-call | tf_op jit(solution)/shard_map/down_out/pallas_call | solution.py:60
  227.5 3.9 %weight_grads.15 = (bf16[1,384,768]{2,1,0:T(8,128)(2,1)S(1)}, bf16[1,384,768]{2,1,0:T(8,128)(2,1)S(1)}) custom-call(s32[1]{0:T(128)} %bitcast.23.at.refs_0_, bf16[1024,768]{1,0:T(8,128)(2,1)} %copy-done.68, bf16[1024,768]{1,0:T(8,128)(2,1)} %get-tuple-element.334.refs_2_.refs_1_, bf16[1024,576]{1,0:T(8,128)(2,1)S(1)} %get-tuple-element.350.refs_3_.refs_0_, ...), custom_call_target="tpu_custom_call" | custom-call | tf_op jit(solution)/shard_map/weight_grads/pallas_call | solution.py:60
  233.7 12.4 %norm_one_back.1 = (bf16[2,128,768]{2,1,0:T(8,128)(2,1)S(1)}, bf16[2,128,768]{2,1,0:T(8,128)(2,1)}, bf16[2,2,128,768]{3,2,1,0:T(8,128)(2,1)S(1)}, f32[1,768]{1,0:T(1,128)S(1)}, f32[1,768]{1,0:T(1,128)S(1)}) custom-call(s32[1]{0:T(128)} %bitcast.14.at, bf16[1024,768]{1,0:T(8,128)(2,1)} %copy-done.11, f32[1024,768]{1,0:T(8,128)} %get-tuple-element.374.dres_ref, ...), custom_call_target="tpu_custom_call" | custom-call | tf_op jit(solution)/shard_map/norm_one_back/pallas_call | solution.py:60
  247.7 5.3 %collective-permute-done.52 = bf16[2,96,768]{2,1,0:T(8,128)(2,1)S(1)} collective-permute-done((bf16[2,96,768]{2,1,0:T(8,128)(2,1)S(1)}, bf16[2,96,768]{2,1,0:T(8,128)(2,1)S(1)}, u32[]{:S(2)}, u32[]{:S(2)}) %collective-permute-start.52) | collective-permute-done | bytes 294944 | tf_op jit(solution)/shard_map/ppermute | solution.py:630
  253.0 35.0 %conditional.3 = (f32[14,768]{1,0:T(8,128)}, f32[96,768]{1,0:T(8,128)S(1)}, f32[3,96,192]{2,1,0:T(8,128)S(1)}, bf16[1,768]{1,0:T(2,128)(2,1)}, bf16[1,768]{1,0:T...) conditional(s32[]{:T(128)} %bitcast.15, () %tuple.163, ...), branch_computations={%region_2.3_spmd, %region_3.4_spmd} | conditional | flops 611328 | bytes 6270400 | solution.py:748
  256.6 5.7 %collective-permute-done.5 = f32[14,768]{1,0:T(8,128)S(1)} collective-permute-done((f32[14,768]{1,0:T(8,128)S(1)}, f32[14,768]{1,0:T(8,128)S(1)}, u32[]{:S(2)}, u32[]{:S(2)}) %collective-permute-start.5) | collective-permute-done | bytes 43040 | tf_op jit(solution)/shard_map/cond/branch_1_fun/ppermute | solution.py:630
  267.5 4.1 %collective-permute-done.8 = f32[14,768]{1,0:T(8,128)S(1)} collective-permute-done((f32[14,768]{1,0:T(8,128)S(1)}, f32[14,768]{1,0:T(8,128)S(1)}, u32[]{:S(2)}, u32[]{:S(2)}) %collective-permute-start.8) | collective-permute-done | bytes 43040 | tf_op jit(solution)/shard_map/cond/branch_1_fun/ppermute | solution.py:630
  278.6 5.1 %collective-permute-done.11 = bf16[1,96,768]{2,1,0:T(8,128)(2,1)S(1)} collective-permute-done((bf16[1,96,768]{2,1,0:T(8,128)(2,1)S(1)}, bf16[1,96,768]{2,1,0:T(8,128)(2,1)S(1)}, u32[]{:S(2)}, u32[]{:S(2)}) %collective-permute-start.11) | collective-permute-done | bytes 147488 | tf_op jit(solution)/shard_map/cond/branch_1_fun/ppermute | solution.py:630
  (370 shorter events, 116.7 us)
Async XLA Ops:
  3.7 12.4 %collective-permute-start.17 = (bf16[2,128,768]{2,1,0:T(8,128)(2,1)}, bf16[2,128,768]{2,1,0:T(8,128)(2,1)}, u32[]{:S(2)}, u32[]{:S(2)}) collective-permute-start(bf16[2,128,768]{2,1,0:T(8,128)(2,1)} %get-tuple-element.463), channel_id=1, source_target_pairs={{0,3},{1,2},{2,1},{3,0},{4,7},{5,6},{6,5},{7,4},{8,11},{9,10},{10,... | collective-permute-start | bytes 1179656 | tf_op jit(solution)/shard_map/ppermute | solution.py:627
  6.4 22.4 %collective-permute-start.16 = (bf16[2,128,768]{2,1,0:T(8,128)(2,1)}, bf16[2,128,768]{2,1,0:T(8,128)(2,1)}, u32[]{:S(2)}, u32[]{:S(2)}) collective-permute-start(bf16[2,128,768]{2,1,0:T(8,128)(2,1)} %get-tuple-element.466), channel_id=1, source_target_pairs={{0,2},{1,3},{2,0},{3,1},{4,6},{5,7},{6,4},{7,5},{8,10},{9,11},{10,... | collective-permute-start | bytes 1179656 | tf_op jit(solution)/shard_map/ppermute | solution.py:627
  7.2 20.0 %collective-permute-start.14 = (bf16[384,576]{1,0:T(8,128)(2,1)S(1)}, bf16[384,576]{1,0:T(8,128)(2,1)S(1)}, u32[]{:S(2)}, u32[]{:S(2)}) collective-permute-start(bf16[384,576]{1,0:T(8,128)(2,1)S(1)} %get-tuple-element.258.refs_0_.refs_4_), channel_id=1, source_target_pairs={{0,1},{1,0},{2,3},{3,2},{4,5},{5,4},{6,7},{7,6},{8,9},{9,8},{10,11... | collective-permute-start | bytes 1327112 | tf_op jit(solution)/shard_map/ppermute | solution.py:627
  7.4 20.0 %collective-permute-start.15 = (bf16[384,576]{1,0:T(8,128)(2,1)S(1)}, bf16[384,576]{1,0:T(8,128)(2,1)S(1)}, u32[]{:S(2)}, u32[]{:S(2)}) collective-permute-start(bf16[384,576]{1,0:T(8,128)(2,1)S(1)} %get-tuple-element.266.refs_1_.refs_5_), channel_id=1, source_target_pairs={{0,1},{1,0},{2,3},{3,2},{4,5},{5,4},{6,7},{7,6},{8,9},{9,8},{10,11... | collective-permute-start | bytes 1327112 | tf_op jit(solution)/shard_map/ppermute | solution.py:627
  11.3 13.7 %collective-permute-start.21 = (f32[2,1152]{1,0:T(2,128)S(1)}, f32[2,1152]{1,0:T(2,128)S(1)}, u32[]{:S(2)}, u32[]{:S(2)}) collective-permute-start(f32[2,1152]{1,0:T(2,128)S(1)} %pad_maximum_fusion.6), channel_id=1, source_target_pairs={{0,2},{1,3},{2,0},{3,1},{4,6},{5,7},{6,4},{7,5},{8,10},{9,11},{10,... | collective-permute-start | bytes 27656 | tf_op jit(solution)/shard_map/ppermute | solution.py:627
  16.2 28.4 %collective-permute-start.20 = (bf16[384,576]{1,0:T(8,128)(2,1)S(1)}, bf16[384,576]{1,0:T(8,128)(2,1)S(1)}, u32[]{:S(2)}, u32[]{:S(2)}) collective-permute-start(bf16[384,576]{1,0:T(8,128)(2,1)S(1)} %get-tuple-element.266.refs_1_.refs_5_), channel_id=1, source_target_pairs={{0,2},{1,3},{2,0},{3,1},{4,6},{5,7},{6,4},{7,5},{8,10},{9,11},{10,... | collective-permute-start | bytes 1327112 | tf_op jit(solution)/shard_map/ppermute | solution.py:627
  25.0 21.1 %collective-permute-start.18 = (bf16[384,576]{1,0:T(8,128)(2,1)S(1)}, bf16[384,576]{1,0:T(8,128)(2,1)S(1)}, u32[]{:S(2)}, u32[]{:S(2)}) collective-permute-start(bf16[384,576]{1,0:T(8,128)(2,1)S(1)} %get-tuple-element.258.refs_0_.refs_4_), channel_id=1, source_target_pairs={{0,2},{1,3},{2,0},{3,1},{4,6},{5,7},{6,4},{7,5},{8,10},{9,11},{10,... | collective-permute-start | bytes 1327112 | tf_op jit(solution)/shard_map/ppermute | solution.py:627
  27.4 39.6 %collective-permute-start.22 = (bf16[576,768]{1,0:T(8,128)(2,1)}, bf16[576,768]{1,0:T(8,128)(2,1)}, u32[]{:S(2)}, u32[]{:S(2)}) collective-permute-start(bf16[576,768]{1,0:T(8,128)(2,1)} %pad_maximum_fusion.1), channel_id=1, source_target_pairs={{0,2},{1,3},{2,0},{3,1},{4,6},{5,7},{6,4},{7,5},{8,10},{9,11},{10,... | collective-permute-start | bytes 2654216 | tf_op jit(solution)/shard_map/ppermute | solution.py:627
  53.2 34.5 %collective-permute-start.25 = (bf16[384,768]{1,0:T(8,128)(2,1)}, bf16[384,768]{1,0:T(8,128)(2,1)S(1)}, u32[]{:S(2)}, u32[]{:S(2)}) collective-permute-start(bf16[384,768]{1,0:T(8,128)(2,1)} %get-tuple-element.288), channel_id=1, source_target_pairs={{0,2},{1,3},{2,0},{3,1},{4,6},{5,7},{6,4},{7,5},{8,10},{9,11},{10,... | collective-permute-start | bytes 1769480 | tf_op jit(solution)/shard_map/ppermute | solution.py:627
  55.2 39.5 %collective-permute-start.28 = (bf16[2,2,128,768]{3,2,1,0:T(8,128)(2,1)}, bf16[2,2,128,768]{3,2,1,0:T(8,128)(2,1)}, u32[]{:S(2)}, u32[]{:S(2)}) collective-permute-start(bf16[2,2,128,768]{3,2,1,0:T(8,128)(2,1)} %bitcast.25), channel_id=1, source_target_pairs={{0,2},{1,3},{2,0},{3,1},{4,6},{5,7},{6,4},{7,5},{8,10},{9,11},{10,... | collective-permute-start | bytes 2359304 | tf_op jit(solution)/shard_map/ppermute | solution.py:627
  68.0 8.0 %collective-permute-start.23 = (bf16[192,768]{1,0:T(8,128)(2,1)S(1)}, bf16[192,768]{1,0:T(8,128)(2,1)S(1)}, u32[]{:S(2)}, u32[]{:S(2)}) collective-permute-start(bf16[192,768]{1,0:T(8,128)(2,1)S(1)} %slice.137.refs_6_.refs_3_), channel_id=1, source_target_pairs={{0,1},{1,0},{2,3},{3,2},{4,5},{5,4},{6,7},{7,6},{8,9},{9,8},{10,11... | collective-permute-start | bytes 884744 | tf_op jit(solution)/shard_map/ppermute | solution.py:627
  72.4 47.2 %collective-permute-start.34 = (bf16[768,768]{1,0:T(8,128)(2,1)}, bf16[768,768]{1,0:T(8,128)(2,1)S(1)}, u32[]{:S(2)}, u32[]{:S(2)}) collective-permute-start(bf16[768,768]{1,0:T(8,128)(2,1)} %refs_4_.3), channel_id=1, source_target_pairs={{0,2},{1,3},{2,0},{3,1},{4,6},{5,7},{6,4},{7,5},{8,10},{9,11},{10,... | collective-permute-start | bytes 3538952 | tf_op jit(solution)/shard_map/ppermute | solution.py:627
  75.7 20.5 %collective-permute-start.24 = (bf16[384,768]{1,0:T(8,128)(2,1)S(1)}, bf16[384,768]{1,0:T(8,128)(2,1)S(1)}, u32[]{:S(2)}, u32[]{:S(2)}) collective-permute-start(bf16[384,768]{1,0:T(8,128)(2,1)S(1)} %slice.140.refs_0_), channel_id=1, source_target_pairs={{0,1},{1,0},{2,3},{3,2},{4,5},{5,4},{6,7},{7,6},{8,9},{9,8},{10,11... | collective-permute-start | bytes 1769480 | tf_op jit(solution)/shard_map/ppermute | solution.py:627
  87.6 8.6 %collective-permute-start.26 = (bf16[384,768]{1,0:T(8,128)(2,1)S(1)}, bf16[384,768]{1,0:T(8,128)(2,1)S(1)}, u32[]{:S(2)}, u32[]{:S(2)}) collective-permute-start(bf16[384,768]{1,0:T(8,128)(2,1)S(1)} %collective-permute-done.25.refs_1_), channel_id=1, source_target_pairs={{0,1},{1,0},{2,3},{3,2},{4,5},{5,4},{6,7},{7,6},{8,9},{9,8},{10,11... | collective-permute-start | bytes 1769480 | tf_op jit(solution)/shard_map/ppermute | solution.py:627
  119.7 13.4 %collective-permute-start.35 = (bf16[768,768]{1,0:T(8,128)(2,1)S(1)}, bf16[768,768]{1,0:T(8,128)(2,1)S(1)}, u32[]{:S(2)}, u32[]{:S(2)}) collective-permute-start(bf16[768,768]{1,0:T(8,128)(2,1)S(1)} %collective-permute-done.34.refs_4_.refs_6_), channel_id=1, source_target_pairs={{0,1},{1,0},{2,3},{3,2},{4,5},{5,4},{6,7},{7,6},{8,9},{9,8},{10,11... | collective-permute-start | bytes 3538952 | tf_op jit(solution)/shard_map/ppermute | solution.py:627
  119.7 31.6 %collective-permute-start.36 = (bf16[1,768,768]{2,1,0:T(8,128)(2,1)}, bf16[1,768,768]{2,1,0:T(8,128)(2,1)}, u32[]{:S(2)}, u32[]{:S(2)}) collective-permute-start(bf16[1,768,768]{2,1,0:T(8,128)(2,1)} %get-tuple-element.324), channel_id=1, source_target_pairs={{0,2},{1,3},{2,0},{3,1},{4,6},{5,7},{6,4},{7,5},{8,10},{9,11},{10,... | collective-permute-start | bytes 3538952 | tf_op jit(solution)/shard_map/ppermute | solution.py:627
  162.3 41.8 %collective-permute-start.44 = (bf16[1,768,768]{2,1,0:T(8,128)(2,1)}, bf16[1,768,768]{2,1,0:T(8,128)(2,1)}, u32[]{:S(2)}, u32[]{:S(2)}) collective-permute-start(bf16[1,768,768]{2,1,0:T(8,128)(2,1)} %get-tuple-element.352), channel_id=1, source_target_pairs={{0,2},{1,3},{2,0},{3,1},{4,6},{5,7},{6,4},{7,5},{8,10},{9,11},{10,... | collective-permute-start | bytes 3538952 | tf_op jit(solution)/shard_map/ppermute | solution.py:627
  162.9 18.8 %collective-permute-start.41 = (bf16[4,96,768]{2,1,0:T(8,128)(2,1)}, bf16[4,96,768]{2,1,0:T(8,128)(2,1)S(1)}, u32[]{:S(2)}, u32[]{:S(2)}) collective-permute-start(bf16[4,96,768]{2,1,0:T(8,128)(2,1)} %get-tuple-element.327), channel_id=1, source_target_pairs={{0,4},{4,0},{8,12},{12,8},{16,20},{20,16},{24,28},{28,24},{1,5},{5... | collective-permute-start | bytes 1769480 | tf_op jit(solution)/shard_map/ppermute | solution.py:630
  192.1 35.4 %collective-permute-start.50 = (bf16[1,768,768]{2,1,0:T(8,128)(2,1)}, bf16[1,768,768]{2,1,0:T(8,128)(2,1)S(1)}, u32[]{:S(2)}, u32[]{:S(2)}) collective-permute-start(bf16[1,768,768]{2,1,0:T(8,128)(2,1)} %weight_grads.13), channel_id=1, source_target_pairs={{0,2},{1,3},{2,0},{3,1},{4,6},{5,7},{6,4},{7,5},{8,10},{9,11},{10,... | collective-permute-start | bytes 3538952 | tf_op jit(solution)/shard_map/ppermute | solution.py:627
  194.3 12.3 %collective-permute-start.45 = (bf16[2,96,768]{2,1,0:T(8,128)(2,1)}, bf16[2,96,768]{2,1,0:T(8,128)(2,1)S(1)}, u32[]{:S(2)}, u32[]{:S(2)}) collective-permute-start(bf16[2,96,768]{2,1,0:T(8,128)(2,1)} %get-tuple-element.344), channel_id=1, source_target_pairs={{0,8},{4,12},{8,0},{12,4},{16,24},{20,28},{24,16},{28,20},{1,9},{5... | collective-permute-start | bytes 884744 | tf_op jit(solution)/shard_map/ppermute | solution.py:630
  206.5 20.7 %collective-permute-start.47 = (bf16[4,96,768]{2,1,0:T(8,128)(2,1)S(1)}, bf16[4,96,768]{2,1,0:T(8,128)(2,1)S(1)}, u32[]{:S(2)}, u32[]{:S(2)}) collective-permute-start(bf16[4,96,768]{2,1,0:T(8,128)(2,1)S(1)} %get-tuple-element.354), channel_id=1, source_target_pairs={{0,4},{4,0},{8,12},{12,8},{16,20},{20,16},{24,28},{28,24},{1,5},{5... | collective-permute-start | bytes 1769480 | tf_op jit(solution)/shard_map/ppermute | solution.py:630
  210.7 16.8 %collective-permute-start.48 = (bf16[768,384]{1,0:T(8,128)(2,1)}, bf16[768,384]{1,0:T(8,128)(2,1)S(1)}, u32[]{:S(2)}, u32[]{:S(2)}) collective-permute-start(bf16[768,384]{1,0:T(8,128)(2,1)} %get-tuple-element.360), channel_id=1, source_target_pairs={{0,1},{1,0},{2,3},{3,2},{4,5},{5,4},{6,7},{7,6},{8,9},{9,8},{10,11... | collective-permute-start | bytes 1769480 | tf_op jit(solution)/shard_map/ppermute | solution.py:627
  214.8 12.7 %collective-permute-start.49 = (bf16[768,384]{1,0:T(8,128)(2,1)S(1)}, bf16[768,384]{1,0:T(8,128)(2,1)S(1)}, u32[]{:S(2)}, u32[]{:S(2)}) collective-permute-start(bf16[768,384]{1,0:T(8,128)(2,1)S(1)} %get-tuple-element.370), channel_id=1, source_target_pairs={{0,1},{1,0},{2,3},{3,2},{4,5},{5,4},{6,7},{7,6},{8,9},{9,8},{10,11... | collective-permute-start | bytes 1769480 | tf_op jit(solution)/shard_map/ppermute | solution.py:627
  214.8 10.8 %collective-permute-start.46 = (bf16[1,96,768]{2,1,0:T(8,128)(2,1)S(1)}, bf16[1,96,768]{2,1,0:T(8,128)(2,1)S(1)}, u32[]{:S(2)}, u32[]{:S(2)}) collective-permute-start(bf16[1,96,768]{2,1,0:T(8,128)(2,1)S(1)} %get-tuple-element.357), channel_id=1, source_target_pairs={{0,16},{4,20},{8,24},{12,28},{16,0},{20,4},{24,8},{28,12},{1,17},{... | collective-permute-start | bytes 442376 | tf_op jit(solution)/shard_map/ppermute | solution.py:630
  225.6 21.3 %collective-permute-start.54 = (bf16[2,2,128,768]{3,2,1,0:T(8,128)(2,1)}, bf16[2,2,128,768]{3,2,1,0:T(8,128)(2,1)S(1)}, u32[]{:S(2)}, u32[]{:S(2)}) collective-permute-start(bf16[2,2,128,768]{3,2,1,0:T(8,128)(2,1)} %get-tuple-element.401), channel_id=1, source_target_pairs={{0,2},{1,3},{2,0},{3,1},{4,6},{5,7},{6,4},{7,5},{8,10},{9,11},{10,... | collective-permute-start | bytes 2359304 | tf_op jit(solution)/shard_map/ppermute | solution.py:627
  231.5 21.6 %collective-permute-start.51 = (bf16[1,384,768]{2,1,0:T(8,128)(2,1)S(1)}, bf16[1,384,768]{2,1,0:T(8,128)(2,1)S(1)}, u32[]{:S(2)}, u32[]{:S(2)}) collective-permute-start(bf16[1,384,768]{2,1,0:T(8,128)(2,1)S(1)} %get-tuple-element.372), channel_id=1, source_target_pairs={{0,8},{4,12},{8,0},{12,4},{16,24},{20,28},{24,16},{28,20},{1,9},{5... | collective-permute-start | bytes 1769480 | tf_op jit(solution)/shard_map/ppermute | solution.py:630
  233.4 19.6 %collective-permute-start.52 = (bf16[2,96,768]{2,1,0:T(8,128)(2,1)S(1)}, bf16[2,96,768]{2,1,0:T(8,128)(2,1)S(1)}, u32[]{:S(2)}, u32[]{:S(2)}) collective-permute-start(bf16[2,96,768]{2,1,0:T(8,128)(2,1)S(1)} %get-tuple-element.368), channel_id=1, source_target_pairs={{0,8},{4,12},{8,0},{12,4},{16,24},{20,28},{24,16},{28,20},{1,9},{5... | collective-permute-start | bytes 884744 | tf_op jit(solution)/shard_map/ppermute | solution.py:630
  246.1 46.5 %collective-permute-start.57 = (bf16[2,2,128,768]{3,2,1,0:T(8,128)(2,1)S(1)}, bf16[2,2,128,768]{3,2,1,0:T(8,128)(2,1)S(1)}, u32[]{:S(2)}, u32[]{:S(2)}) collective-permute-start(bf16[2,2,128,768]{3,2,1,0:T(8,128)(2,1)S(1)} %get-tuple-element.408), channel_id=1, source_target_pairs={{0,2},{1,3},{2,0},{3,1},{4,6},{5,7},{6,4},{7,5},{8,10},{9,11},{10,... | collective-permute-start | bytes 2359304 | tf_op jit(solution)/shard_map/ppermute | solution.py:627
  246.8 42.0 %collective-permute-start.53 = (bf16[2,128,768]{2,1,0:T(8,128)(2,1)}, bf16[2,128,768]{2,1,0:T(8,128)(2,1)}, u32[]{:S(2)}, u32[]{:S(2)}) collective-permute-start(bf16[2,128,768]{2,1,0:T(8,128)(2,1)} %get-tuple-element.399), channel_id=1, source_target_pairs={{0,1},{1,0},{2,3},{3,2},{4,5},{5,4},{6,7},{7,6},{8,9},{9,8},{10,11... | collective-permute-start | bytes 1179656 | tf_op jit(solution)/shard_map/ppermute | solution.py:627
  253.2 10.2 %collective-permute-start.7 = (bf16[2,96,768]{2,1,0:T(8,128)(2,1)S(1)}, bf16[2,96,768]{2,1,0:T(8,128)(2,1)S(1)}, u32[]{:S(2)}, u32[]{:S(2)}) collective-permute-start(bf16[2,96,768]{2,1,0:T(8,128)(2,1)S(1)} %get-tuple-element.48), channel_id=1, source_target_pairs={{0,4},{4,0},{8,12},{12,8},{16,20},{20,16},{24,28},{28,24},{1,5},{5... | collective-permute-start | bytes 884744 | tf_op jit(solution)/shard_map/cond/branch_1_fun/ppermute | solution.py:630
  272.8 10.8 %collective-permute-start.11 = (bf16[1,96,768]{2,1,0:T(8,128)(2,1)S(1)}, bf16[1,96,768]{2,1,0:T(8,128)(2,1)S(1)}, u32[]{:S(2)}, u32[]{:S(2)}) collective-permute-start(bf16[1,96,768]{2,1,0:T(8,128)(2,1)S(1)} %get-tuple-element.56), channel_id=1, source_target_pairs={{0,16},{4,20},{8,24},{12,28},{16,0},{20,4},{24,8},{28,12},{1,17},{... | collective-permute-start | bytes 442376 | tf_op jit(solution)/shard_map/cond/branch_1_fun/ppermute | solution.py:630
  273.7 12.4 %collective-permute-start.10 = (bf16[1,96,768]{2,1,0:T(8,128)(2,1)}, bf16[1,96,768]{2,1,0:T(8,128)(2,1)}, u32[]{:S(2)}, u32[]{:S(2)}) collective-permute-start(bf16[1,96,768]{2,1,0:T(8,128)(2,1)} %get-tuple-element.60), channel_id=1, source_target_pairs={{0,16},{4,20},{8,24},{12,28},{16,0},{20,4},{24,8},{28,12},{1,17},{... | collective-permute-start | bytes 442376 | tf_op jit(solution)/shard_map/cond/branch_1_fun/ppermute | solution.py:630
  (122 other events, 888.5 us)

commit v5 on v4

--- a/solution.py
+++ b/solution.py
@@ -482,7 +482,7 @@
     )
 
 
-def pack(clock, shared, units, projected, me):
+def pack(clock, shared, units, projected, me, cost=0):
     count = len(units)
     first = len(shared)
 
@@ -503,7 +503,7 @@
     operands = (*shared, *units, *projected)
     return call(
         clock, body, out, operands, grid=(1,), in_specs=[whole(v) for v in operands], out_specs=whole(out),
-        scalars=(me.reshape(1),), name="pack",
+        scalars=(me.reshape(1),), name="pack", flops=cost,
     )
 
 
@@ -617,7 +617,7 @@
     )
 
 
-COST_FAR, COST_OUT, COST_END = 14 * 10**9, 4 * 10**9, 2 * 10**9
+COST_FAR, COST_OUT, COST_END = 14 * 10**9, 4 * 10**9, 7 * 10**9
 
 
 def program(dp_size, tensor_size):
@@ -839,55 +839,69 @@
         gin = Exchange(*in_blocks)
         shared = [gain_one, shift_one, gain_two, shift_two, bias_attn, bias_down]
         out.forward()
-        total = pack(clock, shared, bias_up, qkv_sums, t)
         chains += [grads_up, q_own]
         for chain in chains:
-            chain.flight = clock.after(chain.flight)
-
-        def finish(total, state):
+            chain.flight = clock.then(clock.after(chain.flight))
+        total = pack(clock, shared, bias_up, qkv_sums, t, COST_END)
+        out_blocks = out.blocks()
+
+        def moved(values, flip, tensor):
+            flight = pp_tensor(values, flip) if tensor else pp_dp(values, flip)
+            return clock.then(values + clock.after(flight))
+
+        def load(state):
             for chain, (keep, flight) in zip(chains, state):
                 chain.keep, chain.flight = keep, flight
 
-            def reduced(flip, tensor):
-                moved = pp_tensor(total, flip) if tensor else pp_dp(total, flip)
-                return clock.then(total + clock.after(moved))
-
+        def begin(total, state):
+            load(state)
+            for bit in high[:1]:
+                grads_up.step()
             q_own.step()
-            total = reduced(1, True)
-            total = reduced(0, False)
+            total = moved(total, 1, True)
+            for bit in (1, 0)[-bits:]:
+                total = moved(total, bit, False)
+            return total, [(chain.keep, clock.after(chain.flight)) for chain in chains]
+
+        def finish(total, state, blocks):
+            load(state)
+            for bit in high[1:]:
+                grads_up.step()
+            grad_up = clock.then(grads_up.last())
             for bit in high:
                 q_own.step()
-                grads_up.step()
-            for bit in range(1, bits):
-                total = reduced(bit, False)
-            total = reduced(2, True)
+                total = moved(total, bit, False)
+            total = moved(total, 2, True)
+            rows_out = join_rows(clock, blocks, t)
+            first = len(shared)
+            vectors = [total[i] for i in range(first)]
+            vectors.append(lax.dynamic_slice_in_dim(total, first + t, 1)[0, :units])
+            qv = lax.dynamic_slice_in_dim(total, first + tensor_size + t, 1)[0, : 2 * local]
+            vectors.append(qv.reshape(2, local))
             both = q_own.last()
             weights = jnp.stack([both[:, c * local : c * local + local] for c in range(3)])
-            return total, grads_up.last(), weights, both[:, 3 * local :].T
+            return rows_out, vectors, grad_up, weights, both[:, 3 * local :].T
 
         state = [(chain.keep, chain.flight) for chain in chains]
-        total, grad_up, grad_qkv, grad_out = block(finish, total, state)
-        layer_out = join_rows(clock, out.blocks(), t, COST_END)
+        total, state = block(begin, total, state)
         gin.forward()
+        layer_out, vector, grad_up, grad_qkv, grad_out = block(finish, total, state, out_blocks)
         grad_input = join_rows(clock, gin.blocks(), t)
-        first = len(shared)
-        units_sum = lax.dynamic_slice_in_dim(total, first + t, 1)[0, :units]
-        qv_sum = lax.dynamic_slice_in_dim(total, first + tensor_size + t, 1)[0, : 2 * local]
         return (
             layer_out,
             grad_input,
-            total[0],
-            total[1],
+            vector[0],
+            vector[1],
             grad_qkv,
-            qv_sum.reshape(2, local),
+            vector[7],
             grad_out,
-            total[4],
-            total[2],
-            total[3],
+            vector[4],
+            vector[2],
+            vector[3],
             grad_up,
-            units_sum,
+            vector[6],
             grad_down.T,
-            total[5],
+            vector[5],
         )
 
     return on_device

time: 303 us -> 294 us (0.970)
  waiting for transfers between devices: 42.2 us -> 37.4 us
  local copies, waits for them, and re-layouts: 34.9 us -> 30.8 us
  starting transfers between devices: 49 us -> 52.7 us
    ppermute x12, starting transfers between devices: 12.5 us -> 18.6 us  [pp_dp(): lax.ppermute(values, 'dp', [(i, i ^ 1 << bit) for i in range(dp_size)])]
    ppermute x12, waiting for transfers between devices: 22.5 us -> 16.8 us  [pp_dp(): lax.ppermute(values, 'dp', [(i, i ^ 1 << bit) for i in range(dp_size)])]
    unnamed x191 -> x197, local copies, waits for them, and re-layouts: 15.1 us -> 14.4 us
  transfers between devices with their start and end apart: 59 -> 59, of which waited for: 19 -> 18; matrix products, arithmetic and copies ran while one was open for 8% -> 7% of each run, Pallas kernels for 52% -> 53%
where the time goes in v5:
time: 294 us; the launch traced here: 290 us
  Pallas kernels  161 us (55%)
  starting transfers between devices  52.7 us (18%)
  waiting for transfers between devices  37.4 us (13%)
  local copies, waits for them, and re-layouts  30.8 us (10%)
  other arithmetic  5.17 us (2%)
    pallas_call x39, Pallas kernels, call(): pl.pallas_call(body, out_shape=jax.tree.map(lambda v: pltpu.HBM(v.shape,...  161 us
    ppermute x47, starting transfers between devices, pp_tensor(): lax.ppermute(values, 'tensor', [(i, i ^ flip) for i in range(tensor_size)])  34.1 us
    ppermute x47, waiting for transfers between devices, pp_tensor(): lax.ppermute(values, 'tensor', [(i, i ^ flip) for i in range(tensor_size)])  20.6 us
    ppermute x12, starting transfers between devices, pp_dp(): lax.ppermute(values, 'dp', [(i, i ^ 1 << bit) for i in range(dp_size)])  18.6 us
    ppermute x12, waiting for transfers between devices, pp_dp(): lax.ppermute(values, 'dp', [(i, i ^ 1 << bit) for i in range(dp_size)])  16.8 us
    unnamed x197, local copies, waits for them, and re-layouts  14.4 us
  transfers between devices with their start and end apart: 59, of which 18 were waited for; matrix products, arithmetic and copies ran while one was open for 7% of the time, Pallas kernels for 53%

profile of v5, /device:TPU:0, one launch (start us, length us, event | category | flops | bytes accessed | tf_op | source)
XLA Modules:
  0.0 289.6 jit_solution(12684740087614062142)
XLA Ops:
  17.3 7.7 %collective-permute-done.21 = f32[2,1152]{1,0:T(2,128)S(1)} collective-permute-done((f32[2,1152]{1,0:T(2,128)S(1)}, f32[2,1152]{1,0:T(2,128)S(1)}, u32[]{:S(2)}, u32[]{:S(2)}) %collective-permute-start.21) | collective-permute-done | bytes 9248 | tf_op jit(solution)/shard_map/ppermute | solution.py:627
  37.0 6.6 %attend.2 = (bf16[1024,192]{1,0:T(8,128)(2,1)}, bf16[1024,192]{1,0:T(8,128)(2,1)}, bf16[2,6,512,512]{3,2,1,0:T(8,128)(2,1)}, f32[2,6,512]{2,1,0:T(8,128)}) custom-call(s32[2]{0:T(128)S(1)} %dynamic_slice.44.lens.n, bf16[1024,576]{1,0:T(8,128)(2,1)S(1)} %project.5.refs_0_, bf16[1024,576]{1,0:T(8,128)(2,1)S(1)} %project.6.refs_1_), custom_call_target="tpu_custom_call" | custom-call | tf_op jit(solution)/shard_map/attend/pallas_call | solution.py:60
  46.9 6.1 %conditional.3 = (bf16[384,576]{1,0:T(8,128)(2,1)}, bf16[384,576]{1,0:T(8,128)(2,1)}, bf16[1024,576]{1,0:T(8,128)(2,1)S(1)}, bf16[768,768]{1,0:T(8,128)(2,1)}, bf16[768,768]{1,0:T(8,128)(2,1)}) conditional(s32[]{:T(128)} %bitcast.16, () %tuple.123, (bf16[384,576]{1,0:T(8,128)(2,1)S(1)}, bf16[384,576]{1,0:T(8,128)(2,1)S(1)}, f32[576]{0:T(1024)S(1)}, ...), branch_computations={%region_0.1_spmd, %region_1.2_spmd} | conditional | bytes 12980936 | solution.py:748
  55.2 4.5 %project.7.refs_1_ = bf16[1024,576]{1,0:T(8,128)(2,1)S(1)} custom-call(bf16[1024,768]{1,0:T(8,128)(2,1)} %copy-done.68, f32[1,576]{1,0:T(1,128)S(1)} %reshape.187.bias_ref, bf16[384,576]{1,0:T(8,128)(2,1)} %get-tuple-element.300.refs_0_.refs_10_, bf16[384,576]{1,0:T(8,128)(2,1)} %get-tuple-element.302.refs_1_.refs_11_), custom_call_target="tpu_custom_call" | custom-call | tf_op jit(solution)/shard_map/project/pallas_call | solution.py:60
  59.8 6.3 %attend.3 = (bf16[1024,192]{1,0:T(8,128)(2,1)}, bf16[1024,192]{1,0:T(8,128)(2,1)}, bf16[2,6,512,512]{3,2,1,0:T(8,128)(2,1)}, f32[2,6,512]{2,1,0:T(8,128)}) custom-call(s32[2]{0:T(128)S(1)} %dynamic_slice.44.lens.n, bf16[1024,576]{1,0:T(8,128)(2,1)S(1)} %get-tuple-element.363.refs_0_, bf16[1024,576]{1,0:T(8,128)(2,1)S(1)} %project.7.refs_1_), custom_call_target="tpu_custom_call" | custom-call | flops 14000000000 | tf_op jit(solution)/shard_map/attend/pallas_call | solution.py:60
  71.2 3.5 %collective-permute-start.34 = (bf16[768,768]{1,0:T(8,128)(2,1)}, bf16[768,768]{1,0:T(8,128)(2,1)S(1)}, u32[]{:S(2)}, u32[]{:S(2)}) collective-permute-start(bf16[768,768]{1,0:T(8,128)(2,1)} %refs_4_.3), channel_id=1, source_target_pairs={{0,2},{1,3},{2,0},{3,1},{4,6},{5,7},{6,4},{7,5},{8,10},{9,11},{10,... | collective-permute-start | bytes 3538952 | tf_op jit(solution)/shard_map/ppermute | solution.py:627
  76.8 5.4 %attention_out.1 = (f32[1024,768]{1,0:T(8,128)S(1)}, bf16[1024,768]{1,0:T(8,128)(2,1)S(1)}) custom-call(bf16[1024,768]{1,0:T(8,128)(2,1)} %copy-done.11, bf16[1024,192]{1,0:T(8,128)(2,1)} %get-tuple-element.294.refs_0_.refs_4_, bf16[1024,192]{1,0:T(8,128)(2,1)} %get-tuple-element.306.refs_1_.refs_3_, bf16[1024,192]{1,0:T(8,128)(2,1)} %get-tuple-element.304.refs_2_.refs_3_, ...), custom_call_target="tpu_custom_call" | custom-call | tf_op jit(solution)/shard_map/attention_out/pallas_call | solution.py:60
  83.9 3.9 %up.4 = (bf16[1024,768]{1,0:T(8,128)(2,1)}, bf16[1024,768]{1,0:T(8,128)(2,1)}) custom-call(bf16[1024,768]{1,0:T(8,128)(2,1)S(1)} %get-tuple-element.357.h_ref.refs_0_, f32[1,768]{1,0:T(1,128)S(1)} %reshape.191.bias_ref, bf16[768,768]{1,0:T(8,128)(2,1)S(1)} %copy-done.71), custom_call_target="tpu_custom_call" | custom-call | tf_op jit(solution)/shard_map/up/pallas_call | solution.py:60
  88.0 5.2 %up.5 = (bf16[1024,768]{1,0:T(8,128)(2,1)}, bf16[1024,768]{1,0:T(8,128)(2,1)}) custom-call(bf16[1024,768]{1,0:T(8,128)(2,1)S(1)} %get-tuple-element.357.h_ref.refs_0_, f32[1,768]{1,0:T(1,128)S(1)} %reshape.192.bias_ref, bf16[768,768]{1,0:T(8,128)(2,1)} %get-tuple-element.315.refs_0_.refs_1_), custom_call_target="tpu_custom_call" | custom-call | flops 4000000000 | tf_op jit(solution)/shard_map/up/pallas_call | solution.py:60
  96.3 4.2 %up.6 = (bf16[1024,768]{1,0:T(8,128)(2,1)}, bf16[1024,768]{1,0:T(8,128)(2,1)}) custom-call(bf16[1024,768]{1,0:T(8,128)(2,1)S(1)} %get-tuple-element.357.h_ref.refs_0_, f32[1,768]{1,0:T(1,128)S(1)} %get-tuple-element.492.bias_ref, bf16[384,768]{1,0:T(8,128)(2,1)S(1)} %collective-permute-done.24.refs_0_.refs_2_, ...), custom_call_target="tpu_custom_call" | custom-call | tf_op jit(solution)/shard_map/up/pallas_call | solution.py:60
  102.8 4.8 %weight_grads.8 = (bf16[768,384]{1,0:T(8,128)(2,1)S(1)}, bf16[768,384]{1,0:T(8,128)(2,1)S(1)}, bf16[768,384]{1,0:T(8,128)(2,1)S(1)}, bf16[768,384]{1,0:T(8,128)(2,1)S(1)}) custom-call(bf16[1024,768]{1,0:T(8,128)(2,1)S(1)} %get-tuple-element.342.refs_0_.g_ref, bf16[1024,768]{1,0:T(8,128)(2,1)S(1)} %copy-done.12, ...), custom_call_target="tpu_custom_call" | custom-call | tf_op jit(solution)/shard_map/weight_grads/pallas_call | solution.py:60
  108.7 4.2 %up.7 = (bf16[1024,768]{1,0:T(8,128)(2,1)}, bf16[1024,768]{1,0:T(8,128)(2,1)}) custom-call(bf16[1024,768]{1,0:T(8,128)(2,1)S(1)} %get-tuple-element.357.h_ref.refs_0_, f32[1,768]{1,0:T(1,128)S(1)} %get-tuple-element.491.bias_ref, bf16[384,768]{1,0:T(8,128)(2,1)S(1)} %slice.126.refs_0_, bf16[384,768]{1,0:T(8,128)(2,1)S(1)} %collective-permute-done.25.refs_1_), custom_call_target="tpu_custom_call" | custom-call | tf_op jit(solution)/shard_map/up/pallas_call | solution.py:60
  113.0 6.0 %weight_grads.9 = (bf16[1,768,768]{2,1,0:T(8,128)(2,1)S(1)}, bf16[1,768,768]{2,1,0:T(8,128)(2,1)}) custom-call(bf16[1024,768]{1,0:T(8,128)(2,1)} %copy-done.3, bf16[1024,768]{1,0:T(8,128)(2,1)} %get-tuple-element.313.refs_1_.refs_0_, bf16[1024,768]{1,0:T(8,128)(2,1)} %get-tuple-element.331.refs_2_, bf16[768,384]{1,0:T(8,128)(2,1)S(1)} %collective-permute-done.30.refs_3_, ...), custom_call_target="tpu_custom_call" | custom-call | tf_op jit(solution)/shard_map/weight_grads/pallas_call | solution.py:60
  122.7 10.3 %up_back.2 = (bf16[1024,768]{1,0:T(8,128)(2,1)}, bf16[1024,768]{1,0:T(8,128)(2,1)}, f32[1,768]{1,0:T(1,128)}, f32[1,768]{1,0:T(1,128)}, f32[1024,768]{1,0:T(8,128)}) custom-call(bf16[1024,768]{1,0:T(8,128)(2,1)S(1)} %copy-done.4, bf16[768,768]{1,0:T(8,128)(2,1)} %refs_0_.3, bf16[768,768]{1,0:T(8,128)(2,1)} %get-tuple-element.315.refs_0_.refs_1_, ...), custom_call_target="tpu_custom_call" | custom-call | tf_op jit(solution)/shard_map/up_back/pallas_call | solution.py:60
  133.1 11.9 %up_back.3 = (bf16[1024,768]{1,0:T(8,128)(2,1)}, bf16[1024,768]{1,0:T(8,128)(2,1)}, f32[1,768]{1,0:T(1,128)}, f32[1,768]{1,0:T(1,128)}, f32[1024,768]{1,0:T(8,12...) custom-call(bf16[1024,768]{1,0:T(8,128)(2,1)} %copy-done.3, ...), custom_call_target="tpu_custom_call" | custom-call | tf_op jit(solution)/shard_map/up_back/pallas_call | solution.py:60
  145.0 5.3 %weight_grads.10 = (bf16[768,384]{1,0:T(8,128)(2,1)}, bf16[768,384]{1,0:T(8,128)(2,1)}, bf16[768,384]{1,0:T(8,128)(2,1)}, bf16[768,384]{1,0:T(8,128)(2,1)}) custom-call(bf16[1024,768]{1,0:T(8,128)(2,1)S(1)} %get-tuple-element.357.h_ref.refs_0_, bf16[1024,768]{1,0:T(8,128)(2,1)S(1)} %copy-done.40, bf16[1024,768]{1,0:T(8,128)(2,1)} %get-tuple-element.351.refs_2_), custom_call_target="tpu_custom_call" | custom-call | tf_op jit(solution)/shard_map/weight_grads/pallas_call | solution.py:60
  155.0 6.3 %weight_grads.11 = (bf16[1,768,768]{2,1,0:T(8,128)(2,1)S(1)}, bf16[1,768,768]{2,1,0:T(8,128)(2,1)}) custom-call(bf16[1024,768]{1,0:T(8,128)(2,1)} %copy-done.2, bf16[1024,768]{1,0:T(8,128)(2,1)} %get-tuple-element.341.refs_1_, bf16[1024,768]{1,0:T(8,128)(2,1)} %get-tuple-element.348.refs_2_, bf16[768,384]{1,0:T(8,128)(2,1)S(1)} %collective-permute-done.37.refs_3_, ...), custom_call_target="tpu_custom_call" | custom-call | tf_op jit(solution)/shard_map/weight_grads/pallas_call | solution.py:60
  164.4 7.7 %attend_back.2 = (bf16[1024,576]{1,0:T(8,128)(2,1)S(1)}, bf16[1024,576]{1,0:T(8,128)(2,1)S(1)}, f32[1,576]{1,0:T(1,128)S(1)}, f32[1,576]{1,0:T(1,128)S(1)}) custom-call(s32[2]{0:T(128)S(1)} %dynamic_slice.44.lens.n, bf16[1024,576]{1,0:T(8,128)(2,1)S(1)} %copy-done.73, bf16[1024,576]{1,0:T(8,128)(2,1)S(1)} %copy-done.17, bf16[1024,768]{1,0:T(8,128)(2,1)S(1)} %copy-done, ...), custom_call_target="tpu_custom_call" | custom-call | tf_op jit(solution)/shard_map/attend_back/pallas_call | solution.py:60
  173.2 3.6 %weight_grads.12 = (bf16[768,384]{1,0:T(8,128)(2,1)}, bf16[768,384]{1,0:T(8,128)(2,1)}) custom-call(bf16[1024,768]{1,0:T(8,128)(2,1)S(1)} %copy-done.69, bf16[1024,768]{1,0:T(8,128)(2,1)S(1)} %copy-done, bf16[1024,576]{1,0:T(8,128)(2,1)S(1)} %get-tuple-element.369.refs_2_.refs_3_, bf16[1024,192]{1,0:T(8,128)(2,1)S(1)} %copy-done.28), custom_call_target="tpu_custom_call" | custom-call | tf_op jit(solution)/shard_map/weight_grads/pallas_call | solution.py:60
  185.3 4.3 %weight_grads.13 = bf16[1,768,768]{2,1,0:T(8,128)(2,1)} custom-call(bf16[1024,768]{1,0:T(8,128)(2,1)} %copy-done.68, bf16[1024,768]{1,0:T(8,128)(2,1)S(1)} %copy-done, bf16[1024,576]{1,0:T(8,128)(2,1)S(1)} %copy-done.14, bf16[1024,192]{1,0:T(8,128)(2,1)S(1)} %copy-done.26, bf16[768,384]{1,0:T(8,128)(2,1)S(1)} %copy-done.51, ...), custom_call_target="tpu_custom_call" | custom-call | tf_op jit(solution)/shard_map/weight_grads/pallas_call | solution.py:60
  189.5 3.6 %collective-permute-start.50 = (bf16[1,768,768]{2,1,0:T(8,128)(2,1)}, bf16[1,768,768]{2,1,0:T(8,128)(2,1)S(1)}, u32[]{:S(2)}, u32[]{:S(2)}) collective-permute-start(bf16[1,768,768]{2,1,0:T(8,128)(2,1)} %weight_grads.13), channel_id=1, source_target_pairs={{0,2},{1,3},{2,0},{3,1},{4,6},{5,7},{6,4},{7,5},{8,10},{9,11},{10,... | collective-permute-start | bytes 3538952 | tf_op jit(solution)/shard_map/ppermute | solution.py:627
  195.7 7.7 %attend_back.3 = (bf16[1024,576]{1,0:T(8,128)(2,1)S(1)}, bf16[1024,576]{1,0:T(8,128)(2,1)S(1)}, f32[1,576]{1,0:T(1,128)S(1)}, f32[1,576]{1,0:T(1,128)S(1)}) custom-call(s32[2]{0:T(128)S(1)} %dynamic_slice.44.lens.n, bf16[1024,576]{1,0:T(8,128)(2,1)S(1)} %copy-done.7, bf16[1024,576]{1,0:T(8,128)(2,1)S(1)} %copy-done.9, ...), custom_call_target="tpu_custom_call" | custom-call | tf_op jit(solution)/shard_map/attend_back/pallas_call | solution.py:60
  206.0 3.9 %weight_grads.14 = (bf16[768,384]{1,0:T(8,128)(2,1)}, bf16[768,384]{1,0:T(8,128)(2,1)S(1)}) custom-call(bf16[1024,768]{1,0:T(8,128)(2,1)} %copy-done.68, bf16[1024,768]{1,0:T(8,128)(2,1)S(1)} %copy-done.1, bf16[1024,576]{1,0:T(8,128)(2,1)S(1)} %get-tuple-element.391.refs_2_.refs_1_, bf16[1024,192]{1,0:T(8,128)(2,1)S(1)} %copy-done.27), custom_call_target="tpu_custom_call" | custom-call | tf_op jit(solution)/shard_map/weight_grads/pallas_call | solution.py:60
  212.3 6.1 %collective-permute-start.46 = (bf16[1,96,768]{2,1,0:T(8,128)(2,1)S(1)}, bf16[1,96,768]{2,1,0:T(8,128)(2,1)S(1)}, u32[]{:S(2)}, u32[]{:S(2)}) collective-permute-start(bf16[1,96,768]{2,1,0:T(8,128)(2,1)S(1)} %get-tuple-element.389), channel_id=1, source_target_pairs={{0,16},{4,20},{8,24},{12,28},{16,0},{20,4},{24,8},{28,12},{1,17},{... | collective-permute-start | bytes 442376 | tf_op jit(solution)/shard_map/ppermute | solution.py:630
  218.5 9.3 %down_out.1 = (bf16[2,128,768]{2,1,0:T(8,128)(2,1)}, bf16[2,128,768]{2,1,0:T(8,128)(2,1)}, bf16[2,2,128,768]{3,2,1,0:T(8,128)(2,1)S(1)}) custom-call(s32[1]{0:T(128)} %bitcast.17.at, f32[1024,768]{1,0:T(8,128)} %copy-done.5, bf16[1024,768]{1,0:T(8,128)(2,1)S(1)} %copy-done.10, bf16[1024,768]{1,0:T(8,128)(2,1)} %get-tuple-element.316.refs_1_, ...), custom_call_target="tpu_custom_call" | custom-call | tf_op jit(solution)/shard_map/down_out/pallas_call | solution.py:60
  229.0 3.9 %weight_grads.15 = (bf16[1,384,768]{2,1,0:T(8,128)(2,1)S(1)}, bf16[1,384,768]{2,1,0:T(8,128)(2,1)S(1)}) custom-call(s32[1]{0:T(128)} %bitcast.18.at.refs_0_, bf16[1024,768]{1,0:T(8,128)(2,1)} %copy-done.68, bf16[1024,768]{1,0:T(8,128)(2,1)} %get-tuple-element.364.refs_2_.refs_1_, bf16[1024,576]{1,0:T(8,128)(2,1)S(1)} %get-tuple-element.379.refs_3_.refs_0_, ...), custom_call_target="tpu_custom_call" | custom-call | tf_op jit(solution)/shard_map/weight_grads/pallas_call | solution.py:60
  235.2 11.7 %norm_one_back.1 = (bf16[2,128,768]{2,1,0:T(8,128)(2,1)S(1)}, bf16[2,128,768]{2,1,0:T(8,128)(2,1)S(1)}, bf16[2,2,128,768]{3,2,1,0:T(8,128)(2,1)S(1)}, f32[1,768]{1,0:T(1,128)S(1)}, f32[1,768]{1,0:T(1,128)S(1)}) custom-call(s32[1]{0:T(128)} %bitcast.17.at, bf16[1024,768]{1,0:T(8,128)(2,1)} %copy-done.11, f32[1024,768]{1,0:T(8,128)} %get-tuple-element.404.dres_ref, ...), custom_call_target="tpu_custom_call" | custom-call | tf_op jit(solution)/shard_map/norm_one_back/pallas_call | solution.py:60
  248.9 5.1 %collective-permute-done.52 = bf16[2,96,768]{2,1,0:T(8,128)(2,1)S(1)} collective-permute-done((bf16[2,96,768]{2,1,0:T(8,128)(2,1)S(1)}, bf16[2,96,768]{2,1,0:T(8,128)(2,1)S(1)}, u32[]{:S(2)}, u32[]{:S(2)}) %collective-permute-start.52) | collective-permute-done | bytes 294944 | tf_op jit(solution)/shard_map/ppermute | solution.py:630
  254.2 12.8 %conditional.4 = (f32[14,768]{1,0:T(8,128)S(1)}, bf16[1,96,768]{2,1,0:T(8,128)(2,1)S(1)}, bf16[1,96,768]{2,1,0:T(8,128)(2,1)}, bf16[2,96,768]{2,1,0:T(8,128)(2,1)}, bf16[2,96,768]{2,1,0:T(8,128)(2,1)}) conditional(s32[]{:T(128)} %bitcast.16, () %tuple.118, (f32[14,768]{1,0:T(8,128)S(1)}, s32[]{:T(128)}, bf16[1,384,768]{2,1,0:T(8,128)(2,1)S(1)}, ...), branch_computations={%region_2.3_spmd, %region_3.4_spmd} | conditional | flops 32256 | bytes 2672880 | solution.py:748
  259.0 3.8 %collective-permute-done.5 = f32[14,768]{1,0:T(8,128)S(1)} collective-permute-done((f32[14,768]{1,0:T(8,128)S(1)}, f32[14,768]{1,0:T(8,128)S(1)}, u32[]{:S(2)}, u32[]{:S(2)}) %collective-permute-start.5) | collective-permute-done | bytes 43040 | tf_op jit(solution)/shard_map/cond/branch_1_fun/ppermute | solution.py:630
  262.9 4.1 %collective-permute-done.6 = f32[14,768]{1,0:T(8,128)S(1)} collective-permute-done((f32[14,768]{1,0:T(8,128)S(1)}, f32[14,768]{1,0:T(8,128)S(1)}, u32[]{:S(2)}, u32[]{:S(2)}) %collective-permute-start.6) | collective-permute-done | bytes 43040 | tf_op jit(solution)/shard_map/cond/branch_1_fun/ppermute | solution.py:630
  270.1 17.9 %conditional.5 = (bf16[8,128,768]{2,1,0:T(8,128)(2,1)}, f32[768]{0:T(1024)S(1)}, f32[768]{0:T(1024)S(1)}, f32[768]{0:T(1024)S(1)}, f32[768]{0:T(1024)S(1)}, /*in...) conditional(s32[]{:T(128)} %bitcast.16, () %tuple.117, ...), branch_computations={%region_4.5_spmd, %region_5.6_spmd} | conditional | flops 574472 | bytes 6746484 | solution.py:748
  (380 shorter events, 116.4 us)
Async XLA Ops:
  3.7 12.4 %collective-permute-start.17 = (bf16[2,128,768]{2,1,0:T(8,128)(2,1)}, bf16[2,128,768]{2,1,0:T(8,128)(2,1)}, u32[]{:S(2)}, u32[]{:S(2)}) collective-permute-start(bf16[2,128,768]{2,1,0:T(8,128)(2,1)} %get-tuple-element.485), channel_id=1, source_target_pairs={{0,3},{1,2},{2,1},{3,0},{4,7},{5,6},{6,5},{7,4},{8,11},{9,10},{10,... | collective-permute-start | bytes 1179656 | tf_op jit(solution)/shard_map/ppermute | solution.py:627
  6.4 22.4 %collective-permute-start.16 = (bf16[2,128,768]{2,1,0:T(8,128)(2,1)}, bf16[2,128,768]{2,1,0:T(8,128)(2,1)}, u32[]{:S(2)}, u32[]{:S(2)}) collective-permute-start(bf16[2,128,768]{2,1,0:T(8,128)(2,1)} %get-tuple-element.488), channel_id=1, source_target_pairs={{0,2},{1,3},{2,0},{3,1},{4,6},{5,7},{6,4},{7,5},{8,10},{9,11},{10,... | collective-permute-start | bytes 1179656 | tf_op jit(solution)/shard_map/ppermute | solution.py:627
  7.2 20.0 %collective-permute-start.14 = (bf16[384,576]{1,0:T(8,128)(2,1)S(1)}, bf16[384,576]{1,0:T(8,128)(2,1)S(1)}, u32[]{:S(2)}, u32[]{:S(2)}) collective-permute-start(bf16[384,576]{1,0:T(8,128)(2,1)S(1)} %get-tuple-element.289.refs_0_.refs_4_), channel_id=1, source_target_pairs={{0,1},{1,0},{2,3},{3,2},{4,5},{5,4},{6,7},{7,6},{8,9},{9,8},{10,11... | collective-permute-start | bytes 1327112 | tf_op jit(solution)/shard_map/ppermute | solution.py:627
  7.4 20.0 %collective-permute-start.15 = (bf16[384,576]{1,0:T(8,128)(2,1)S(1)}, bf16[384,576]{1,0:T(8,128)(2,1)S(1)}, u32[]{:S(2)}, u32[]{:S(2)}) collective-permute-start(bf16[384,576]{1,0:T(8,128)(2,1)S(1)} %get-tuple-element.296.refs_1_.refs_5_), channel_id=1, source_target_pairs={{0,1},{1,0},{2,3},{3,2},{4,5},{5,4},{6,7},{7,6},{8,9},{9,8},{10,11... | collective-permute-start | bytes 1327112 | tf_op jit(solution)/shard_map/ppermute | solution.py:627
  11.3 13.7 %collective-permute-start.21 = (f32[2,1152]{1,0:T(2,128)S(1)}, f32[2,1152]{1,0:T(2,128)S(1)}, u32[]{:S(2)}, u32[]{:S(2)}) collective-permute-start(f32[2,1152]{1,0:T(2,128)S(1)} %pad_maximum_fusion.6), channel_id=1, source_target_pairs={{0,2},{1,3},{2,0},{3,1},{4,6},{5,7},{6,4},{7,5},{8,10},{9,11},{10,... | collective-permute-start | bytes 27656 | tf_op jit(solution)/shard_map/ppermute | solution.py:627
  16.2 27.5 %collective-permute-start.20 = (bf16[384,576]{1,0:T(8,128)(2,1)S(1)}, bf16[384,576]{1,0:T(8,128)(2,1)S(1)}, u32[]{:S(2)}, u32[]{:S(2)}) collective-permute-start(bf16[384,576]{1,0:T(8,128)(2,1)S(1)} %get-tuple-element.296.refs_1_.refs_5_), channel_id=1, source_target_pairs={{0,2},{1,3},{2,0},{3,1},{4,6},{5,7},{6,4},{7,5},{8,10},{9,11},{10,... | collective-permute-start | bytes 1327112 | tf_op jit(solution)/shard_map/ppermute | solution.py:627
  25.0 21.1 %collective-permute-start.18 = (bf16[384,576]{1,0:T(8,128)(2,1)S(1)}, bf16[384,576]{1,0:T(8,128)(2,1)S(1)}, u32[]{:S(2)}, u32[]{:S(2)}) collective-permute-start(bf16[384,576]{1,0:T(8,128)(2,1)S(1)} %get-tuple-element.289.refs_0_.refs_4_), channel_id=1, source_target_pairs={{0,2},{1,3},{2,0},{3,1},{4,6},{5,7},{6,4},{7,5},{8,10},{9,11},{10,... | collective-permute-start | bytes 1327112 | tf_op jit(solution)/shard_map/ppermute | solution.py:627
  27.4 38.7 %collective-permute-start.22 = (bf16[576,768]{1,0:T(8,128)(2,1)}, bf16[576,768]{1,0:T(8,128)(2,1)}, u32[]{:S(2)}, u32[]{:S(2)}) collective-permute-start(bf16[576,768]{1,0:T(8,128)(2,1)} %pad_maximum_fusion.1), channel_id=1, source_target_pairs={{0,2},{1,3},{2,0},{3,1},{4,6},{5,7},{6,4},{7,5},{8,10},{9,11},{10,... | collective-permute-start | bytes 2654216 | tf_op jit(solution)/shard_map/ppermute | solution.py:627
  53.0 34.7 %collective-permute-start.25 = (bf16[384,768]{1,0:T(8,128)(2,1)}, bf16[384,768]{1,0:T(8,128)(2,1)S(1)}, u32[]{:S(2)}, u32[]{:S(2)}) collective-permute-start(bf16[384,768]{1,0:T(8,128)(2,1)} %get-tuple-element.318), channel_id=1, source_target_pairs={{0,2},{1,3},{2,0},{3,1},{4,6},{5,7},{6,4},{7,5},{8,10},{9,11},{10,... | collective-permute-start | bytes 1769480 | tf_op jit(solution)/shard_map/ppermute | solution.py:627
  55.2 39.5 %collective-permute-start.28 = (bf16[2,2,128,768]{3,2,1,0:T(8,128)(2,1)}, bf16[2,2,128,768]{3,2,1,0:T(8,128)(2,1)}, u32[]{:S(2)}, u32[]{:S(2)}) collective-permute-start(bf16[2,2,128,768]{3,2,1,0:T(8,128)(2,1)} %bitcast.26), channel_id=1, source_target_pairs={{0,2},{1,3},{2,0},{3,1},{4,6},{5,7},{6,4},{7,5},{8,10},{9,11},{10,... | collective-permute-start | bytes 2359304 | tf_op jit(solution)/shard_map/ppermute | solution.py:627
  71.2 48.5 %collective-permute-start.34 = (bf16[768,768]{1,0:T(8,128)(2,1)}, bf16[768,768]{1,0:T(8,128)(2,1)S(1)}, u32[]{:S(2)}, u32[]{:S(2)}) collective-permute-start(bf16[768,768]{1,0:T(8,128)(2,1)} %refs_4_.3), channel_id=1, source_target_pairs={{0,2},{1,3},{2,0},{3,1},{4,6},{5,7},{6,4},{7,5},{8,10},{9,11},{10,... | collective-permute-start | bytes 3538952 | tf_op jit(solution)/shard_map/ppermute | solution.py:627
  75.8 20.5 %collective-permute-start.24 = (bf16[384,768]{1,0:T(8,128)(2,1)S(1)}, bf16[384,768]{1,0:T(8,128)(2,1)S(1)}, u32[]{:S(2)}, u32[]{:S(2)}) collective-permute-start(bf16[384,768]{1,0:T(8,128)(2,1)S(1)} %slice.126.refs_0_), channel_id=1, source_target_pairs={{0,1},{1,0},{2,3},{3,2},{4,5},{5,4},{6,7},{7,6},{8,9},{9,8},{10,11... | collective-permute-start | bytes 1769480 | tf_op jit(solution)/shard_map/ppermute | solution.py:627
  119.7 13.4 %collective-permute-start.35 = (bf16[768,768]{1,0:T(8,128)(2,1)S(1)}, bf16[768,768]{1,0:T(8,128)(2,1)S(1)}, u32[]{:S(2)}, u32[]{:S(2)}) collective-permute-start(bf16[768,768]{1,0:T(8,128)(2,1)S(1)} %collective-permute-done.34.refs_4_.refs_6_), channel_id=1, source_target_pairs={{0,1},{1,0},{2,3},{3,2},{4,5},{5,4},{6,7},{7,6},{8,9},{9,8},{10,11... | collective-permute-start | bytes 3538952 | tf_op jit(solution)/shard_map/ppermute | solution.py:627
  119.7 31.6 %collective-permute-start.36 = (bf16[1,768,768]{2,1,0:T(8,128)(2,1)}, bf16[1,768,768]{2,1,0:T(8,128)(2,1)}, u32[]{:S(2)}, u32[]{:S(2)}) collective-permute-start(bf16[1,768,768]{2,1,0:T(8,128)(2,1)} %get-tuple-element.354), channel_id=1, source_target_pairs={{0,2},{1,3},{2,0},{3,1},{4,6},{5,7},{6,4},{7,5},{8,10},{9,11},{10,... | collective-permute-start | bytes 3538952 | tf_op jit(solution)/shard_map/ppermute | solution.py:627
  162.4 41.1 %collective-permute-start.44 = (bf16[1,768,768]{2,1,0:T(8,128)(2,1)}, bf16[1,768,768]{2,1,0:T(8,128)(2,1)}, u32[]{:S(2)}, u32[]{:S(2)}) collective-permute-start(bf16[1,768,768]{2,1,0:T(8,128)(2,1)} %get-tuple-element.381), channel_id=1, source_target_pairs={{0,2},{1,3},{2,0},{3,1},{4,6},{5,7},{6,4},{7,5},{8,10},{9,11},{10,... | collective-permute-start | bytes 3538952 | tf_op jit(solution)/shard_map/ppermute | solution.py:627
  162.9 16.2 %collective-permute-start.41 = (bf16[4,96,768]{2,1,0:T(8,128)(2,1)}, bf16[4,96,768]{2,1,0:T(8,128)(2,1)S(1)}, u32[]{:S(2)}, u32[]{:S(2)}) collective-permute-start(bf16[4,96,768]{2,1,0:T(8,128)(2,1)} %get-tuple-element.356), channel_id=1, source_target_pairs={{0,4},{4,0},{8,12},{12,8},{16,20},{20,16},{24,28},{28,24},{1,5},{5... | collective-permute-start | bytes 1769480 | tf_op jit(solution)/shard_map/ppermute | solution.py:630
  189.5 39.4 %collective-permute-start.50 = (bf16[1,768,768]{2,1,0:T(8,128)(2,1)}, bf16[1,768,768]{2,1,0:T(8,128)(2,1)S(1)}, u32[]{:S(2)}, u32[]{:S(2)}) collective-permute-start(bf16[1,768,768]{2,1,0:T(8,128)(2,1)} %weight_grads.13), channel_id=1, source_target_pairs={{0,2},{1,3},{2,0},{3,1},{4,6},{5,7},{6,4},{7,5},{8,10},{9,11},{10,... | collective-permute-start | bytes 3538952 | tf_op jit(solution)/shard_map/ppermute | solution.py:627
  193.1 12.8 %collective-permute-start.45 = (bf16[2,96,768]{2,1,0:T(8,128)(2,1)}, bf16[2,96,768]{2,1,0:T(8,128)(2,1)S(1)}, u32[]{:S(2)}, u32[]{:S(2)}) collective-permute-start(bf16[2,96,768]{2,1,0:T(8,128)(2,1)} %get-tuple-element.373), channel_id=1, source_target_pairs={{0,8},{4,12},{8,0},{12,4},{16,24},{20,28},{24,16},{28,20},{1,9},{5... | collective-permute-start | bytes 884744 | tf_op jit(solution)/shard_map/ppermute | solution.py:630
  205.8 22.9 %collective-permute-start.47 = (bf16[4,96,768]{2,1,0:T(8,128)(2,1)S(1)}, bf16[4,96,768]{2,1,0:T(8,128)(2,1)S(1)}, u32[]{:S(2)}, u32[]{:S(2)}) collective-permute-start(bf16[4,96,768]{2,1,0:T(8,128)(2,1)S(1)} %get-tuple-element.385), channel_id=1, source_target_pairs={{0,4},{4,0},{8,12},{12,8},{16,20},{20,16},{24,28},{28,24},{1,5},{5... | collective-permute-start | bytes 1769480 | tf_op jit(solution)/shard_map/ppermute | solution.py:630
  209.9 19.0 %collective-permute-start.48 = (bf16[768,384]{1,0:T(8,128)(2,1)}, bf16[768,384]{1,0:T(8,128)(2,1)S(1)}, u32[]{:S(2)}, u32[]{:S(2)}) collective-permute-start(bf16[768,384]{1,0:T(8,128)(2,1)} %get-tuple-element.392), channel_id=1, source_target_pairs={{0,1},{1,0},{2,3},{3,2},{4,5},{5,4},{6,7},{7,6},{8,9},{9,8},{10,11... | collective-permute-start | bytes 1769480 | tf_op jit(solution)/shard_map/ppermute | solution.py:627
  212.3 16.7 %collective-permute-start.49 = (bf16[768,384]{1,0:T(8,128)(2,1)S(1)}, bf16[768,384]{1,0:T(8,128)(2,1)S(1)}, u32[]{:S(2)}, u32[]{:S(2)}) collective-permute-start(bf16[768,384]{1,0:T(8,128)(2,1)S(1)} %get-tuple-element.400), channel_id=1, source_target_pairs={{0,1},{1,0},{2,3},{3,2},{4,5},{5,4},{6,7},{7,6},{8,9},{9,8},{10,11... | collective-permute-start | bytes 1769480 | tf_op jit(solution)/shard_map/ppermute | solution.py:627
  212.3 15.5 %collective-permute-start.46 = (bf16[1,96,768]{2,1,0:T(8,128)(2,1)S(1)}, bf16[1,96,768]{2,1,0:T(8,128)(2,1)S(1)}, u32[]{:S(2)}, u32[]{:S(2)}) collective-permute-start(bf16[1,96,768]{2,1,0:T(8,128)(2,1)S(1)} %get-tuple-element.389), channel_id=1, source_target_pairs={{0,16},{4,20},{8,24},{12,28},{16,0},{20,4},{24,8},{28,12},{1,17},{... | collective-permute-start | bytes 442376 | tf_op jit(solution)/shard_map/ppermute | solution.py:630
  227.8 20.3 %collective-permute-start.54 = (bf16[2,2,128,768]{3,2,1,0:T(8,128)(2,1)S(1)}, bf16[2,2,128,768]{3,2,1,0:T(8,128)(2,1)S(1)}, u32[]{:S(2)}, u32[]{:S(2)}) collective-permute-start(bf16[2,2,128,768]{3,2,1,0:T(8,128)(2,1)S(1)} %get-tuple-element.435), channel_id=1, source_target_pairs={{0,2},{1,3},{2,0},{3,1},{4,6},{5,7},{6,4},{7,5},{8,10},{9,11},{10,... | collective-permute-start | bytes 2359304 | tf_op jit(solution)/shard_map/ppermute | solution.py:627
  233.0 21.1 %collective-permute-start.51 = (bf16[1,384,768]{2,1,0:T(8,128)(2,1)S(1)}, bf16[1,384,768]{2,1,0:T(8,128)(2,1)S(1)}, u32[]{:S(2)}, u32[]{:S(2)}) collective-permute-start(bf16[1,384,768]{2,1,0:T(8,128)(2,1)S(1)} %get-tuple-element.402), channel_id=1, source_target_pairs={{0,8},{4,12},{8,0},{12,4},{16,24},{20,28},{24,16},{28,20},{1,9},{5... | collective-permute-start | bytes 1769480 | tf_op jit(solution)/shard_map/ppermute | solution.py:630
  233.0 21.0 %collective-permute-start.52 = (bf16[2,96,768]{2,1,0:T(8,128)(2,1)S(1)}, bf16[2,96,768]{2,1,0:T(8,128)(2,1)S(1)}, u32[]{:S(2)}, u32[]{:S(2)}) collective-permute-start(bf16[2,96,768]{2,1,0:T(8,128)(2,1)S(1)} %get-tuple-element.398), channel_id=1, source_target_pairs={{0,8},{4,12},{8,0},{12,4},{16,24},{20,28},{24,16},{28,20},{1,9},{5... | collective-permute-start | bytes 884744 | tf_op jit(solution)/shard_map/ppermute | solution.py:630
  246.9 20.7 %collective-permute-start.57 = (bf16[2,2,128,768]{3,2,1,0:T(8,128)(2,1)S(1)}, bf16[2,2,128,768]{3,2,1,0:T(8,128)(2,1)S(1)}, u32[]{:S(2)}, u32[]{:S(2)}) collective-permute-start(bf16[2,2,128,768]{3,2,1,0:T(8,128)(2,1)S(1)} %get-tuple-element.443), channel_id=1, source_target_pairs={{0,2},{1,3},{2,0},{3,1},{4,6},{5,7},{6,4},{7,5},{8,10},{9,11},{10,... | collective-permute-start | bytes 2359304 | tf_op jit(solution)/shard_map/ppermute | solution.py:627
  248.1 22.0 %collective-permute-start.53 = (bf16[2,128,768]{2,1,0:T(8,128)(2,1)}, bf16[2,128,768]{2,1,0:T(8,128)(2,1)}, u32[]{:S(2)}, u32[]{:S(2)}) collective-permute-start(bf16[2,128,768]{2,1,0:T(8,128)(2,1)} %get-tuple-element.433), channel_id=1, source_target_pairs={{0,1},{1,0},{2,3},{3,2},{4,5},{5,4},{6,7},{7,6},{8,9},{9,8},{10,11... | collective-permute-start | bytes 1179656 | tf_op jit(solution)/shard_map/ppermute | solution.py:627
  255.1 11.8 %collective-permute-start.8 = (bf16[2,96,768]{2,1,0:T(8,128)(2,1)S(1)}, bf16[2,96,768]{2,1,0:T(8,128)(2,1)}, u32[]{:S(2)}, u32[]{:S(2)}) collective-permute-start(bf16[2,96,768]{2,1,0:T(8,128)(2,1)S(1)} %get-tuple-element.64), channel_id=1, source_target_pairs={{0,4},{4,0},{8,12},{12,8},{16,20},{20,16},{24,28},{28,24},{1,5},{5... | collective-permute-start | bytes 884744 | tf_op jit(solution)/shard_map/cond/branch_1_fun/ppermute | solution.py:630
  257.1 9.9 %collective-permute-start.7 = (bf16[1,96,768]{2,1,0:T(8,128)(2,1)S(1)}, bf16[1,96,768]{2,1,0:T(8,128)(2,1)}, u32[]{:S(2)}, u32[]{:S(2)}) collective-permute-start(bf16[1,96,768]{2,1,0:T(8,128)(2,1)S(1)} %get-tuple-element.60), channel_id=1, source_target_pairs={{0,16},{4,20},{8,24},{12,28},{16,0},{20,4},{24,8},{28,12},{1,17},{... | collective-permute-start | bytes 442376 | tf_op jit(solution)/shard_map/cond/branch_1_fun/ppermute | solution.py:630
  267.1 21.0 %collective-permute-start.56 = (bf16[2,128,768]{2,1,0:T(8,128)(2,1)S(1)}, bf16[2,128,768]{2,1,0:T(8,128)(2,1)S(1)}, u32[]{:S(2)}, u32[]{:S(2)}) collective-permute-start(bf16[2,128,768]{2,1,0:T(8,128)(2,1)S(1)} %copy-done.60), channel_id=1, source_target_pairs={{0,1},{1,0},{2,3},{3,2},{4,5},{5,4},{6,7},{7,6},{8,9},{9,8},{10,11... | collective-permute-start | bytes 1179656 | tf_op jit(solution)/shard_map/ppermute | solution.py:627
  268.3 19.7 %collective-permute-start.58 = (bf16[2,128,768]{2,1,0:T(8,128)(2,1)}, bf16[2,128,768]{2,1,0:T(8,128)(2,1)S(1)}, u32[]{:S(2)}, u32[]{:S(2)}) collective-permute-start(bf16[2,128,768]{2,1,0:T(8,128)(2,1)} %dynamic-slice_bitcast_fusion), channel_id=1, source_target_pairs={{0,1},{1,0},{2,3},{3,2},{4,5},{5,4},{6,7},{7,6},{8,9},{9,8},{10,11... | collective-permute-start | bytes 1179656 | tf_op jit(solution)/shard_map/ppermute | solution.py:627
  276.7 9.7 %collective-permute-start.11 = (bf16[1,96,768]{2,1,0:T(8,128)(2,1)S(1)}, bf16[1,96,768]{2,1,0:T(8,128)(2,1)S(1)}, u32[]{:S(2)}, u32[]{:S(2)}) collective-permute-start(bf16[1,96,768]{2,1,0:T(8,128)(2,1)S(1)} %get-tuple-element.82), channel_id=1, source_target_pairs={{0,16},{4,20},{8,24},{12,28},{16,0},{20,4},{24,8},{28,12},{1,17},{... | collective-permute-start | bytes 442376 | tf_op jit(solution)/shard_map/cond/branch_1_fun/ppermute | solution.py:630
  (127 other events, 948.6 us)

commit v6 on v5

--- a/solution.py
+++ b/solution.py
@@ -305,19 +305,39 @@
     )
 
 
-def join_rows(clock, blocks, me, cost=0):
+def split_texts(clock, values, index, me, texts, stacked):
+    count = index.shape[0] // texts
+    block = (texts,) + values.shape[1:]
+
+    def body(at, text_at, values_ref, *refs):
+        for r in range(count):
+            for i in range(texts):
+                rows = values_ref[pl.ds(text_at[r * texts + i], 1)]
+                if stacked and r >= 2:
+                    refs[2][pl.ds((at[0] ^ r) % 2, 1), i : i + 1] = rows[None]
+                else:
+                    refs[r][i : i + 1] = rows
+
+    out = [shape_of(block)] * 2 + ([shape_of((2, *block))] if stacked else [shape_of(block)] * (count - 2))
+    return call(
+        clock, body, out, (values,), grid=(1,), in_specs=[whole(values)], out_specs=[whole(v) for v in out],
+        scalars=(me.reshape(1), index), name="split_texts",
+    )
+
+
+def join_rows(clock, blocks, me, index):
     texts = blocks[0].shape[0]
     count = len(blocks)
 
-    def body(at, *refs):
+    def body(at, text_at, *refs):
         for r in range(count):
             for i in range(texts):
-                refs[count][pl.ds((at[0] ^ r) * texts + i, 1)] = block_of(refs, at, r, i)[None]
+                refs[count][pl.ds(text_at[r * texts + i], 1)] = block_of(refs, at, r, i)[None]
 
     out = shape_of((texts * count,) + blocks[0].shape[1:])
     return call(
         clock, body, out, blocks, grid=(1,), in_specs=[whole(v) for v in blocks], out_specs=whole(out),
-        scalars=(me.reshape(1),), name="join_rows", flops=cost,
+        scalars=(me.reshape(1), index), name="join_rows",
     )
 
 
@@ -617,7 +637,7 @@
     )
 
 
-COST_FAR, COST_OUT, COST_END = 14 * 10**9, 4 * 10**9, 7 * 10**9
+COST_FAR, COST_OUT, COST_END = 14 * 10**9, 6 * 10**9, 7 * 10**9
 
 
 def program(dp_size, tensor_size):
@@ -663,10 +683,17 @@
         def pick(values, index, axis):
             return lax.dynamic_index_in_dim(values, index, axis, keepdims=False)
 
-        def text_blocks(values):
-            return [
-                lax.dynamic_slice(values, ((t ^ r) * texts, 0, 0), (texts, part, D)) for r in rels
-            ]
+        number = jnp.arange(texts_all)
+        ahead = (lengths[None] > lengths[:, None]) | (
+            (lengths[None] == lengths[:, None]) & (number[None] < number[:, None])
+        )
+        rank = jnp.sum(ahead, 1)
+        dealt = []
+        for r in rels:
+            for i in range(texts):
+                dealt.append(i * tensor_size + ((t ^ r) if i % 2 == 0 else tensor_size - 1 - (t ^ r)))
+        text_at = jnp.sum(jnp.where(rank[None] == jnp.stack(dealt)[:, None], number[None], 0), 1).astype(jnp.int32)
+        lens = jnp.sum(jnp.where(rank[None] == jnp.stack(dealt[:texts])[:, None], lengths[None], 0), 1).astype(jnp.int32)
 
         def exchange(blocks):
             far = {r: pp_tensor(blocks[r], r) for r in (3, 2, 1)}
@@ -754,7 +781,7 @@
         def from_near(lefts, slots):
             return [pp_tensor(v, 1) for v in weight_grads(clock, lefts, slots, pieces=True)]
 
-        x_own = text_blocks(inputs)
+        x_own = split_texts(clock, inputs, text_at, t, texts, False)
         x_blocks = exchange(x_own)
         wq_own = side_by_side(clock, tie(w_qkv, *x_own[1:]))
         wq_near = [pp_tensor(v, 1) for v in wq_own]
@@ -766,7 +793,6 @@
             jnp.concatenate([s[:local], jnp.zeros((local,), F32), s[local : 2 * local]]) for s in small
         ]
         bup = [s[2 * local :] for s in small]
-        lens = lax.dynamic_slice_in_dim(lengths, t * texts, texts)
 
 
         x_blocks[0] = tie(x_blocks[0], wo_near, *wq_near)
@@ -774,9 +800,7 @@
         cut = w_up.shape[0] // 2
         up_first, up_second = jnp.concatenate([w_up[:cut], w_out], 0), w_up[cut:]
         first_far, second_far = [pp_tensor(tie(v, x_blocks[3]), 2) for v in (up_first, up_second)]
-        cot_far = lax.dynamic_slice_in_dim(cotangent, (t // 2 ^ 1) * 2 * texts, 2 * texts)
-        cot_own = text_blocks(cotangent)
-        cot = Exchange(cot_own[0], cot_own[1], tie(cot_far, x_blocks[3]).reshape(2, texts, part, D))
+        cot = Exchange(*split_texts(clock, tie(cotangent, x_blocks[1]), text_at, t, texts, True))
         wd_far = pp_tensor(tie(w_down, x_blocks[3]), 2)
         x, h1 = join_norm(clock, x_blocks, t, ln1_gain, ln1_bias)
         wq = [wq_own, wq_near]
@@ -872,7 +896,7 @@
                 q_own.step()
                 total = moved(total, bit, False)
             total = moved(total, 2, True)
-            rows_out = join_rows(clock, blocks, t)
+            rows_out = join_rows(clock, blocks, t, text_at)
             first = len(shared)
             vectors = [total[i] for i in range(first)]
             vectors.append(lax.dynamic_slice_in_dim(total, first + t, 1)[0, :units])
@@ -886,7 +910,7 @@
         total, state = block(begin, total, state)
         gin.forward()
         layer_out, vector, grad_up, grad_qkv, grad_out = block(finish, total, state, out_blocks)
-        grad_input = join_rows(clock, gin.blocks(), t)
+        grad_input = join_rows(clock, gin.blocks(), t, text_at)
         return (
             layer_out,
             grad_input,

time: 294 us -> 296 us (level)
  Pallas kernels: 161 us -> 170 us
  starting transfers between devices: 52.7 us -> 47.3 us
    pallas_call x39 -> x41, Pallas kernels: 161 us -> 170 us  [call(): pl.pallas_call(body, out_shape=jax.tree.map(lambda v: pltpu.HBM(v.shape,...]
    ppermute x47, starting transfers between devices: 34.1 us -> 28 us  [pp_tensor(): lax.ppermute(values, 'tensor', [(i, i ^ flip) for i in range(tensor_size)])]
    dynamic_slice x4 -> x0, local copies, waits for them, and re-layouts: 5.88 us -> none  [the longest x2 3.76 us: text_blocks(): lax.dynamic_slice(values, ((t ^ r) * texts, 0, 0), (texts, part, D))]
    unnamed x197 -> x213, local copies, waits for them, and re-layouts: 14.4 us -> 18.8 us
  transfers between devices with their start and end apart: 59 -> 59, of which waited for: 18 -> 17; matrix products, arithmetic and copies ran while one was open for 7% -> 6% of each run, Pallas kernels for 53% -> 55%
where the time goes in v6:
time: 296 us; the launch traced here: 291 us
  Pallas kernels  170 us (57%)
  starting transfers between devices  47.3 us (16%)
  waiting for transfers between devices  35.8 us (12%)
  local copies, waits for them, and re-layouts  29.6 us (10%)
  other arithmetic  6.52 us (2%)
    pallas_call x41, Pallas kernels, call(): pl.pallas_call(body, out_shape=jax.tree.map(lambda v: pltpu.HBM(v.shape,...  170 us
    ppermute x47, starting transfers between devices, pp_tensor(): lax.ppermute(values, 'tensor', [(i, i ^ flip) for i in range(tensor_size)])  28 us
    ppermute x47, waiting for transfers between devices, pp_tensor(): lax.ppermute(values, 'tensor', [(i, i ^ flip) for i in range(tensor_size)])  21.6 us
    ppermute x12, starting transfers between devices, pp_dp(): lax.ppermute(values, 'dp', [(i, i ^ 1 << bit) for i in range(dp_size)])  19.3 us
    unnamed x213, local copies, waits for them, and re-layouts  18.8 us
    ppermute x12, waiting for transfers between devices, pp_dp(): lax.ppermute(values, 'dp', [(i, i ^ 1 << bit) for i in range(dp_size)])  14.2 us
  transfers between devices with their start and end apart: 59, of which 17 were waited for; matrix products, arithmetic and copies ran while one was open for 6% of the time, Pallas kernels for 55%

profile of v6, /device:TPU:0, one launch (start us, length us, event | category | flops | bytes accessed | tf_op | source)
XLA Modules:
  0.0 291.4 jit_solution(16807873090924858281)
XLA Ops:
  20.2 7.2 %collective-permute-done.21 = f32[2,1152]{1,0:T(2,128)S(1)} collective-permute-done((f32[2,1152]{1,0:T(2,128)S(1)}, f32[2,1152]{1,0:T(2,128)S(1)}, u32[]{:S(2)}, u32[]{:S(2)}) %collective-permute-start.21) | collective-permute-done | bytes 9248 | tf_op jit(solution)/shard_map/ppermute | solution.py:647
  40.0 7.4 %attend.2 = (bf16[1024,192]{1,0:T(8,128)(2,1)}, bf16[1024,192]{1,0:T(8,128)(2,1)}, bf16[2,6,512,512]{3,2,1,0:T(8,128)(2,1)}, f32[2,6,512]{2,1,0:T(8,128)}) custom-call(s32[2]{0:T(128)S(1)} %fusion.8.lens.n, bf16[1024,576]{1,0:T(8,128)(2,1)S(1)} %project.5.refs_0_, bf16[1024,576]{1,0:T(8,128)(2,1)S(1)} %project.6.refs_1_), custom_call_target="tpu_custom_call" | custom-call | tf_op jit(solution)/shard_map/attend/pallas_call | solution.py:60
  49.3 6.1 %conditional.3 = (bf16[384,576]{1,0:T(8,128)(2,1)}, bf16[384,576]{1,0:T(8,128)(2,1)}, bf16[1024,576]{1,0:T(8,128)(2,1)S(1)}, bf16[768,768]{1,0:T(8,128)(2,1)}, bf16[768,768]{1,0:T(8,128)(2,1)}) conditional(s32[]{:T(128)} %bitcast.16, () %tuple.128, (bf16[384,576]{1,0:T(8,128)(2,1)S(1)}, bf16[384,576]{1,0:T(8,128)(2,1)S(1)}, f32[576]{0:T(1024)S(1)}, ...), branch_computations={%region_3.4_spmd, %region_4.5_spmd} | conditional | bytes 12980936 | solution.py:775
  57.6 4.4 %project.7.refs_1_ = bf16[1024,576]{1,0:T(8,128)(2,1)S(1)} custom-call(bf16[1024,768]{1,0:T(8,128)(2,1)} %copy-done.75, f32[1,576]{1,0:T(1,128)S(1)} %reshape.191.bias_ref, bf16[384,576]{1,0:T(8,128)(2,1)} %get-tuple-element.320.refs_0_.refs_10_, bf16[384,576]{1,0:T(8,128)(2,1)} %get-tuple-element.322.refs_1_.refs_11_), custom_call_target="tpu_custom_call" | custom-call | tf_op jit(solution)/shard_map/project/pallas_call | solution.py:60
  62.0 7.1 %attend.3 = (bf16[1024,192]{1,0:T(8,128)(2,1)}, bf16[1024,192]{1,0:T(8,128)(2,1)}, bf16[2,6,512,512]{3,2,1,0:T(8,128)(2,1)}, f32[2,6,512]{2,1,0:T(8,128)}) custom-call(s32[2]{0:T(128)S(1)} %fusion.8.lens.n, bf16[1024,576]{1,0:T(8,128)(2,1)S(1)} %get-tuple-element.384.refs_0_, bf16[1024,576]{1,0:T(8,128)(2,1)S(1)} %project.7.refs_1_), custom_call_target="tpu_custom_call" | custom-call | flops 14000000000 | tf_op jit(solution)/shard_map/attend/pallas_call | solution.py:60
  76.0 5.4 %attention_out.1 = (f32[1024,768]{1,0:T(8,128)S(1)}, bf16[1024,768]{1,0:T(8,128)(2,1)S(1)}) custom-call(bf16[1024,768]{1,0:T(8,128)(2,1)} %copy-done.11, bf16[1024,192]{1,0:T(8,128)(2,1)} %get-tuple-element.314.refs_0_.refs_4_, bf16[1024,192]{1,0:T(8,128)(2,1)} %get-tuple-element.326.refs_1_.refs_3_, bf16[1024,192]{1,0:T(8,128)(2,1)} %get-tuple-element.324.refs_2_.refs_3_, ...), custom_call_target="tpu_custom_call" | custom-call | tf_op jit(solution)/shard_map/attention_out/pallas_call | solution.py:60
  83.1 3.8 %up.4 = (bf16[1024,768]{1,0:T(8,128)(2,1)}, bf16[1024,768]{1,0:T(8,128)(2,1)}) custom-call(bf16[1024,768]{1,0:T(8,128)(2,1)S(1)} %get-tuple-element.378.h_ref.refs_0_, f32[1,768]{1,0:T(1,128)S(1)} %reshape.195.bias_ref, bf16[768,768]{1,0:T(8,128)(2,1)S(1)} %copy-done.78), custom_call_target="tpu_custom_call" | custom-call | tf_op jit(solution)/shard_map/up/pallas_call | solution.py:60
  87.4 5.3 %up.5 = (bf16[1024,768]{1,0:T(8,128)(2,1)}, bf16[1024,768]{1,0:T(8,128)(2,1)}) custom-call(bf16[1024,768]{1,0:T(8,128)(2,1)S(1)} %get-tuple-element.378.h_ref.refs_0_, f32[1,768]{1,0:T(1,128)S(1)} %reshape.196.bias_ref, bf16[768,768]{1,0:T(8,128)(2,1)} %get-tuple-element.335.refs_0_.refs_1_), custom_call_target="tpu_custom_call" | custom-call | flops 6000000000 | tf_op jit(solution)/shard_map/up/pallas_call | solution.py:60
  92.6 4.4 %collective-permute-done.28.refs_2_ = bf16[2,2,128,768]{3,2,1,0:T(8,128)(2,1)} collective-permute-done((bf16[2,2,128,768]{3,2,1,0:T(8,128)(2,1)}, bf16[2,2,128,768]{3,2,1,0:T(8,128)(2,1)}, u32[]{:S(2)}, u32[]{:S(2)}) %collective-permute-start.28) | collective-permute-done | bytes 786464 | tf_op jit(solution)/shard_map/ppermute | solution.py:647
  98.7 4.2 %up.6 = (bf16[1024,768]{1,0:T(8,128)(2,1)}, bf16[1024,768]{1,0:T(8,128)(2,1)}) custom-call(bf16[1024,768]{1,0:T(8,128)(2,1)S(1)} %get-tuple-element.378.h_ref.refs_0_, f32[1,768]{1,0:T(1,128)S(1)} %get-tuple-element.521.bias_ref, bf16[384,768]{1,0:T(8,128)(2,1)S(1)} %collective-permute-done.24.refs_0_.refs_2_, ...), custom_call_target="tpu_custom_call" | custom-call | tf_op jit(solution)/shard_map/up/pallas_call | solution.py:60
  105.2 4.8 %weight_grads.8 = (bf16[768,384]{1,0:T(8,128)(2,1)S(1)}, bf16[768,384]{1,0:T(8,128)(2,1)S(1)}, bf16[768,384]{1,0:T(8,128)(2,1)S(1)}, bf16[768,384]{1,0:T(8,128)(2,1)S(1)}) custom-call(bf16[1024,768]{1,0:T(8,128)(2,1)S(1)} %get-tuple-element.363.refs_0_.g_ref, bf16[1024,768]{1,0:T(8,128)(2,1)S(1)} %copy-done.12, ...), custom_call_target="tpu_custom_call" | custom-call | tf_op jit(solution)/shard_map/weight_grads/pallas_call | solution.py:60
  111.1 4.2 %up.7 = (bf16[1024,768]{1,0:T(8,128)(2,1)}, bf16[1024,768]{1,0:T(8,128)(2,1)}) custom-call(bf16[1024,768]{1,0:T(8,128)(2,1)S(1)} %get-tuple-element.378.h_ref.refs_0_, f32[1,768]{1,0:T(1,128)S(1)} %get-tuple-element.520.bias_ref, bf16[384,768]{1,0:T(8,128)(2,1)S(1)} %slice.126.refs_0_, bf16[384,768]{1,0:T(8,128)(2,1)S(1)} %collective-permute-done.25.refs_1_), custom_call_target="tpu_custom_call" | custom-call | tf_op jit(solution)/shard_map/up/pallas_call | solution.py:60
  115.4 6.0 %weight_grads.9 = (bf16[1,768,768]{2,1,0:T(8,128)(2,1)S(1)}, bf16[1,768,768]{2,1,0:T(8,128)(2,1)}) custom-call(bf16[1024,768]{1,0:T(8,128)(2,1)} %copy-done.3, bf16[1024,768]{1,0:T(8,128)(2,1)} %get-tuple-element.333.refs_1_.refs_0_, bf16[1024,768]{1,0:T(8,128)(2,1)} %get-tuple-element.352.refs_2_, bf16[768,384]{1,0:T(8,128)(2,1)S(1)} %collective-permute-done.30.refs_3_, ...), custom_call_target="tpu_custom_call" | custom-call | tf_op jit(solution)/shard_map/weight_grads/pallas_call | solution.py:60
  125.1 10.3 %up_back.2 = (bf16[1024,768]{1,0:T(8,128)(2,1)}, bf16[1024,768]{1,0:T(8,128)(2,1)}, f32[1,768]{1,0:T(1,128)}, f32[1,768]{1,0:T(1,128)}, f32[1024,768]{1,0:T(8,128)}) custom-call(bf16[1024,768]{1,0:T(8,128)(2,1)S(1)} %copy-done.4, bf16[768,768]{1,0:T(8,128)(2,1)} %refs_0_.3, bf16[768,768]{1,0:T(8,128)(2,1)} %get-tuple-element.335.refs_0_.refs_1_, ...), custom_call_target="tpu_custom_call" | custom-call | tf_op jit(solution)/shard_map/up_back/pallas_call | solution.py:60
  135.5 11.8 %up_back.3 = (bf16[1024,768]{1,0:T(8,128)(2,1)}, bf16[1024,768]{1,0:T(8,128)(2,1)}, f32[1,768]{1,0:T(1,128)}, f32[1,768]{1,0:T(1,128)}, f32[1024,768]{1,0:T(8,12...) custom-call(bf16[1024,768]{1,0:T(8,128)(2,1)} %copy-done.3, ...), custom_call_target="tpu_custom_call" | custom-call | tf_op jit(solution)/shard_map/up_back/pallas_call | solution.py:60
  147.4 5.3 %weight_grads.10 = (bf16[768,384]{1,0:T(8,128)(2,1)}, bf16[768,384]{1,0:T(8,128)(2,1)}, bf16[768,384]{1,0:T(8,128)(2,1)}, bf16[768,384]{1,0:T(8,128)(2,1)}) custom-call(bf16[1024,768]{1,0:T(8,128)(2,1)S(1)} %get-tuple-element.378.h_ref.refs_0_, bf16[1024,768]{1,0:T(8,128)(2,1)S(1)} %copy-done.42, bf16[1024,768]{1,0:T(8,128)(2,1)} %get-tuple-element.372.refs_2_), custom_call_target="tpu_custom_call" | custom-call | tf_op jit(solution)/shard_map/weight_grads/pallas_call | solution.py:60
  153.7 3.3 %add_split.11 = (bf16[4,96,768]{2,1,0:T(8,128)(2,1)}, bf16[4,96,768]{2,1,0:T(8,128)(2,1)S(1)}) custom-call(s32[1]{0:T(128)} %bitcast.26.at, bf16[4,2,96,768]{3,2,1,0:T(8,128)(2,1)S(1)} %bitcast.63, bf16[4,2,96,768]{3,2,1,0:T(8,128)(2,1)} %bitcast.35.arrived_ref), custom_call_target="tpu_custom_call" | custom-call | tf_op jit(solution)/shard_map/add_split/pallas_call | solution.py:60
  157.4 6.3 %weight_grads.11 = (bf16[1,768,768]{2,1,0:T(8,128)(2,1)S(1)}, bf16[1,768,768]{2,1,0:T(8,128)(2,1)}) custom-call(bf16[1024,768]{1,0:T(8,128)(2,1)} %copy-done.2, bf16[1024,768]{1,0:T(8,128)(2,1)} %get-tuple-element.362.refs_1_, bf16[1024,768]{1,0:T(8,128)(2,1)} %get-tuple-element.369.refs_2_, bf16[768,384]{1,0:T(8,128)(2,1)S(1)} %collective-permute-done.37.refs_3_, ...), custom_call_target="tpu_custom_call" | custom-call | tf_op jit(solution)/shard_map/weight_grads/pallas_call | solution.py:60
  166.9 9.4 %attend_back.2 = (bf16[1024,576]{1,0:T(8,128)(2,1)S(1)}, bf16[1024,576]{1,0:T(8,128)(2,1)S(1)}, f32[1,576]{1,0:T(1,128)S(1)}, f32[1,576]{1,0:T(1,128)S(1)}) custom-call(s32[2]{0:T(128)S(1)} %fusion.8.lens.n, bf16[1024,576]{1,0:T(8,128)(2,1)S(1)} %copy-done.80, bf16[1024,576]{1,0:T(8,128)(2,1)S(1)} %copy-done.17, bf16[1024,768]{1,0:T(8,128)(2,1)S(1)} %copy-done, ...), custom_call_target="tpu_custom_call" | custom-call | tf_op jit(solution)/shard_map/attend_back/pallas_call | solution.py:60
  177.4 3.4 %weight_grads.12 = (bf16[768,384]{1,0:T(8,128)(2,1)}, bf16[768,384]{1,0:T(8,128)(2,1)}) custom-call(bf16[1024,768]{1,0:T(8,128)(2,1)S(1)} %copy-done.76, bf16[1024,768]{1,0:T(8,128)(2,1)S(1)} %copy-done, bf16[1024,576]{1,0:T(8,128)(2,1)S(1)} %get-tuple-element.390.refs_2_.refs_3_, bf16[1024,192]{1,0:T(8,128)(2,1)S(1)} %copy-done.28), custom_call_target="tpu_custom_call" | custom-call | tf_op jit(solution)/shard_map/weight_grads/pallas_call | solution.py:60
  187.5 4.3 %weight_grads.13 = bf16[1,768,768]{2,1,0:T(8,128)(2,1)} custom-call(bf16[1024,768]{1,0:T(8,128)(2,1)} %copy-done.75, bf16[1024,768]{1,0:T(8,128)(2,1)S(1)} %copy-done, bf16[1024,576]{1,0:T(8,128)(2,1)S(1)} %copy-done.14, bf16[1024,192]{1,0:T(8,128)(2,1)S(1)} %copy-done.26, bf16[768,384]{1,0:T(8,128)(2,1)S(1)} %copy-done.52, ...), custom_call_target="tpu_custom_call" | custom-call | tf_op jit(solution)/shard_map/weight_grads/pallas_call | solution.py:60
  191.7 3.7 %collective-permute-start.50 = (bf16[1,768,768]{2,1,0:T(8,128)(2,1)}, bf16[1,768,768]{2,1,0:T(8,128)(2,1)S(1)}, u32[]{:S(2)}, u32[]{:S(2)}) collective-permute-start(bf16[1,768,768]{2,1,0:T(8,128)(2,1)} %weight_grads.13), channel_id=1, source_target_pairs={{0,2},{1,3},{2,0},{3,1},{4,6},{5,7},{6,4},{7,5},{8,10},{9,11},{10,... | collective-permute-start | bytes 3538952 | tf_op jit(solution)/shard_map/ppermute | solution.py:647
  198.3 9.3 %attend_back.3 = (bf16[1024,576]{1,0:T(8,128)(2,1)S(1)}, bf16[1024,576]{1,0:T(8,128)(2,1)S(1)}, f32[1,576]{1,0:T(1,128)S(1)}, f32[1,576]{1,0:T(1,128)S(1)}) custom-call(s32[2]{0:T(128)S(1)} %fusion.8.lens.n, bf16[1024,576]{1,0:T(8,128)(2,1)S(1)} %copy-done.7, bf16[1024,576]{1,0:T(8,128)(2,1)S(1)} %copy-done.9, ...), custom_call_target="tpu_custom_call" | custom-call | tf_op jit(solution)/shard_map/attend_back/pallas_call | solution.py:60
  210.3 4.0 %weight_grads.14 = (bf16[768,384]{1,0:T(8,128)(2,1)}, bf16[768,384]{1,0:T(8,128)(2,1)S(1)}) custom-call(bf16[1024,768]{1,0:T(8,128)(2,1)} %copy-done.75, bf16[1024,768]{1,0:T(8,128)(2,1)S(1)} %copy-done.1, bf16[1024,576]{1,0:T(8,128)(2,1)S(1)} %get-tuple-element.412.refs_2_.refs_1_, bf16[1024,192]{1,0:T(8,128)(2,1)S(1)} %copy-done.27), custom_call_target="tpu_custom_call" | custom-call | tf_op jit(solution)/shard_map/weight_grads/pallas_call | solution.py:60
  214.7 4.6 %collective-permute-start.46 = (bf16[1,96,768]{2,1,0:T(8,128)(2,1)S(1)}, bf16[1,96,768]{2,1,0:T(8,128)(2,1)S(1)}, u32[]{:S(2)}, u32[]{:S(2)}) collective-permute-start(bf16[1,96,768]{2,1,0:T(8,128)(2,1)S(1)} %get-tuple-element.410), channel_id=1, source_target_pairs={{0,16},{4,20},{8,24},{12,28},{16,0},{20,4},{24,8},{28,12},{1,17},{... | collective-permute-start | bytes 442376 | tf_op jit(solution)/shard_map/ppermute | solution.py:650
  219.3 9.3 %down_out.1 = (bf16[2,128,768]{2,1,0:T(8,128)(2,1)}, bf16[2,128,768]{2,1,0:T(8,128)(2,1)}, bf16[2,2,128,768]{3,2,1,0:T(8,128)(2,1)S(1)}) custom-call(s32[1]{0:T(128)} %bitcast.17.at, f32[1024,768]{1,0:T(8,128)} %copy-done.5, bf16[1024,768]{1,0:T(8,128)(2,1)S(1)} %copy-done.10, bf16[1024,768]{1,0:T(8,128)(2,1)} %get-tuple-element.336.refs_1_, ...), custom_call_target="tpu_custom_call" | custom-call | tf_op jit(solution)/shard_map/down_out/pallas_call | solution.py:60
  229.1 3.9 %weight_grads.15 = (bf16[1,384,768]{2,1,0:T(8,128)(2,1)S(1)}, bf16[1,384,768]{2,1,0:T(8,128)(2,1)S(1)}) custom-call(s32[1]{0:T(128)} %bitcast.25.at.refs_0_, bf16[1024,768]{1,0:T(8,128)(2,1)} %copy-done.75, bf16[1024,768]{1,0:T(8,128)(2,1)} %get-tuple-element.385.refs_2_.refs_1_, bf16[1024,576]{1,0:T(8,128)(2,1)S(1)} %get-tuple-element.400.refs_3_.refs_0_, ...), custom_call_target="tpu_custom_call" | custom-call | tf_op jit(solution)/shard_map/weight_grads/pallas_call | solution.py:60
  235.2 11.7 %norm_one_back.1 = (bf16[2,128,768]{2,1,0:T(8,128)(2,1)S(1)}, bf16[2,128,768]{2,1,0:T(8,128)(2,1)S(1)}, bf16[2,2,128,768]{3,2,1,0:T(8,128)(2,1)S(1)}, f32[1,768]{1,0:T(1,128)S(1)}, f32[1,768]{1,0:T(1,128)S(1)}) custom-call(s32[1]{0:T(128)} %bitcast.17.at, bf16[1024,768]{1,0:T(8,128)(2,1)} %copy-done.11, f32[1024,768]{1,0:T(8,128)} %get-tuple-element.425.dres_ref, ...), custom_call_target="tpu_custom_call" | custom-call | tf_op jit(solution)/shard_map/norm_one_back/pallas_call | solution.py:60
  249.9 5.0 %collective-permute-done.52 = bf16[2,96,768]{2,1,0:T(8,128)(2,1)S(1)} collective-permute-done((bf16[2,96,768]{2,1,0:T(8,128)(2,1)S(1)}, bf16[2,96,768]{2,1,0:T(8,128)(2,1)S(1)}, u32[]{:S(2)}, u32[]{:S(2)}) %collective-permute-start.52) | collective-permute-done | bytes 294944 | tf_op jit(solution)/shard_map/ppermute | solution.py:650
  255.1 12.8 %conditional.4 = (f32[14,768]{1,0:T(8,128)S(1)}, bf16[1,96,768]{2,1,0:T(8,128)(2,1)S(1)}, bf16[1,96,768]{2,1,0:T(8,128)(2,1)}, bf16[2,96,768]{2,1,0:T(8,128)(2,1)}, bf16[2,96,768]{2,1,0:T(8,128)(2,1)}) conditional(s32[]{:T(128)} %bitcast.16, () %tuple.120, (f32[14,768]{1,0:T(8,128)S(1)}, s32[]{:T(128)}, bf16[1,384,768]{2,1,0:T(8,128)(2,1)S(1)}, ...), branch_computations={%region_5.6_spmd, %region_6.7_spmd} | conditional | flops 32256 | bytes 2672880 | solution.py:775
  271.0 18.3 %conditional.5 = (bf16[8,128,768]{2,1,0:T(8,128)(2,1)}, f32[768]{0:T(1024)S(1)}, f32[768]{0:T(1024)S(1)}, f32[768]{0:T(1024)S(1)}, f32[768]{0:T(1024)S(1)}, /*in...) conditional(s32[]{:T(128)} %bitcast.16, () %tuple.119, ...), branch_computations={%region_7.8_spmd, %region_8.9_spmd} | conditional | flops 574472 | bytes 6746484 | solution.py:775
  271.0 3.3 %collective-permute-start.9 = (f32[14,768]{1,0:T(8,128)S(1)}, f32[14,768]{1,0:T(8,128)S(1)}, u32[]{:S(2)}, u32[]{:S(2)}) collective-permute-start(f32[14,768]{1,0:T(8,128)S(1)} %get-tuple-element.77), channel_id=1, source_target_pairs={{0,16},{4,20},{8,24},{12,28},{16,0},{20,4},{24,8},{28,12},{1,17},{... | collective-permute-start | bytes 129032 | tf_op jit(solution)/shard_map/cond/branch_1_fun/ppermute | solution.py:650
  (399 shorter events, 115.9 us)
Async XLA Ops:
  6.1 14.1 %collective-permute-start.17 = (bf16[2,128,768]{2,1,0:T(8,128)(2,1)}, bf16[2,128,768]{2,1,0:T(8,128)(2,1)}, u32[]{:S(2)}, u32[]{:S(2)}) collective-permute-start(bf16[2,128,768]{2,1,0:T(8,128)(2,1)} %get-tuple-element.297), channel_id=1, source_target_pairs={{0,3},{1,2},{2,1},{3,0},{4,7},{5,6},{6,5},{7,4},{8,11},{9,10},{10,... | collective-permute-start | bytes 1179656 | tf_op jit(solution)/shard_map/ppermute | solution.py:647
  8.8 23.2 %collective-permute-start.16 = (bf16[2,128,768]{2,1,0:T(8,128)(2,1)}, bf16[2,128,768]{2,1,0:T(8,128)(2,1)}, u32[]{:S(2)}, u32[]{:S(2)}) collective-permute-start(bf16[2,128,768]{2,1,0:T(8,128)(2,1)} %get-tuple-element.296), channel_id=1, source_target_pairs={{0,2},{1,3},{2,0},{3,1},{4,6},{5,7},{6,4},{7,5},{8,10},{9,11},{10,... | collective-permute-start | bytes 1179656 | tf_op jit(solution)/shard_map/ppermute | solution.py:647
  9.6 20.0 %collective-permute-start.14 = (bf16[384,576]{1,0:T(8,128)(2,1)S(1)}, bf16[384,576]{1,0:T(8,128)(2,1)S(1)}, u32[]{:S(2)}, u32[]{:S(2)}) collective-permute-start(bf16[384,576]{1,0:T(8,128)(2,1)S(1)} %get-tuple-element.309.refs_0_.refs_4_), channel_id=1, source_target_pairs={{0,1},{1,0},{2,3},{3,2},{4,5},{5,4},{6,7},{7,6},{8,9},{9,8},{10,11... | collective-permute-start | bytes 1327112 | tf_op jit(solution)/shard_map/ppermute | solution.py:647
  9.8 20.0 %collective-permute-start.15 = (bf16[384,576]{1,0:T(8,128)(2,1)S(1)}, bf16[384,576]{1,0:T(8,128)(2,1)S(1)}, u32[]{:S(2)}, u32[]{:S(2)}) collective-permute-start(bf16[384,576]{1,0:T(8,128)(2,1)S(1)} %get-tuple-element.316.refs_1_.refs_5_), channel_id=1, source_target_pairs={{0,1},{1,0},{2,3},{3,2},{4,5},{5,4},{6,7},{7,6},{8,9},{9,8},{10,11... | collective-permute-start | bytes 1327112 | tf_op jit(solution)/shard_map/ppermute | solution.py:647
  14.8 12.6 %collective-permute-start.21 = (f32[2,1152]{1,0:T(2,128)S(1)}, f32[2,1152]{1,0:T(2,128)S(1)}, u32[]{:S(2)}, u32[]{:S(2)}) collective-permute-start(f32[2,1152]{1,0:T(2,128)S(1)} %pad_maximum_fusion.6), channel_id=1, source_target_pairs={{0,2},{1,3},{2,0},{3,1},{4,6},{5,7},{6,4},{7,5},{8,10},{9,11},{10,... | collective-permute-start | bytes 27656 | tf_op jit(solution)/shard_map/ppermute | solution.py:647
  20.2 27.2 %collective-permute-start.20 = (bf16[384,576]{1,0:T(8,128)(2,1)S(1)}, bf16[384,576]{1,0:T(8,128)(2,1)S(1)}, u32[]{:S(2)}, u32[]{:S(2)}) collective-permute-start(bf16[384,576]{1,0:T(8,128)(2,1)S(1)} %get-tuple-element.316.refs_1_.refs_5_), channel_id=1, source_target_pairs={{0,2},{1,3},{2,0},{3,1},{4,6},{5,7},{6,4},{7,5},{8,10},{9,11},{10,... | collective-permute-start | bytes 1327112 | tf_op jit(solution)/shard_map/ppermute | solution.py:647
  27.5 21.1 %collective-permute-start.18 = (bf16[384,576]{1,0:T(8,128)(2,1)S(1)}, bf16[384,576]{1,0:T(8,128)(2,1)S(1)}, u32[]{:S(2)}, u32[]{:S(2)}) collective-permute-start(bf16[384,576]{1,0:T(8,128)(2,1)S(1)} %get-tuple-element.309.refs_0_.refs_4_), channel_id=1, source_target_pairs={{0,2},{1,3},{2,0},{3,1},{4,6},{5,7},{6,4},{7,5},{8,10},{9,11},{10,... | collective-permute-start | bytes 1327112 | tf_op jit(solution)/shard_map/ppermute | solution.py:647
  29.8 39.3 %collective-permute-start.22 = (bf16[576,768]{1,0:T(8,128)(2,1)}, bf16[576,768]{1,0:T(8,128)(2,1)}, u32[]{:S(2)}, u32[]{:S(2)}) collective-permute-start(bf16[576,768]{1,0:T(8,128)(2,1)} %pad_maximum_fusion.1), channel_id=1, source_target_pairs={{0,2},{1,3},{2,0},{3,1},{4,6},{5,7},{6,4},{7,5},{8,10},{9,11},{10,... | collective-permute-start | bytes 2654216 | tf_op jit(solution)/shard_map/ppermute | solution.py:647
  55.4 31.5 %collective-permute-start.25 = (bf16[384,768]{1,0:T(8,128)(2,1)}, bf16[384,768]{1,0:T(8,128)(2,1)S(1)}, u32[]{:S(2)}, u32[]{:S(2)}) collective-permute-start(bf16[384,768]{1,0:T(8,128)(2,1)} %get-tuple-element.338), channel_id=1, source_target_pairs={{0,2},{1,3},{2,0},{3,1},{4,6},{5,7},{6,4},{7,5},{8,10},{9,11},{10,... | collective-permute-start | bytes 1769480 | tf_op jit(solution)/shard_map/ppermute | solution.py:647
  70.2 26.9 %collective-permute-start.28 = (bf16[2,2,128,768]{3,2,1,0:T(8,128)(2,1)}, bf16[2,2,128,768]{3,2,1,0:T(8,128)(2,1)}, u32[]{:S(2)}, u32[]{:S(2)}) collective-permute-start(bf16[2,2,128,768]{3,2,1,0:T(8,128)(2,1)} %get-tuple-element.345), channel_id=1, source_target_pairs={{0,2},{1,3},{2,0},{3,1},{4,6},{5,7},{6,4},{7,5},{8,10},{9,11},{10,... | collective-permute-start | bytes 2359304 | tf_op jit(solution)/shard_map/ppermute | solution.py:647
  73.9 48.2 %collective-permute-start.34 = (bf16[768,768]{1,0:T(8,128)(2,1)}, bf16[768,768]{1,0:T(8,128)(2,1)S(1)}, u32[]{:S(2)}, u32[]{:S(2)}) collective-permute-start(bf16[768,768]{1,0:T(8,128)(2,1)} %refs_4_.3), channel_id=1, source_target_pairs={{0,2},{1,3},{2,0},{3,1},{4,6},{5,7},{6,4},{7,5},{8,10},{9,11},{10,... | collective-permute-start | bytes 3538952 | tf_op jit(solution)/shard_map/ppermute | solution.py:647
  75.2 23.5 %collective-permute-start.24 = (bf16[384,768]{1,0:T(8,128)(2,1)S(1)}, bf16[384,768]{1,0:T(8,128)(2,1)S(1)}, u32[]{:S(2)}, u32[]{:S(2)}) collective-permute-start(bf16[384,768]{1,0:T(8,128)(2,1)S(1)} %slice.126.refs_0_), channel_id=1, source_target_pairs={{0,1},{1,0},{2,3},{3,2},{4,5},{5,4},{6,7},{7,6},{8,9},{9,8},{10,11... | collective-permute-start | bytes 1769480 | tf_op jit(solution)/shard_map/ppermute | solution.py:647
  86.9 11.9 %collective-permute-start.26 = (bf16[384,768]{1,0:T(8,128)(2,1)S(1)}, bf16[384,768]{1,0:T(8,128)(2,1)S(1)}, u32[]{:S(2)}, u32[]{:S(2)}) collective-permute-start(bf16[384,768]{1,0:T(8,128)(2,1)S(1)} %collective-permute-done.25.refs_1_), channel_id=1, source_target_pairs={{0,1},{1,0},{2,3},{3,2},{4,5},{5,4},{6,7},{7,6},{8,9},{9,8},{10,11... | collective-permute-start | bytes 1769480 | tf_op jit(solution)/shard_map/ppermute | solution.py:647
  122.1 13.4 %collective-permute-start.35 = (bf16[768,768]{1,0:T(8,128)(2,1)S(1)}, bf16[768,768]{1,0:T(8,128)(2,1)S(1)}, u32[]{:S(2)}, u32[]{:S(2)}) collective-permute-start(bf16[768,768]{1,0:T(8,128)(2,1)S(1)} %collective-permute-done.34.refs_4_.refs_6_), channel_id=1, source_target_pairs={{0,1},{1,0},{2,3},{3,2},{4,5},{5,4},{6,7},{7,6},{8,9},{9,8},{10,11... | collective-permute-start | bytes 3538952 | tf_op jit(solution)/shard_map/ppermute | solution.py:647
  122.1 31.6 %collective-permute-start.36 = (bf16[1,768,768]{2,1,0:T(8,128)(2,1)}, bf16[1,768,768]{2,1,0:T(8,128)(2,1)}, u32[]{:S(2)}, u32[]{:S(2)}) collective-permute-start(bf16[1,768,768]{2,1,0:T(8,128)(2,1)} %get-tuple-element.375), channel_id=1, source_target_pairs={{0,2},{1,3},{2,0},{3,1},{4,6},{5,7},{6,4},{7,5},{8,10},{9,11},{10,... | collective-permute-start | bytes 3538952 | tf_op jit(solution)/shard_map/ppermute | solution.py:647
  164.8 42.9 %collective-permute-start.44 = (bf16[1,768,768]{2,1,0:T(8,128)(2,1)}, bf16[1,768,768]{2,1,0:T(8,128)(2,1)}, u32[]{:S(2)}, u32[]{:S(2)}) collective-permute-start(bf16[1,768,768]{2,1,0:T(8,128)(2,1)} %get-tuple-element.402), channel_id=1, source_target_pairs={{0,2},{1,3},{2,0},{3,1},{4,6},{5,7},{6,4},{7,5},{8,10},{9,11},{10,... | collective-permute-start | bytes 3538952 | tf_op jit(solution)/shard_map/ppermute | solution.py:647
  165.3 16.1 %collective-permute-start.41 = (bf16[4,96,768]{2,1,0:T(8,128)(2,1)}, bf16[4,96,768]{2,1,0:T(8,128)(2,1)S(1)}, u32[]{:S(2)}, u32[]{:S(2)}) collective-permute-start(bf16[4,96,768]{2,1,0:T(8,128)(2,1)} %get-tuple-element.377), channel_id=1, source_target_pairs={{0,4},{4,0},{8,12},{12,8},{16,20},{20,16},{24,28},{28,24},{1,5},{5... | collective-permute-start | bytes 1769480 | tf_op jit(solution)/shard_map/ppermute | solution.py:650
  191.7 37.3 %collective-permute-start.50 = (bf16[1,768,768]{2,1,0:T(8,128)(2,1)}, bf16[1,768,768]{2,1,0:T(8,128)(2,1)S(1)}, u32[]{:S(2)}, u32[]{:S(2)}) collective-permute-start(bf16[1,768,768]{2,1,0:T(8,128)(2,1)} %weight_grads.13), channel_id=1, source_target_pairs={{0,2},{1,3},{2,0},{3,1},{4,6},{5,7},{6,4},{7,5},{8,10},{9,11},{10,... | collective-permute-start | bytes 3538952 | tf_op jit(solution)/shard_map/ppermute | solution.py:647
  195.4 14.7 %collective-permute-start.45 = (bf16[2,96,768]{2,1,0:T(8,128)(2,1)}, bf16[2,96,768]{2,1,0:T(8,128)(2,1)S(1)}, u32[]{:S(2)}, u32[]{:S(2)}) collective-permute-start(bf16[2,96,768]{2,1,0:T(8,128)(2,1)} %get-tuple-element.394), channel_id=1, source_target_pairs={{0,8},{4,12},{8,0},{12,4},{16,24},{20,28},{24,16},{28,20},{1,9},{5... | collective-permute-start | bytes 884744 | tf_op jit(solution)/shard_map/ppermute | solution.py:650
  210.0 18.8 %collective-permute-start.47 = (bf16[4,96,768]{2,1,0:T(8,128)(2,1)S(1)}, bf16[4,96,768]{2,1,0:T(8,128)(2,1)S(1)}, u32[]{:S(2)}, u32[]{:S(2)}) collective-permute-start(bf16[4,96,768]{2,1,0:T(8,128)(2,1)S(1)} %get-tuple-element.406), channel_id=1, source_target_pairs={{0,4},{4,0},{8,12},{12,8},{16,20},{20,16},{24,28},{28,24},{1,5},{5... | collective-permute-start | bytes 1769480 | tf_op jit(solution)/shard_map/ppermute | solution.py:650
  214.2 14.8 %collective-permute-start.48 = (bf16[768,384]{1,0:T(8,128)(2,1)}, bf16[768,384]{1,0:T(8,128)(2,1)S(1)}, u32[]{:S(2)}, u32[]{:S(2)}) collective-permute-start(bf16[768,384]{1,0:T(8,128)(2,1)} %get-tuple-element.413), channel_id=1, source_target_pairs={{0,1},{1,0},{2,3},{3,2},{4,5},{5,4},{6,7},{7,6},{8,9},{9,8},{10,11... | collective-permute-start | bytes 1769480 | tf_op jit(solution)/shard_map/ppermute | solution.py:647
  214.2 14.8 %collective-permute-start.49 = (bf16[768,384]{1,0:T(8,128)(2,1)S(1)}, bf16[768,384]{1,0:T(8,128)(2,1)S(1)}, u32[]{:S(2)}, u32[]{:S(2)}) collective-permute-start(bf16[768,384]{1,0:T(8,128)(2,1)S(1)} %get-tuple-element.421), channel_id=1, source_target_pairs={{0,1},{1,0},{2,3},{3,2},{4,5},{5,4},{6,7},{7,6},{8,9},{9,8},{10,11... | collective-permute-start | bytes 1769480 | tf_op jit(solution)/shard_map/ppermute | solution.py:647
  214.7 14.0 %collective-permute-start.46 = (bf16[1,96,768]{2,1,0:T(8,128)(2,1)S(1)}, bf16[1,96,768]{2,1,0:T(8,128)(2,1)S(1)}, u32[]{:S(2)}, u32[]{:S(2)}) collective-permute-start(bf16[1,96,768]{2,1,0:T(8,128)(2,1)S(1)} %get-tuple-element.410), channel_id=1, source_target_pairs={{0,16},{4,20},{8,24},{12,28},{16,0},{20,4},{24,8},{28,12},{1,17},{... | collective-permute-start | bytes 442376 | tf_op jit(solution)/shard_map/ppermute | solution.py:650
  228.7 20.3 %collective-permute-start.54 = (bf16[2,2,128,768]{3,2,1,0:T(8,128)(2,1)S(1)}, bf16[2,2,128,768]{3,2,1,0:T(8,128)(2,1)S(1)}, u32[]{:S(2)}, u32[]{:S(2)}) collective-permute-start(bf16[2,2,128,768]{3,2,1,0:T(8,128)(2,1)S(1)} %get-tuple-element.456), channel_id=1, source_target_pairs={{0,2},{1,3},{2,0},{3,1},{4,6},{5,7},{6,4},{7,5},{8,10},{9,11},{10,... | collective-permute-start | bytes 2359304 | tf_op jit(solution)/shard_map/ppermute | solution.py:647
  233.0 21.9 %collective-permute-start.51 = (bf16[1,384,768]{2,1,0:T(8,128)(2,1)S(1)}, bf16[1,384,768]{2,1,0:T(8,128)(2,1)S(1)}, u32[]{:S(2)}, u32[]{:S(2)}) collective-permute-start(bf16[1,384,768]{2,1,0:T(8,128)(2,1)S(1)} %get-tuple-element.423), channel_id=1, source_target_pairs={{0,8},{4,12},{8,0},{12,4},{16,24},{20,28},{24,16},{28,20},{1,9},{5... | collective-permute-start | bytes 1769480 | tf_op jit(solution)/shard_map/ppermute | solution.py:650
  234.8 20.1 %collective-permute-start.52 = (bf16[2,96,768]{2,1,0:T(8,128)(2,1)S(1)}, bf16[2,96,768]{2,1,0:T(8,128)(2,1)S(1)}, u32[]{:S(2)}, u32[]{:S(2)}) collective-permute-start(bf16[2,96,768]{2,1,0:T(8,128)(2,1)S(1)} %get-tuple-element.419), channel_id=1, source_target_pairs={{0,8},{4,12},{8,0},{12,4},{16,24},{20,28},{24,16},{28,20},{1,9},{5... | collective-permute-start | bytes 884744 | tf_op jit(solution)/shard_map/ppermute | solution.py:650
  246.9 21.5 %collective-permute-start.57 = (bf16[2,2,128,768]{3,2,1,0:T(8,128)(2,1)S(1)}, bf16[2,2,128,768]{3,2,1,0:T(8,128)(2,1)S(1)}, u32[]{:S(2)}, u32[]{:S(2)}) collective-permute-start(bf16[2,2,128,768]{3,2,1,0:T(8,128)(2,1)S(1)} %get-tuple-element.464), channel_id=1, source_target_pairs={{0,2},{1,3},{2,0},{3,1},{4,6},{5,7},{6,4},{7,5},{8,10},{9,11},{10,... | collective-permute-start | bytes 2359304 | tf_op jit(solution)/shard_map/ppermute | solution.py:647
  249.0 21.9 %collective-permute-start.53 = (bf16[2,128,768]{2,1,0:T(8,128)(2,1)}, bf16[2,128,768]{2,1,0:T(8,128)(2,1)}, u32[]{:S(2)}, u32[]{:S(2)}) collective-permute-start(bf16[2,128,768]{2,1,0:T(8,128)(2,1)} %get-tuple-element.454), channel_id=1, source_target_pairs={{0,1},{1,0},{2,3},{3,2},{4,5},{5,4},{6,7},{7,6},{8,9},{9,8},{10,11... | collective-permute-start | bytes 1179656 | tf_op jit(solution)/shard_map/ppermute | solution.py:647
  256.0 11.9 %collective-permute-start.8 = (bf16[2,96,768]{2,1,0:T(8,128)(2,1)S(1)}, bf16[2,96,768]{2,1,0:T(8,128)(2,1)}, u32[]{:S(2)}, u32[]{:S(2)}) collective-permute-start(bf16[2,96,768]{2,1,0:T(8,128)(2,1)S(1)} %get-tuple-element.66), channel_id=1, source_target_pairs={{0,4},{4,0},{8,12},{12,8},{16,20},{20,16},{24,28},{28,24},{1,5},{5... | collective-permute-start | bytes 884744 | tf_op jit(solution)/shard_map/cond/branch_1_fun/ppermute | solution.py:650
  257.7 10.1 %collective-permute-start.7 = (bf16[1,96,768]{2,1,0:T(8,128)(2,1)S(1)}, bf16[1,96,768]{2,1,0:T(8,128)(2,1)}, u32[]{:S(2)}, u32[]{:S(2)}) collective-permute-start(bf16[1,96,768]{2,1,0:T(8,128)(2,1)S(1)} %get-tuple-element.62), channel_id=1, source_target_pairs={{0,16},{4,20},{8,24},{12,28},{16,0},{20,4},{24,8},{28,12},{1,17},{... | collective-permute-start | bytes 442376 | tf_op jit(solution)/shard_map/cond/branch_1_fun/ppermute | solution.py:650
  267.9 21.4 %collective-permute-start.56 = (bf16[2,128,768]{2,1,0:T(8,128)(2,1)S(1)}, bf16[2,128,768]{2,1,0:T(8,128)(2,1)S(1)}, u32[]{:S(2)}, u32[]{:S(2)}) collective-permute-start(bf16[2,128,768]{2,1,0:T(8,128)(2,1)S(1)} %copy-done.65), channel_id=1, source_target_pairs={{0,1},{1,0},{2,3},{3,2},{4,5},{5,4},{6,7},{7,6},{8,9},{9,8},{10,11... | collective-permute-start | bytes 1179656 | tf_op jit(solution)/shard_map/ppermute | solution.py:647
  269.2 20.1 %collective-permute-start.58 = (bf16[2,128,768]{2,1,0:T(8,128)(2,1)}, bf16[2,128,768]{2,1,0:T(8,128)(2,1)S(1)}, u32[]{:S(2)}, u32[]{:S(2)}) collective-permute-start(bf16[2,128,768]{2,1,0:T(8,128)(2,1)} %dynamic-slice_bitcast_fusion), channel_id=1, source_target_pairs={{0,1},{1,0},{2,3},{3,2},{4,5},{5,4},{6,7},{7,6},{8,9},{9,8},{10,11... | collective-permute-start | bytes 1179656 | tf_op jit(solution)/shard_map/ppermute | solution.py:647
  (135 other events, 986.1 us)

commit v7 on v6

--- a/solution.py
+++ b/solution.py
@@ -858,7 +858,7 @@
         out = Exchange(*down_out(clock, resid, acts, wd, b_down, t, texts))
         grad_down = clock.then(down.last())
         grads_up.step()
-        q_own = Chain([h1, dres_low], [[(0, dqkv[0]), (1, ctx[0])]], near, [1, 0] + high, clock.after(q_far))
+        q_own = Chain([h1, dres_low], [[(0, dqkv[0]), (1, ctx[0])]], near, [0, 1] + high, clock.after(q_far))
         in_blocks, gain_one, shift_one = norm_one_back(clock, x, dres, dqkv, wq, ln1_gain, t, texts)
         gin = Exchange(*in_blocks)
         shared = [gain_one, shift_one, gain_two, shift_two, bias_attn, bias_down]
@@ -883,7 +883,7 @@
                 grads_up.step()
             q_own.step()
             total = moved(total, 1, True)
-            for bit in (1, 0)[-bits:]:
+            for bit in (0, 1)[:bits]:
                 total = moved(total, bit, False)
             return total, [(chain.keep, clock.after(chain.flight)) for chain in chains]
 

time: 296 us -> 291 us (0.983)
  starting transfers between devices: 47.3 us -> 40.2 us
    ppermute x47, waiting for transfers between devices: 21.6 us -> 25.8 us  [pp_tensor(): lax.ppermute(values, 'tensor', [(i, i ^ flip) for i in range(tensor_size)])]
    ppermute x47, starting transfers between devices: 28 us -> 24.3 us  [pp_tensor(): lax.ppermute(values, 'tensor', [(i, i ^ flip) for i in range(tensor_size)])]
    ppermute x12, starting transfers between devices: 19.3 us -> 15.9 us  [pp_dp(): lax.ppermute(values, 'dp', [(i, i ^ 1 << bit) for i in range(dp_size)])]
  transfers between devices with their start and end apart: 59 -> 59, of which waited for: 17 -> 20; matrix products, arithmetic and copies ran while one was open for 6% -> 6% of each run, Pallas kernels for 55% -> 56%
where the time goes in v7:
time: 291 us; the launch traced here: 286 us
  Pallas kernels  170 us (58%)
  starting transfers between devices  40.2 us (14%)
  waiting for transfers between devices  37.3 us (13%)
  local copies, waits for them, and re-layouts  29.6 us (10%)
  other arithmetic  6.52 us (2%)
    pallas_call x41, Pallas kernels, call(): pl.pallas_call(body, out_shape=jax.tree.map(lambda v: pltpu.HBM(v.shape,...  170 us
    ppermute x47, waiting for transfers between devices, pp_tensor(): lax.ppermute(values, 'tensor', [(i, i ^ flip) for i in range(tensor_size)])  25.8 us
    ppermute x47, starting transfers between devices, pp_tensor(): lax.ppermute(values, 'tensor', [(i, i ^ flip) for i in range(tensor_size)])  24.3 us
    unnamed x213, local copies, waits for them, and re-layouts  18.8 us
    ppermute x12, starting transfers between devices, pp_dp(): lax.ppermute(values, 'dp', [(i, i ^ 1 << bit) for i in range(dp_size)])  15.9 us
    ppermute x12, waiting for transfers between devices, pp_dp(): lax.ppermute(values, 'dp', [(i, i ^ 1 << bit) for i in range(dp_size)])  11.5 us
  transfers between devices with their start and end apart: 59, of which 20 were waited for; matrix products, arithmetic and copies ran while one was open for 6% of the time, Pallas kernels for 56%

profile of v7, /device:TPU:0, one launch (start us, length us, event | category | flops | bytes accessed | tf_op | source)
XLA Modules:
  0.0 285.8 jit_solution(7008990816514557110)
XLA Ops:
  20.2 7.2 %collective-permute-done.21 = f32[2,1152]{1,0:T(2,128)S(1)} collective-permute-done((f32[2,1152]{1,0:T(2,128)S(1)}, f32[2,1152]{1,0:T(2,128)S(1)}, u32[]{:S(2)}, u32[]{:S(2)}) %collective-permute-start.21) | collective-permute-done | bytes 9248 | tf_op jit(solution)/shard_map/ppermute | solution.py:647
  40.0 7.4 %attend.2 = (bf16[1024,192]{1,0:T(8,128)(2,1)}, bf16[1024,192]{1,0:T(8,128)(2,1)}, bf16[2,6,512,512]{3,2,1,0:T(8,128)(2,1)}, f32[2,6,512]{2,1,0:T(8,128)}) custom-call(s32[2]{0:T(128)S(1)} %fusion.8.lens.n, bf16[1024,576]{1,0:T(8,128)(2,1)S(1)} %project.5.refs_0_, bf16[1024,576]{1,0:T(8,128)(2,1)S(1)} %project.6.refs_1_), custom_call_target="tpu_custom_call" | custom-call | tf_op jit(solution)/shard_map/attend/pallas_call | solution.py:60
  49.3 6.1 %conditional.3 = (bf16[384,576]{1,0:T(8,128)(2,1)}, bf16[384,576]{1,0:T(8,128)(2,1)}, bf16[1024,576]{1,0:T(8,128)(2,1)S(1)}, bf16[768,768]{1,0:T(8,128)(2,1)}, bf16[768,768]{1,0:T(8,128)(2,1)}) conditional(s32[]{:T(128)} %bitcast.16, () %tuple.128, (bf16[384,576]{1,0:T(8,128)(2,1)S(1)}, bf16[384,576]{1,0:T(8,128)(2,1)S(1)}, f32[576]{0:T(1024)S(1)}, ...), branch_computations={%region_3.4_spmd, %region_4.5_spmd} | conditional | bytes 12980936 | solution.py:775
  57.6 4.4 %project.7.refs_1_ = bf16[1024,576]{1,0:T(8,128)(2,1)S(1)} custom-call(bf16[1024,768]{1,0:T(8,128)(2,1)} %copy-done.75, f32[1,576]{1,0:T(1,128)S(1)} %reshape.191.bias_ref, bf16[384,576]{1,0:T(8,128)(2,1)} %get-tuple-element.320.refs_0_.refs_10_, bf16[384,576]{1,0:T(8,128)(2,1)} %get-tuple-element.322.refs_1_.refs_11_), custom_call_target="tpu_custom_call" | custom-call | tf_op jit(solution)/shard_map/project/pallas_call | solution.py:60
  62.0 7.1 %attend.3 = (bf16[1024,192]{1,0:T(8,128)(2,1)}, bf16[1024,192]{1,0:T(8,128)(2,1)}, bf16[2,6,512,512]{3,2,1,0:T(8,128)(2,1)}, f32[2,6,512]{2,1,0:T(8,128)}) custom-call(s32[2]{0:T(128)S(1)} %fusion.8.lens.n, bf16[1024,576]{1,0:T(8,128)(2,1)S(1)} %get-tuple-element.384.refs_0_, bf16[1024,576]{1,0:T(8,128)(2,1)S(1)} %project.7.refs_1_), custom_call_target="tpu_custom_call" | custom-call | flops 14000000000 | tf_op jit(solution)/shard_map/attend/pallas_call | solution.py:60
  76.0 5.4 %attention_out.1 = (f32[1024,768]{1,0:T(8,128)S(1)}, bf16[1024,768]{1,0:T(8,128)(2,1)S(1)}) custom-call(bf16[1024,768]{1,0:T(8,128)(2,1)} %copy-done.11, bf16[1024,192]{1,0:T(8,128)(2,1)} %get-tuple-element.314.refs_0_.refs_4_, bf16[1024,192]{1,0:T(8,128)(2,1)} %get-tuple-element.326.refs_1_.refs_3_, bf16[1024,192]{1,0:T(8,128)(2,1)} %get-tuple-element.324.refs_2_.refs_3_, ...), custom_call_target="tpu_custom_call" | custom-call | tf_op jit(solution)/shard_map/attention_out/pallas_call | solution.py:60
  83.1 3.8 %up.4 = (bf16[1024,768]{1,0:T(8,128)(2,1)}, bf16[1024,768]{1,0:T(8,128)(2,1)}) custom-call(bf16[1024,768]{1,0:T(8,128)(2,1)S(1)} %get-tuple-element.378.h_ref.refs_0_, f32[1,768]{1,0:T(1,128)S(1)} %reshape.195.bias_ref, bf16[768,768]{1,0:T(8,128)(2,1)S(1)} %copy-done.78), custom_call_target="tpu_custom_call" | custom-call | tf_op jit(solution)/shard_map/up/pallas_call | solution.py:60
  87.4 5.3 %up.5 = (bf16[1024,768]{1,0:T(8,128)(2,1)}, bf16[1024,768]{1,0:T(8,128)(2,1)}) custom-call(bf16[1024,768]{1,0:T(8,128)(2,1)S(1)} %get-tuple-element.378.h_ref.refs_0_, f32[1,768]{1,0:T(1,128)S(1)} %reshape.196.bias_ref, bf16[768,768]{1,0:T(8,128)(2,1)} %get-tuple-element.335.refs_0_.refs_1_), custom_call_target="tpu_custom_call" | custom-call | flops 6000000000 | tf_op jit(solution)/shard_map/up/pallas_call | solution.py:60
  92.6 4.4 %collective-permute-done.28.refs_2_ = bf16[2,2,128,768]{3,2,1,0:T(8,128)(2,1)} collective-permute-done((bf16[2,2,128,768]{3,2,1,0:T(8,128)(2,1)}, bf16[2,2,128,768]{3,2,1,0:T(8,128)(2,1)}, u32[]{:S(2)}, u32[]{:S(2)}) %collective-permute-start.28) | collective-permute-done | bytes 786464 | tf_op jit(solution)/shard_map/ppermute | solution.py:647
  98.7 4.2 %up.6 = (bf16[1024,768]{1,0:T(8,128)(2,1)}, bf16[1024,768]{1,0:T(8,128)(2,1)}) custom-call(bf16[1024,768]{1,0:T(8,128)(2,1)S(1)} %get-tuple-element.378.h_ref.refs_0_, f32[1,768]{1,0:T(1,128)S(1)} %get-tuple-element.521.bias_ref, bf16[384,768]{1,0:T(8,128)(2,1)S(1)} %collective-permute-done.24.refs_0_.refs_2_, ...), custom_call_target="tpu_custom_call" | custom-call | tf_op jit(solution)/shard_map/up/pallas_call | solution.py:60
  105.2 4.8 %weight_grads.8 = (bf16[768,384]{1,0:T(8,128)(2,1)S(1)}, bf16[768,384]{1,0:T(8,128)(2,1)S(1)}, bf16[768,384]{1,0:T(8,128)(2,1)S(1)}, bf16[768,384]{1,0:T(8,128)(2,1)S(1)}) custom-call(bf16[1024,768]{1,0:T(8,128)(2,1)S(1)} %get-tuple-element.363.refs_0_.g_ref, bf16[1024,768]{1,0:T(8,128)(2,1)S(1)} %copy-done.12, ...), custom_call_target="tpu_custom_call" | custom-call | tf_op jit(solution)/shard_map/weight_grads/pallas_call | solution.py:60
  111.1 4.2 %up.7 = (bf16[1024,768]{1,0:T(8,128)(2,1)}, bf16[1024,768]{1,0:T(8,128)(2,1)}) custom-call(bf16[1024,768]{1,0:T(8,128)(2,1)S(1)} %get-tuple-element.378.h_ref.refs_0_, f32[1,768]{1,0:T(1,128)S(1)} %get-tuple-element.520.bias_ref, bf16[384,768]{1,0:T(8,128)(2,1)S(1)} %slice.126.refs_0_, bf16[384,768]{1,0:T(8,128)(2,1)S(1)} %collective-permute-done.25.refs_1_), custom_call_target="tpu_custom_call" | custom-call | tf_op jit(solution)/shard_map/up/pallas_call | solution.py:60
  115.4 6.0 %weight_grads.9 = (bf16[1,768,768]{2,1,0:T(8,128)(2,1)S(1)}, bf16[1,768,768]{2,1,0:T(8,128)(2,1)}) custom-call(bf16[1024,768]{1,0:T(8,128)(2,1)} %copy-done.3, bf16[1024,768]{1,0:T(8,128)(2,1)} %get-tuple-element.333.refs_1_.refs_0_, bf16[1024,768]{1,0:T(8,128)(2,1)} %get-tuple-element.352.refs_2_, bf16[768,384]{1,0:T(8,128)(2,1)S(1)} %collective-permute-done.30.refs_3_, ...), custom_call_target="tpu_custom_call" | custom-call | tf_op jit(solution)/shard_map/weight_grads/pallas_call | solution.py:60
  125.1 10.3 %up_back.2 = (bf16[1024,768]{1,0:T(8,128)(2,1)}, bf16[1024,768]{1,0:T(8,128)(2,1)}, f32[1,768]{1,0:T(1,128)}, f32[1,768]{1,0:T(1,128)}, f32[1024,768]{1,0:T(8,128)}) custom-call(bf16[1024,768]{1,0:T(8,128)(2,1)S(1)} %copy-done.4, bf16[768,768]{1,0:T(8,128)(2,1)} %refs_0_.3, bf16[768,768]{1,0:T(8,128)(2,1)} %get-tuple-element.335.refs_0_.refs_1_, ...), custom_call_target="tpu_custom_call" | custom-call | tf_op jit(solution)/shard_map/up_back/pallas_call | solution.py:60
  135.5 11.8 %up_back.3 = (bf16[1024,768]{1,0:T(8,128)(2,1)}, bf16[1024,768]{1,0:T(8,128)(2,1)}, f32[1,768]{1,0:T(1,128)}, f32[1,768]{1,0:T(1,128)}, f32[1024,768]{1,0:T(8,12...) custom-call(bf16[1024,768]{1,0:T(8,128)(2,1)} %copy-done.3, ...), custom_call_target="tpu_custom_call" | custom-call | tf_op jit(solution)/shard_map/up_back/pallas_call | solution.py:60
  147.4 5.3 %weight_grads.10 = (bf16[768,384]{1,0:T(8,128)(2,1)}, bf16[768,384]{1,0:T(8,128)(2,1)}, bf16[768,384]{1,0:T(8,128)(2,1)}, bf16[768,384]{1,0:T(8,128)(2,1)}) custom-call(bf16[1024,768]{1,0:T(8,128)(2,1)S(1)} %get-tuple-element.378.h_ref.refs_0_, bf16[1024,768]{1,0:T(8,128)(2,1)S(1)} %copy-done.42, bf16[1024,768]{1,0:T(8,128)(2,1)} %get-tuple-element.372.refs_2_), custom_call_target="tpu_custom_call" | custom-call | tf_op jit(solution)/shard_map/weight_grads/pallas_call | solution.py:60
  153.7 3.3 %add_split.11 = (bf16[4,96,768]{2,1,0:T(8,128)(2,1)}, bf16[4,96,768]{2,1,0:T(8,128)(2,1)S(1)}) custom-call(s32[1]{0:T(128)} %bitcast.25.at.refs_0_, bf16[4,2,96,768]{3,2,1,0:T(8,128)(2,1)S(1)} %bitcast.63, bf16[4,2,96,768]{3,2,1,0:T(8,128)(2,1)} %bitcast.35.arrived_ref), custom_call_target="tpu_custom_call" | custom-call | tf_op jit(solution)/shard_map/add_split/pallas_call | solution.py:60
  157.4 6.3 %weight_grads.11 = (bf16[1,768,768]{2,1,0:T(8,128)(2,1)S(1)}, bf16[1,768,768]{2,1,0:T(8,128)(2,1)}) custom-call(bf16[1024,768]{1,0:T(8,128)(2,1)} %copy-done.2, bf16[1024,768]{1,0:T(8,128)(2,1)} %get-tuple-element.362.refs_1_, bf16[1024,768]{1,0:T(8,128)(2,1)} %get-tuple-element.369.refs_2_, bf16[768,384]{1,0:T(8,128)(2,1)S(1)} %collective-permute-done.37.refs_3_, ...), custom_call_target="tpu_custom_call" | custom-call | tf_op jit(solution)/shard_map/weight_grads/pallas_call | solution.py:60
  166.9 9.4 %attend_back.2 = (bf16[1024,576]{1,0:T(8,128)(2,1)S(1)}, bf16[1024,576]{1,0:T(8,128)(2,1)S(1)}, f32[1,576]{1,0:T(1,128)S(1)}, f32[1,576]{1,0:T(1,128)S(1)}) custom-call(s32[2]{0:T(128)S(1)} %fusion.8.lens.n, bf16[1024,576]{1,0:T(8,128)(2,1)S(1)} %copy-done.80, bf16[1024,576]{1,0:T(8,128)(2,1)S(1)} %copy-done.17, bf16[1024,768]{1,0:T(8,128)(2,1)S(1)} %copy-done, ...), custom_call_target="tpu_custom_call" | custom-call | tf_op jit(solution)/shard_map/attend_back/pallas_call | solution.py:60
  177.4 3.4 %weight_grads.12 = (bf16[768,384]{1,0:T(8,128)(2,1)}, bf16[768,384]{1,0:T(8,128)(2,1)}) custom-call(bf16[1024,768]{1,0:T(8,128)(2,1)S(1)} %copy-done.76, bf16[1024,768]{1,0:T(8,128)(2,1)S(1)} %copy-done, bf16[1024,576]{1,0:T(8,128)(2,1)S(1)} %get-tuple-element.390.refs_2_.refs_3_, bf16[1024,192]{1,0:T(8,128)(2,1)S(1)} %copy-done.28), custom_call_target="tpu_custom_call" | custom-call | tf_op jit(solution)/shard_map/weight_grads/pallas_call | solution.py:60
  187.5 4.3 %weight_grads.13 = bf16[1,768,768]{2,1,0:T(8,128)(2,1)} custom-call(bf16[1024,768]{1,0:T(8,128)(2,1)} %copy-done.75, bf16[1024,768]{1,0:T(8,128)(2,1)S(1)} %copy-done, bf16[1024,576]{1,0:T(8,128)(2,1)S(1)} %copy-done.14, bf16[1024,192]{1,0:T(8,128)(2,1)S(1)} %copy-done.26, bf16[768,384]{1,0:T(8,128)(2,1)S(1)} %copy-done.52, ...), custom_call_target="tpu_custom_call" | custom-call | tf_op jit(solution)/shard_map/weight_grads/pallas_call | solution.py:60
  192.2 3.5 %collective-permute-start.45 = (bf16[2,96,768]{2,1,0:T(8,128)(2,1)}, bf16[2,96,768]{2,1,0:T(8,128)(2,1)S(1)}, u32[]{:S(2)}, u32[]{:S(2)}) collective-permute-start(bf16[2,96,768]{2,1,0:T(8,128)(2,1)} %get-tuple-element.394), channel_id=1, source_target_pairs={{0,8},{4,12},{8,0},{12,4},{16,24},{20,28},{24,16},{28,20},{1,9},{5... | collective-permute-start | bytes 884744 | tf_op jit(solution)/shard_map/ppermute | solution.py:650
  197.0 9.3 %attend_back.3 = (bf16[1024,576]{1,0:T(8,128)(2,1)S(1)}, bf16[1024,576]{1,0:T(8,128)(2,1)S(1)}, f32[1,576]{1,0:T(1,128)S(1)}, f32[1,576]{1,0:T(1,128)S(1)}) custom-call(s32[2]{0:T(128)S(1)} %fusion.8.lens.n, bf16[1024,576]{1,0:T(8,128)(2,1)S(1)} %copy-done.7, bf16[1024,576]{1,0:T(8,128)(2,1)S(1)} %copy-done.9, ...), custom_call_target="tpu_custom_call" | custom-call | tf_op jit(solution)/shard_map/attend_back/pallas_call | solution.py:60
  208.7 2.8 collective-permute-start.47
  211.7 4.0 %weight_grads.14 = (bf16[768,384]{1,0:T(8,128)(2,1)}, bf16[768,384]{1,0:T(8,128)(2,1)S(1)}) custom-call(bf16[1024,768]{1,0:T(8,128)(2,1)} %copy-done.75, bf16[1024,768]{1,0:T(8,128)(2,1)S(1)} %copy-done.1, bf16[1024,576]{1,0:T(8,128)(2,1)S(1)} %get-tuple-element.412.refs_2_.refs_1_, bf16[1024,192]{1,0:T(8,128)(2,1)S(1)} %copy-done.27), custom_call_target="tpu_custom_call" | custom-call | tf_op jit(solution)/shard_map/weight_grads/pallas_call | solution.py:60
  217.9 9.3 %down_out.1 = (bf16[2,128,768]{2,1,0:T(8,128)(2,1)}, bf16[2,128,768]{2,1,0:T(8,128)(2,1)}, bf16[2,2,128,768]{3,2,1,0:T(8,128)(2,1)S(1)}) custom-call(s32[1]{0:T(128)} %bitcast.17.at, f32[1024,768]{1,0:T(8,128)} %copy-done.5, bf16[1024,768]{1,0:T(8,128)(2,1)S(1)} %copy-done.10, bf16[1024,768]{1,0:T(8,128)(2,1)} %get-tuple-element.336.refs_1_, ...), custom_call_target="tpu_custom_call" | custom-call | tf_op jit(solution)/shard_map/down_out/pallas_call | solution.py:60
  228.8 3.9 %weight_grads.15 = (bf16[1,384,768]{2,1,0:T(8,128)(2,1)S(1)}, bf16[1,384,768]{2,1,0:T(8,128)(2,1)S(1)}) custom-call(s32[1]{0:T(128)} %bitcast.25.at.refs_0_, bf16[1024,768]{1,0:T(8,128)(2,1)} %copy-done.75, bf16[1024,768]{1,0:T(8,128)(2,1)} %get-tuple-element.385.refs_2_.refs_1_, bf16[1024,576]{1,0:T(8,128)(2,1)S(1)} %get-tuple-element.400.refs_3_.refs_0_, ...), custom_call_target="tpu_custom_call" | custom-call | tf_op jit(solution)/shard_map/weight_grads/pallas_call | solution.py:60
  234.0 11.7 %norm_one_back.1 = (bf16[2,128,768]{2,1,0:T(8,128)(2,1)S(1)}, bf16[2,128,768]{2,1,0:T(8,128)(2,1)S(1)}, bf16[2,2,128,768]{3,2,1,0:T(8,128)(2,1)S(1)}, f32[1,768]{1,0:T(1,128)S(1)}, f32[1,768]{1,0:T(1,128)S(1)}) custom-call(s32[1]{0:T(128)} %bitcast.17.at, bf16[1024,768]{1,0:T(8,128)(2,1)} %copy-done.11, f32[1024,768]{1,0:T(8,128)} %get-tuple-element.425.dres_ref, ...), custom_call_target="tpu_custom_call" | custom-call | tf_op jit(solution)/shard_map/norm_one_back/pallas_call | solution.py:60
  248.2 13.3 %conditional.4 = (f32[14,768]{1,0:T(8,128)S(1)}, bf16[1,96,768]{2,1,0:T(8,128)(2,1)S(1)}, bf16[1,96,768]{2,1,0:T(8,128)(2,1)}, bf16[2,96,768]{2,1,0:T(8,128)(2,1)}, bf16[2,96,768]{2,1,0:T(8,128)(2,1)}) conditional(s32[]{:T(128)} %bitcast.16, () %tuple.120, (f32[14,768]{1,0:T(8,128)S(1)}, s32[]{:T(128)}, bf16[1,384,768]{2,1,0:T(8,128)(2,1)S(1)}, ...), branch_computations={%region_5.6_spmd, %region_6.7_spmd} | conditional | flops 32256 | bytes 2672880 | solution.py:775
  257.1 4.3 %collective-permute-done.6 = f32[14,768]{1,0:T(8,128)S(1)} collective-permute-done((f32[14,768]{1,0:T(8,128)S(1)}, f32[14,768]{1,0:T(8,128)S(1)}, u32[]{:S(2)}, u32[]{:S(2)}) %collective-permute-start.6) | collective-permute-done | bytes 43040 | tf_op jit(solution)/shard_map/cond/branch_1_fun/ppermute | solution.py:650
  266.8 16.8 %conditional.5 = (bf16[8,128,768]{2,1,0:T(8,128)(2,1)}, f32[768]{0:T(1024)S(1)}, f32[768]{0:T(1024)S(1)}, f32[768]{0:T(1024)S(1)}, f32[768]{0:T(1024)S(1)}, /*in...) conditional(s32[]{:T(128)} %bitcast.16, () %tuple.119, ...), branch_computations={%region_7.8_spmd, %region_8.9_spmd} | conditional | flops 574472 | bytes 6746484 | solution.py:775
  276.2 3.1 %join_rows.2 = bf16[8,128,768]{2,1,0:T(8,128)(2,1)} custom-call(s32[1]{0:T(128)} %bitcast.6.at, s32[8]{0:T(128)S(1)} %get-tuple-element.75.text_at, bf16[2,128,768]{2,1,0:T(8,128)(2,1)S(1)} %copy-done.88, bf16[2,128,768]{2,1,0:T(8,128)(2,1)} %get-tuple-element.89.refs_1_, bf16[2,2,128,768]{3,2,1,0:T(8,128)(2,1)} %get-tuple-element.90.refs_2_, ...), custom_call_target="tpu_custom_call" | custom-call | tf_op jit(solution)/shard_map/cond/branch_1_fun/join_rows/pallas_call | solution.py:60
  (399 shorter events, 113.1 us)
Async XLA Ops:
  6.1 14.1 %collective-permute-start.17 = (bf16[2,128,768]{2,1,0:T(8,128)(2,1)}, bf16[2,128,768]{2,1,0:T(8,128)(2,1)}, u32[]{:S(2)}, u32[]{:S(2)}) collective-permute-start(bf16[2,128,768]{2,1,0:T(8,128)(2,1)} %get-tuple-element.297), channel_id=1, source_target_pairs={{0,3},{1,2},{2,1},{3,0},{4,7},{5,6},{6,5},{7,4},{8,11},{9,10},{10,... | collective-permute-start | bytes 1179656 | tf_op jit(solution)/shard_map/ppermute | solution.py:647
  8.8 23.2 %collective-permute-start.16 = (bf16[2,128,768]{2,1,0:T(8,128)(2,1)}, bf16[2,128,768]{2,1,0:T(8,128)(2,1)}, u32[]{:S(2)}, u32[]{:S(2)}) collective-permute-start(bf16[2,128,768]{2,1,0:T(8,128)(2,1)} %get-tuple-element.296), channel_id=1, source_target_pairs={{0,2},{1,3},{2,0},{3,1},{4,6},{5,7},{6,4},{7,5},{8,10},{9,11},{10,... | collective-permute-start | bytes 1179656 | tf_op jit(solution)/shard_map/ppermute | solution.py:647
  9.6 20.0 %collective-permute-start.14 = (bf16[384,576]{1,0:T(8,128)(2,1)S(1)}, bf16[384,576]{1,0:T(8,128)(2,1)S(1)}, u32[]{:S(2)}, u32[]{:S(2)}) collective-permute-start(bf16[384,576]{1,0:T(8,128)(2,1)S(1)} %get-tuple-element.309.refs_0_.refs_4_), channel_id=1, source_target_pairs={{0,1},{1,0},{2,3},{3,2},{4,5},{5,4},{6,7},{7,6},{8,9},{9,8},{10,11... | collective-permute-start | bytes 1327112 | tf_op jit(solution)/shard_map/ppermute | solution.py:647
  9.8 20.0 %collective-permute-start.15 = (bf16[384,576]{1,0:T(8,128)(2,1)S(1)}, bf16[384,576]{1,0:T(8,128)(2,1)S(1)}, u32[]{:S(2)}, u32[]{:S(2)}) collective-permute-start(bf16[384,576]{1,0:T(8,128)(2,1)S(1)} %get-tuple-element.316.refs_1_.refs_5_), channel_id=1, source_target_pairs={{0,1},{1,0},{2,3},{3,2},{4,5},{5,4},{6,7},{7,6},{8,9},{9,8},{10,11... | collective-permute-start | bytes 1327112 | tf_op jit(solution)/shard_map/ppermute | solution.py:647
  14.8 12.6 %collective-permute-start.21 = (f32[2,1152]{1,0:T(2,128)S(1)}, f32[2,1152]{1,0:T(2,128)S(1)}, u32[]{:S(2)}, u32[]{:S(2)}) collective-permute-start(f32[2,1152]{1,0:T(2,128)S(1)} %pad_maximum_fusion.6), channel_id=1, source_target_pairs={{0,2},{1,3},{2,0},{3,1},{4,6},{5,7},{6,4},{7,5},{8,10},{9,11},{10,... | collective-permute-start | bytes 27656 | tf_op jit(solution)/shard_map/ppermute | solution.py:647
  20.2 27.2 %collective-permute-start.20 = (bf16[384,576]{1,0:T(8,128)(2,1)S(1)}, bf16[384,576]{1,0:T(8,128)(2,1)S(1)}, u32[]{:S(2)}, u32[]{:S(2)}) collective-permute-start(bf16[384,576]{1,0:T(8,128)(2,1)S(1)} %get-tuple-element.316.refs_1_.refs_5_), channel_id=1, source_target_pairs={{0,2},{1,3},{2,0},{3,1},{4,6},{5,7},{6,4},{7,5},{8,10},{9,11},{10,... | collective-permute-start | bytes 1327112 | tf_op jit(solution)/shard_map/ppermute | solution.py:647
  27.5 21.1 %collective-permute-start.18 = (bf16[384,576]{1,0:T(8,128)(2,1)S(1)}, bf16[384,576]{1,0:T(8,128)(2,1)S(1)}, u32[]{:S(2)}, u32[]{:S(2)}) collective-permute-start(bf16[384,576]{1,0:T(8,128)(2,1)S(1)} %get-tuple-element.309.refs_0_.refs_4_), channel_id=1, source_target_pairs={{0,2},{1,3},{2,0},{3,1},{4,6},{5,7},{6,4},{7,5},{8,10},{9,11},{10,... | collective-permute-start | bytes 1327112 | tf_op jit(solution)/shard_map/ppermute | solution.py:647
  29.8 39.3 %collective-permute-start.22 = (bf16[576,768]{1,0:T(8,128)(2,1)}, bf16[576,768]{1,0:T(8,128)(2,1)}, u32[]{:S(2)}, u32[]{:S(2)}) collective-permute-start(bf16[576,768]{1,0:T(8,128)(2,1)} %pad_maximum_fusion.1), channel_id=1, source_target_pairs={{0,2},{1,3},{2,0},{3,1},{4,6},{5,7},{6,4},{7,5},{8,10},{9,11},{10,... | collective-permute-start | bytes 2654216 | tf_op jit(solution)/shard_map/ppermute | solution.py:647
  55.4 31.5 %collective-permute-start.25 = (bf16[384,768]{1,0:T(8,128)(2,1)}, bf16[384,768]{1,0:T(8,128)(2,1)S(1)}, u32[]{:S(2)}, u32[]{:S(2)}) collective-permute-start(bf16[384,768]{1,0:T(8,128)(2,1)} %get-tuple-element.338), channel_id=1, source_target_pairs={{0,2},{1,3},{2,0},{3,1},{4,6},{5,7},{6,4},{7,5},{8,10},{9,11},{10,... | collective-permute-start | bytes 1769480 | tf_op jit(solution)/shard_map/ppermute | solution.py:647
  70.2 26.9 %collective-permute-start.28 = (bf16[2,2,128,768]{3,2,1,0:T(8,128)(2,1)}, bf16[2,2,128,768]{3,2,1,0:T(8,128)(2,1)}, u32[]{:S(2)}, u32[]{:S(2)}) collective-permute-start(bf16[2,2,128,768]{3,2,1,0:T(8,128)(2,1)} %get-tuple-element.345), channel_id=1, source_target_pairs={{0,2},{1,3},{2,0},{3,1},{4,6},{5,7},{6,4},{7,5},{8,10},{9,11},{10,... | collective-permute-start | bytes 2359304 | tf_op jit(solution)/shard_map/ppermute | solution.py:647
  72.6 49.5 %collective-permute-start.34 = (bf16[768,768]{1,0:T(8,128)(2,1)}, bf16[768,768]{1,0:T(8,128)(2,1)S(1)}, u32[]{:S(2)}, u32[]{:S(2)}) collective-permute-start(bf16[768,768]{1,0:T(8,128)(2,1)} %refs_4_.3), channel_id=1, source_target_pairs={{0,2},{1,3},{2,0},{3,1},{4,6},{5,7},{6,4},{7,5},{8,10},{9,11},{10,... | collective-permute-start | bytes 3538952 | tf_op jit(solution)/shard_map/ppermute | solution.py:647
  75.2 23.5 %collective-permute-start.24 = (bf16[384,768]{1,0:T(8,128)(2,1)S(1)}, bf16[384,768]{1,0:T(8,128)(2,1)S(1)}, u32[]{:S(2)}, u32[]{:S(2)}) collective-permute-start(bf16[384,768]{1,0:T(8,128)(2,1)S(1)} %slice.126.refs_0_), channel_id=1, source_target_pairs={{0,1},{1,0},{2,3},{3,2},{4,5},{5,4},{6,7},{7,6},{8,9},{9,8},{10,11... | collective-permute-start | bytes 1769480 | tf_op jit(solution)/shard_map/ppermute | solution.py:647
  86.9 11.9 %collective-permute-start.26 = (bf16[384,768]{1,0:T(8,128)(2,1)S(1)}, bf16[384,768]{1,0:T(8,128)(2,1)S(1)}, u32[]{:S(2)}, u32[]{:S(2)}) collective-permute-start(bf16[384,768]{1,0:T(8,128)(2,1)S(1)} %collective-permute-done.25.refs_1_), channel_id=1, source_target_pairs={{0,1},{1,0},{2,3},{3,2},{4,5},{5,4},{6,7},{7,6},{8,9},{9,8},{10,11... | collective-permute-start | bytes 1769480 | tf_op jit(solution)/shard_map/ppermute | solution.py:647
  122.1 13.4 %collective-permute-start.35 = (bf16[768,768]{1,0:T(8,128)(2,1)S(1)}, bf16[768,768]{1,0:T(8,128)(2,1)S(1)}, u32[]{:S(2)}, u32[]{:S(2)}) collective-permute-start(bf16[768,768]{1,0:T(8,128)(2,1)S(1)} %collective-permute-done.34.refs_4_.refs_6_), channel_id=1, source_target_pairs={{0,1},{1,0},{2,3},{3,2},{4,5},{5,4},{6,7},{7,6},{8,9},{9,8},{10,11... | collective-permute-start | bytes 3538952 | tf_op jit(solution)/shard_map/ppermute | solution.py:647
  122.1 31.6 %collective-permute-start.36 = (bf16[1,768,768]{2,1,0:T(8,128)(2,1)}, bf16[1,768,768]{2,1,0:T(8,128)(2,1)}, u32[]{:S(2)}, u32[]{:S(2)}) collective-permute-start(bf16[1,768,768]{2,1,0:T(8,128)(2,1)} %get-tuple-element.375), channel_id=1, source_target_pairs={{0,2},{1,3},{2,0},{3,1},{4,6},{5,7},{6,4},{7,5},{8,10},{9,11},{10,... | collective-permute-start | bytes 3538952 | tf_op jit(solution)/shard_map/ppermute | solution.py:647
  164.8 41.5 %collective-permute-start.44 = (bf16[1,768,768]{2,1,0:T(8,128)(2,1)}, bf16[1,768,768]{2,1,0:T(8,128)(2,1)}, u32[]{:S(2)}, u32[]{:S(2)}) collective-permute-start(bf16[1,768,768]{2,1,0:T(8,128)(2,1)} %get-tuple-element.402), channel_id=1, source_target_pairs={{0,2},{1,3},{2,0},{3,1},{4,6},{5,7},{6,4},{7,5},{8,10},{9,11},{10,... | collective-permute-start | bytes 3538952 | tf_op jit(solution)/shard_map/ppermute | solution.py:647
  165.3 16.1 %collective-permute-start.41 = (bf16[4,96,768]{2,1,0:T(8,128)(2,1)}, bf16[4,96,768]{2,1,0:T(8,128)(2,1)S(1)}, u32[]{:S(2)}, u32[]{:S(2)}) collective-permute-start(bf16[4,96,768]{2,1,0:T(8,128)(2,1)} %get-tuple-element.377), channel_id=1, source_target_pairs={{0,4},{4,0},{8,12},{12,8},{16,20},{20,16},{24,28},{28,24},{1,5},{5... | collective-permute-start | bytes 1769480 | tf_op jit(solution)/shard_map/ppermute | solution.py:650
  191.7 37.1 %collective-permute-start.50 = (bf16[1,768,768]{2,1,0:T(8,128)(2,1)}, bf16[1,768,768]{2,1,0:T(8,128)(2,1)S(1)}, u32[]{:S(2)}, u32[]{:S(2)}) collective-permute-start(bf16[1,768,768]{2,1,0:T(8,128)(2,1)} %weight_grads.13), channel_id=1, source_target_pairs={{0,2},{1,3},{2,0},{3,1},{4,6},{5,7},{6,4},{7,5},{8,10},{9,11},{10,... | collective-permute-start | bytes 3538952 | tf_op jit(solution)/shard_map/ppermute | solution.py:647
  192.2 19.3 %collective-permute-start.45 = (bf16[2,96,768]{2,1,0:T(8,128)(2,1)}, bf16[2,96,768]{2,1,0:T(8,128)(2,1)S(1)}, u32[]{:S(2)}, u32[]{:S(2)}) collective-permute-start(bf16[2,96,768]{2,1,0:T(8,128)(2,1)} %get-tuple-element.394), channel_id=1, source_target_pairs={{0,8},{4,12},{8,0},{12,4},{16,24},{20,28},{24,16},{28,20},{1,9},{5... | collective-permute-start | bytes 884744 | tf_op jit(solution)/shard_map/ppermute | solution.py:650
  208.7 19.9 %collective-permute-start.47 = (bf16[4,96,768]{2,1,0:T(8,128)(2,1)S(1)}, bf16[4,96,768]{2,1,0:T(8,128)(2,1)S(1)}, u32[]{:S(2)}, u32[]{:S(2)}) collective-permute-start(bf16[4,96,768]{2,1,0:T(8,128)(2,1)S(1)} %get-tuple-element.406), channel_id=1, source_target_pairs={{0,4},{4,0},{8,12},{12,8},{16,20},{20,16},{24,28},{28,24},{1,5},{5... | collective-permute-start | bytes 1769480 | tf_op jit(solution)/shard_map/ppermute | solution.py:650
  215.6 13.2 %collective-permute-start.48 = (bf16[768,384]{1,0:T(8,128)(2,1)}, bf16[768,384]{1,0:T(8,128)(2,1)S(1)}, u32[]{:S(2)}, u32[]{:S(2)}) collective-permute-start(bf16[768,384]{1,0:T(8,128)(2,1)} %get-tuple-element.413), channel_id=1, source_target_pairs={{0,1},{1,0},{2,3},{3,2},{4,5},{5,4},{6,7},{7,6},{8,9},{9,8},{10,11... | collective-permute-start | bytes 1769480 | tf_op jit(solution)/shard_map/ppermute | solution.py:647
  215.6 13.2 %collective-permute-start.49 = (bf16[768,384]{1,0:T(8,128)(2,1)S(1)}, bf16[768,384]{1,0:T(8,128)(2,1)S(1)}, u32[]{:S(2)}, u32[]{:S(2)}) collective-permute-start(bf16[768,384]{1,0:T(8,128)(2,1)S(1)} %get-tuple-element.421), channel_id=1, source_target_pairs={{0,1},{1,0},{2,3},{3,2},{4,5},{5,4},{6,7},{7,6},{8,9},{9,8},{10,11... | collective-permute-start | bytes 1769480 | tf_op jit(solution)/shard_map/ppermute | solution.py:647
  216.1 11.1 %collective-permute-start.46 = (bf16[1,96,768]{2,1,0:T(8,128)(2,1)S(1)}, bf16[1,96,768]{2,1,0:T(8,128)(2,1)S(1)}, u32[]{:S(2)}, u32[]{:S(2)}) collective-permute-start(bf16[1,96,768]{2,1,0:T(8,128)(2,1)S(1)} %get-tuple-element.410), channel_id=1, source_target_pairs={{0,16},{4,20},{8,24},{12,28},{16,0},{20,4},{24,8},{28,12},{1,17},{... | collective-permute-start | bytes 442376 | tf_op jit(solution)/shard_map/ppermute | solution.py:650
  227.2 19.4 %collective-permute-start.54 = (bf16[2,2,128,768]{3,2,1,0:T(8,128)(2,1)S(1)}, bf16[2,2,128,768]{3,2,1,0:T(8,128)(2,1)S(1)}, u32[]{:S(2)}, u32[]{:S(2)}) collective-permute-start(bf16[2,2,128,768]{3,2,1,0:T(8,128)(2,1)S(1)} %get-tuple-element.456), channel_id=1, source_target_pairs={{0,2},{1,3},{2,0},{3,1},{4,6},{5,7},{6,4},{7,5},{8,10},{9,11},{10,... | collective-permute-start | bytes 2359304 | tf_op jit(solution)/shard_map/ppermute | solution.py:647
  232.8 15.2 %collective-permute-start.51 = (bf16[1,384,768]{2,1,0:T(8,128)(2,1)S(1)}, bf16[1,384,768]{2,1,0:T(8,128)(2,1)S(1)}, u32[]{:S(2)}, u32[]{:S(2)}) collective-permute-start(bf16[1,384,768]{2,1,0:T(8,128)(2,1)S(1)} %get-tuple-element.423), channel_id=1, source_target_pairs={{0,4},{4,0},{8,12},{12,8},{16,20},{20,16},{24,28},{28,24},{1,5},{5... | collective-permute-start | bytes 1769480 | tf_op jit(solution)/shard_map/ppermute | solution.py:650
  233.2 14.3 %collective-permute-start.52 = (bf16[2,96,768]{2,1,0:T(8,128)(2,1)S(1)}, bf16[2,96,768]{2,1,0:T(8,128)(2,1)S(1)}, u32[]{:S(2)}, u32[]{:S(2)}) collective-permute-start(bf16[2,96,768]{2,1,0:T(8,128)(2,1)S(1)} %get-tuple-element.419), channel_id=1, source_target_pairs={{0,8},{4,12},{8,0},{12,4},{16,24},{20,28},{24,16},{28,20},{1,9},{5... | collective-permute-start | bytes 884744 | tf_op jit(solution)/shard_map/ppermute | solution.py:650
  245.7 18.7 %collective-permute-start.57 = (bf16[2,2,128,768]{3,2,1,0:T(8,128)(2,1)S(1)}, bf16[2,2,128,768]{3,2,1,0:T(8,128)(2,1)S(1)}, u32[]{:S(2)}, u32[]{:S(2)}) collective-permute-start(bf16[2,2,128,768]{3,2,1,0:T(8,128)(2,1)S(1)} %get-tuple-element.464), channel_id=1, source_target_pairs={{0,2},{1,3},{2,0},{3,1},{4,6},{5,7},{6,4},{7,5},{8,10},{9,11},{10,... | collective-permute-start | bytes 2359304 | tf_op jit(solution)/shard_map/ppermute | solution.py:647
  245.8 21.0 %collective-permute-start.53 = (bf16[2,128,768]{2,1,0:T(8,128)(2,1)}, bf16[2,128,768]{2,1,0:T(8,128)(2,1)}, u32[]{:S(2)}, u32[]{:S(2)}) collective-permute-start(bf16[2,128,768]{2,1,0:T(8,128)(2,1)} %get-tuple-element.454), channel_id=1, source_target_pairs={{0,1},{1,0},{2,3},{3,2},{4,5},{5,4},{6,7},{7,6},{8,9},{9,8},{10,11... | collective-permute-start | bytes 1179656 | tf_op jit(solution)/shard_map/ppermute | solution.py:647
  249.1 12.3 %collective-permute-start.8 = (bf16[2,96,768]{2,1,0:T(8,128)(2,1)S(1)}, bf16[2,96,768]{2,1,0:T(8,128)(2,1)}, u32[]{:S(2)}, u32[]{:S(2)}) collective-permute-start(bf16[2,96,768]{2,1,0:T(8,128)(2,1)S(1)} %get-tuple-element.66), channel_id=1, source_target_pairs={{0,8},{4,12},{8,0},{12,4},{16,24},{20,28},{24,16},{28,20},{1,9},{5... | collective-permute-start | bytes 884744 | tf_op jit(solution)/shard_map/cond/branch_1_fun/ppermute | solution.py:650
  249.6 11.9 %collective-permute-start.7 = (bf16[1,96,768]{2,1,0:T(8,128)(2,1)S(1)}, bf16[1,96,768]{2,1,0:T(8,128)(2,1)}, u32[]{:S(2)}, u32[]{:S(2)}) collective-permute-start(bf16[1,96,768]{2,1,0:T(8,128)(2,1)S(1)} %get-tuple-element.62), channel_id=1, source_target_pairs={{0,16},{4,20},{8,24},{12,28},{16,0},{20,4},{24,8},{28,12},{1,17},{... | collective-permute-start | bytes 442376 | tf_op jit(solution)/shard_map/cond/branch_1_fun/ppermute | solution.py:650
  261.5 22.1 %collective-permute-start.56 = (bf16[2,128,768]{2,1,0:T(8,128)(2,1)S(1)}, bf16[2,128,768]{2,1,0:T(8,128)(2,1)S(1)}, u32[]{:S(2)}, u32[]{:S(2)}) collective-permute-start(bf16[2,128,768]{2,1,0:T(8,128)(2,1)S(1)} %copy-done.65), channel_id=1, source_target_pairs={{0,1},{1,0},{2,3},{3,2},{4,5},{5,4},{6,7},{7,6},{8,9},{9,8},{10,11... | collective-permute-start | bytes 1179656 | tf_op jit(solution)/shard_map/ppermute | solution.py:647
  265.2 18.5 %collective-permute-start.58 = (bf16[2,128,768]{2,1,0:T(8,128)(2,1)}, bf16[2,128,768]{2,1,0:T(8,128)(2,1)S(1)}, u32[]{:S(2)}, u32[]{:S(2)}) collective-permute-start(bf16[2,128,768]{2,1,0:T(8,128)(2,1)} %dynamic-slice_bitcast_fusion), channel_id=1, source_target_pairs={{0,1},{1,0},{2,3},{3,2},{4,5},{5,4},{6,7},{7,6},{8,9},{9,8},{10,11... | collective-permute-start | bytes 1179656 | tf_op jit(solution)/shard_map/ppermute | solution.py:647
  (135 other events, 918.4 us)

commit v8 on v7

--- a/solution.py
+++ b/solution.py
@@ -891,11 +891,11 @@
             load(state)
             for bit in high[1:]:
                 grads_up.step()
-            grad_up = clock.then(grads_up.last())
             for bit in high:
                 q_own.step()
                 total = moved(total, bit, False)
             total = moved(total, 2, True)
+            grad_up = clock.then(grads_up.last())
             rows_out = join_rows(clock, blocks, t, text_at)
             first = len(shared)
             vectors = [total[i] for i in range(first)]

time: 291 us -> 292 us (level)
    ppermute x47, starting transfers between devices: 24.3 us -> 28.3 us  [pp_tensor(): lax.ppermute(values, 'tensor', [(i, i ^ flip) for i in range(tensor_size)])]
  transfers between devices with their start and end apart: 59 -> 59, of which waited for: 20 -> 18; matrix products, arithmetic and copies ran while one was open for 6% -> 6% of each run, Pallas kernels for 56% -> 56%
where the time goes in v8:
time: 292 us; the launch traced here: 288 us
  Pallas kernels  170 us (58%)
  starting transfers between devices  41.8 us (14%)
  waiting for transfers between devices  37.1 us (13%)
  local copies, waits for them, and re-layouts  29.9 us (10%)
  other arithmetic  6.52 us (2%)
    pallas_call x41, Pallas kernels, call(): pl.pallas_call(body, out_shape=jax.tree.map(lambda v: pltpu.HBM(v.shape,...  170 us
    ppermute x47, starting transfers between devices, pp_tensor(): lax.ppermute(values, 'tensor', [(i, i ^ flip) for i in range(tensor_size)])  28.3 us
    ppermute x47, waiting for transfers between devices, pp_tensor(): lax.ppermute(values, 'tensor', [(i, i ^ flip) for i in range(tensor_size)])  23.7 us
    unnamed x213, local copies, waits for them, and re-layouts  18.8 us
    ppermute x12, starting transfers between devices, pp_dp(): lax.ppermute(values, 'dp', [(i, i ^ 1 << bit) for i in range(dp_size)])  13.5 us
    ppermute x12, waiting for transfers between devices, pp_dp(): lax.ppermute(values, 'dp', [(i, i ^ 1 << bit) for i in range(dp_size)])  13.4 us
  transfers between devices with their start and end apart: 59, of which 18 were waited for; matrix products, arithmetic and copies ran while one was open for 6% of the time, Pallas kernels for 56%

profile of v8, /device:TPU:0, one launch (start us, length us, event | category | flops | bytes accessed | tf_op | source)
XLA Modules:
  0.0 287.6 jit_solution(6816970950801634461)
XLA Ops:
  20.2 7.2 %collective-permute-done.21 = f32[2,1152]{1,0:T(2,128)S(1)} collective-permute-done((f32[2,1152]{1,0:T(2,128)S(1)}, f32[2,1152]{1,0:T(2,128)S(1)}, u32[]{:S(2)}, u32[]{:S(2)}) %collective-permute-start.21) | collective-permute-done | bytes 9248 | tf_op jit(solution)/shard_map/ppermute | solution.py:647
  40.0 7.4 %attend.2 = (bf16[1024,192]{1,0:T(8,128)(2,1)}, bf16[1024,192]{1,0:T(8,128)(2,1)}, bf16[2,6,512,512]{3,2,1,0:T(8,128)(2,1)}, f32[2,6,512]{2,1,0:T(8,128)}) custom-call(s32[2]{0:T(128)S(1)} %fusion.8.lens.n, bf16[1024,576]{1,0:T(8,128)(2,1)S(1)} %project.5.refs_0_, bf16[1024,576]{1,0:T(8,128)(2,1)S(1)} %project.6.refs_1_), custom_call_target="tpu_custom_call" | custom-call | tf_op jit(solution)/shard_map/attend/pallas_call | solution.py:60
  49.3 6.1 %conditional.3 = (bf16[384,576]{1,0:T(8,128)(2,1)}, bf16[384,576]{1,0:T(8,128)(2,1)}, bf16[1024,576]{1,0:T(8,128)(2,1)S(1)}, bf16[768,768]{1,0:T(8,128)(2,1)}, bf16[768,768]{1,0:T(8,128)(2,1)}) conditional(s32[]{:T(128)} %bitcast.16, () %tuple.127, (bf16[384,576]{1,0:T(8,128)(2,1)S(1)}, bf16[384,576]{1,0:T(8,128)(2,1)S(1)}, f32[576]{0:T(1024)S(1)}, ...), branch_computations={%region_3.4_spmd, %region_4.5_spmd} | conditional | bytes 12980936 | solution.py:775
  57.6 4.4 %project.7.refs_1_ = bf16[1024,576]{1,0:T(8,128)(2,1)S(1)} custom-call(bf16[1024,768]{1,0:T(8,128)(2,1)} %copy-done.75, f32[1,576]{1,0:T(1,128)S(1)} %reshape.191.bias_ref, bf16[384,576]{1,0:T(8,128)(2,1)} %get-tuple-element.319.refs_0_.refs_10_, bf16[384,576]{1,0:T(8,128)(2,1)} %get-tuple-element.321.refs_1_.refs_11_), custom_call_target="tpu_custom_call" | custom-call | tf_op jit(solution)/shard_map/project/pallas_call | solution.py:60
  62.0 7.1 %attend.3 = (bf16[1024,192]{1,0:T(8,128)(2,1)}, bf16[1024,192]{1,0:T(8,128)(2,1)}, bf16[2,6,512,512]{3,2,1,0:T(8,128)(2,1)}, f32[2,6,512]{2,1,0:T(8,128)}) custom-call(s32[2]{0:T(128)S(1)} %fusion.8.lens.n, bf16[1024,576]{1,0:T(8,128)(2,1)S(1)} %get-tuple-element.383.refs_0_, bf16[1024,576]{1,0:T(8,128)(2,1)S(1)} %project.7.refs_1_), custom_call_target="tpu_custom_call" | custom-call | flops 14000000000 | tf_op jit(solution)/shard_map/attend/pallas_call | solution.py:60
  76.0 5.4 %attention_out.1 = (f32[1024,768]{1,0:T(8,128)S(1)}, bf16[1024,768]{1,0:T(8,128)(2,1)S(1)}) custom-call(bf16[1024,768]{1,0:T(8,128)(2,1)} %copy-done.11, bf16[1024,192]{1,0:T(8,128)(2,1)} %get-tuple-element.313.refs_0_.refs_4_, bf16[1024,192]{1,0:T(8,128)(2,1)} %get-tuple-element.325.refs_1_.refs_3_, bf16[1024,192]{1,0:T(8,128)(2,1)} %get-tuple-element.323.refs_2_.refs_3_, ...), custom_call_target="tpu_custom_call" | custom-call | tf_op jit(solution)/shard_map/attention_out/pallas_call | solution.py:60
  83.1 3.8 %up.4 = (bf16[1024,768]{1,0:T(8,128)(2,1)}, bf16[1024,768]{1,0:T(8,128)(2,1)}) custom-call(bf16[1024,768]{1,0:T(8,128)(2,1)S(1)} %get-tuple-element.377.h_ref.refs_0_, f32[1,768]{1,0:T(1,128)S(1)} %reshape.195.bias_ref, bf16[768,768]{1,0:T(8,128)(2,1)S(1)} %copy-done.78), custom_call_target="tpu_custom_call" | custom-call | tf_op jit(solution)/shard_map/up/pallas_call | solution.py:60
  87.4 5.3 %up.5 = (bf16[1024,768]{1,0:T(8,128)(2,1)}, bf16[1024,768]{1,0:T(8,128)(2,1)}) custom-call(bf16[1024,768]{1,0:T(8,128)(2,1)S(1)} %get-tuple-element.377.h_ref.refs_0_, f32[1,768]{1,0:T(1,128)S(1)} %reshape.196.bias_ref, bf16[768,768]{1,0:T(8,128)(2,1)} %get-tuple-element.334.refs_0_.refs_1_), custom_call_target="tpu_custom_call" | custom-call | flops 6000000000 | tf_op jit(solution)/shard_map/up/pallas_call | solution.py:60
  92.6 4.4 %collective-permute-done.28.refs_2_ = bf16[2,2,128,768]{3,2,1,0:T(8,128)(2,1)} collective-permute-done((bf16[2,2,128,768]{3,2,1,0:T(8,128)(2,1)}, bf16[2,2,128,768]{3,2,1,0:T(8,128)(2,1)}, u32[]{:S(2)}, u32[]{:S(2)}) %collective-permute-start.28) | collective-permute-done | bytes 786464 | tf_op jit(solution)/shard_map/ppermute | solution.py:647
  98.7 4.2 %up.6 = (bf16[1024,768]{1,0:T(8,128)(2,1)}, bf16[1024,768]{1,0:T(8,128)(2,1)}) custom-call(bf16[1024,768]{1,0:T(8,128)(2,1)S(1)} %get-tuple-element.377.h_ref.refs_0_, f32[1,768]{1,0:T(1,128)S(1)} %get-tuple-element.520.bias_ref, bf16[384,768]{1,0:T(8,128)(2,1)S(1)} %collective-permute-done.24.refs_0_.refs_2_, ...), custom_call_target="tpu_custom_call" | custom-call | tf_op jit(solution)/shard_map/up/pallas_call | solution.py:60
  105.2 4.8 %weight_grads.8 = (bf16[768,384]{1,0:T(8,128)(2,1)S(1)}, bf16[768,384]{1,0:T(8,128)(2,1)S(1)}, bf16[768,384]{1,0:T(8,128)(2,1)S(1)}, bf16[768,384]{1,0:T(8,128)(2,1)S(1)}) custom-call(bf16[1024,768]{1,0:T(8,128)(2,1)S(1)} %get-tuple-element.362.refs_0_.g_ref, bf16[1024,768]{1,0:T(8,128)(2,1)S(1)} %copy-done.12, ...), custom_call_target="tpu_custom_call" | custom-call | tf_op jit(solution)/shard_map/weight_grads/pallas_call | solution.py:60
  111.1 4.2 %up.7 = (bf16[1024,768]{1,0:T(8,128)(2,1)}, bf16[1024,768]{1,0:T(8,128)(2,1)}) custom-call(bf16[1024,768]{1,0:T(8,128)(2,1)S(1)} %get-tuple-element.377.h_ref.refs_0_, f32[1,768]{1,0:T(1,128)S(1)} %get-tuple-element.519.bias_ref, bf16[384,768]{1,0:T(8,128)(2,1)S(1)} %slice.126.refs_0_, bf16[384,768]{1,0:T(8,128)(2,1)S(1)} %collective-permute-done.25.refs_1_), custom_call_target="tpu_custom_call" | custom-call | tf_op jit(solution)/shard_map/up/pallas_call | solution.py:60
  115.4 6.0 %weight_grads.9 = (bf16[1,768,768]{2,1,0:T(8,128)(2,1)S(1)}, bf16[1,768,768]{2,1,0:T(8,128)(2,1)}) custom-call(bf16[1024,768]{1,0:T(8,128)(2,1)} %copy-done.3, bf16[1024,768]{1,0:T(8,128)(2,1)} %get-tuple-element.332.refs_1_.refs_0_, bf16[1024,768]{1,0:T(8,128)(2,1)} %get-tuple-element.351.refs_2_, bf16[768,384]{1,0:T(8,128)(2,1)S(1)} %collective-permute-done.30.refs_3_, ...), custom_call_target="tpu_custom_call" | custom-call | tf_op jit(solution)/shard_map/weight_grads/pallas_call | solution.py:60
  125.1 10.3 %up_back.2 = (bf16[1024,768]{1,0:T(8,128)(2,1)}, bf16[1024,768]{1,0:T(8,128)(2,1)}, f32[1,768]{1,0:T(1,128)}, f32[1,768]{1,0:T(1,128)}, f32[1024,768]{1,0:T(8,128)}) custom-call(bf16[1024,768]{1,0:T(8,128)(2,1)S(1)} %copy-done.4, bf16[768,768]{1,0:T(8,128)(2,1)} %refs_0_.3, bf16[768,768]{1,0:T(8,128)(2,1)} %get-tuple-element.334.refs_0_.refs_1_, ...), custom_call_target="tpu_custom_call" | custom-call | tf_op jit(solution)/shard_map/up_back/pallas_call | solution.py:60
  135.5 11.8 %up_back.3 = (bf16[1024,768]{1,0:T(8,128)(2,1)}, bf16[1024,768]{1,0:T(8,128)(2,1)}, f32[1,768]{1,0:T(1,128)}, f32[1,768]{1,0:T(1,128)}, f32[1024,768]{1,0:T(8,12...) custom-call(bf16[1024,768]{1,0:T(8,128)(2,1)} %copy-done.3, ...), custom_call_target="tpu_custom_call" | custom-call | tf_op jit(solution)/shard_map/up_back/pallas_call | solution.py:60
  147.4 5.3 %weight_grads.10 = (bf16[768,384]{1,0:T(8,128)(2,1)}, bf16[768,384]{1,0:T(8,128)(2,1)}, bf16[768,384]{1,0:T(8,128)(2,1)}, bf16[768,384]{1,0:T(8,128)(2,1)}) custom-call(bf16[1024,768]{1,0:T(8,128)(2,1)S(1)} %get-tuple-element.377.h_ref.refs_0_, bf16[1024,768]{1,0:T(8,128)(2,1)S(1)} %copy-done.42, bf16[1024,768]{1,0:T(8,128)(2,1)} %get-tuple-element.371.refs_2_), custom_call_target="tpu_custom_call" | custom-call | tf_op jit(solution)/shard_map/weight_grads/pallas_call | solution.py:60
  153.7 3.3 %add_split.11 = (bf16[4,96,768]{2,1,0:T(8,128)(2,1)}, bf16[4,96,768]{2,1,0:T(8,128)(2,1)S(1)}) custom-call(s32[1]{0:T(128)} %bitcast.25.at.refs_0_, bf16[4,2,96,768]{3,2,1,0:T(8,128)(2,1)S(1)} %bitcast.63, bf16[4,2,96,768]{3,2,1,0:T(8,128)(2,1)} %bitcast.35.arrived_ref), custom_call_target="tpu_custom_call" | custom-call | tf_op jit(solution)/shard_map/add_split/pallas_call | solution.py:60
  157.4 6.3 %weight_grads.11 = (bf16[1,768,768]{2,1,0:T(8,128)(2,1)S(1)}, bf16[1,768,768]{2,1,0:T(8,128)(2,1)}) custom-call(bf16[1024,768]{1,0:T(8,128)(2,1)} %copy-done.2, bf16[1024,768]{1,0:T(8,128)(2,1)} %get-tuple-element.361.refs_1_, bf16[1024,768]{1,0:T(8,128)(2,1)} %get-tuple-element.368.refs_2_, bf16[768,384]{1,0:T(8,128)(2,1)S(1)} %collective-permute-done.37.refs_3_, ...), custom_call_target="tpu_custom_call" | custom-call | tf_op jit(solution)/shard_map/weight_grads/pallas_call | solution.py:60
  166.9 9.4 %attend_back.2 = (bf16[1024,576]{1,0:T(8,128)(2,1)S(1)}, bf16[1024,576]{1,0:T(8,128)(2,1)S(1)}, f32[1,576]{1,0:T(1,128)S(1)}, f32[1,576]{1,0:T(1,128)S(1)}) custom-call(s32[2]{0:T(128)S(1)} %fusion.8.lens.n, bf16[1024,576]{1,0:T(8,128)(2,1)S(1)} %copy-done.80, bf16[1024,576]{1,0:T(8,128)(2,1)S(1)} %copy-done.17, bf16[1024,768]{1,0:T(8,128)(2,1)S(1)} %copy-done, ...), custom_call_target="tpu_custom_call" | custom-call | tf_op jit(solution)/shard_map/attend_back/pallas_call | solution.py:60
  177.4 3.4 %weight_grads.12 = (bf16[768,384]{1,0:T(8,128)(2,1)}, bf16[768,384]{1,0:T(8,128)(2,1)}) custom-call(bf16[1024,768]{1,0:T(8,128)(2,1)S(1)} %copy-done.76, bf16[1024,768]{1,0:T(8,128)(2,1)S(1)} %copy-done, bf16[1024,576]{1,0:T(8,128)(2,1)S(1)} %get-tuple-element.389.refs_2_.refs_3_, bf16[1024,192]{1,0:T(8,128)(2,1)S(1)} %copy-done.28), custom_call_target="tpu_custom_call" | custom-call | tf_op jit(solution)/shard_map/weight_grads/pallas_call | solution.py:60
  187.5 4.3 %weight_grads.13 = bf16[1,768,768]{2,1,0:T(8,128)(2,1)} custom-call(bf16[1024,768]{1,0:T(8,128)(2,1)} %copy-done.75, bf16[1024,768]{1,0:T(8,128)(2,1)S(1)} %copy-done, bf16[1024,576]{1,0:T(8,128)(2,1)S(1)} %copy-done.14, bf16[1024,192]{1,0:T(8,128)(2,1)S(1)} %copy-done.26, bf16[768,384]{1,0:T(8,128)(2,1)S(1)} %copy-done.52, ...), custom_call_target="tpu_custom_call" | custom-call | tf_op jit(solution)/shard_map/weight_grads/pallas_call | solution.py:60
  198.3 9.3 %attend_back.3 = (bf16[1024,576]{1,0:T(8,128)(2,1)S(1)}, bf16[1024,576]{1,0:T(8,128)(2,1)S(1)}, f32[1,576]{1,0:T(1,128)S(1)}, f32[1,576]{1,0:T(1,128)S(1)}) custom-call(s32[2]{0:T(128)S(1)} %fusion.8.lens.n, bf16[1024,576]{1,0:T(8,128)(2,1)S(1)} %copy-done.7, bf16[1024,576]{1,0:T(8,128)(2,1)S(1)} %copy-done.9, ...), custom_call_target="tpu_custom_call" | custom-call | tf_op jit(solution)/shard_map/attend_back/pallas_call | solution.py:60
  210.3 4.0 %weight_grads.14 = (bf16[768,384]{1,0:T(8,128)(2,1)}, bf16[768,384]{1,0:T(8,128)(2,1)S(1)}) custom-call(bf16[1024,768]{1,0:T(8,128)(2,1)} %copy-done.75, bf16[1024,768]{1,0:T(8,128)(2,1)S(1)} %copy-done.1, bf16[1024,576]{1,0:T(8,128)(2,1)S(1)} %get-tuple-element.411.refs_2_.refs_1_, bf16[1024,192]{1,0:T(8,128)(2,1)S(1)} %copy-done.27), custom_call_target="tpu_custom_call" | custom-call | tf_op jit(solution)/shard_map/weight_grads/pallas_call | solution.py:60
  217.4 9.3 %down_out.1 = (bf16[2,128,768]{2,1,0:T(8,128)(2,1)}, bf16[2,128,768]{2,1,0:T(8,128)(2,1)}, bf16[2,2,128,768]{3,2,1,0:T(8,128)(2,1)S(1)}) custom-call(s32[1]{0:T(128)} %bitcast.17.at, f32[1024,768]{1,0:T(8,128)} %copy-done.5, bf16[1024,768]{1,0:T(8,128)(2,1)S(1)} %copy-done.10, bf16[1024,768]{1,0:T(8,128)(2,1)} %get-tuple-element.335.refs_1_, ...), custom_call_target="tpu_custom_call" | custom-call | tf_op jit(solution)/shard_map/down_out/pallas_call | solution.py:60
  228.6 3.9 %weight_grads.15 = (bf16[1,384,768]{2,1,0:T(8,128)(2,1)S(1)}, bf16[1,384,768]{2,1,0:T(8,128)(2,1)S(1)}) custom-call(s32[1]{0:T(128)} %bitcast.25.at.refs_0_, bf16[1024,768]{1,0:T(8,128)(2,1)} %copy-done.75, bf16[1024,768]{1,0:T(8,128)(2,1)} %get-tuple-element.384.refs_2_.refs_1_, bf16[1024,576]{1,0:T(8,128)(2,1)S(1)} %get-tuple-element.399.refs_3_.refs_0_, ...), custom_call_target="tpu_custom_call" | custom-call | tf_op jit(solution)/shard_map/weight_grads/pallas_call | solution.py:60
  235.4 11.7 %norm_one_back.1 = (bf16[2,128,768]{2,1,0:T(8,128)(2,1)S(1)}, bf16[2,128,768]{2,1,0:T(8,128)(2,1)S(1)}, bf16[2,2,128,768]{3,2,1,0:T(8,128)(2,1)S(1)}, f32[1,768]{1,0:T(1,128)S(1)}, f32[1,768]{1,0:T(1,128)S(1)}) custom-call(s32[1]{0:T(128)} %bitcast.17.at, bf16[1024,768]{1,0:T(8,128)(2,1)} %copy-done.11, f32[1024,768]{1,0:T(8,128)} %get-tuple-element.424.dres_ref, ...), custom_call_target="tpu_custom_call" | custom-call | tf_op jit(solution)/shard_map/norm_one_back/pallas_call | solution.py:60
  249.3 14.5 %conditional.4 = (f32[14,768]{1,0:T(8,128)S(1)}, bf16[1,96,768]{2,1,0:T(8,128)(2,1)S(1)}, bf16[1,96,768]{2,1,0:T(8,128)(2,1)}, bf16[2,96,768]{2,1,0:T(8,128)(2,1)}, bf16[2,96,768]{2,1,0:T(8,128)(2,1)}) conditional(s32[]{:T(128)} %bitcast.16, () %tuple.119, (f32[14,768]{1,0:T(8,128)S(1)}, s32[]{:T(128)}, bf16[1,384,768]{2,1,0:T(8,128)(2,1)S(1)}, ...), branch_computations={%region_5.6_spmd, %region_6.7_spmd} | conditional | flops 32256 | bytes 2672880 | solution.py:775
  253.3 3.3 %collective-permute-done.5 = f32[14,768]{1,0:T(8,128)S(1)} collective-permute-done((f32[14,768]{1,0:T(8,128)S(1)}, f32[14,768]{1,0:T(8,128)S(1)}, u32[]{:S(2)}, u32[]{:S(2)}) %collective-permute-start.5) | collective-permute-done | bytes 43040 | tf_op jit(solution)/shard_map/cond/branch_1_fun/ppermute | solution.py:650
  258.2 5.6 %collective-permute-done.6 = f32[14,768]{1,0:T(8,128)S(1)} collective-permute-done((f32[14,768]{1,0:T(8,128)S(1)}, f32[14,768]{1,0:T(8,128)S(1)}, u32[]{:S(2)}, u32[]{:S(2)}) %collective-permute-start.6) | collective-permute-done | bytes 43040 | tf_op jit(solution)/shard_map/cond/branch_1_fun/ppermute | solution.py:650
  268.0 17.5 %conditional.5 = (bf16[8,128,768]{2,1,0:T(8,128)(2,1)}, f32[768]{0:T(1024)S(1)}, f32[768]{0:T(1024)S(1)}, f32[768]{0:T(1024)S(1)}, f32[768]{0:T(1024)S(1)}, /*in...) conditional(s32[]{:T(128)} %bitcast.16, () %tuple.118, ...), branch_computations={%region_7.8_spmd, %region_8.9_spmd} | conditional | flops 574472 | bytes 6746484 | solution.py:775
  269.8 3.3 %collective-permute-done.9 = f32[14,768]{1,0:T(8,128)S(1)} collective-permute-done((f32[14,768]{1,0:T(8,128)S(1)}, f32[14,768]{1,0:T(8,128)S(1)}, u32[]{:S(2)}, u32[]{:S(2)}) %collective-permute-start.9) | collective-permute-done | bytes 43040 | tf_op jit(solution)/shard_map/cond/branch_1_fun/ppermute | solution.py:650
  279.4 3.1 %join_rows.2 = bf16[8,128,768]{2,1,0:T(8,128)(2,1)} custom-call(s32[1]{0:T(128)} %bitcast.6.at, s32[8]{0:T(128)S(1)} %get-tuple-element.75.text_at, bf16[2,128,768]{2,1,0:T(8,128)(2,1)S(1)} %copy-done.88, bf16[2,128,768]{2,1,0:T(8,128)(2,1)} %get-tuple-element.88.refs_1_, bf16[2,2,128,768]{3,2,1,0:T(8,128)(2,1)} %get-tuple-element.89.refs_2_, ...), custom_call_target="tpu_custom_call" | custom-call | tf_op jit(solution)/shard_map/cond/branch_1_fun/join_rows/pallas_call | solution.py:60
  (399 shorter events, 113.3 us)
Async XLA Ops:
  6.1 14.1 %collective-permute-start.17 = (bf16[2,128,768]{2,1,0:T(8,128)(2,1)}, bf16[2,128,768]{2,1,0:T(8,128)(2,1)}, u32[]{:S(2)}, u32[]{:S(2)}) collective-permute-start(bf16[2,128,768]{2,1,0:T(8,128)(2,1)} %get-tuple-element.296), channel_id=1, source_target_pairs={{0,3},{1,2},{2,1},{3,0},{4,7},{5,6},{6,5},{7,4},{8,11},{9,10},{10,... | collective-permute-start | bytes 1179656 | tf_op jit(solution)/shard_map/ppermute | solution.py:647
  8.8 23.2 %collective-permute-start.16 = (bf16[2,128,768]{2,1,0:T(8,128)(2,1)}, bf16[2,128,768]{2,1,0:T(8,128)(2,1)}, u32[]{:S(2)}, u32[]{:S(2)}) collective-permute-start(bf16[2,128,768]{2,1,0:T(8,128)(2,1)} %get-tuple-element.295), channel_id=1, source_target_pairs={{0,2},{1,3},{2,0},{3,1},{4,6},{5,7},{6,4},{7,5},{8,10},{9,11},{10,... | collective-permute-start | bytes 1179656 | tf_op jit(solution)/shard_map/ppermute | solution.py:647
  9.6 20.0 %collective-permute-start.14 = (bf16[384,576]{1,0:T(8,128)(2,1)S(1)}, bf16[384,576]{1,0:T(8,128)(2,1)S(1)}, u32[]{:S(2)}, u32[]{:S(2)}) collective-permute-start(bf16[384,576]{1,0:T(8,128)(2,1)S(1)} %get-tuple-element.308.refs_0_.refs_4_), channel_id=1, source_target_pairs={{0,1},{1,0},{2,3},{3,2},{4,5},{5,4},{6,7},{7,6},{8,9},{9,8},{10,11... | collective-permute-start | bytes 1327112 | tf_op jit(solution)/shard_map/ppermute | solution.py:647
  9.8 20.0 %collective-permute-start.15 = (bf16[384,576]{1,0:T(8,128)(2,1)S(1)}, bf16[384,576]{1,0:T(8,128)(2,1)S(1)}, u32[]{:S(2)}, u32[]{:S(2)}) collective-permute-start(bf16[384,576]{1,0:T(8,128)(2,1)S(1)} %get-tuple-element.315.refs_1_.refs_5_), channel_id=1, source_target_pairs={{0,1},{1,0},{2,3},{3,2},{4,5},{5,4},{6,7},{7,6},{8,9},{9,8},{10,11... | collective-permute-start | bytes 1327112 | tf_op jit(solution)/shard_map/ppermute | solution.py:647
  14.8 12.6 %collective-permute-start.21 = (f32[2,1152]{1,0:T(2,128)S(1)}, f32[2,1152]{1,0:T(2,128)S(1)}, u32[]{:S(2)}, u32[]{:S(2)}) collective-permute-start(f32[2,1152]{1,0:T(2,128)S(1)} %pad_maximum_fusion.6), channel_id=1, source_target_pairs={{0,2},{1,3},{2,0},{3,1},{4,6},{5,7},{6,4},{7,5},{8,10},{9,11},{10,... | collective-permute-start | bytes 27656 | tf_op jit(solution)/shard_map/ppermute | solution.py:647
  20.2 27.2 %collective-permute-start.20 = (bf16[384,576]{1,0:T(8,128)(2,1)S(1)}, bf16[384,576]{1,0:T(8,128)(2,1)S(1)}, u32[]{:S(2)}, u32[]{:S(2)}) collective-permute-start(bf16[384,576]{1,0:T(8,128)(2,1)S(1)} %get-tuple-element.315.refs_1_.refs_5_), channel_id=1, source_target_pairs={{0,2},{1,3},{2,0},{3,1},{4,6},{5,7},{6,4},{7,5},{8,10},{9,11},{10,... | collective-permute-start | bytes 1327112 | tf_op jit(solution)/shard_map/ppermute | solution.py:647
  27.5 21.1 %collective-permute-start.18 = (bf16[384,576]{1,0:T(8,128)(2,1)S(1)}, bf16[384,576]{1,0:T(8,128)(2,1)S(1)}, u32[]{:S(2)}, u32[]{:S(2)}) collective-permute-start(bf16[384,576]{1,0:T(8,128)(2,1)S(1)} %get-tuple-element.308.refs_0_.refs_4_), channel_id=1, source_target_pairs={{0,2},{1,3},{2,0},{3,1},{4,6},{5,7},{6,4},{7,5},{8,10},{9,11},{10,... | collective-permute-start | bytes 1327112 | tf_op jit(solution)/shard_map/ppermute | solution.py:647
  29.8 39.3 %collective-permute-start.22 = (bf16[576,768]{1,0:T(8,128)(2,1)}, bf16[576,768]{1,0:T(8,128)(2,1)}, u32[]{:S(2)}, u32[]{:S(2)}) collective-permute-start(bf16[576,768]{1,0:T(8,128)(2,1)} %pad_maximum_fusion.1), channel_id=1, source_target_pairs={{0,2},{1,3},{2,0},{3,1},{4,6},{5,7},{6,4},{7,5},{8,10},{9,11},{10,... | collective-permute-start | bytes 2654216 | tf_op jit(solution)/shard_map/ppermute | solution.py:647
  55.4 31.5 %collective-permute-start.25 = (bf16[384,768]{1,0:T(8,128)(2,1)}, bf16[384,768]{1,0:T(8,128)(2,1)S(1)}, u32[]{:S(2)}, u32[]{:S(2)}) collective-permute-start(bf16[384,768]{1,0:T(8,128)(2,1)} %get-tuple-element.337), channel_id=1, source_target_pairs={{0,2},{1,3},{2,0},{3,1},{4,6},{5,7},{6,4},{7,5},{8,10},{9,11},{10,... | collective-permute-start | bytes 1769480 | tf_op jit(solution)/shard_map/ppermute | solution.py:647
  70.2 26.9 %collective-permute-start.28 = (bf16[2,2,128,768]{3,2,1,0:T(8,128)(2,1)}, bf16[2,2,128,768]{3,2,1,0:T(8,128)(2,1)}, u32[]{:S(2)}, u32[]{:S(2)}) collective-permute-start(bf16[2,2,128,768]{3,2,1,0:T(8,128)(2,1)} %get-tuple-element.344), channel_id=1, source_target_pairs={{0,2},{1,3},{2,0},{3,1},{4,6},{5,7},{6,4},{7,5},{8,10},{9,11},{10,... | collective-permute-start | bytes 2359304 | tf_op jit(solution)/shard_map/ppermute | solution.py:647
  73.9 48.1 %collective-permute-start.34 = (bf16[768,768]{1,0:T(8,128)(2,1)}, bf16[768,768]{1,0:T(8,128)(2,1)S(1)}, u32[]{:S(2)}, u32[]{:S(2)}) collective-permute-start(bf16[768,768]{1,0:T(8,128)(2,1)} %refs_4_.3), channel_id=1, source_target_pairs={{0,2},{1,3},{2,0},{3,1},{4,6},{5,7},{6,4},{7,5},{8,10},{9,11},{10,... | collective-permute-start | bytes 3538952 | tf_op jit(solution)/shard_map/ppermute | solution.py:647
  75.2 23.5 %collective-permute-start.24 = (bf16[384,768]{1,0:T(8,128)(2,1)S(1)}, bf16[384,768]{1,0:T(8,128)(2,1)S(1)}, u32[]{:S(2)}, u32[]{:S(2)}) collective-permute-start(bf16[384,768]{1,0:T(8,128)(2,1)S(1)} %slice.126.refs_0_), channel_id=1, source_target_pairs={{0,1},{1,0},{2,3},{3,2},{4,5},{5,4},{6,7},{7,6},{8,9},{9,8},{10,11... | collective-permute-start | bytes 1769480 | tf_op jit(solution)/shard_map/ppermute | solution.py:647
  86.9 11.9 %collective-permute-start.26 = (bf16[384,768]{1,0:T(8,128)(2,1)S(1)}, bf16[384,768]{1,0:T(8,128)(2,1)S(1)}, u32[]{:S(2)}, u32[]{:S(2)}) collective-permute-start(bf16[384,768]{1,0:T(8,128)(2,1)S(1)} %collective-permute-done.25.refs_1_), channel_id=1, source_target_pairs={{0,1},{1,0},{2,3},{3,2},{4,5},{5,4},{6,7},{7,6},{8,9},{9,8},{10,11... | collective-permute-start | bytes 1769480 | tf_op jit(solution)/shard_map/ppermute | solution.py:647
  122.1 13.4 %collective-permute-start.35 = (bf16[768,768]{1,0:T(8,128)(2,1)S(1)}, bf16[768,768]{1,0:T(8,128)(2,1)S(1)}, u32[]{:S(2)}, u32[]{:S(2)}) collective-permute-start(bf16[768,768]{1,0:T(8,128)(2,1)S(1)} %collective-permute-done.34.refs_4_.refs_6_), channel_id=1, source_target_pairs={{0,1},{1,0},{2,3},{3,2},{4,5},{5,4},{6,7},{7,6},{8,9},{9,8},{10,11... | collective-permute-start | bytes 3538952 | tf_op jit(solution)/shard_map/ppermute | solution.py:647
  122.1 31.6 %collective-permute-start.36 = (bf16[1,768,768]{2,1,0:T(8,128)(2,1)}, bf16[1,768,768]{2,1,0:T(8,128)(2,1)}, u32[]{:S(2)}, u32[]{:S(2)}) collective-permute-start(bf16[1,768,768]{2,1,0:T(8,128)(2,1)} %get-tuple-element.374), channel_id=1, source_target_pairs={{0,2},{1,3},{2,0},{3,1},{4,6},{5,7},{6,4},{7,5},{8,10},{9,11},{10,... | collective-permute-start | bytes 3538952 | tf_op jit(solution)/shard_map/ppermute | solution.py:647
  164.8 42.9 %collective-permute-start.44 = (bf16[1,768,768]{2,1,0:T(8,128)(2,1)}, bf16[1,768,768]{2,1,0:T(8,128)(2,1)}, u32[]{:S(2)}, u32[]{:S(2)}) collective-permute-start(bf16[1,768,768]{2,1,0:T(8,128)(2,1)} %get-tuple-element.401), channel_id=1, source_target_pairs={{0,2},{1,3},{2,0},{3,1},{4,6},{5,7},{6,4},{7,5},{8,10},{9,11},{10,... | collective-permute-start | bytes 3538952 | tf_op jit(solution)/shard_map/ppermute | solution.py:647
  165.3 16.1 %collective-permute-start.41 = (bf16[4,96,768]{2,1,0:T(8,128)(2,1)}, bf16[4,96,768]{2,1,0:T(8,128)(2,1)S(1)}, u32[]{:S(2)}, u32[]{:S(2)}) collective-permute-start(bf16[4,96,768]{2,1,0:T(8,128)(2,1)} %get-tuple-element.376), channel_id=1, source_target_pairs={{0,4},{4,0},{8,12},{12,8},{16,20},{20,16},{24,28},{28,24},{1,5},{5... | collective-permute-start | bytes 1769480 | tf_op jit(solution)/shard_map/ppermute | solution.py:650
  191.7 36.9 %collective-permute-start.50 = (bf16[1,768,768]{2,1,0:T(8,128)(2,1)}, bf16[1,768,768]{2,1,0:T(8,128)(2,1)S(1)}, u32[]{:S(2)}, u32[]{:S(2)}) collective-permute-start(bf16[1,768,768]{2,1,0:T(8,128)(2,1)} %weight_grads.13), channel_id=1, source_target_pairs={{0,2},{1,3},{2,0},{3,1},{4,6},{5,7},{6,4},{7,5},{8,10},{9,11},{10,... | collective-permute-start | bytes 3538952 | tf_op jit(solution)/shard_map/ppermute | solution.py:647
  194.3 15.8 %collective-permute-start.45 = (bf16[2,96,768]{2,1,0:T(8,128)(2,1)}, bf16[2,96,768]{2,1,0:T(8,128)(2,1)S(1)}, u32[]{:S(2)}, u32[]{:S(2)}) collective-permute-start(bf16[2,96,768]{2,1,0:T(8,128)(2,1)} %get-tuple-element.393), channel_id=1, source_target_pairs={{0,8},{4,12},{8,0},{12,4},{16,24},{20,28},{24,16},{28,20},{1,9},{5... | collective-permute-start | bytes 884744 | tf_op jit(solution)/shard_map/ppermute | solution.py:650
  210.0 18.3 %collective-permute-start.47 = (bf16[4,96,768]{2,1,0:T(8,128)(2,1)S(1)}, bf16[4,96,768]{2,1,0:T(8,128)(2,1)S(1)}, u32[]{:S(2)}, u32[]{:S(2)}) collective-permute-start(bf16[4,96,768]{2,1,0:T(8,128)(2,1)S(1)} %get-tuple-element.405), channel_id=1, source_target_pairs={{0,4},{4,0},{8,12},{12,8},{16,20},{20,16},{24,28},{28,24},{1,5},{5... | collective-permute-start | bytes 1769480 | tf_op jit(solution)/shard_map/ppermute | solution.py:650
  214.2 14.4 %collective-permute-start.48 = (bf16[768,384]{1,0:T(8,128)(2,1)}, bf16[768,384]{1,0:T(8,128)(2,1)S(1)}, u32[]{:S(2)}, u32[]{:S(2)}) collective-permute-start(bf16[768,384]{1,0:T(8,128)(2,1)} %get-tuple-element.412), channel_id=1, source_target_pairs={{0,1},{1,0},{2,3},{3,2},{4,5},{5,4},{6,7},{7,6},{8,9},{9,8},{10,11... | collective-permute-start | bytes 1769480 | tf_op jit(solution)/shard_map/ppermute | solution.py:647
  214.3 14.3 %collective-permute-start.49 = (bf16[768,384]{1,0:T(8,128)(2,1)S(1)}, bf16[768,384]{1,0:T(8,128)(2,1)S(1)}, u32[]{:S(2)}, u32[]{:S(2)}) collective-permute-start(bf16[768,384]{1,0:T(8,128)(2,1)S(1)} %get-tuple-element.420), channel_id=1, source_target_pairs={{0,1},{1,0},{2,3},{3,2},{4,5},{5,4},{6,7},{7,6},{8,9},{9,8},{10,11... | collective-permute-start | bytes 1769480 | tf_op jit(solution)/shard_map/ppermute | solution.py:647
  214.7 12.0 %collective-permute-start.46 = (bf16[1,96,768]{2,1,0:T(8,128)(2,1)S(1)}, bf16[1,96,768]{2,1,0:T(8,128)(2,1)S(1)}, u32[]{:S(2)}, u32[]{:S(2)}) collective-permute-start(bf16[1,96,768]{2,1,0:T(8,128)(2,1)S(1)} %get-tuple-element.409), channel_id=1, source_target_pairs={{0,16},{4,20},{8,24},{12,28},{16,0},{20,4},{24,8},{28,12},{1,17},{... | collective-permute-start | bytes 442376 | tf_op jit(solution)/shard_map/ppermute | solution.py:650
  226.7 21.6 %collective-permute-start.54 = (bf16[2,2,128,768]{3,2,1,0:T(8,128)(2,1)S(1)}, bf16[2,2,128,768]{3,2,1,0:T(8,128)(2,1)S(1)}, u32[]{:S(2)}, u32[]{:S(2)}) collective-permute-start(bf16[2,2,128,768]{3,2,1,0:T(8,128)(2,1)S(1)} %get-tuple-element.455), channel_id=1, source_target_pairs={{0,2},{1,3},{2,0},{3,1},{4,6},{5,7},{6,4},{7,5},{8,10},{9,11},{10,... | collective-permute-start | bytes 2359304 | tf_op jit(solution)/shard_map/ppermute | solution.py:647
  232.6 16.6 %collective-permute-start.51 = (bf16[1,384,768]{2,1,0:T(8,128)(2,1)S(1)}, bf16[1,384,768]{2,1,0:T(8,128)(2,1)S(1)}, u32[]{:S(2)}, u32[]{:S(2)}) collective-permute-start(bf16[1,384,768]{2,1,0:T(8,128)(2,1)S(1)} %get-tuple-element.422), channel_id=1, source_target_pairs={{0,4},{4,0},{8,12},{12,8},{16,20},{20,16},{24,28},{28,24},{1,5},{5... | collective-permute-start | bytes 1769480 | tf_op jit(solution)/shard_map/ppermute | solution.py:650
  234.3 14.8 %collective-permute-start.52 = (bf16[2,96,768]{2,1,0:T(8,128)(2,1)S(1)}, bf16[2,96,768]{2,1,0:T(8,128)(2,1)S(1)}, u32[]{:S(2)}, u32[]{:S(2)}) collective-permute-start(bf16[2,96,768]{2,1,0:T(8,128)(2,1)S(1)} %get-tuple-element.418), channel_id=1, source_target_pairs={{0,8},{4,12},{8,0},{12,4},{16,24},{20,28},{24,16},{28,20},{1,9},{5... | collective-permute-start | bytes 884744 | tf_op jit(solution)/shard_map/ppermute | solution.py:650
  247.1 18.4 %collective-permute-start.57 = (bf16[2,2,128,768]{3,2,1,0:T(8,128)(2,1)S(1)}, bf16[2,2,128,768]{3,2,1,0:T(8,128)(2,1)S(1)}, u32[]{:S(2)}, u32[]{:S(2)}) collective-permute-start(bf16[2,2,128,768]{3,2,1,0:T(8,128)(2,1)S(1)} %get-tuple-element.463), channel_id=1, source_target_pairs={{0,2},{1,3},{2,0},{3,1},{4,6},{5,7},{6,4},{7,5},{8,10},{9,11},{10,... | collective-permute-start | bytes 2359304 | tf_op jit(solution)/shard_map/ppermute | solution.py:647
  248.3 19.7 %collective-permute-start.53 = (bf16[2,128,768]{2,1,0:T(8,128)(2,1)}, bf16[2,128,768]{2,1,0:T(8,128)(2,1)}, u32[]{:S(2)}, u32[]{:S(2)}) collective-permute-start(bf16[2,128,768]{2,1,0:T(8,128)(2,1)} %get-tuple-element.453), channel_id=1, source_target_pairs={{0,1},{1,0},{2,3},{3,2},{4,5},{5,4},{6,7},{7,6},{8,9},{9,8},{10,11... | collective-permute-start | bytes 1179656 | tf_op jit(solution)/shard_map/ppermute | solution.py:647
  250.2 13.6 %collective-permute-start.8 = (bf16[2,96,768]{2,1,0:T(8,128)(2,1)S(1)}, bf16[2,96,768]{2,1,0:T(8,128)(2,1)}, u32[]{:S(2)}, u32[]{:S(2)}) collective-permute-start(bf16[2,96,768]{2,1,0:T(8,128)(2,1)S(1)} %get-tuple-element.66), channel_id=1, source_target_pairs={{0,8},{4,12},{8,0},{12,4},{16,24},{20,28},{24,16},{28,20},{1,9},{5... | collective-permute-start | bytes 884744 | tf_op jit(solution)/shard_map/cond/branch_1_fun/ppermute | solution.py:650
  251.0 12.9 %collective-permute-start.7 = (bf16[1,96,768]{2,1,0:T(8,128)(2,1)S(1)}, bf16[1,96,768]{2,1,0:T(8,128)(2,1)}, u32[]{:S(2)}, u32[]{:S(2)}) collective-permute-start(bf16[1,96,768]{2,1,0:T(8,128)(2,1)S(1)} %get-tuple-element.62), channel_id=1, source_target_pairs={{0,16},{4,20},{8,24},{12,28},{16,0},{20,4},{24,8},{28,12},{1,17},{... | collective-permute-start | bytes 442376 | tf_op jit(solution)/shard_map/cond/branch_1_fun/ppermute | solution.py:650
  264.0 21.5 %collective-permute-start.56 = (bf16[2,128,768]{2,1,0:T(8,128)(2,1)S(1)}, bf16[2,128,768]{2,1,0:T(8,128)(2,1)S(1)}, u32[]{:S(2)}, u32[]{:S(2)}) collective-permute-start(bf16[2,128,768]{2,1,0:T(8,128)(2,1)S(1)} %copy-done.65), channel_id=1, source_target_pairs={{0,1},{1,0},{2,3},{3,2},{4,5},{5,4},{6,7},{7,6},{8,9},{9,8},{10,11... | collective-permute-start | bytes 1179656 | tf_op jit(solution)/shard_map/ppermute | solution.py:647
  266.3 19.2 %collective-permute-start.58 = (bf16[2,128,768]{2,1,0:T(8,128)(2,1)}, bf16[2,128,768]{2,1,0:T(8,128)(2,1)S(1)}, u32[]{:S(2)}, u32[]{:S(2)}) collective-permute-start(bf16[2,128,768]{2,1,0:T(8,128)(2,1)} %dynamic-slice_bitcast_fusion), channel_id=1, source_target_pairs={{0,1},{1,0},{2,3},{3,2},{4,5},{5,4},{6,7},{7,6},{8,9},{9,8},{10,11... | collective-permute-start | bytes 1179656 | tf_op jit(solution)/shard_map/ppermute | solution.py:647
  (135 other events, 933.7 us)
